TPU v7x, 32 devices: a whole 2x2x4 slice. The times are simulated.
32 devices in a mesh: rows: 16 (over z, y, x), cols: 2 (over core).
Axes of the slice: x: 2, y: 2, z: 4, core: 2. Of those that a mesh axis runs over, the one named last changes fastest.
Arguments:
- sketch: bfloat16 [131072, 256], P(('rows', 'cols')), may hold values from -6 to 6
- blocks: bfloat16 [256, 256, 256], P(('rows', 'cols')), may hold values from -0.375 to 0.375
- block_rows: int32 [256], P(('rows', 'cols')), may hold values from 0 to 3, as said below
- block_cols: int32 [256], P(('rows', 'cols')), may hold values from 0 to 255
- counts: int32 [32], P(('rows', 'cols')), may hold values from 1 to 8, as said below
Outputs:
- basis: float32 [16384, 256], P(('rows', 'cols'))
- factor: float32 [256, 256], replicated
Inputs may be any that keep to these rules, and one draw needn't show every extreme that they name: Within one device's 8 slots the pairs (block_rows, block_cols) are distinct. `counts`: some device has exactly 8 live slots.
All inputs are finite; a program needn't handle non-finite values.
Results may differ from a plain program's by a relative error of at most 0.0003.
Values may be sent and summed in bfloat16 or wider, within the bound.
No kernel may reach another device: no remote copies, remote signals or barrier semaphores. Data moves between devices by JAX's collectives and lax.ppermute only.
A program may use at most 64 MiB of HBM per device.

v0:
```python
import jax
import jax.numpy as jnp
from jax import lax
from jax.sharding import PartitionSpec as P

RB = 4


def local(sketch, blocks, block_rows, block_cols, counts):
    highest = lax.Precision.HIGHEST
    slots, width, _ = blocks.shape
    columns = sketch.shape[1]
    live_count = counts[0]
    starts = block_cols * width
    panel = lax.all_gather(sketch, "rows", axis=0, tiled=True)
    chosen = jax.vmap(lambda offset: lax.dynamic_slice_in_dim(panel, offset, width, 0))(starts)
    products = jnp.einsum("bij,bjk->bik", blocks, chosen, preferred_element_type=jnp.float32)
    selector = (
        (block_rows[:, None] == jnp.arange(RB, dtype=jnp.int32)[None, :])
        & (jnp.arange(slots, dtype=jnp.int32) < live_count)[:, None]
    ).astype(jnp.float32)
    partial_rows = jnp.einsum("br,bik->rik", selector, products, precision=highest)
    partial_rows = partial_rows.reshape(RB * width, columns)
    total_rows = RB * width * lax.axis_size("rows")
    slab_total = lax.psum(partial_rows, "cols")
    gram_matrix = lax.psum(jnp.dot(slab_total.T, slab_total, precision=highest), "rows")
    share_rows = slab_total.shape[0] // lax.axis_size("cols")
    own_rows = lax.dynamic_slice_in_dim(
        slab_total, lax.axis_index("cols") * share_rows, share_rows, 0
    )
    lower_factor = jnp.linalg.cholesky(gram_matrix)
    root_rows = jnp.sqrt(jnp.float32(total_rows))
    solved = lax.linalg.triangular_solve(
        lower_factor, own_rows, left_side=False, lower=True, transpose_a=True
    )
    return (solved * root_rows, lower_factor.T / root_rows)


def solution(mesh):
    in_specs = (
        P(("rows", "cols"), None),
        P(("rows", "cols"), None, None),
        P(("rows", "cols")),
        P(("rows", "cols")),
        P(("rows", "cols")),
    )
    out_specs = (P(("rows", "cols"), None), P())
    return jax.shard_map(local, mesh=mesh, in_specs=in_specs, out_specs=out_specs, check_vma=False)
```

profile of v0, /device:TPU:0, one launch (start us, length us, event | category | flops | bytes accessed | tf_op | source)
XLA Modules:
  0.0 591.6 jit_solution(11298626235763234377)
XLA Ops:
  7.2 0.0 copy-start
  7.2 0.0 copy-start.3
  7.2 0.0 all-gather.2.cloned.1.call-start
  7.2 0.7 all-gather.2.cloned.1.call-update
  7.9 0.0 all-reduce.5.cloned.1.call-start
  8.0 0.0 copy-done.3
  8.7 355.7 %all-gather.2.cloned.1.call-done = bf16[65536,256]{1,0:T(8,128)(2,1)} async-done(((bf16[4096,256]{1,0:T(8,128)(2,1)}), bf16[65536,256]{1,0:T(8,128)(2,1)}) %all-gather.2.cloned.1.call-update) | async-done | bytes 33554448 | tf_op jit(solution)/shard_map/all_gather | solution.py:15
  364.4 16.8 %while.2 = (s32[]{:T(128)}, bf16[65536,256]{1,0:T(8,128)(2,1)}, s32[8,2]{0,1:T(2,128)S(1)}, bf16[8,256,256]{2,1,0:T(8,128)(2,1)S(1)}, s32[]{:T(128)}) while((s32[]{:T(128)}, bf16[65536,256]{1,0:T(8,128)(2,1)}, s32[8,2]{0,1:T(2,128)S(1)}, bf16[8,256,256]{2,1,0:T(8,128)(2,1)S(1)}, s32[]{:T(128)}) %tuple.41), condition=%wide.while_cond, body=%wide.while_body.sunk | while | flops 2 | bytes 262241 | solution.py:16
  364.4 0.1 constant_dynamic-slice_fusion.4
  364.5 0.5 slice.69
  365.0 1.5 bitcast_dynamic-update-slice_fusion.4
  366.5 0.1 constant_dynamic-slice_fusion.4
  366.6 0.5 slice.69
  367.1 1.5 bitcast_dynamic-update-slice_fusion.4
  368.6 0.1 constant_dynamic-slice_fusion.4
  368.7 0.5 slice.69
  369.2 1.5 bitcast_dynamic-update-slice_fusion.4
  370.7 0.1 constant_dynamic-slice_fusion.4
  370.8 0.5 slice.69
  371.3 1.5 bitcast_dynamic-update-slice_fusion.4
  372.8 0.1 constant_dynamic-slice_fusion.4
  372.9 0.5 slice.69
  373.4 1.5 bitcast_dynamic-update-slice_fusion.4
  374.9 0.1 constant_dynamic-slice_fusion.4
  375.0 0.5 slice.69
  375.5 1.5 bitcast_dynamic-update-slice_fusion.4
  377.0 0.1 constant_dynamic-slice_fusion.4
  377.1 0.5 slice.69
  377.6 1.5 bitcast_dynamic-update-slice_fusion.4
  379.1 0.1 constant_dynamic-slice_fusion.4
  379.2 0.5 slice.69
  379.7 1.5 bitcast_dynamic-update-slice_fusion.4
  381.2 0.0 copy-done
  381.2 1.8 fusion.19
  383.0 2.2 copy.16
  385.3 1.1 fusion
  386.4 1.2 copy.11
  387.6 0.0 all-reduce.5.cloned.1.call-update
  387.6 0.2 all-reduce.7.cloned.1.call-start
  387.8 17.7 %all-reduce.5.cloned.1.call-done = f32[1024,256]{1,0:T(8,128)} async-done(((f32[1024,256]{1,0:T(8,128)}), f32[1024,256]{1,0:T(8,128)}) %all-reduce.5.cloned.1.call-update) | async-done | bytes 1048592 | tf_op jit(solution)/shard_map/psum | solution.py:25
  405.5 4.1 fusion.20
  409.6 0.0 all-reduce.7.cloned.1.call-update
  409.7 110.4 %all-reduce.7.cloned.1.call-done = f32[256,256]{0,1:T(8,128)} async-done(((f32[256,256]{0,1:T(8,128)}), f32[256,256]{0,1:T(8,128)}) %all-reduce.7.cloned.1.call-update) | async-done | bytes 262160 | tf_op jit(solution)/shard_map/psum | solution.py:26
  520.1 1.1 copy.13
  521.2 1.0 fusion.4
  522.2 11.7 %cholesky.50 = f32[128,128]{1,0:T(8,128)S(1)} custom-call(f32[128,128]{1,0:T(8,128)S(1)} %cholesky.118), custom_call_target="Cholesky" | custom-call | tf_op jit(solution)/shard_map/jit(cholesky)/cholesky | solution.py:31
  533.9 9.8 %custom-call.14 = f32[1,128,128]{1,2,0:T(8,128)S(1)} custom-call(f32[1,128,128]{2,1,0:T(8,128)S(1)} %get-tuple-element.45), custom_call_target="InvertDiagBlocksLowerTriangular" | custom-call | tf_op jit(solution)/shard_map/jit(cholesky)/cholesky | solution.py:31
  543.8 0.2 constant_dynamic-update-slice_fusion.1
  544.0 0.3 convolution_subtract_fusion.1
  544.3 11.7 %cholesky.105 = f32[128,128]{1,0:T(8,128)S(1)} custom-call(f32[128,128]{1,0:T(8,128)S(1)} %convolution_subtract_fusion.1), custom_call_target="Cholesky" | custom-call | tf_op jit(solution)/shard_map/jit(cholesky)/cholesky | solution.py:31
  556.0 0.8 compare_reduce_fusion
  558.1 0.1 triangular_solve.58
  558.2 3.8 while.3
  558.2 0.6 fusion.30
  558.8 1.3 bitcast_dynamic-update-slice_fusion.5
  560.1 0.6 fusion.30
  560.7 1.3 bitcast_dynamic-update-slice_fusion.5
  562.0 19.7 %custom-call.15 = f32[2,128,128]{1,2,0:T(8,128)S(1)} custom-call(f32[2,128,128]{2,1,0:T(8,128)S(1)} %get-tuple-element.17), custom_call_target="InvertDiagBlocksLowerTriangular" | custom-call | tf_op jit(solution)/shard_map/triangular_solve | solution.py:33
  581.7 0.0 copy-done.1
  581.7 0.4 fusion.2
  582.1 0.6 convolution_subtract_fusion
  582.8 0.4 fusion.6
  583.2 1.0 copy.14
  584.2 0.8 copy.15
  (17 shorter events, 0.2 us)
Async XLA Ops:
  7.2 374.0 %copy-start = (bf16[8,256,256]{2,1,0:T(8,128)(2,1)S(1)}, bf16[8,256,256]{2,1,0:T(8,128)(2,1)}, u32[]{:S(2)}) copy-start(bf16[8,256,256]{2,1,0:T(8,128)(2,1)} %param.6) | copy-start | bytes 3145732
  7.2 0.8 copy-start.3
  7.2 357.2 %all-gather.2.cloned.1.call-start = ((), (), s32[]{:S(2)}) async-start(), calls=%async_computation | async-start | bytes 35651584 | tf_op jit(solution)/shard_map/all_gather | solution.py:15
  7.9 397.6 %all-reduce.5.cloned.1.call-start = ((), (), s32[]{:S(2)}) async-start(), calls=%async_computation.1 | async-start | bytes 2097152 | tf_op jit(solution)/shard_map/psum | solution.py:25
  383.0 2.2 copy-start.2
  387.6 132.5 %all-reduce.7.cloned.1.call-start = ((), (), s32[]{:S(2)}) async-start(), calls=%async_computation.2 | async-start | bytes 524288 | tf_op jit(solution)/shard_map/psum | solution.py:26
  409.7 172.0 %copy-start.1 = (f32[1024,256]{1,0:T(8,128)S(1)}, f32[1024,256]{1,0:T(8,128)}, u32[]{:S(2)}) copy-start(f32[1024,256]{1,0:T(8,128)} %all-reduce.5.cloned.1.call-done) | copy-start | bytes 3145732
Sparse Core Ops, SparseCore 0:
  10.8 353.5 all-gather.1
  387.7 17.7 all-reduce.4
  412.2 107.8 all-reduce.6
where the time goes:
time: 592 us
  waiting for transfers between devices  485 us (82%)
  other arithmetic  54.9 us (9%)
  local copies, waits for them, and re-layouts  26.9 us (5%)
  between operations  15.8 us (3%)
  matrix products  8.89 us (2%)
    all_gather x1, waiting for transfers between devices, local(): panel = lax.all_gather(sketch, 'rows', axis=0, tiled=True)  356 us
    psum x1, waiting for transfers between devices, local(): lax.psum(jnp.dot(slab_total.T, slab_total, precision=highest), 'rows')  110 us
    another operation x6, other arithmetic, local(): lower_factor = jnp.linalg.cholesky(gram_matrix)  34.2 us
    another operation x2, other arithmetic, local(): lax.linalg.triangular_solve(lower_factor, own_rows, left_side=False, lowe...  19.7 us
    psum x1, waiting for transfers between devices, local(): slab_total = lax.psum(partial_rows, 'cols')  17.7 us
    gather x24, local copies, waits for them, and re-layouts  16.7 us
  transfers between devices with their start and end apart: 3, of which 3 were waited for; matrix products, arithmetic and copies ran while one was open for 0% of the time, Pallas kernels for 0%

commit v1 on v0

v1 whole, which is shorter than its diff:
```python
import functools

import jax
import jax.numpy as jnp
from jax import lax
from jax.experimental import pallas as pl
from jax.experimental.pallas import tpu as pltpu
from jax.sharding import PartitionSpec as P

RB = 4
HIGHEST = lax.Precision.HIGHEST
VMEM = pl.BlockSpec(memory_space=pltpu.VMEM)
SMEM = pl.BlockSpec(memory_space=pltpu.SMEM)
MIB = 1024 * 1024


def pick_kernel(index_ref, stripes_ref, out_ref):
    def body(i, carry):
        out_ref[i] = stripes_ref[index_ref[i]]
        return carry

    lax.fori_loop(0, out_ref.shape[0], body, 0, unroll=8)


def pick(indices, stripes):
    count = indices.shape[0]
    _, height, columns = stripes.shape
    return pl.pallas_call(
        pick_kernel,
        out_shape=jax.ShapeDtypeStruct((count, height, columns), stripes.dtype),
        in_specs=[SMEM, VMEM],
        out_specs=VMEM,
        compiler_params=pltpu.CompilerParams(vmem_limit_bytes=24 * MIB),
        name="pick_stripes",
    )(indices, stripes)


def product_kernel(rows_ref, counts_ref, blocks_ref, chosen_ref, out_ref):
    slots, width, _ = blocks_ref.shape
    columns = out_ref.shape[1]
    out_ref[...] = jnp.zeros_like(out_ref)
    for s in range(slots):

        @pl.when(s < counts_ref[0])
        def _():
            piece = chosen_ref[:, s].reshape(width, columns)
            product = jnp.dot(blocks_ref[s], piece, preferred_element_type=jnp.float32)
            at = pl.ds(pl.multiple_of(rows_ref[s] * width, width), width)
            out_ref[at, :] += product


def block_products(block_rows, counts, blocks, chosen):
    _, width, _ = blocks.shape
    columns = chosen.shape[-1]
    return pl.pallas_call(
        product_kernel,
        out_shape=jax.ShapeDtypeStruct((RB * width, columns), jnp.float32),
        in_specs=[SMEM, SMEM, VMEM, VMEM],
        out_specs=VMEM,
        compiler_params=pltpu.CompilerParams(vmem_limit_bytes=24 * MIB),
        name="block_products",
    )(block_rows, counts, blocks, chosen)


def gram_kernel(kept_ref, other_ref, total_ref, gram_ref):
    total = kept_ref[...] + other_ref[...]
    total_ref[...] = total
    gram_ref[...] = lax.dot_general(
        total, total, (((0,), (0,)), ((), ())), precision=HIGHEST, preferred_element_type=jnp.float32
    )


def sum_and_gram(kept, other):
    rows, columns = kept.shape
    return pl.pallas_call(
        gram_kernel,
        out_shape=(
            jax.ShapeDtypeStruct((rows, columns), jnp.float32),
            jax.ShapeDtypeStruct((columns, columns), jnp.float32),
        ),
        in_specs=[VMEM, VMEM],
        out_specs=(VMEM, VMEM),
        compiler_params=pltpu.CompilerParams(vmem_limit_bytes=24 * MIB),
        name="sum_and_gram",
    )(kept, other)


def matmul(a, b, precision):
    return jnp.dot(a, b, precision=precision, preferred_element_type=jnp.float32)


def matmul_nt(a, b, precision):
    return lax.dot_general(
        a, b, (((1,), (1,)), ((), ())), precision=precision, preferred_element_type=jnp.float32
    )


def factor_kernel(total_rows, gram_ref, own_ref, basis_ref, factor_ref, scaled, inverse):
    n = gram_ref.shape[0]
    row_ids = lax.broadcasted_iota(jnp.int32, (n, n), 0)
    col_ids = lax.broadcasted_iota(jnp.int32, (n, n), 1)
    diagonal = row_ids == col_ids
    identity = diagonal.astype(jnp.float32)
    half = jnp.where(row_ids > col_ids, 1.0, jnp.where(diagonal, 0.5, 0.0))
    gram = gram_ref[...]
    on_diagonal = jnp.where(diagonal, gram, 0.0)
    down = jnp.sqrt(jnp.sum(on_diagonal, axis=1, keepdims=True))
    across = jnp.sqrt(jnp.sum(on_diagonal, axis=0, keepdims=True))
    up_down = 1.0 / down
    up_across = 1.0 / across
    scaled[...] = gram * up_down * up_across

    def refine(precision):
        w = inverse[...]
        residual = matmul_nt(matmul(w, scaled[...], precision), w, precision) - identity
        inverse[...] = w - matmul(residual * half, w, precision)
        return jnp.sum(residual * residual)

    inverse[...] = identity - (scaled[...] - identity) * half
    refine(lax.Precision.DEFAULT)

    def going(state):
        step, size = state
        return (step < 8) & (size > 1e-6)

    def advance(state):
        return state[0] + 1, refine(HIGHEST)

    _, size = lax.while_loop(going, advance, (jnp.int32(0), jnp.float32(1.0)))

    @pl.when(jnp.logical_not(size <= 1e-6))
    def _():
        inverse[...] = identity
        ids = lax.broadcasted_iota(jnp.int32, (n, 1), 0)

        def eliminate(j, carry):
            pivot_row = scaled[pl.ds(j, 1), :]
            inverse_row = inverse[pl.ds(j, 1), :]
            column = jnp.sum(jnp.where(col_ids == j, scaled[...], 0.0), axis=1, keepdims=True)
            pivot = jnp.sum(jnp.where(ids == j, column, 0.0), axis=0, keepdims=True)
            root = 1.0 / jnp.sqrt(pivot)
            ratio = jnp.where(ids > j, column / pivot, jnp.where(ids == j, 1.0 - root, 0.0))
            scaled[...] = scaled[...] - ratio * pivot_row
            inverse[...] = inverse[...] - ratio * inverse_row
            return carry

        lax.fori_loop(0, n, eliminate, 0)
        scaled[...] = gram_ref[...] * up_down * up_across

    w = inverse[...]
    root_rows = jnp.sqrt(jnp.float32(total_rows))
    upper = matmul(w, scaled[...], HIGHEST) * across / root_rows
    factor_ref[...] = jnp.where(row_ids <= col_ids, upper, 0.0)
    basis_ref[...] = matmul_nt(own_ref[...] * up_across, w, HIGHEST) * root_rows


def factor_and_basis(total_rows, gram, own):
    columns = gram.shape[0]
    return pl.pallas_call(
        functools.partial(factor_kernel, total_rows),
        out_shape=(
            jax.ShapeDtypeStruct(own.shape, jnp.float32),
            jax.ShapeDtypeStruct((columns, columns), jnp.float32),
        ),
        in_specs=[VMEM, VMEM],
        out_specs=(VMEM, VMEM),
        scratch_shapes=[pltpu.VMEM((columns, columns), jnp.float32)] * 2,
        compiler_params=pltpu.CompilerParams(vmem_limit_bytes=24 * MIB),
        name="factor_and_basis",
    )(gram, own)


def sum_everywhere(gram, axes, devices):
    columns = gram.shape[0]
    if columns % devices:
        return lax.psum(gram, axes)
    pieces = gram.reshape(devices, columns // devices, columns)
    pieces = lax.all_to_all(pieces, axes, split_axis=0, concat_axis=0, tiled=True)
    return lax.all_gather(jnp.sum(pieces, axis=0), axes, axis=0, tiled=True)


def local(sketch, blocks, block_rows, block_cols, counts):
    slots, width, _ = blocks.shape
    columns = sketch.shape[1]
    rows = lax.axis_size("rows")
    cols = lax.axis_size("cols")
    height = width // rows
    stripes = sketch.reshape(-1, rows, height, columns).swapaxes(0, 1)
    stripes = lax.all_to_all(stripes, "rows", split_axis=0, concat_axis=0, tiled=True)
    stripes = stripes.reshape(-1, height, columns)
    wanted = lax.all_gather(block_cols, "rows", axis=0, tiled=True)
    sent = pick(wanted, stripes).reshape(rows, slots, height, columns)
    chosen = lax.all_to_all(sent, "rows", split_axis=0, concat_axis=0, tiled=True)
    if height % 16:
        chosen = chosen.swapaxes(0, 1).reshape(1, slots, width, columns)
    partial_rows = block_products(block_rows, counts, blocks, chosen)
    share = RB * width // cols
    me = lax.axis_index("cols")
    if cols == 2:
        kept = lax.dynamic_slice_in_dim(partial_rows, me * share, share, 0)
        given = lax.dynamic_slice_in_dim(partial_rows, (1 - me) * share, share, 0)
        other = lax.ppermute(given, "cols", [(0, 1), (1, 0)])
    else:
        kept = lax.psum_scatter(partial_rows, "cols", scatter_dimension=0, tiled=True)
        other = jnp.zeros_like(kept)
    own, gram = sum_and_gram(kept, other)
    gram = sum_everywhere(gram, ("rows", "cols"), rows * cols)
    return factor_and_basis(RB * width * rows, gram, own)


def solution(mesh):
    in_specs = (
        P(("rows", "cols"), None),
        P(("rows", "cols"), None, None),
        P(("rows", "cols")),
        P(("rows", "cols")),
        P(("rows", "cols")),
    )
    out_specs = (P(("rows", "cols"), None), P())
    return jax.shard_map(local, mesh=mesh, in_specs=in_specs, out_specs=out_specs, check_vma=False)
```

time: 592 us -> 212 us (0.36)
  waiting for transfers between devices: 485 us -> 24.5 us
  blocking collectives: 0 us -> 102 us
  Pallas kernels: 0 us -> 65.9 us
  other arithmetic: 54.9 us -> 0.04 us
  local copies, waits for them, and re-layouts: 26.9 us -> 4.09 us
  between operations: 15.8 us -> 2.03 us
  starting transfers between devices: 0.3 us -> 13.6 us
  matrix products: 8.89 us -> 0 us
    all_gather x1 -> x0, waiting for transfers between devices: 356 us -> none  [local(): panel = lax.all_gather(sketch, 'rows', axis=0, tiled=True)]
    psum x2 -> x0, waiting for transfers between devices: 128 us -> none  [the longest x1 110 us: local(): lax.psum(jnp.dot(slab_total.T, slab_total, precision=highest), 'rows')]
    pallas_call x0 -> x4, Pallas kernels: none -> 65.9 us  [the longest x1 62.6 us: factor_and_basis(): pl.pallas_call(functools.partial(factor_kernel, total_rows), out_shape=(j...]
    another operation x8 -> x0, other arithmetic: 53.8 us -> none  [the longest x6 34.2 us: local(): lower_factor = jnp.linalg.cholesky(gram_matrix)]
    unnamed x0 -> x1, blocking collectives: none -> 46.9 us
    all_gather x0 -> x1, blocking collectives: none -> 39 us  [sum_everywhere(): return lax.all_gather(jnp.sum(pieces, axis=0), axes, axis=0, tiled=True)]
    all_to_all x0 -> x2, waiting for transfers between devices: none -> 22.6 us  [the longest x1 22.6 us: local(): lax.all_to_all(sent, 'rows', split_axis=0, concat_axis=0, tiled=True)]
    gather x24 -> x0, local copies, waits for them, and re-layouts: 16.7 us -> none
  transfers between devices with their start and end apart: 3 -> 3, of which waited for: 3 -> 2; matrix products, arithmetic and copies ran while one was open for 0% -> 0% of each run, Pallas kernels for 0% -> 0%
where the time goes in v1:
time: 212 us
  blocking collectives  102 us (48%)
  Pallas kernels  65.9 us (31%)
  waiting for transfers between devices  24.5 us (12%)
  starting transfers between devices  13.6 us (6%)
  local copies, waits for them, and re-layouts  4.09 us (2%)
    pallas_call x1, Pallas kernels, factor_and_basis(): pl.pallas_call(functools.partial(factor_kernel, total_rows), out_shape=(j...  62.6 us
    unnamed x1, blocking collectives  46.9 us
    all_gather x1, blocking collectives, sum_everywhere(): return lax.all_gather(jnp.sum(pieces, axis=0), axes, axis=0, tiled=True)  39 us
    all_to_all x1, waiting for transfers between devices, local(): lax.all_to_all(sent, 'rows', split_axis=0, concat_axis=0, tiled=True)  22.6 us
    all_to_all x1, blocking collectives, sum_everywhere(): lax.all_to_all(pieces, axes, split_axis=0, concat_axis=0, tiled=True)  16.2 us
    all_to_all x1, starting transfers between devices, local(): lax.all_to_all(stripes, 'rows', split_axis=0, concat_axis=0, tiled=True)  8.44 us
    all_to_all x1, starting transfers between devices, local(): lax.all_to_all(sent, 'rows', split_axis=0, concat_axis=0, tiled=True)  5.09 us
  transfers between devices with their start and end apart: 3, of which 2 were waited for; matrix products, arithmetic and copies ran while one was open for 0% of the time, Pallas kernels for 0%

profile of v1, /device:TPU:0, one launch (start us, length us, event | category | flops | bytes accessed | tf_op | source)
XLA Modules:
  0.0 212.3 jit_solution(4846090880574024388)
XLA Ops:
  0.6 3.2 %copy.9 = bf16[16,16,16,256]{3,2,0,1:T(8,128)(2,1)} copy(bf16[16,16,16,256]{3,2,1,0:T(8,128)(2,1)} %bitcast.11) | data formatting | bytes 4194304 | tf_op jit(solution)/shard_map/reshape | solution.py:188
  3.8 0.0 copy-start.3
  3.8 0.0 copy-start.2
  3.8 8.4 %all-to-all-start = ((bf16[16,16,16,256]{3,2,1,0:T(8,128)(2,1)}), bf16[16,16,16,256]{3,2,1,0:T(8,128)(2,1)S(1)}, u32[]{:S(2)}, u32[]{:S(2)}) async-start(bf16[16,16,16,256]{3,2,1,0:T(8,128)(2,1)} %bitcast.10), calls=%async_computation | async-start | bytes 4194304 | tf_op jit(solution)/shard_map/all_to_all | solution.py:189
  12.3 0.0 copy-done.3
  12.3 0.6 dynamic-slice
  13.5 0.0 copy-done.2
  13.5 0.2 dynamic-update-slice
  13.8 46.9 %all-reduce.index_ref = s32[128]{0:T(128)S(1)} all-reduce(s32[128]{0:T(128)S(1)} %dynamic-update-slice), channel_id=1, replica_groups=mesh['rows'=16,'cols'=2] {'rows'}, use_global_device_ids=true, to_apply=%add | all-reduce | flops 128 | bytes 1024
  60.6 0.0 all-to-all-done
  60.6 0.0 copy-start
  60.6 0.0 copy-start.1
  60.6 1.7 pick_stripes.1
  62.4 5.1 %all-to-all-start.1 = ((bf16[16,8,16,256]{3,2,1,0:T(8,128)(2,1)}), bf16[16,8,16,256]{3,2,1,0:T(8,128)(2,1)S(1)}, u32[]{:S(2)}, u32[]{:S(2)}) async-start(bf16[16,8,16,256]{3,2,1,0:T(8,128)(2,1)} %bitcast.4), calls=%async_computation.1 | async-start | bytes 2097152 | tf_op jit(solution)/shard_map/all_to_all | solution.py:193
  68.1 22.6 %all-to-all-done.1.chosen_ref = bf16[16,8,16,256]{3,2,1,0:T(8,128)(2,1)S(1)} async-done(((bf16[16,8,16,256]{3,2,1,0:T(8,128)(2,1)}), bf16[16,8,16,256]{3,2,1,0:T(8,128)(2,1)S(1)}, u32[]{:S(2)}, u32[]{:S(2)}) %all-to-all-start.1) | async-done | bytes 1048608 | tf_op jit(solution)/shard_map/all_to_all | solution.py:193
  90.7 0.0 copy-done
  90.8 0.0 copy-done.1
  90.8 0.8 block_products.1
  91.5 0.1 constant_dynamic-slice_fusion
  91.6 0.1 collective-permute-start
  91.7 1.9 collective-permute-done.other_ref
  93.6 0.8 sum_and_gram.1
  94.4 16.2 %all_to_all.15 = f32[32,8,256]{2,1,0:T(8,128)S(1)} all-to-all(f32[32,8,256]{2,1,0:T(8,128)S(1)} %bitcast.9), channel_id=1, replica_groups=mesh['rows'=16,'cols'=2] {'rows','cols'}, dimensions={0} | all-to-all | bytes 524288 | tf_op jit(solution)/shard_map/all_to_all | solution.py:178
  110.6 39.0 %all_gather.7.gram_ref = f32[256,256]{1,0:T(8,128)S(1)} all-gather(f32[8,256]{1,0:T(8,128)S(1)} %reduce_sum.9), channel_id=1, replica_groups=mesh['rows'=16,'cols'=2] {'rows','cols'}, dimensions={0}, use_global_device_ids=true | all-gather | bytes 270336 | tf_op jit(solution)/shard_map/all_gather | solution.py:179
  149.7 62.6 %factor_and_basis.1 = (f32[512,256]{1,0:T(8,128)}, f32[256,256]{1,0:T(8,128)}) custom-call(f32[256,256]{1,0:T(8,128)S(1)} %all_gather.7.gram_ref, f32[512,256]{1,0:T(8,128)S(1)} %get-tuple-element.5.own_ref), custom_call_target="tpu_custom_call" | custom-call | tf_op jit(solution)/shard_map/factor_and_basis/pallas_call | solution.py:159
  (2 shorter events, 0.0 us)
Async XLA Ops:
  3.8 8.5 %copy-start.3 = (u32[32]{0:T(128)S(1)}, u32[32]{0:T(128)}, u32[]{:S(2)}) copy-start(u32[32]{0:T(128)} %constant.20) | copy-start | bytes 388
  3.8 9.7 %copy-start.2 = (s32[8]{0:T(128)S(1)}, s32[8]{0:T(128)}, u32[]{:S(2)}) copy-start(s32[8]{0:T(128)} %param.8) | copy-start | bytes 100
  3.8 56.8 %all-to-all-start = ((bf16[16,16,16,256]{3,2,1,0:T(8,128)(2,1)}), bf16[16,16,16,256]{3,2,1,0:T(8,128)(2,1)S(1)}, u32[]{:S(2)}, u32[]{:S(2)}) async-start(bf16[16,16,16,256]{3,2,1,0:T(8,128)(2,1)} %bitcast.10), calls=%async_computation | async-start | bytes 4194304 | tf_op jit(solution)/shard_map/all_to_all | solution.py:189
  60.6 30.1 %copy-start = (bf16[8,256,256]{2,1,0:T(8,128)(2,1)S(1)}, bf16[8,256,256]{2,1,0:T(8,128)(2,1)}, u32[]{:S(2)}) copy-start(bf16[8,256,256]{2,1,0:T(8,128)(2,1)} %blocks_ref.1) | copy-start | bytes 3145732
  60.6 30.1 %copy-start.1 = (s32[8]{0:T(128)S(1)}, s32[8]{0:T(128)}, u32[]{:S(2)}) copy-start(s32[8]{0:T(128)} %rows_ref.1) | copy-start | bytes 100
  62.4 28.4 %all-to-all-start.1 = ((bf16[16,8,16,256]{3,2,1,0:T(8,128)(2,1)}), bf16[16,8,16,256]{3,2,1,0:T(8,128)(2,1)S(1)}, u32[]{:S(2)}, u32[]{:S(2)}) async-start(bf16[16,8,16,256]{3,2,1,0:T(8,128)(2,1)} %bitcast.4), calls=%async_computation.1 | async-start | bytes 2097152 | tf_op jit(solution)/shard_map/all_to_all | solution.py:193
  91.6 2.0 collective-permute-start

commit v2 on v1

--- a/solution.py
+++ b/solution.py
@@ -14,25 +14,102 @@
 MIB = 1024 * 1024
 
 
-def pick_kernel(index_ref, stripes_ref, out_ref):
-    def body(i, carry):
-        out_ref[i] = stripes_ref[index_ref[i]]
-        return carry
-
-    lax.fori_loop(0, out_ref.shape[0], body, 0, unroll=8)
-
-
-def pick(indices, stripes):
-    count = indices.shape[0]
-    _, height, columns = stripes.shape
-    return pl.pallas_call(
-        pick_kernel,
-        out_shape=jax.ShapeDtypeStruct((count, height, columns), stripes.dtype),
+KEPT = 8
+
+
+def plan_kernel(per, table_ref, places_ref, kept_ref, most_ref):
+    devices = table_ref.shape[0]
+    slots = places_ref.shape[1]
+    panel = per * lax.axis_size("rows")
+    cols = lax.axis_size("cols")
+    table = table_ref[...]
+    block = lax.broadcasted_iota(jnp.int32, (devices, panel), 1)
+    device = lax.broadcasted_iota(jnp.int32, (devices, panel), 0)
+    asked = [(table[:, s : s + 1] == block) & (s < table[:, slots : slots + 1]) for s in range(slots)]
+    some = functools.reduce(jnp.logical_or, asked)
+    first = lax.broadcasted_iota(jnp.int32, (panel, panel), 0)
+    second = lax.broadcasted_iota(jnp.int32, (panel, panel), 1)
+    before = (first // per == second // per) & (first < second)
+    before = jnp.where(before, 1.0, 0.0).astype(jnp.bfloat16)
+    touched = [
+        jnp.max(jnp.where(some & (device % cols == c), 1.0, 0.0), axis=0, keepdims=True) for c in range(cols)
+    ]
+    line = lax.broadcasted_iota(jnp.int32, (8, panel), 0)
+    touched = sum(jnp.where(line == c, touched[c], 0.0) for c in range(cols))
+    rank = jnp.dot(touched.astype(jnp.bfloat16), before, preferred_element_type=jnp.float32)
+    most = jnp.max(rank + touched, axis=(0, 1), keepdims=True)
+    most_ref[...] = jnp.broadcast_to(most, most_ref.shape).astype(jnp.int32)
+    here = line == lax.axis_index("cols")
+    touched = jnp.max(jnp.where(here, touched, 0.0), axis=0, keepdims=True)
+    rank = jnp.max(jnp.where(here, rank, 0.0), axis=0, keepdims=True)
+    ids = lax.broadcasted_iota(jnp.int32, (1, panel), 1)
+    place = (ids // per * KEPT).astype(jnp.float32) + rank
+    slot = lax.broadcasted_iota(jnp.int32, places_ref.shape, 1)
+    places = jnp.zeros(places_ref.shape, jnp.float32)
+    for s in range(slots):
+        found = jnp.sum(jnp.where(asked[s], place, 0.0), axis=1, keepdims=True)
+        places = jnp.where(slot == s, found, places)
+    places_ref[...] = jnp.minimum(places.astype(jnp.int32), panel // per * KEPT - 1)
+    mine = (touched > 0.5) & (ids // per == lax.axis_index("rows"))
+    wanted_rank = lax.broadcasted_iota(jnp.int32, (KEPT, panel), 0).astype(jnp.float32)
+    chosen = jnp.where(mine & (rank == wanted_rank), (ids % per).astype(jnp.float32), 0.0)
+    chosen = jnp.sum(chosen, axis=1, keepdims=True).astype(jnp.int32)
+    kept_ref[...] = jnp.broadcast_to(chosen, kept_ref.shape)
+
+
+def plan(table, slots, per):
+    devices = table.shape[0]
+    return pl.pallas_call(
+        functools.partial(plan_kernel, per),
+        out_shape=(
+            jax.ShapeDtypeStruct((devices, slots), jnp.int32),
+            jax.ShapeDtypeStruct((KEPT, 128), jnp.int32),
+            jax.ShapeDtypeStruct((8, 128), jnp.int32),
+        ),
+        in_specs=[VMEM],
+        out_specs=(VMEM, VMEM, VMEM),
+        name="plan",
+    )(table)
+
+
+def keep_kernel(kept_ref, sketch_ref, out_ref):
+    for k in range(out_ref.shape[1]):
+        out_ref[:, k] = sketch_ref[kept_ref[k]]
+
+
+def keep(kept, sketch):
+    _, rows, height, columns = sketch.shape
+    return pl.pallas_call(
+        keep_kernel,
+        out_shape=jax.ShapeDtypeStruct((rows, KEPT, height, columns), sketch.dtype),
         in_specs=[SMEM, VMEM],
         out_specs=VMEM,
         compiler_params=pltpu.CompilerParams(vmem_limit_bytes=24 * MIB),
+        name="keep_blocks",
+    )(kept, sketch)
+
+
+def pick_kernel(places_ref, stripes_ref, out_ref):
+    slots = out_ref.shape[1]
+
+    def body(r, carry):
+        for s in range(slots):
+            out_ref[r, s] = stripes_ref[places_ref[r, s]]
+        return carry
+
+    lax.fori_loop(0, out_ref.shape[0], body, 0)
+
+
+def pick(places, stripes):
+    _, height, columns = stripes.shape
+    return pl.pallas_call(
+        pick_kernel,
+        out_shape=jax.ShapeDtypeStruct((*places.shape, height, columns), stripes.dtype),
+        in_specs=[SMEM, VMEM],
+        out_specs=VMEM,
+        compiler_params=pltpu.CompilerParams(vmem_limit_bytes=24 * MIB),
         name="pick_stripes",
-    )(indices, stripes)
+    )(places, stripes)
 
 
 def product_kernel(rows_ref, counts_ref, blocks_ref, chosen_ref, out_ref):
@@ -176,7 +253,40 @@
         return lax.psum(gram, axes)
     pieces = gram.reshape(devices, columns // devices, columns)
     pieces = lax.all_to_all(pieces, axes, split_axis=0, concat_axis=0, tiled=True)
-    return lax.all_gather(jnp.sum(pieces, axis=0), axes, axis=0, tiled=True)
+    return spread(jnp.sum(pieces, axis=0), axes, devices).reshape(columns, columns)
+
+
+def spread(piece, axes, devices):
+    copies = jnp.broadcast_to(piece[None], (devices, *piece.shape))
+    return lax.all_to_all(copies, axes, split_axis=0, concat_axis=0, tiled=True)
+
+
+def turn(stripes):
+    stripes = lax.all_to_all(stripes, "rows", split_axis=0, concat_axis=0, tiled=True)
+    return stripes.reshape(-1, *stripes.shape[2:])
+
+
+def stripes_for_panel(sketch, block_cols, counts, slots, rows, cols):
+    per = sketch.shape[0]
+    if per <= KEPT:
+        wanted = lax.all_gather(block_cols, "rows", axis=0, tiled=False)
+        return pick(wanted, turn(sketch.swapaxes(0, 1)))
+    devices = rows * cols
+    line = jnp.concatenate([block_cols, counts, jnp.zeros((7,), jnp.int32)])
+    table = spread(line, ("rows", "cols"), devices)
+    places, kept, most = plan(table, slots, per)
+
+    def mine(values):
+        values = values.reshape(rows, cols, -1)
+        return lax.dynamic_index_in_dim(values, lax.axis_index("cols"), 1, keepdims=False)
+
+    def some():
+        return pick(mine(places), turn(keep(kept[:, 0], sketch)))
+
+    def every():
+        return pick(mine(table)[:, :slots], turn(sketch.swapaxes(0, 1)))
+
+    return lax.cond(most[0, 0] <= KEPT, some, every)
 
 
 def local(sketch, blocks, block_rows, block_cols, counts):
@@ -185,11 +295,8 @@
     rows = lax.axis_size("rows")
     cols = lax.axis_size("cols")
     height = width // rows
-    stripes = sketch.reshape(-1, rows, height, columns).swapaxes(0, 1)
-    stripes = lax.all_to_all(stripes, "rows", split_axis=0, concat_axis=0, tiled=True)
-    stripes = stripes.reshape(-1, height, columns)
-    wanted = lax.all_gather(block_cols, "rows", axis=0, tiled=True)
-    sent = pick(wanted, stripes).reshape(rows, slots, height, columns)
+    sketch = sketch.reshape(-1, rows, height, columns)
+    sent = stripes_for_panel(sketch, block_cols, counts, slots, rows, cols)
     chosen = lax.all_to_all(sent, "rows", split_axis=0, concat_axis=0, tiled=True)
     if height % 16:
         chosen = chosen.swapaxes(0, 1).reshape(1, slots, width, columns)

time: 212 us -> 177 us (0.83)
  blocking collectives: 102 us -> 41.7 us
  waiting for transfers between devices: 24.5 us -> 49.8 us
  Pallas kernels: 65.9 us -> 70.8 us
  starting transfers between devices: 13.6 us -> 9.95 us
  local copies, waits for them, and re-layouts: 4.09 us -> 1.44 us
    unnamed x1 -> x0, blocking collectives: 46.9 us -> none
    all_gather x1 -> x0, blocking collectives: 39 us -> none  [sum_everywhere(): return lax.all_gather(jnp.sum(pieces, axis=0), axes, axis=0, tiled=True)]
    all_to_all x0 -> x2, blocking collectives: none -> 27.1 us  [spread(): return lax.all_to_all(copies, axes, split_axis=0, concat_axis=0, tiled=True)]
    all_to_all x1, waiting for transfers between devices: 0.01 us -> 24.5 us  [turn(): lax.all_to_all(stripes, 'rows', split_axis=0, concat_axis=0, tiled=True)]
    all_to_all x1, starting transfers between devices: 8.44 us -> 3.65 us  [turn(): lax.all_to_all(stripes, 'rows', split_axis=0, concat_axis=0, tiled=True)]
    pallas_call x1 -> x3, Pallas kernels: 1.73 us -> 5.52 us  [the longest x1 2.65 us: keep(): pl.pallas_call(keep_kernel, out_shape=jax.ShapeDtypeStruct((rows, KEPT, h...]
    reshape x1 -> x0, local copies, waits for them, and re-layouts: 3.16 us -> none  [local(): stripes = sketch.reshape(-1, rows, height, columns).swapaxes(0, 1)]
  transfers between devices with their start and end apart: 3 -> 3, of which waited for: 2 -> 3; matrix products, arithmetic and copies ran while one was open for 0% -> 0% of each run, Pallas kernels for 0% -> 0%
where the time goes in v2:
time: 177 us; the launch traced here: 176 us
  Pallas kernels  70.8 us (40%)
  waiting for transfers between devices  49.8 us (28%)
  blocking collectives  41.7 us (24%)
  starting transfers between devices  9.95 us (6%)
  between operations  2 us (1%)
    pallas_call x1, Pallas kernels, factor_and_basis(): pl.pallas_call(functools.partial(factor_kernel, total_rows), out_shape=(j...  62.6 us
    all_to_all x2, blocking collectives, spread(): return lax.all_to_all(copies, axes, split_axis=0, concat_axis=0, tiled=True)  27.1 us
    all_to_all x1, waiting for transfers between devices, turn(): lax.all_to_all(stripes, 'rows', split_axis=0, concat_axis=0, tiled=True)  24.5 us
    all_to_all x1, waiting for transfers between devices, local(): lax.all_to_all(sent, 'rows', split_axis=0, concat_axis=0, tiled=True)  23.3 us
    all_to_all x1, blocking collectives, sum_everywhere(): lax.all_to_all(pieces, axes, split_axis=0, concat_axis=0, tiled=True)  14.7 us
    all_to_all x1, starting transfers between devices, local(): lax.all_to_all(sent, 'rows', split_axis=0, concat_axis=0, tiled=True)  6.22 us
    all_to_all x1, starting transfers between devices, turn(): lax.all_to_all(stripes, 'rows', split_axis=0, concat_axis=0, tiled=True)  3.65 us
  transfers between devices with their start and end apart: 3, of which 3 were waited for; matrix products, arithmetic and copies ran while one was open for 0% of the time, Pallas kernels for 0%

profile of v2, /device:TPU:0, one launch (start us, length us, event | category | flops | bytes accessed | tf_op | source)
XLA Modules:
  0.0 176.5 jit_solution(6210600223675439916)
XLA Ops:
  1.3 0.7 pad_add_fusion
  2.0 14.3 %all_to_all.31 = s32[32,1,16]{2,1,0:T(1,128)S(1)} all-to-all(s32[32,1,16]{2,1,0:T(1,128)S(1)} %broadcast_in_dim.4), channel_id=1, replica_groups=mesh['rows'=16,'cols'=2] {'rows','cols'}, dimensions={0} | all-to-all | bytes 4096 | tf_op jit(solution)/shard_map/all_to_all | solution.py:261
  16.3 1.0 plan.1
  17.3 1.2 slice.9
  19.2 32.9 %conditional.1 = (bf16[16,8,16,256]{3,2,1,0:T(8,128)(2,1)}) conditional(s32[]{:T(128)} %bitcast.9, (s32[32,16]{1,0:T(8,128)S(1)}, bf16[16,16,16,256]{3,2,1,0:T(8,128)(2,1)}) %tuple.26, (s32[32,8]{1,0:T(8,128)S(1)}, s32[8,128]{1,0:T(8,128)S(1)}, bf16[16,16,16,256]{3,2,1,0:T(8,128)(2,1)}) %tuple.25), branch_computations={%region_0.1_spmd, %region_1.2_spmd} | conditional | flops 5 | bytes 10487906 | solution.py:289
  19.2 0.1 copy.20
  19.3 2.6 %keep_blocks.1 = bf16[16,8,16,256]{3,2,1,0:T(8,128)(2,1)} custom-call(s32[8]{0:T(128)S(1)} %slice_bitcast_fusion.kept_ref, bf16[16,16,16,256]{3,2,1,0:T(8,128)(2,1)} %get-tuple-element.17.sketch_ref), custom_call_target="tpu_custom_call" | custom-call | tf_op jit(solution)/shard_map/cond/branch_1_fun/keep_blocks/pallas_call | solution.py:82
  21.9 3.7 %all-to-all-start.1 = ((bf16[16,8,16,256]{3,2,1,0:T(8,128)(2,1)}), bf16[16,8,16,256]{3,2,1,0:T(8,128)(2,1)S(1)}, u32[]{:S(2)}, u32[]{:S(2)}) async-start(bf16[16,8,16,256]{3,2,1,0:T(8,128)(2,1)} %keep_blocks.1), calls=%async_computation.1 | async-start | bytes 2097152 | tf_op jit(solution)/shard_map/cond/branch_1_fun/all_to_all | solution.py:265
  25.6 24.5 %all-to-all-done.1 = bf16[16,8,16,256]{3,2,1,0:T(8,128)(2,1)S(1)} async-done(((bf16[16,8,16,256]{3,2,1,0:T(8,128)(2,1)}), bf16[16,8,16,256]{3,2,1,0:T(8,128)(2,1)S(1)}, u32[]{:S(2)}, u32[]{:S(2)}) %all-to-all-start.1) | async-done | bytes 1048608 | tf_op jit(solution)/shard_map/cond/branch_1_fun/all_to_all | solution.py:265
  50.1 1.9 %pick_stripes.3 = bf16[16,8,16,256]{3,2,1,0:T(8,128)(2,1)} custom-call(s32[16,8]{1,0:T(8,128)S(1)} %bitcast.22, bf16[128,16,256]{2,1,0:T(8,128)(2,1)S(1)} %bitcast.18), custom_call_target="tpu_custom_call" | custom-call | tf_op jit(solution)/shard_map/cond/branch_1_fun/pick_stripes/pallas_call | solution.py:105
  52.0 0.0 copy-start
  52.0 0.0 copy-start.1
  52.0 6.2 %all-to-all-start.3 = ((bf16[16,8,16,256]{3,2,1,0:T(8,128)(2,1)}), bf16[16,8,16,256]{3,2,1,0:T(8,128)(2,1)S(1)}, u32[]{:S(2)}, u32[]{:S(2)}) async-start(bf16[16,8,16,256]{3,2,1,0:T(8,128)(2,1)} %get-tuple-element.47), calls=%async_computation.3 | async-start | bytes 2097152 | tf_op jit(solution)/shard_map/all_to_all | solution.py:300
  58.2 23.3 %all-to-all-done.3.chosen_ref = bf16[16,8,16,256]{3,2,1,0:T(8,128)(2,1)S(1)} async-done(((bf16[16,8,16,256]{3,2,1,0:T(8,128)(2,1)}), bf16[16,8,16,256]{3,2,1,0:T(8,128)(2,1)S(1)}, u32[]{:S(2)}, u32[]{:S(2)}) %all-to-all-start.3) | async-done | bytes 1048608 | tf_op jit(solution)/shard_map/all_to_all | solution.py:300
  81.6 0.0 copy-done
  81.6 0.0 copy-done.1
  81.6 1.9 %block_products.1 = f32[1024,256]{1,0:T(8,128)S(1)} custom-call(s32[8]{0:T(128)S(1)} %copy-done.1, s32[1]{0:T(128)S(6)} %copy.26.counts_ref, bf16[8,256,256]{2,1,0:T(8,128)(2,1)S(1)} %copy-done, bf16[16,8,16,256]{3,2,1,0:T(8,128)(2,1)S(1)} %all-to-all-done.3.chosen_ref), custom_call_target="tpu_custom_call" | custom-call | tf_op jit(solution)/shard_map/block_products/pallas_call | solution.py:132
  83.5 0.1 constant_dynamic-slice_fusion.2
  83.6 0.1 collective-permute-start
  83.7 1.9 %collective-permute-done.other_ref = f32[512,256]{1,0:T(8,128)S(1)} collective-permute-done((f32[512,256]{1,0:T(8,128)S(1)}, f32[512,256]{1,0:T(8,128)S(1)}, u32[]{:S(2)}, u32[]{:S(2)}) %collective-permute-start) | collective-permute-done | bytes 524320 | tf_op jit(solution)/shard_map/ppermute | solution.py:309
  85.6 0.8 sum_and_gram.1
  86.3 14.7 %all_to_all.32 = f32[32,8,256]{2,1,0:T(8,128)S(1)} all-to-all(f32[32,8,256]{2,1,0:T(8,128)S(1)} %bitcast.20), channel_id=1, replica_groups=mesh['rows'=16,'cols'=2] {'rows','cols'}, dimensions={0} | all-to-all | bytes 524288 | tf_op jit(solution)/shard_map/all_to_all | solution.py:255
  101.1 12.8 %all_to_all.33 = f32[32,8,256]{2,1,0:T(8,128)S(1)} all-to-all(f32[32,8,256]{2,1,0:T(8,128)S(1)} %broadcast_in_dim.5), channel_id=1, replica_groups=mesh['rows'=16,'cols'=2] {'rows','cols'}, dimensions={0} | all-to-all | bytes 524288 | tf_op jit(solution)/shard_map/all_to_all | solution.py:261
  113.9 62.6 %factor_and_basis.1 = (f32[512,256]{1,0:T(8,128)}, f32[256,256]{1,0:T(8,128)}) custom-call(f32[256,256]{1,0:T(8,128)S(1)} %bitcast.19, f32[512,256]{1,0:T(8,128)S(1)} %get-tuple-element.29.own_ref), custom_call_target="tpu_custom_call" | custom-call | tf_op jit(solution)/shard_map/factor_and_basis/pallas_call | solution.py:236
  (6 shorter events, 0.1 us)
Async XLA Ops:
  21.9 28.2 %all-to-all-start.1 = ((bf16[16,8,16,256]{3,2,1,0:T(8,128)(2,1)}), bf16[16,8,16,256]{3,2,1,0:T(8,128)(2,1)S(1)}, u32[]{:S(2)}, u32[]{:S(2)}) async-start(bf16[16,8,16,256]{3,2,1,0:T(8,128)(2,1)} %keep_blocks.1), calls=%async_computation.1 | async-start | bytes 2097152 | tf_op jit(solution)/shard_map/cond/branch_1_fun/all_to_all | solution.py:265
  52.0 29.6 %copy-start = (bf16[8,256,256]{2,1,0:T(8,128)(2,1)S(1)}, bf16[8,256,256]{2,1,0:T(8,128)(2,1)}, u32[]{:S(2)}) copy-start(bf16[8,256,256]{2,1,0:T(8,128)(2,1)} %blocks_ref.1) | copy-start | bytes 3145732
  52.0 29.6 %copy-start.1 = (s32[8]{0:T(128)S(1)}, s32[8]{0:T(128)}, u32[]{:S(2)}) copy-start(s32[8]{0:T(128)} %rows_ref.1) | copy-start | bytes 100
  52.0 29.6 %all-to-all-start.3 = ((bf16[16,8,16,256]{3,2,1,0:T(8,128)(2,1)}), bf16[16,8,16,256]{3,2,1,0:T(8,128)(2,1)S(1)}, u32[]{:S(2)}, u32[]{:S(2)}) async-start(bf16[16,8,16,256]{3,2,1,0:T(8,128)(2,1)} %get-tuple-element.47), calls=%async_computation.3 | async-start | bytes 2097152 | tf_op jit(solution)/shard_map/all_to_all | solution.py:300
  83.6 2.0 %collective-permute-start = (f32[512,256]{1,0:T(8,128)S(1)}, f32[512,256]{1,0:T(8,128)S(1)}, u32[]{:S(2)}, u32[]{:S(2)}) collective-permute-start(f32[512,256]{1,0:T(8,128)S(1)} %get-tuple-element.45), channel_id=1, source_target_pairs={{0,1},{1,0},{2,3},{3,2},{4,5},{5,4},{6,7},{7,6},{8,9},{9,8},{10,11... | collective-permute-start | bytes 1572872 | tf_op jit(solution)/shard_map/ppermute | solution.py:309

commit v3 on v1

--- a/solution.py
+++ b/solution.py
@@ -14,25 +14,147 @@
 MIB = 1024 * 1024
 
 
-def pick_kernel(index_ref, stripes_ref, out_ref):
-    def body(i, carry):
-        out_ref[i] = stripes_ref[index_ref[i]]
-        return carry
-
-    lax.fori_loop(0, out_ref.shape[0], body, 0, unroll=8)
-
-
-def pick(indices, stripes):
-    count = indices.shape[0]
-    _, height, columns = stripes.shape
-    return pl.pallas_call(
-        pick_kernel,
-        out_shape=jax.ShapeDtypeStruct((count, height, columns), stripes.dtype),
+LEVELS = (16, 24)
+
+
+def cut_kernel(sketch_ref, out_ref, sems):
+    copies = [
+        pltpu.make_async_copy(sketch_ref.at[:, j], out_ref.at[j], sems.at[j]) for j in range(out_ref.shape[0])
+    ]
+    for copy in copies:
+        copy.start()
+    for copy in copies:
+        copy.wait()
+
+
+def cut(sketch):
+    blocks, pieces, height, columns = sketch.shape
+    return pl.pallas_call(
+        cut_kernel,
+        out_shape=jax.ShapeDtypeStruct((pieces, blocks, height, columns), sketch.dtype),
+        in_specs=[pl.BlockSpec(memory_space=pl.ANY)],
+        out_specs=pl.BlockSpec(memory_space=pl.ANY),
+        scratch_shapes=[pltpu.SemaphoreType.DMA((pieces,))],
+        name="cut_stripes",
+    )(sketch)
+
+
+def plan_kernel(per, table_ref, places_ref, list_ref, most_ref):
+    devices = table_ref.shape[0]
+    slots = places_ref.shape[1]
+    rows, cols = lax.axis_size("rows"), lax.axis_size("cols")
+    panel = per * rows
+    part = panel // 2
+    table = table_ref[...]
+    block = lax.broadcasted_iota(jnp.int32, (devices, panel), 1)
+    device = lax.broadcasted_iota(jnp.int32, (devices, panel), 0)
+    asked = [(table[:, s : s + 1] == block) & (s < table[:, slots : slots + 1]) for s in range(slots)]
+    some = functools.reduce(jnp.logical_or, asked) & (device // (devices // 2) != block // part)
+    lines = -(-2 * cols // 8) * 8
+    line = lax.broadcasted_iota(jnp.int32, (lines, panel), 0)
+    touched = jnp.zeros((lines, panel), jnp.float32)
+    for h in range(2):
+        for c in range(cols):
+            group = some & (device // (devices // 2) == h) & (device % cols == c)
+            found = jnp.max(jnp.where(group, 1.0, 0.0), axis=0, keepdims=True)
+            touched = jnp.where(line == h * cols + c, found, touched)
+    most = jnp.max(jnp.sum(touched, axis=1, keepdims=True), axis=0, keepdims=True)
+    most_ref[...] = jnp.broadcast_to(most, most_ref.shape).astype(jnp.int32)
+    touched = touched.astype(jnp.bfloat16)
+    first = lax.broadcasted_iota(jnp.int32, (panel, panel), 0)
+    second = lax.broadcasted_iota(jnp.int32, (panel, panel), 1)
+    after = jnp.where(first > second, 1.0, 0.0).astype(jnp.bfloat16)
+    same = jnp.where(first == second, 1.0, 0.0).astype(jnp.bfloat16)
+    nt = (((1,), (1,)), ((), ()))
+    half = lax.axis_index("rows") // (rows // 2)
+    c = lax.axis_index("cols")
+    rank = lax.dot_general(touched, after, nt, preferred_element_type=jnp.float32)
+    rank = jnp.sum(jnp.where(line == half * cols + c, rank, 0.0), axis=0, keepdims=True)
+    ids = lax.broadcasted_iota(jnp.int32, (1, panel), 1)
+    place = jnp.where(ids // part == half, ids - half * part, part + rank.astype(jnp.int32))
+    slot = lax.broadcasted_iota(jnp.int32, places_ref.shape, 1)
+    places = jnp.zeros(places_ref.shape, jnp.int32)
+    for s in range(slots):
+        found = jnp.sum(jnp.where(asked[s], place, 0), axis=1, keepdims=True)
+        places = jnp.where(slot == s, found, places)
+    places_ref[...] = places
+    line = lax.broadcasted_iota(jnp.int32, (panel, lines), 1)
+    mine = line == (1 - half) * cols + c
+    there = lax.dot_general(same, touched, nt, preferred_element_type=jnp.float32)
+    there = jnp.sum(jnp.where(mine, there, 0.0), axis=1, keepdims=True)
+    rank = lax.dot_general(after, touched, nt, preferred_element_type=jnp.float32)
+    rank = jnp.sum(jnp.where(mine, rank, 0.0), axis=1, keepdims=True).astype(jnp.int32)
+    ids = lax.broadcasted_iota(jnp.int32, (panel, list_ref.shape[1]), 0)
+    number = lax.broadcasted_iota(jnp.int32, (panel, list_ref.shape[1]), 1)
+    listed = jnp.where((there > 0.5) & (rank == number), ids - half * part, 0)
+    list_ref[...] = jnp.broadcast_to(jnp.sum(listed, axis=0, keepdims=True), list_ref.shape)
+
+
+def plan(table, slots, per):
+    devices = table.shape[0]
+    return pl.pallas_call(
+        functools.partial(plan_kernel, per),
+        out_shape=(
+            jax.ShapeDtypeStruct((devices, slots), jnp.int32),
+            jax.ShapeDtypeStruct((8, 128), jnp.int32),
+            jax.ShapeDtypeStruct((8, 128), jnp.int32),
+        ),
+        in_specs=[VMEM],
+        out_specs=(VMEM, VMEM, VMEM),
+        name="plan",
+    )(table)
+
+
+def list_kernel(list_ref, stripes_ref, out_ref):
+    for k in range(out_ref.shape[0]):
+        out_ref[k] = stripes_ref[list_ref[0, k]]
+
+
+def listed(numbers, stripes, count):
+    return pl.pallas_call(
+        list_kernel,
+        out_shape=jax.ShapeDtypeStruct((count, *stripes.shape[1:]), stripes.dtype),
         in_specs=[SMEM, VMEM],
         out_specs=VMEM,
         compiler_params=pltpu.CompilerParams(vmem_limit_bytes=24 * MIB),
+        name="listed_stripes",
+    )(numbers, stripes)
+
+
+def pick_kernel(places_ref, own_ref, other_ref, out_ref):
+    members, slots = out_ref.shape[:2]
+    rows, cols = lax.axis_size("rows"), lax.axis_size("cols")
+    here = own_ref.shape[0]
+    half = lax.axis_index("rows") // (rows // 2)
+    c = lax.axis_index("cols")
+
+    def body(m, carry):
+        device = (half * members + m) * cols + c
+        for s in range(slots):
+            place = places_ref[device, s]
+
+            @pl.when(place < here)
+            def _():
+                out_ref[m, s] = own_ref[jnp.minimum(place, here - 1)]
+
+            @pl.when(place >= here)
+            def _():
+                out_ref[m, s] = other_ref[jnp.clip(place - here, 0, other_ref.shape[0] - 1)]
+
+        return carry
+
+    lax.fori_loop(0, members, body, 0)
+
+
+def pick(places, own, other, members):
+    return pl.pallas_call(
+        pick_kernel,
+        out_shape=jax.ShapeDtypeStruct((members, places.shape[1], *own.shape[1:]), own.dtype),
+        in_specs=[SMEM, VMEM, VMEM],
+        out_specs=VMEM,
+        compiler_params=pltpu.CompilerParams(vmem_limit_bytes=24 * MIB),
         name="pick_stripes",
-    )(indices, stripes)
+    )(places, own, other)
 
 
 def product_kernel(rows_ref, counts_ref, blocks_ref, chosen_ref, out_ref):
@@ -62,27 +184,31 @@
     )(block_rows, counts, blocks, chosen)
 
 
-def gram_kernel(kept_ref, other_ref, total_ref, gram_ref):
-    total = kept_ref[...] + other_ref[...]
-    total_ref[...] = total
+def gram_kernel(mine_ref, other_ref, own_ref, gram_ref, slab):
+    c = lax.axis_index("cols")
+    share, width = own_ref.shape[0], gram_ref.shape[1]
+    slab[...] = mine_ref[...] + other_ref[...]
+    own_ref[...] = slab[pl.ds(pl.multiple_of(c * share, share), share), :]
+    right = slab[:, pl.ds(pl.multiple_of(c * width, width), width)]
     gram_ref[...] = lax.dot_general(
-        total, total, (((0,), (0,)), ((), ())), precision=HIGHEST, preferred_element_type=jnp.float32
+        slab[...], right, (((0,), (0,)), ((), ())), precision=HIGHEST, preferred_element_type=jnp.float32
     )
 
 
-def sum_and_gram(kept, other):
-    rows, columns = kept.shape
+def sum_and_gram(mine, other):
+    rows, columns = mine.shape
     return pl.pallas_call(
         gram_kernel,
         out_shape=(
-            jax.ShapeDtypeStruct((rows, columns), jnp.float32),
-            jax.ShapeDtypeStruct((columns, columns), jnp.float32),
+            jax.ShapeDtypeStruct((rows // 2, columns), jnp.float32),
+            jax.ShapeDtypeStruct((columns, columns // 2), jnp.float32),
         ),
         in_specs=[VMEM, VMEM],
         out_specs=(VMEM, VMEM),
+        scratch_shapes=[pltpu.VMEM((rows, columns), jnp.float32)],
         compiler_params=pltpu.CompilerParams(vmem_limit_bytes=24 * MIB),
         name="sum_and_gram",
-    )(kept, other)
+    )(mine, other)
 
 
 def matmul(a, b, precision):
@@ -95,14 +221,17 @@
     )
 
 
-def factor_kernel(total_rows, gram_ref, own_ref, basis_ref, factor_ref, scaled, inverse):
-    n = gram_ref.shape[0]
+def factor_kernel(total_rows, gram_ref, own_ref, basis_ref, factor_ref, whole, scaled, inverse):
+    n = factor_ref.shape[0]
+    width = gram_ref.shape[-1]
+    for c in range(n // width):
+        whole[:, c * width : (c + 1) * width] = gram_ref[:, c].reshape(n, width)
     row_ids = lax.broadcasted_iota(jnp.int32, (n, n), 0)
     col_ids = lax.broadcasted_iota(jnp.int32, (n, n), 1)
     diagonal = row_ids == col_ids
     identity = diagonal.astype(jnp.float32)
     half = jnp.where(row_ids > col_ids, 1.0, jnp.where(diagonal, 0.5, 0.0))
-    gram = gram_ref[...]
+    gram = whole[...]
     on_diagonal = jnp.where(diagonal, gram, 0.0)
     down = jnp.sqrt(jnp.sum(on_diagonal, axis=1, keepdims=True))
     across = jnp.sqrt(jnp.sum(on_diagonal, axis=0, keepdims=True))
@@ -145,7 +274,7 @@
             return carry
 
         lax.fori_loop(0, n, eliminate, 0)
-        scaled[...] = gram_ref[...] * up_down * up_across
+        scaled[...] = whole[...] * up_down * up_across
 
     w = inverse[...]
     root_rows = jnp.sqrt(jnp.float32(total_rows))
@@ -155,7 +284,7 @@
 
 
 def factor_and_basis(total_rows, gram, own):
-    columns = gram.shape[0]
+    columns = own.shape[1]
     return pl.pallas_call(
         functools.partial(factor_kernel, total_rows),
         out_shape=(
@@ -164,47 +293,69 @@
         ),
         in_specs=[VMEM, VMEM],
         out_specs=(VMEM, VMEM),
-        scratch_shapes=[pltpu.VMEM((columns, columns), jnp.float32)] * 2,
+        scratch_shapes=[pltpu.VMEM((columns, columns), jnp.float32)] * 3,
         compiler_params=pltpu.CompilerParams(vmem_limit_bytes=24 * MIB),
         name="factor_and_basis",
     )(gram, own)
 
 
-def sum_everywhere(gram, axes, devices):
-    columns = gram.shape[0]
-    if columns % devices:
-        return lax.psum(gram, axes)
-    pieces = gram.reshape(devices, columns // devices, columns)
-    pieces = lax.all_to_all(pieces, axes, split_axis=0, concat_axis=0, tiled=True)
-    return lax.all_gather(jnp.sum(pieces, axis=0), axes, axis=0, tiled=True)
+def spread(piece, axes, devices):
+    copies = jnp.broadcast_to(piece[None], (devices, *piece.shape))
+    return lax.all_to_all(copies, axes, split_axis=0, concat_axis=0, tiled=True)
+
+
+def exchange(pieces, rows):
+    groups = [list(range(rows // 2)), list(range(rows // 2, rows))]
+    return lax.all_to_all(pieces, "rows", split_axis=0, concat_axis=0, axis_index_groups=groups, tiled=True)
+
+
+def fetch(sketch, block_cols, counts, slots, width):
+    rows, cols = lax.axis_size("rows"), lax.axis_size("cols")
+    members = rows // 2
+    height = width // members
+    columns = sketch.shape[1]
+    sketch = sketch.reshape(-1, members, height, columns)
+    per = sketch.shape[0]
+    stripes = exchange(cut(sketch), rows).reshape(-1, height, columns)
+    devices = rows * cols
+    line = jnp.concatenate([block_cols, counts, jnp.zeros((7,), jnp.int32)])
+    table = spread(line, ("rows", "cols"), devices)
+    places, numbers, most = plan(table, slots, per)
+    swap = [(r, (r + members) % rows) for r in range(rows)]
+    largest = min(per * members, slots * members, 128)
+
+    def with_other(count):
+        def run():
+            other = lax.ppermute(listed(numbers, stripes, count), "rows", swap)
+            return pick(places, stripes, other, members)
+
+        return run
+
+    levels = [level for level in LEVELS if level < largest]
+    level = sum((most[0, 0] > level).astype(jnp.int32) for level in levels)
+    picked = lax.switch(level, [with_other(count) for count in (*levels, largest)])
+    return exchange(picked, rows)
 
 
 def local(sketch, blocks, block_rows, block_cols, counts):
     slots, width, _ = blocks.shape
     columns = sketch.shape[1]
-    rows = lax.axis_size("rows")
-    cols = lax.axis_size("cols")
-    height = width // rows
-    stripes = sketch.reshape(-1, rows, height, columns).swapaxes(0, 1)
-    stripes = lax.all_to_all(stripes, "rows", split_axis=0, concat_axis=0, tiled=True)
-    stripes = stripes.reshape(-1, height, columns)
-    wanted = lax.all_gather(block_cols, "rows", axis=0, tiled=True)
-    sent = pick(wanted, stripes).reshape(rows, slots, height, columns)
-    chosen = lax.all_to_all(sent, "rows", split_axis=0, concat_axis=0, tiled=True)
-    if height % 16:
+    rows, cols = lax.axis_size("rows"), lax.axis_size("cols")
+    chosen = fetch(sketch, block_cols, counts, slots, width)
+    if chosen.shape[2] % 16:
         chosen = chosen.swapaxes(0, 1).reshape(1, slots, width, columns)
     partial_rows = block_products(block_rows, counts, blocks, chosen)
-    share = RB * width // cols
-    me = lax.axis_index("cols")
     if cols == 2:
-        kept = lax.dynamic_slice_in_dim(partial_rows, me * share, share, 0)
-        given = lax.dynamic_slice_in_dim(partial_rows, (1 - me) * share, share, 0)
-        other = lax.ppermute(given, "cols", [(0, 1), (1, 0)])
+        other = lax.ppermute(partial_rows, "cols", [(0, 1), (1, 0)])
+        own, gram = sum_and_gram(partial_rows, other)
+        pieces = gram.reshape(rows, -1, columns // 2)
+        pieces = lax.all_to_all(pieces, "rows", split_axis=0, concat_axis=0, tiled=True)
+        gram = spread(jnp.sum(pieces, axis=0), ("rows", "cols"), rows * cols)
+        gram = gram.reshape(rows, cols, -1, columns // 2)
     else:
-        kept = lax.psum_scatter(partial_rows, "cols", scatter_dimension=0, tiled=True)
-        other = jnp.zeros_like(kept)
-    own, gram = sum_and_gram(kept, other)
-    gram = sum_everywhere(gram, ("rows", "cols"), rows * cols)
+        own = lax.psum_scatter(partial_rows, "cols", scatter_dimension=0, tiled=True)
+        gram = lax.psum(matmul(own.T, own, HIGHEST), ("rows", "cols"))
+        gram = gram.reshape(1, 1, columns, columns)
     return factor_and_basis(RB * width * rows, gram, own)
 
 

time: 212 us -> 242 us (1.14)
  Pallas kernels: 65.9 us -> 135 us
  blocking collectives: 102 us -> 44.9 us
  waiting for transfers between devices: 24.5 us -> 41.1 us
    pallas_call x2 -> x5, Pallas kernels: 2.49 us -> 70.2 us  [the longest x1 64.7 us: cut(): pl.pallas_call(cut_kernel, out_shape=jax.ShapeDtypeStruct((pieces, blocks...]
    unnamed x1 -> x0, blocking collectives: 46.9 us -> none
    all_gather x1 -> x0, blocking collectives: 39 us -> none  [sum_everywhere(): return lax.all_gather(jnp.sum(pieces, axis=0), axes, axis=0, tiled=True)]
    all_to_all x1 -> x3, blocking collectives: 16.2 us -> 44.9 us  [the longest x1 21.5 us: exchange(): lax.all_to_all(pieces, 'rows', split_axis=0, concat_axis=0, axis_index_gr...]
    ppermute x1 -> x2, waiting for transfers between devices: 1.9 us -> 19 us  [the longest x1 16.4 us: run(): other = lax.ppermute(listed(numbers, stripes, count), 'rows', swap)]
    reshape x1 -> x0, local copies, waits for them, and re-layouts: 3.16 us -> none  [local(): stripes = sketch.reshape(-1, rows, height, columns).swapaxes(0, 1)]
    ppermute x1 -> x2, starting transfers between devices: 0.07 us -> 2.6 us  [the longest x1 2.53 us: run(): other = lax.ppermute(listed(numbers, stripes, count), 'rows', swap)]
  transfers between devices with their start and end apart: 3 -> 4, of which waited for: 2 -> 3; matrix products, arithmetic and copies ran while one was open for 0% -> 0% of each run, Pallas kernels for 0% -> 27%
where the time goes in v3:
time: 242 us; the launch traced here: 241 us
  Pallas kernels  135 us (56%)
  blocking collectives  44.9 us (19%)
  waiting for transfers between devices  41.1 us (17%)
  starting transfers between devices  14.7 us (6%)
  between operations  2.68 us (1%)
  local copies, waits for them, and re-layouts  2.45 us (1%)
    pallas_call x1, Pallas kernels, cut(): pl.pallas_call(cut_kernel, out_shape=jax.ShapeDtypeStruct((pieces, blocks...  64.7 us
    pallas_call x1, Pallas kernels, factor_and_basis(): pl.pallas_call(functools.partial(factor_kernel, total_rows), out_shape=(j...  62.6 us
    all_to_all x1, waiting for transfers between devices, exchange(): lax.all_to_all(pieces, 'rows', split_axis=0, concat_axis=0, axis_index_gr...  22 us
    all_to_all x1, blocking collectives, exchange(): lax.all_to_all(pieces, 'rows', split_axis=0, concat_axis=0, axis_index_gr...  21.5 us
    ppermute x1, waiting for transfers between devices, run(): other = lax.ppermute(listed(numbers, stripes, count), 'rows', swap)  16.4 us
    all_to_all x1, blocking collectives, spread(): return lax.all_to_all(copies, axes, split_axis=0, concat_axis=0, tiled=True)  12.5 us
    all_to_all x1, blocking collectives, local(): lax.all_to_all(pieces, 'rows', split_axis=0, concat_axis=0, tiled=True)  10.9 us
    all_to_all x1, starting transfers between devices, spread(): return lax.all_to_all(copies, axes, split_axis=0, concat_axis=0, tiled=True)  7.3 us
  transfers between devices with their start and end apart: 4, of which 3 were waited for; matrix products, arithmetic and copies ran while one was open for 0% of the time, Pallas kernels for 27%

profile of v3, /device:TPU:0, one launch (start us, length us, event | category | flops | bytes accessed | tf_op | source)
XLA Modules:
  0.0 241.2 jit_solution(18406687061578363589)
XLA Ops:
  1.3 0.7 pad_add_fusion
  2.0 0.6 broadcast_in_dim.4
  2.6 7.3 %all-to-all-start = ((s32[32,1,16]{2,1,0:T(1,128)}), s32[32,1,16]{2,1,0:T(1,128)S(1)}, u32[]{:S(2)}, u32[]{:S(2)}) async-start(s32[32,1,16]{2,1,0:T(1,128)} %broadcast_in_dim.4), calls=%async_computation | async-start | bytes 32768 | tf_op jit(solution)/shard_map/all_to_all | solution.py:304
  9.9 64.7 %cut_stripes.1 = bf16[8,16,32,256]{3,2,1,0:T(8,128)(2,1)} custom-call(bf16[16,8,32,256]{3,2,1,0:T(8,128)(2,1)} %bitcast.11), custom_call_target="tpu_custom_call" | custom-call | tf_op jit(solution)/shard_map/cut_stripes/pallas_call | solution.py:32
  74.7 0.0 all-to-all-done
  74.7 0.0 copy-start.2
  74.7 0.6 copy-done.2
  75.3 4.8 %all-to-all-start.1 = ((bf16[8,16,32,256]{3,2,1,0:T(8,128)(2,1)}), bf16[8,16,32,256]{3,2,1,0:T(8,128)(2,1)S(1)}, u32[]{:S(2)}, u32[]{:S(2)}) async-start(bf16[8,16,32,256]{3,2,1,0:T(8,128)(2,1)} %cut_stripes.1), calls=%async_computation.1 | async-start | bytes 4194304 | tf_op jit(solution)/shard_map/all_to_all | solution.py:309
  80.1 1.6 plan.1
  81.7 1.2 slice.4
  84.2 22.0 %all-to-all-done.1 = bf16[8,16,32,256]{3,2,1,0:T(8,128)(2,1)S(1)} async-done(((bf16[8,16,32,256]{3,2,1,0:T(8,128)(2,1)}), bf16[8,16,32,256]{3,2,1,0:T(8,128)(2,1)S(1)}, u32[]{:S(2)}, u32[]{:S(2)}) %all-to-all-start.1) | async-done | bytes 2097184 | tf_op jit(solution)/shard_map/all_to_all | solution.py:309
  106.2 21.4 %conditional.1 = (bf16[8,8,32,256]{3,2,1,0:T(8,128)(2,1)S(1)}) conditional(s32[]{:T(128)} %bitcast.1, (s32[8,128]{1,0:T(8,128)S(1)}, bf16[128,32,256]{2,1,0:T(8,128)(2,1)S(1)}, s32[32,8]{1,0:T(8,128)S(1)}) %tuple.20, (s32[8,128]{1,0:T(8,128)S(1)}, bf16[128,32,256]{2,1,0:T(8,128)(2,1)S(1)}, s32[32,8]{1,0:T(8,128)S(1)}) %tuple.21, ...), branch_computations={%region_0.0_spmd, %region_1.0_spmd, %region_2.0_spmd} | conditional | bytes 4194352 | solution.py:336
  106.2 0.6 listed_stripes.4
  106.9 2.5 %collective-permute-start.1 = (bf16[24,32,256]{2,1,0:T(8,128)(2,1)S(1)}, bf16[24,32,256]{2,1,0:T(8,128)(2,1)S(1)}, u32[]{:S(2)}, u32[]{:S(2)}) collective-permute-start(bf16[24,32,256]{2,1,0:T(8,128)(2,1)S(1)} %listed_stripes.4), channel_id=1, source_target_pairs={{0,16},{2,18},{4,20},{6,22},{8,24},{10,26},{12,28},{14,30},{16,0},... | collective-permute-start | bytes 1179656 | tf_op jit(solution)/shard_map/cond/branch_1_fun/ppermute | solution.py:329
  109.4 16.4 %collective-permute-done.1.other_ref = bf16[24,32,256]{2,1,0:T(8,128)(2,1)S(1)} collective-permute-done((bf16[24,32,256]{2,1,0:T(8,128)(2,1)S(1)}, bf16[24,32,256]{2,1,0:T(8,128)(2,1)S(1)}, u32[]{:S(2)}, u32[]{:S(2)}) %collective-permute-start.1) | collective-permute-done | bytes 393248 | tf_op jit(solution)/shard_map/cond/branch_1_fun/ppermute | solution.py:329
  125.8 1.8 pick_stripes.4
  127.6 0.0 copy-start
  127.7 0.0 copy-start.1
  127.7 21.5 %all_to_all.28.chosen_ref = bf16[8,8,32,256]{3,2,1,0:T(8,128)(2,1)S(1)} all-to-all(bf16[8,8,32,256]{3,2,1,0:T(8,128)(2,1)S(1)} %get-tuple-element.43), channel_id=1, replica_groups={{0,2,4,6,8,10,12,14},{16,18,20,22,24,26,28,30},{1,3,5,7,9,11,13,15},{17..., dimensions={0} | all-to-all | bytes 2097152 | tf_op jit(solution)/shard_map/all_to_all | solution.py:309
  149.1 0.0 copy-done
  149.1 0.0 copy-done.1
  149.1 1.9 block_products.1.mine_ref
  151.0 0.1 collective-permute-start.3
  151.1 2.6 %collective-permute-done.3.other_ref = f32[1024,256]{1,0:T(8,128)S(1)} collective-permute-done((f32[1024,256]{1,0:T(8,128)S(1)}, f32[1024,256]{1,0:T(8,128)S(1)}, u32[]{:S(2)}, u32[]{:S(2)}) %collective-permute-start.3) | collective-permute-done | bytes 1048608 | tf_op jit(solution)/shard_map/ppermute | solution.py:349
  153.7 1.4 sum_and_gram.1
  155.2 10.9 %all_to_all.29 = f32[16,16,128]{2,1,0:T(8,128)S(1)} all-to-all(f32[16,16,128]{2,1,0:T(8,128)S(1)} %bitcast.7), channel_id=1, replica_groups=mesh['rows'=16,'cols'=2] {'rows'}, dimensions={0} | all-to-all | bytes 262144 | tf_op jit(solution)/shard_map/all_to_all | solution.py:352
  166.1 12.5 %all_to_all.30 = f32[32,16,128]{2,1,0:T(8,128)S(1)} all-to-all(f32[32,16,128]{2,1,0:T(8,128)S(1)} %broadcast_in_dim.5), channel_id=1, replica_groups=mesh['rows'=16,'cols'=2] {'rows','cols'}, dimensions={0} | all-to-all | bytes 524288 | tf_op jit(solution)/shard_map/all_to_all | solution.py:304
  178.6 62.6 %factor_and_basis.1 = (f32[512,256]{1,0:T(8,128)}, f32[256,256]{1,0:T(8,128)}) custom-call(f32[16,2,16,128]{3,2,1,0:T(8,128)S(1)} %bitcast.6, f32[512,256]{1,0:T(8,128)S(1)} %get-tuple-element.42.own_ref), custom_call_target="tpu_custom_call" | custom-call | tf_op jit(solution)/shard_map/factor_and_basis/pallas_call | solution.py:288
  (3 shorter events, 0.0 us)
Async XLA Ops:
  2.6 72.0 %all-to-all-start = ((s32[32,1,16]{2,1,0:T(1,128)}), s32[32,1,16]{2,1,0:T(1,128)S(1)}, u32[]{:S(2)}, u32[]{:S(2)}) async-start(s32[32,1,16]{2,1,0:T(1,128)} %broadcast_in_dim.4), calls=%async_computation | async-start | bytes 32768 | tf_op jit(solution)/shard_map/all_to_all | solution.py:304
  74.7 0.6 copy-start.2
  75.3 31.0 %all-to-all-start.1 = ((bf16[8,16,32,256]{3,2,1,0:T(8,128)(2,1)}), bf16[8,16,32,256]{3,2,1,0:T(8,128)(2,1)S(1)}, u32[]{:S(2)}, u32[]{:S(2)}) async-start(bf16[8,16,32,256]{3,2,1,0:T(8,128)(2,1)} %cut_stripes.1), calls=%async_computation.1 | async-start | bytes 4194304 | tf_op jit(solution)/shard_map/all_to_all | solution.py:309
  106.9 18.9 %collective-permute-start.1 = (bf16[24,32,256]{2,1,0:T(8,128)(2,1)S(1)}, bf16[24,32,256]{2,1,0:T(8,128)(2,1)S(1)}, u32[]{:S(2)}, u32[]{:S(2)}) collective-permute-start(bf16[24,32,256]{2,1,0:T(8,128)(2,1)S(1)} %listed_stripes.4), channel_id=1, source_target_pairs={{0,16},{2,18},{4,20},{6,22},{8,24},{10,26},{12,28},{14,30},{16,0},... | collective-permute-start | bytes 1179656 | tf_op jit(solution)/shard_map/cond/branch_1_fun/ppermute | solution.py:329
  127.6 21.5 %copy-start = (bf16[8,256,256]{2,1,0:T(8,128)(2,1)S(1)}, bf16[8,256,256]{2,1,0:T(8,128)(2,1)}, u32[]{:S(2)}) copy-start(bf16[8,256,256]{2,1,0:T(8,128)(2,1)} %blocks_ref.1) | copy-start | bytes 3145732
  127.7 21.5 %copy-start.1 = (s32[8]{0:T(128)S(1)}, s32[8]{0:T(128)}, u32[]{:S(2)}) copy-start(s32[8]{0:T(128)} %rows_ref.1) | copy-start | bytes 100
  151.0 2.7 %collective-permute-start.3 = (f32[1024,256]{1,0:T(8,128)S(1)}, f32[1024,256]{1,0:T(8,128)S(1)}, u32[]{:S(2)}, u32[]{:S(2)}) collective-permute-start(f32[1024,256]{1,0:T(8,128)S(1)} %block_products.1.mine_ref), channel_id=1, source_target_pairs={{0,1},{1,0},{2,3},{3,2},{4,5},{5,4},{6,7},{7,6},{8,9},{9,8},{10,11... | collective-permute-start | bytes 3145736 | tf_op jit(solution)/shard_map/ppermute | solution.py:349

commit v4 on v3

--- a/solution.py
+++ b/solution.py
@@ -14,38 +14,43 @@
 MIB = 1024 * 1024
 
 
-LEVELS = (16, 24)
-
-
-def cut_kernel(sketch_ref, out_ref, sems):
-    copies = [
-        pltpu.make_async_copy(sketch_ref.at[:, j], out_ref.at[j], sems.at[j]) for j in range(out_ref.shape[0])
-    ]
-    for copy in copies:
-        copy.start()
-    for copy in copies:
-        copy.wait()
-
-
-def cut(sketch):
-    blocks, pieces, height, columns = sketch.shape
+LEVELS = (12, 14, 16, 18, 20, 22, 24)
+
+
+def cut_kernel(cols_ref, counts_ref, sketch_ref, table_ref, *out_refs):
+    members = len(out_refs)
+    me = lax.axis_index("rows") % members
+    for d in range(members):
+        out_refs[d][...] = sketch_ref[:, me ^ d]
+    lane = lax.broadcasted_iota(jnp.int32, table_ref.shape, 2)
+    table = jnp.where(lane == cols_ref.shape[0], counts_ref[0], 0)
+    for s in range(cols_ref.shape[0]):
+        table = jnp.where(lane == s, cols_ref[s], table)
+    table_ref[...] = table
+
+
+def cut(block_cols, counts, sketch, devices):
+    blocks, members, height, columns = sketch.shape
     return pl.pallas_call(
         cut_kernel,
-        out_shape=jax.ShapeDtypeStruct((pieces, blocks, height, columns), sketch.dtype),
-        in_specs=[pl.BlockSpec(memory_space=pl.ANY)],
-        out_specs=pl.BlockSpec(memory_space=pl.ANY),
-        scratch_shapes=[pltpu.SemaphoreType.DMA((pieces,))],
+        out_shape=(
+            jax.ShapeDtypeStruct((devices, 1, 128), jnp.int32),
+            *[jax.ShapeDtypeStruct((blocks, height, columns), sketch.dtype)] * members,
+        ),
+        in_specs=[SMEM, SMEM, VMEM],
+        out_specs=(VMEM,) * (members + 1),
+        compiler_params=pltpu.CompilerParams(vmem_limit_bytes=24 * MIB),
         name="cut_stripes",
-    )(sketch)
-
-
-def plan_kernel(per, table_ref, places_ref, list_ref, most_ref):
+    )(block_cols, counts, sketch)
+
+
+def plan_kernel(per, levels, table_ref, places_ref, list_ref, level_ref):
     devices = table_ref.shape[0]
     slots = places_ref.shape[1]
     rows, cols = lax.axis_size("rows"), lax.axis_size("cols")
     panel = per * rows
     part = panel // 2
-    table = table_ref[...]
+    table = table_ref[:, 0, :]
     block = lax.broadcasted_iota(jnp.int32, (devices, panel), 1)
     device = lax.broadcasted_iota(jnp.int32, (devices, panel), 0)
     asked = [(table[:, s : s + 1] == block) & (s < table[:, slots : slots + 1]) for s in range(slots)]
@@ -58,8 +63,8 @@
             group = some & (device // (devices // 2) == h) & (device % cols == c)
             found = jnp.max(jnp.where(group, 1.0, 0.0), axis=0, keepdims=True)
             touched = jnp.where(line == h * cols + c, found, touched)
-    most = jnp.max(jnp.sum(touched, axis=1, keepdims=True), axis=0, keepdims=True)
-    most_ref[...] = jnp.broadcast_to(most, most_ref.shape).astype(jnp.int32)
+    most = jnp.max(jnp.sum(touched, axis=1, keepdims=True)).astype(jnp.int32)
+    level_ref[0] = sum((most > level).astype(jnp.int32) for level in levels)
     touched = touched.astype(jnp.bfloat16)
     first = lax.broadcasted_iota(jnp.int32, (panel, panel), 0)
     second = lax.broadcasted_iota(jnp.int32, (panel, panel), 1)
@@ -90,82 +95,99 @@
     list_ref[...] = jnp.broadcast_to(jnp.sum(listed, axis=0, keepdims=True), list_ref.shape)
 
 
-def plan(table, slots, per):
+def plan(table, slots, per, levels):
     devices = table.shape[0]
     return pl.pallas_call(
-        functools.partial(plan_kernel, per),
+        functools.partial(plan_kernel, per, levels),
         out_shape=(
             jax.ShapeDtypeStruct((devices, slots), jnp.int32),
             jax.ShapeDtypeStruct((8, 128), jnp.int32),
-            jax.ShapeDtypeStruct((8, 128), jnp.int32),
+            jax.ShapeDtypeStruct((1,), jnp.int32),
         ),
         in_specs=[VMEM],
-        out_specs=(VMEM, VMEM, VMEM),
+        out_specs=(VMEM, VMEM, SMEM),
+        compiler_params=pltpu.CompilerParams(vmem_limit_bytes=48 * MIB),
         name="plan",
     )(table)
 
 
-def list_kernel(list_ref, stripes_ref, out_ref):
+def list_kernel(list_ref, *refs):
+    *stripe_refs, out_ref, all_ref = refs
+    members = len(stripe_refs)
+    me = lax.axis_index("rows") % members
+    per = stripe_refs[0].shape[0]
+    for d in range(members):
+        all_ref[pl.ds((me ^ d) * per, per)] = stripe_refs[d][...]
     for k in range(out_ref.shape[0]):
-        out_ref[k] = stripes_ref[list_ref[0, k]]
+        out_ref[k] = all_ref[list_ref[0, k]]
 
 
 def listed(numbers, stripes, count):
+    per, height, columns = stripes[0].shape
     return pl.pallas_call(
         list_kernel,
-        out_shape=jax.ShapeDtypeStruct((count, *stripes.shape[1:]), stripes.dtype),
-        in_specs=[SMEM, VMEM],
-        out_specs=VMEM,
+        out_shape=(
+            jax.ShapeDtypeStruct((count, height, columns), stripes[0].dtype),
+            jax.ShapeDtypeStruct((len(stripes) * per, height, columns), stripes[0].dtype),
+        ),
+        in_specs=[SMEM] + [VMEM] * len(stripes),
+        out_specs=(VMEM, VMEM),
         compiler_params=pltpu.CompilerParams(vmem_limit_bytes=24 * MIB),
         name="listed_stripes",
-    )(numbers, stripes)
-
-
-def pick_kernel(places_ref, own_ref, other_ref, out_ref):
-    members, slots = out_ref.shape[:2]
+    )(numbers, *stripes)
+
+
+def pick_kernel(places_ref, own_ref, other_ref, *out_refs):
+    members = len(out_refs)
     rows, cols = lax.axis_size("rows"), lax.axis_size("cols")
     here = own_ref.shape[0]
-    half = lax.axis_index("rows") // (rows // 2)
+    me = lax.axis_index("rows")
     c = lax.axis_index("cols")
-
-    def body(m, carry):
-        device = (half * members + m) * cols + c
-        for s in range(slots):
+    for d in range(members):
+        out_ref = out_refs[d]
+        device = (me ^ d) * cols + c
+
+        def body(s, carry):
             place = places_ref[device, s]
 
             @pl.when(place < here)
             def _():
-                out_ref[m, s] = own_ref[jnp.minimum(place, here - 1)]
+                out_ref[s] = own_ref[jnp.minimum(place, here - 1)]
 
             @pl.when(place >= here)
             def _():
-                out_ref[m, s] = other_ref[jnp.clip(place - here, 0, other_ref.shape[0] - 1)]
-
-        return carry
-
-    lax.fori_loop(0, members, body, 0)
+                out_ref[s] = other_ref[jnp.clip(place - here, 0, other_ref.shape[0] - 1)]
+
+            return carry
+
+        lax.fori_loop(0, out_ref.shape[0], body, 0)
 
 
 def pick(places, own, other, members):
     return pl.pallas_call(
         pick_kernel,
-        out_shape=jax.ShapeDtypeStruct((members, places.shape[1], *own.shape[1:]), own.dtype),
+        out_shape=(jax.ShapeDtypeStruct((places.shape[1], *own.shape[1:]), own.dtype),) * members,
         in_specs=[SMEM, VMEM, VMEM],
-        out_specs=VMEM,
+        out_specs=(VMEM,) * members,
         compiler_params=pltpu.CompilerParams(vmem_limit_bytes=24 * MIB),
         name="pick_stripes",
     )(places, own, other)
 
 
-def product_kernel(rows_ref, counts_ref, blocks_ref, chosen_ref, out_ref):
+def product_kernel(rows_ref, counts_ref, blocks_ref, *refs):
+    *chosen_refs, out_ref, whole = refs
     slots, width, _ = blocks_ref.shape
     columns = out_ref.shape[1]
+    members = len(chosen_refs)
+    me = lax.axis_index("rows") % members
+    for d in range(members):
+        whole[me ^ d] = chosen_refs[d][...]
     out_ref[...] = jnp.zeros_like(out_ref)
     for s in range(slots):
 
         @pl.when(s < counts_ref[0])
         def _():
-            piece = chosen_ref[:, s].reshape(width, columns)
+            piece = whole[:, s].reshape(width, columns)
             product = jnp.dot(blocks_ref[s], piece, preferred_element_type=jnp.float32)
             at = pl.ds(pl.multiple_of(rows_ref[s] * width, width), width)
             out_ref[at, :] += product
@@ -173,15 +195,16 @@
 
 def block_products(block_rows, counts, blocks, chosen):
     _, width, _ = blocks.shape
-    columns = chosen.shape[-1]
+    columns = chosen[0].shape[-1]
     return pl.pallas_call(
         product_kernel,
         out_shape=jax.ShapeDtypeStruct((RB * width, columns), jnp.float32),
-        in_specs=[SMEM, SMEM, VMEM, VMEM],
+        in_specs=[SMEM, SMEM, VMEM] + [VMEM] * len(chosen),
         out_specs=VMEM,
+        scratch_shapes=[pltpu.VMEM((len(chosen), *chosen[0].shape), chosen[0].dtype)],
         compiler_params=pltpu.CompilerParams(vmem_limit_bytes=24 * MIB),
         name="block_products",
-    )(block_rows, counts, blocks, chosen)
+    )(block_rows, counts, blocks, *chosen)
 
 
 def gram_kernel(mine_ref, other_ref, own_ref, gram_ref, slab):
@@ -305,8 +328,9 @@
 
 
 def exchange(pieces, rows):
-    groups = [list(range(rows // 2)), list(range(rows // 2, rows))]
-    return lax.all_to_all(pieces, "rows", split_axis=0, concat_axis=0, axis_index_groups=groups, tiled=True)
+    return [pieces[0]] + [
+        lax.ppermute(piece, "rows", [(r, r ^ d) for r in range(rows)]) for d, piece in enumerate(pieces) if d
+    ]
 
 
 def fetch(sketch, block_cols, counts, slots, width):
@@ -316,24 +340,23 @@
     columns = sketch.shape[1]
     sketch = sketch.reshape(-1, members, height, columns)
     per = sketch.shape[0]
-    stripes = exchange(cut(sketch), rows).reshape(-1, height, columns)
     devices = rows * cols
-    line = jnp.concatenate([block_cols, counts, jnp.zeros((7,), jnp.int32)])
-    table = spread(line, ("rows", "cols"), devices)
-    places, numbers, most = plan(table, slots, per)
+    table, *stripes = cut(block_cols, counts, sketch, devices)
+    stripes = exchange(stripes, rows)
+    table = lax.all_to_all(table, ("rows", "cols"), split_axis=0, concat_axis=0, tiled=True)
     swap = [(r, (r + members) % rows) for r in range(rows)]
     largest = min(per * members, slots * members, 128)
+    levels = tuple(level for level in LEVELS if level < largest)
+    places, numbers, level = plan(table, slots, per, levels)
 
     def with_other(count):
         def run():
-            other = lax.ppermute(listed(numbers, stripes, count), "rows", swap)
-            return pick(places, stripes, other, members)
+            sent, own = listed(numbers, stripes, count)
+            return pick(places, own, lax.ppermute(sent, "rows", swap), members)
 
         return run
 
-    levels = [level for level in LEVELS if level < largest]
-    level = sum((most[0, 0] > level).astype(jnp.int32) for level in levels)
-    picked = lax.switch(level, [with_other(count) for count in (*levels, largest)])
+    picked = lax.switch(level[0], [with_other(count) for count in (*levels, largest)])
     return exchange(picked, rows)
 
 
@@ -342,8 +365,9 @@
     columns = sketch.shape[1]
     rows, cols = lax.axis_size("rows"), lax.axis_size("cols")
     chosen = fetch(sketch, block_cols, counts, slots, width)
-    if chosen.shape[2] % 16:
-        chosen = chosen.swapaxes(0, 1).reshape(1, slots, width, columns)
+    if chosen[0].shape[1] % 16:
+        order = lax.axis_index("rows") % len(chosen) ^ jnp.arange(len(chosen))
+        chosen = [jnp.stack(chosen)[order].swapaxes(0, 1).reshape(1, slots, width, columns)[0]]
     partial_rows = block_products(block_rows, counts, blocks, chosen)
     if cols == 2:
         other = lax.ppermute(partial_rows, "cols", [(0, 1), (1, 0)])

time: 242 us -> 168 us (0.69)
  Pallas kernels: 135 us -> 71.6 us
  waiting for transfers between devices: 41.1 us -> 26.3 us
  starting transfers between devices: 14.7 us -> 21.3 us
    pallas_call x4, Pallas kernels: 68.7 us -> 5.89 us  [the longest x1 2.22 us: pick(): pl.pallas_call(pick_kernel, out_shape=(jax.ShapeDtypeStruct((places.shape...]
    all_to_all x2 -> x0, waiting for transfers between devices: 22 us -> none  [the longest x1 22 us: exchange(): lax.all_to_all(pieces, 'rows', split_axis=0, concat_axis=0, axis_index_gr...]
    ppermute x1 -> x15, starting transfers between devices: 2.53 us -> 21.3 us  [the longest x14 20.5 us: exchange(): lax.ppermute(piece, 'rows', [(r, r ^ d) for r in range(rows)])]
    all_to_all x2 -> x0, starting transfers between devices: 12.1 us -> none  [the longest x1 7.3 us: spread(): return lax.all_to_all(copies, axes, split_axis=0, concat_axis=0, tiled=True)]
    ppermute x1 -> x15, waiting for transfers between devices: 16.4 us -> 23.7 us  [the longest x1 12.4 us: run(): return pick(places, own, lax.ppermute(sent, 'rows', swap), members)]
    all_to_all x1, blocking collectives: 21.5 us -> 18.7 us  [fetch(): lax.all_to_all(table, ('rows', 'cols'), split_axis=0, concat_axis=0, tile...]
  transfers between devices with their start and end apart: 4 -> 16, of which waited for: 3 -> 9; matrix products, arithmetic and copies ran while one was open for 0% -> 0% of each run, Pallas kernels for 27% -> 1%
where the time goes in v4:
time: 168 us; the launch traced here: 167 us
  Pallas kernels  71.6 us (43%)
  blocking collectives  43 us (26%)
  waiting for transfers between devices  26.3 us (16%)
  starting transfers between devices  21.3 us (13%)
  local copies, waits for them, and re-layouts  2.27 us (1%)
  between operations  2.06 us (1%)
    pallas_call x1, Pallas kernels, factor_and_basis(): pl.pallas_call(functools.partial(factor_kernel, total_rows), out_shape=(j...  62.6 us
    ppermute x14, starting transfers between devices, exchange(): lax.ppermute(piece, 'rows', [(r, r ^ d) for r in range(rows)])  20.5 us
    all_to_all x1, blocking collectives, fetch(): lax.all_to_all(table, ('rows', 'cols'), split_axis=0, concat_axis=0, tile...  18.7 us
    all_to_all x1, blocking collectives, spread(): return lax.all_to_all(copies, axes, split_axis=0, concat_axis=0, tiled=True)  12.5 us
    ppermute x1, waiting for transfers between devices, run(): return pick(places, own, lax.ppermute(sent, 'rows', swap), members)  12.4 us
    all_to_all x1, blocking collectives, local(): lax.all_to_all(pieces, 'rows', split_axis=0, concat_axis=0, tiled=True)  11.8 us
    ppermute x14, waiting for transfers between devices, exchange(): lax.ppermute(piece, 'rows', [(r, r ^ d) for r in range(rows)])  11.3 us
  transfers between devices with their start and end apart: 16, of which 9 were waited for; matrix products, arithmetic and copies ran while one was open for 0% of the time, Pallas kernels for 1%

profile of v4, /device:TPU:0, one launch (start us, length us, event | category | flops | bytes accessed | tf_op | source)
XLA Modules:
  0.0 166.6 jit_solution(7816378581342604786)
XLA Ops:
  1.3 0.0 copy-start
  1.3 1.6 copy-done
  2.9 0.0 copy-start.3
  2.9 0.7 copy-done.3
  3.5 0.7 cut_stripes.1
  4.2 3.0 %collective-permute-start.8 = (bf16[16,32,256]{2,1,0:T(8,128)(2,1)S(1)}, bf16[16,32,256]{2,1,0:T(8,128)(2,1)S(1)}, u32[]{:S(2)}, u32[]{:S(2)}) collective-permute-start(bf16[16,32,256]{2,1,0:T(8,128)(2,1)S(1)} %get-tuple-element.284), channel_id=1, source_target_pairs={{0,2},{2,0},{4,6},{6,4},{8,10},{10,8},{12,14},{14,12},{16,18},{18,... | collective-permute-start | bytes 786440 | tf_op jit(solution)/shard_map/ppermute | solution.py:332
  7.2 1.5 collective-permute-start.9
  8.8 0.0 collective-permute-start.10
  8.8 2.0 %collective-permute-start.11 = (bf16[16,32,256]{2,1,0:T(8,128)(2,1)S(1)}, bf16[16,32,256]{2,1,0:T(8,128)(2,1)S(1)}, u32[]{:S(2)}, u32[]{:S(2)}) collective-permute-start(bf16[16,32,256]{2,1,0:T(8,128)(2,1)S(1)} %get-tuple-element.287), channel_id=1, source_target_pairs={{0,8},{2,10},{4,12},{6,14},{8,0},{10,2},{12,4},{14,6},{16,24},{18,... | collective-permute-start | bytes 786440 | tf_op jit(solution)/shard_map/ppermute | solution.py:332
  10.8 1.4 collective-permute-start.12
  12.2 2.2 %collective-permute-done.8 = bf16[16,32,256]{2,1,0:T(8,128)(2,1)S(1)} collective-permute-done((bf16[16,32,256]{2,1,0:T(8,128)(2,1)S(1)}, bf16[16,32,256]{2,1,0:T(8,128)(2,1)S(1)}, u32[]{:S(2)}, u32[]{:S(2)}) %collective-permute-start.8) | collective-permute-done | bytes 262176 | tf_op jit(solution)/shard_map/ppermute | solution.py:332
  14.4 3.1 %collective-permute-start.13 = (bf16[16,32,256]{2,1,0:T(8,128)(2,1)S(1)}, bf16[16,32,256]{2,1,0:T(8,128)(2,1)S(1)}, u32[]{:S(2)}, u32[]{:S(2)}) collective-permute-start(bf16[16,32,256]{2,1,0:T(8,128)(2,1)S(1)} %get-tuple-element.289), channel_id=1, source_target_pairs={{0,12},{2,14},{4,8},{6,10},{8,4},{10,6},{12,0},{14,2},{16,28},{18,... | collective-permute-start | bytes 786440 | tf_op jit(solution)/shard_map/ppermute | solution.py:332
  17.5 0.0 collective-permute-done.9
  17.5 1.8 %collective-permute-start.14 = (bf16[16,32,256]{2,1,0:T(8,128)(2,1)S(1)}, bf16[16,32,256]{2,1,0:T(8,128)(2,1)S(1)}, u32[]{:S(2)}, u32[]{:S(2)}) collective-permute-start(bf16[16,32,256]{2,1,0:T(8,128)(2,1)S(1)} %get-tuple-element.290), channel_id=1, source_target_pairs={{0,14},{2,12},{4,10},{6,8},{8,6},{10,4},{12,2},{14,0},{16,30},{18,... | collective-permute-start | bytes 786440 | tf_op jit(solution)/shard_map/ppermute | solution.py:332
  19.2 18.7 %all_to_all.15.table_ref = s32[32,1,128]{2,1,0:T(1,128)S(1)} all-to-all(s32[32,1,128]{2,1,0:T(1,128)S(1)} %get-tuple-element.280), channel_id=1, replica_groups=mesh['rows'=16,'cols'=2] {'rows','cols'}, dimensions={0} | all-to-all | bytes 32768 | tf_op jit(solution)/shard_map/all_to_all | solution.py:346
  38.0 2.2 %plan.1 = (s32[32,8]{1,0:T(8,128)S(1)}, s32[8,128]{1,0:T(8,128)S(1)}, s32[1]{0:T(128)}) custom-call(s32[32,1,128]{2,1,0:T(1,128)S(1)} %all_to_all.15.table_ref), custom_call_target="tpu_custom_call" | custom-call | tf_op jit(solution)/shard_map/plan/pallas_call | solution.py:100
  40.8 0.0 collective-permute-done.10
  40.8 0.0 collective-permute-done.11
  40.8 0.0 collective-permute-done.12
  40.9 0.0 collective-permute-done.13
  40.9 0.0 collective-permute-done.14
  40.9 0.0 copy-start.1
  40.9 0.0 copy-start.2
  40.9 16.2 %conditional.1 = ((bf16[8,32,256]{2,1,0:T(8,128)(2,1)S(1)}, bf16[8,32,256]{2,1,0:T(8,128)(2,1)S(1)}, bf16[8,32,256]{2,1,0:T(8,128)(2,1)S(1)}, bf16[8,32,256]{2,1...) conditional(s32[]{:T(128)} %bitcast.1, ...), branch_computations={%region_0.0_spmd, %region_1.0_spmd, %region_2.0_spmd, %region_3.0_... | conditional | bytes 4194352 | solution.py:359
  40.9 0.8 listed_stripes.9
  41.7 0.7 collective-permute-start.1
  42.4 12.4 %collective-permute-done.1.other_ref = bf16[14,32,256]{2,1,0:T(8,128)(2,1)S(1)} collective-permute-done((bf16[14,32,256]{2,1,0:T(8,128)(2,1)S(1)}, bf16[14,32,256]{2,1,0:T(8,128)(2,1)S(1)}, u32[]{:S(2)}, u32[]{:S(2)}) %collective-permute-start.1) | collective-permute-done | bytes 229408 | tf_op jit(solution)/shard_map/cond/branch_1_fun/ppermute | solution.py:355
  54.8 2.2 %pick_stripes.9 = (bf16[8,32,256]{2,1,0:T(8,128)(2,1)S(1)}, bf16[8,32,256]{2,1,0:T(8,128)(2,1)S(1)}, bf16[8,32,256]{2,1,0:T(8,128)(2,1)S(1)}, bf16[8,32,256]{2,1...) custom-call(s32[32,8]{1,0:T(8,128)S(1)} %get-tuple-element.172.place, ...), custom_call_target="tpu_custom_call" | custom-call | tf_op jit(solution)/shard_map/cond/branch_1_fun/pick_stripes/pallas_call | solution.py:167
  57.1 0.9 collective-permute-start.15
  58.0 0.5 collective-permute-start.16
  58.5 2.1 %collective-permute-start.17 = (bf16[8,32,256]{2,1,0:T(8,128)(2,1)S(1)}, bf16[8,32,256]{2,1,0:T(8,128)(2,1)S(1)}, u32[]{:S(2)}, u32[]{:S(2)}) collective-permute-start(bf16[8,32,256]{2,1,0:T(8,128)(2,1)S(1)} %get-tuple-element.295), channel_id=1, source_target_pairs={{0,6},{2,4},{4,2},{6,0},{8,14},{10,12},{12,10},{14,8},{16,22},{18,... | collective-permute-start | bytes 393224 | tf_op jit(solution)/shard_map/ppermute | solution.py:332
  60.7 0.0 collective-permute-start.18
  60.7 2.3 %collective-permute-start.19 = (bf16[8,32,256]{2,1,0:T(8,128)(2,1)S(1)}, bf16[8,32,256]{2,1,0:T(8,128)(2,1)S(1)}, u32[]{:S(2)}, u32[]{:S(2)}) collective-permute-start(bf16[8,32,256]{2,1,0:T(8,128)(2,1)S(1)} %get-tuple-element.297), channel_id=1, source_target_pairs={{0,10},{2,8},{4,14},{6,12},{8,2},{10,0},{12,6},{14,4},{16,26},{18,... | collective-permute-start | bytes 393224 | tf_op jit(solution)/shard_map/ppermute | solution.py:332
  63.0 0.5 collective-permute-done.15.refs_1_
  63.5 0.0 collective-permute-start.20
  63.5 1.2 collective-permute-done.16.refs_2_
  64.7 1.8 %collective-permute-start.21 = (bf16[8,32,256]{2,1,0:T(8,128)(2,1)S(1)}, bf16[8,32,256]{2,1,0:T(8,128)(2,1)S(1)}, u32[]{:S(2)}, u32[]{:S(2)}) collective-permute-start(bf16[8,32,256]{2,1,0:T(8,128)(2,1)S(1)} %get-tuple-element.299), channel_id=1, source_target_pairs={{0,14},{2,12},{4,10},{6,8},{8,6},{10,4},{12,2},{14,0},{16,30},{18,... | collective-permute-start | bytes 393224 | tf_op jit(solution)/shard_map/ppermute | solution.py:332
  66.5 0.5 collective-permute-done.17.refs_3_
  67.0 0.0 collective-permute-done.18.refs_4_
  67.1 3.1 %collective-permute-done.19.refs_5_ = bf16[8,32,256]{2,1,0:T(8,128)(2,1)S(1)} collective-permute-done((bf16[8,32,256]{2,1,0:T(8,128)(2,1)S(1)}, bf16[8,32,256]{2,1,0:T(8,128)(2,1)S(1)}, u32[]{:S(2)}, u32[]{:S(2)}) %collective-permute-start.19) | collective-permute-done | bytes 131104 | tf_op jit(solution)/shard_map/ppermute | solution.py:332
  70.2 2.2 %collective-permute-done.20.refs_6_ = bf16[8,32,256]{2,1,0:T(8,128)(2,1)S(1)} collective-permute-done((bf16[8,32,256]{2,1,0:T(8,128)(2,1)S(1)}, bf16[8,32,256]{2,1,0:T(8,128)(2,1)S(1)}, u32[]{:S(2)}, u32[]{:S(2)}) %collective-permute-start.20) | collective-permute-done | bytes 131104 | tf_op jit(solution)/shard_map/ppermute | solution.py:332
  72.4 1.5 collective-permute-done.21.refs_7_
  73.9 0.0 copy-done.1
  73.9 0.0 copy-done.2
  73.9 1.7 block_products.1.mine_ref
  75.6 0.1 collective-permute-start.22
  75.6 2.6 %collective-permute-done.22.other_ref = f32[1024,256]{1,0:T(8,128)S(1)} collective-permute-done((f32[1024,256]{1,0:T(8,128)S(1)}, f32[1024,256]{1,0:T(8,128)S(1)}, u32[]{:S(2)}, u32[]{:S(2)}) %collective-permute-start.22) | collective-permute-done | bytes 1048608 | tf_op jit(solution)/shard_map/ppermute | solution.py:373
  78.3 1.4 sum_and_gram.1
  79.7 11.8 %all_to_all.16 = f32[16,16,128]{2,1,0:T(8,128)S(1)} all-to-all(f32[16,16,128]{2,1,0:T(8,128)S(1)} %bitcast.6), channel_id=1, replica_groups=mesh['rows'=16,'cols'=2] {'rows'}, dimensions={0} | all-to-all | bytes 262144 | tf_op jit(solution)/shard_map/all_to_all | solution.py:376
  91.5 12.5 %all_to_all.17 = f32[32,16,128]{2,1,0:T(8,128)S(1)} all-to-all(f32[32,16,128]{2,1,0:T(8,128)S(1)} %broadcast_in_dim.2), channel_id=1, replica_groups=mesh['rows'=16,'cols'=2] {'rows','cols'}, dimensions={0} | all-to-all | bytes 524288 | tf_op jit(solution)/shard_map/all_to_all | solution.py:327
  104.1 62.6 %factor_and_basis.1 = (f32[512,256]{1,0:T(8,128)}, f32[256,256]{1,0:T(8,128)}) custom-call(f32[16,2,16,128]{3,2,1,0:T(8,128)S(1)} %bitcast.5, f32[512,256]{1,0:T(8,128)S(1)} %get-tuple-element.301.own_ref), custom_call_target="tpu_custom_call" | custom-call | tf_op jit(solution)/shard_map/factor_and_basis/pallas_call | solution.py:311
  (2 shorter events, 0.0 us)
Async XLA Ops:
  1.3 1.6 copy-start
  2.9 0.7 copy-start.3
  4.2 10.1 %collective-permute-start.8 = (bf16[16,32,256]{2,1,0:T(8,128)(2,1)S(1)}, bf16[16,32,256]{2,1,0:T(8,128)(2,1)S(1)}, u32[]{:S(2)}, u32[]{:S(2)}) collective-permute-start(bf16[16,32,256]{2,1,0:T(8,128)(2,1)S(1)} %get-tuple-element.284), channel_id=1, source_target_pairs={{0,2},{2,0},{4,6},{6,4},{8,10},{10,8},{12,14},{14,12},{16,18},{18,... | collective-permute-start | bytes 786440 | tf_op jit(solution)/shard_map/ppermute | solution.py:332
  7.2 10.2 %collective-permute-start.9 = (bf16[16,32,256]{2,1,0:T(8,128)(2,1)S(1)}, bf16[16,32,256]{2,1,0:T(8,128)(2,1)S(1)}, u32[]{:S(2)}, u32[]{:S(2)}) collective-permute-start(bf16[16,32,256]{2,1,0:T(8,128)(2,1)S(1)} %get-tuple-element.285), channel_id=1, source_target_pairs={{0,4},{2,6},{4,0},{6,2},{8,12},{10,14},{12,8},{14,10},{16,20},{18,... | collective-permute-start | bytes 786440 | tf_op jit(solution)/shard_map/ppermute | solution.py:332
  8.8 32.1 %collective-permute-start.10 = (bf16[16,32,256]{2,1,0:T(8,128)(2,1)S(1)}, bf16[16,32,256]{2,1,0:T(8,128)(2,1)S(1)}, u32[]{:S(2)}, u32[]{:S(2)}) collective-permute-start(bf16[16,32,256]{2,1,0:T(8,128)(2,1)S(1)} %get-tuple-element.286), channel_id=1, source_target_pairs={{0,6},{2,4},{4,2},{6,0},{8,14},{10,12},{12,10},{14,8},{16,22},{18,... | collective-permute-start | bytes 786440 | tf_op jit(solution)/shard_map/ppermute | solution.py:332
  8.8 32.1 %collective-permute-start.11 = (bf16[16,32,256]{2,1,0:T(8,128)(2,1)S(1)}, bf16[16,32,256]{2,1,0:T(8,128)(2,1)S(1)}, u32[]{:S(2)}, u32[]{:S(2)}) collective-permute-start(bf16[16,32,256]{2,1,0:T(8,128)(2,1)S(1)} %get-tuple-element.287), channel_id=1, source_target_pairs={{0,8},{2,10},{4,12},{6,14},{8,0},{10,2},{12,4},{14,6},{16,24},{18,... | collective-permute-start | bytes 786440 | tf_op jit(solution)/shard_map/ppermute | solution.py:332
  10.8 30.0 %collective-permute-start.12 = (bf16[16,32,256]{2,1,0:T(8,128)(2,1)S(1)}, bf16[16,32,256]{2,1,0:T(8,128)(2,1)S(1)}, u32[]{:S(2)}, u32[]{:S(2)}) collective-permute-start(bf16[16,32,256]{2,1,0:T(8,128)(2,1)S(1)} %get-tuple-element.288), channel_id=1, source_target_pairs={{0,10},{2,8},{4,14},{6,12},{8,2},{10,0},{12,6},{14,4},{16,26},{18,... | collective-permute-start | bytes 786440 | tf_op jit(solution)/shard_map/ppermute | solution.py:332
  14.4 26.5 %collective-permute-start.13 = (bf16[16,32,256]{2,1,0:T(8,128)(2,1)S(1)}, bf16[16,32,256]{2,1,0:T(8,128)(2,1)S(1)}, u32[]{:S(2)}, u32[]{:S(2)}) collective-permute-start(bf16[16,32,256]{2,1,0:T(8,128)(2,1)S(1)} %get-tuple-element.289), channel_id=1, source_target_pairs={{0,12},{2,14},{4,8},{6,10},{8,4},{10,6},{12,0},{14,2},{16,28},{18,... | collective-permute-start | bytes 786440 | tf_op jit(solution)/shard_map/ppermute | solution.py:332
  17.5 23.4 %collective-permute-start.14 = (bf16[16,32,256]{2,1,0:T(8,128)(2,1)S(1)}, bf16[16,32,256]{2,1,0:T(8,128)(2,1)S(1)}, u32[]{:S(2)}, u32[]{:S(2)}) collective-permute-start(bf16[16,32,256]{2,1,0:T(8,128)(2,1)S(1)} %get-tuple-element.290), channel_id=1, source_target_pairs={{0,14},{2,12},{4,10},{6,8},{8,6},{10,4},{12,2},{14,0},{16,30},{18,... | collective-permute-start | bytes 786440 | tf_op jit(solution)/shard_map/ppermute | solution.py:332
  40.9 33.0 %copy-start.1 = (bf16[8,256,256]{2,1,0:T(8,128)(2,1)S(1)}, bf16[8,256,256]{2,1,0:T(8,128)(2,1)}, u32[]{:S(2)}) copy-start(bf16[8,256,256]{2,1,0:T(8,128)(2,1)} %blocks_ref.1) | copy-start | bytes 3145732
  40.9 33.0 %copy-start.2 = (s32[8]{0:T(128)S(1)}, s32[8]{0:T(128)}, u32[]{:S(2)}) copy-start(s32[8]{0:T(128)} %rows_ref.1) | copy-start | bytes 100
  41.7 13.1 %collective-permute-start.1 = (bf16[14,32,256]{2,1,0:T(8,128)(2,1)S(1)}, bf16[14,32,256]{2,1,0:T(8,128)(2,1)S(1)}, u32[]{:S(2)}, u32[]{:S(2)}) collective-permute-start(bf16[14,32,256]{2,1,0:T(8,128)(2,1)S(1)} %get-tuple-element.183), channel_id=1, source_target_pairs={{0,16},{2,18},{4,20},{6,22},{8,24},{10,26},{12,28},{14,30},{16,0},... | collective-permute-start | bytes 688136 | tf_op jit(solution)/shard_map/cond/branch_1_fun/ppermute | solution.py:355
  57.1 6.4 %collective-permute-start.15 = (bf16[8,32,256]{2,1,0:T(8,128)(2,1)S(1)}, bf16[8,32,256]{2,1,0:T(8,128)(2,1)S(1)}, u32[]{:S(2)}, u32[]{:S(2)}) collective-permute-start(bf16[8,32,256]{2,1,0:T(8,128)(2,1)S(1)} %get-tuple-element.293), channel_id=1, source_target_pairs={{0,2},{2,0},{4,6},{6,4},{8,10},{10,8},{12,14},{14,12},{16,18},{18,... | collective-permute-start | bytes 393224 | tf_op jit(solution)/shard_map/ppermute | solution.py:332
  58.0 6.7 %collective-permute-start.16 = (bf16[8,32,256]{2,1,0:T(8,128)(2,1)S(1)}, bf16[8,32,256]{2,1,0:T(8,128)(2,1)S(1)}, u32[]{:S(2)}, u32[]{:S(2)}) collective-permute-start(bf16[8,32,256]{2,1,0:T(8,128)(2,1)S(1)} %get-tuple-element.294), channel_id=1, source_target_pairs={{0,4},{2,6},{4,0},{6,2},{8,12},{10,14},{12,8},{14,10},{16,20},{18,... | collective-permute-start | bytes 393224 | tf_op jit(solution)/shard_map/ppermute | solution.py:332
  58.5 8.5 %collective-permute-start.17 = (bf16[8,32,256]{2,1,0:T(8,128)(2,1)S(1)}, bf16[8,32,256]{2,1,0:T(8,128)(2,1)S(1)}, u32[]{:S(2)}, u32[]{:S(2)}) collective-permute-start(bf16[8,32,256]{2,1,0:T(8,128)(2,1)S(1)} %get-tuple-element.295), channel_id=1, source_target_pairs={{0,6},{2,4},{4,2},{6,0},{8,14},{10,12},{12,10},{14,8},{16,22},{18,... | collective-permute-start | bytes 393224 | tf_op jit(solution)/shard_map/ppermute | solution.py:332
  60.7 6.4 %collective-permute-start.18 = (bf16[8,32,256]{2,1,0:T(8,128)(2,1)S(1)}, bf16[8,32,256]{2,1,0:T(8,128)(2,1)S(1)}, u32[]{:S(2)}, u32[]{:S(2)}) collective-permute-start(bf16[8,32,256]{2,1,0:T(8,128)(2,1)S(1)} %get-tuple-element.296), channel_id=1, source_target_pairs={{0,8},{2,10},{4,12},{6,14},{8,0},{10,2},{12,4},{14,6},{16,24},{18,... | collective-permute-start | bytes 393224 | tf_op jit(solution)/shard_map/ppermute | solution.py:332
  60.7 9.5 %collective-permute-start.19 = (bf16[8,32,256]{2,1,0:T(8,128)(2,1)S(1)}, bf16[8,32,256]{2,1,0:T(8,128)(2,1)S(1)}, u32[]{:S(2)}, u32[]{:S(2)}) collective-permute-start(bf16[8,32,256]{2,1,0:T(8,128)(2,1)S(1)} %get-tuple-element.297), channel_id=1, source_target_pairs={{0,10},{2,8},{4,14},{6,12},{8,2},{10,0},{12,6},{14,4},{16,26},{18,... | collective-permute-start | bytes 393224 | tf_op jit(solution)/shard_map/ppermute | solution.py:332
  63.5 8.9 %collective-permute-start.20 = (bf16[8,32,256]{2,1,0:T(8,128)(2,1)S(1)}, bf16[8,32,256]{2,1,0:T(8,128)(2,1)S(1)}, u32[]{:S(2)}, u32[]{:S(2)}) collective-permute-start(bf16[8,32,256]{2,1,0:T(8,128)(2,1)S(1)} %get-tuple-element.298), channel_id=1, source_target_pairs={{0,12},{2,14},{4,8},{6,10},{8,4},{10,6},{12,0},{14,2},{16,28},{18,... | collective-permute-start | bytes 393224 | tf_op jit(solution)/shard_map/ppermute | solution.py:332
  64.7 9.2 %collective-permute-start.21 = (bf16[8,32,256]{2,1,0:T(8,128)(2,1)S(1)}, bf16[8,32,256]{2,1,0:T(8,128)(2,1)S(1)}, u32[]{:S(2)}, u32[]{:S(2)}) collective-permute-start(bf16[8,32,256]{2,1,0:T(8,128)(2,1)S(1)} %get-tuple-element.299), channel_id=1, source_target_pairs={{0,14},{2,12},{4,10},{6,8},{8,6},{10,4},{12,2},{14,0},{16,30},{18,... | collective-permute-start | bytes 393224 | tf_op jit(solution)/shard_map/ppermute | solution.py:332
  75.6 2.7 %collective-permute-start.22 = (f32[1024,256]{1,0:T(8,128)S(1)}, f32[1024,256]{1,0:T(8,128)S(1)}, u32[]{:S(2)}, u32[]{:S(2)}) collective-permute-start(f32[1024,256]{1,0:T(8,128)S(1)} %block_products.1.mine_ref), channel_id=1, source_target_pairs={{0,1},{1,0},{2,3},{3,2},{4,5},{5,4},{6,7},{7,6},{8,9},{9,8},{10,11... | collective-permute-start | bytes 3145736 | tf_op jit(solution)/shard_map/ppermute | solution.py:373

commit v5 on v4

--- a/solution.py
+++ b/solution.py
@@ -14,55 +14,83 @@
 MIB = 1024 * 1024
 
 
-LEVELS = (12, 14, 16, 18, 20, 22, 24)
-
-
-def cut_kernel(cols_ref, counts_ref, sketch_ref, table_ref, *out_refs):
+LEVELS = (12, 14, 16, 18, 20, 24)
+TABLE_ROWS = 16
+
+
+def row_kernel(cols_ref, counts_ref, out_ref):
+    slots = cols_ref.shape[0]
+    rows, cols = lax.axis_size("rows"), lax.axis_size("cols")
+    mine = lax.axis_index("rows") // (rows // 2) * cols + lax.axis_index("cols")
+    row = lax.broadcasted_iota(jnp.int32, out_ref.shape, 0)
+    lane = lax.broadcasted_iota(jnp.int32, out_ref.shape, 1)
+    table = jnp.where(lane == slots, counts_ref[0], 0)
+    for s in range(slots):
+        table = jnp.where(lane == s, cols_ref[s], table)
+    out_ref[...] = jnp.where(row == mine, table, 0).astype(jnp.float32).astype(out_ref.dtype)
+
+
+def table_row(block_cols, counts, columns, dtype):
+    return pl.pallas_call(
+        row_kernel,
+        out_shape=jax.ShapeDtypeStruct((TABLE_ROWS, columns), dtype),
+        in_specs=[SMEM, SMEM],
+        out_specs=VMEM,
+        name="table_row",
+    )(block_cols, counts)
+
+
+def cut_kernel(sketch_ref, here_ref, across_ref, *out_refs):
     members = len(out_refs)
     me = lax.axis_index("rows") % members
+    blocks, _, height, columns = sketch_ref.shape
+    unit = out_refs[0].shape[1]
+    pieces = blocks * height // unit
+    table = (here_ref[...].astype(jnp.float32) + across_ref[...].astype(jnp.float32)).astype(here_ref.dtype)
     for d in range(members):
-        out_refs[d][...] = sketch_ref[:, me ^ d]
-    lane = lax.broadcasted_iota(jnp.int32, table_ref.shape, 2)
-    table = jnp.where(lane == cols_ref.shape[0], counts_ref[0], 0)
-    for s in range(cols_ref.shape[0]):
-        table = jnp.where(lane == s, cols_ref[s], table)
-    table_ref[...] = table
-
-
-def cut(block_cols, counts, sketch, devices):
+        out_refs[d][:pieces] = sketch_ref[:, me ^ d].reshape(pieces, unit, columns)
+        out_refs[d][pieces:] = table.reshape(-1, unit, columns)
+
+
+def cut(sketch, here, across):
     blocks, members, height, columns = sketch.shape
+    unit = min(height, TABLE_ROWS)
+    pieces = (blocks * height + TABLE_ROWS) // unit
     return pl.pallas_call(
         cut_kernel,
-        out_shape=(
-            jax.ShapeDtypeStruct((devices, 1, 128), jnp.int32),
-            *[jax.ShapeDtypeStruct((blocks, height, columns), sketch.dtype)] * members,
-        ),
-        in_specs=[SMEM, SMEM, VMEM],
-        out_specs=(VMEM,) * (members + 1),
+        out_shape=(jax.ShapeDtypeStruct((pieces, unit, columns), sketch.dtype),) * members,
+        in_specs=[VMEM] * 3,
+        out_specs=(VMEM,) * members,
         compiler_params=pltpu.CompilerParams(vmem_limit_bytes=24 * MIB),
         name="cut_stripes",
-    )(block_cols, counts, sketch)
-
-
-def plan_kernel(per, levels, table_ref, places_ref, list_ref, level_ref):
-    devices = table_ref.shape[0]
+    )(sketch, here, across)
+
+
+def plan_kernel(levels, *refs):
+    *stripe_refs, all_ref, places_ref, list_ref, level_ref = refs
+    rows, cols = lax.axis_size("rows"), lax.axis_size("cols")
+    members = len(stripe_refs)
+    me = lax.axis_index("rows") % members
+    half = lax.axis_index("rows") // members
+    c = lax.axis_index("cols")
+    part, height, columns = all_ref.shape
+    per = part // members
+    panel = part * 2
     slots = places_ref.shape[1]
-    rows, cols = lax.axis_size("rows"), lax.axis_size("cols")
-    panel = per * rows
-    part = panel // 2
-    table = table_ref[:, 0, :]
-    block = lax.broadcasted_iota(jnp.int32, (devices, panel), 1)
-    device = lax.broadcasted_iota(jnp.int32, (devices, panel), 0)
+    unit = stripe_refs[0].shape[1]
+    pieces = per * height // unit
+    lines = places_ref.shape[0] // members
+    tables = []
+    for d in range(members):
+        all_ref[pl.ds((me ^ d) * per, per)] = stripe_refs[d][:pieces].reshape(per, height, columns)
+        tables.append(stripe_refs[d][pieces:].reshape(TABLE_ROWS, columns).astype(jnp.float32)[:lines])
+    table = jnp.concatenate(tables, axis=0).astype(jnp.int32)
+    block = lax.broadcasted_iota(jnp.int32, (members * lines, panel), 1)
+    line = lax.broadcasted_iota(jnp.int32, (members * lines, panel), 0) % lines
     asked = [(table[:, s : s + 1] == block) & (s < table[:, slots : slots + 1]) for s in range(slots)]
-    some = functools.reduce(jnp.logical_or, asked) & (device // (devices // 2) != block // part)
-    lines = -(-2 * cols // 8) * 8
-    line = lax.broadcasted_iota(jnp.int32, (lines, panel), 0)
-    touched = jnp.zeros((lines, panel), jnp.float32)
-    for h in range(2):
-        for c in range(cols):
-            group = some & (device // (devices // 2) == h) & (device % cols == c)
-            found = jnp.max(jnp.where(group, 1.0, 0.0), axis=0, keepdims=True)
-            touched = jnp.where(line == h * cols + c, found, touched)
+    some = functools.reduce(jnp.logical_or, asked) & (line // cols != block // part)
+    some = jnp.where(some, 1.0, 0.0)
+    touched = functools.reduce(jnp.maximum, [some[d * lines : (d + 1) * lines] for d in range(members)])
     most = jnp.max(jnp.sum(touched, axis=1, keepdims=True)).astype(jnp.int32)
     level_ref[0] = sum((most > level).astype(jnp.int32) for level in levels)
     touched = touched.astype(jnp.bfloat16)
@@ -71,9 +99,8 @@
     after = jnp.where(first > second, 1.0, 0.0).astype(jnp.bfloat16)
     same = jnp.where(first == second, 1.0, 0.0).astype(jnp.bfloat16)
     nt = (((1,), (1,)), ((), ()))
-    half = lax.axis_index("rows") // (rows // 2)
-    c = lax.axis_index("cols")
     rank = lax.dot_general(touched, after, nt, preferred_element_type=jnp.float32)
+    line = lax.broadcasted_iota(jnp.int32, (lines, panel), 0)
     rank = jnp.sum(jnp.where(line == half * cols + c, rank, 0.0), axis=0, keepdims=True)
     ids = lax.broadcasted_iota(jnp.int32, (1, panel), 1)
     place = jnp.where(ids // part == half, ids - half * part, part + rank.astype(jnp.int32))
@@ -95,72 +122,58 @@
     list_ref[...] = jnp.broadcast_to(jnp.sum(listed, axis=0, keepdims=True), list_ref.shape)
 
 
-def plan(table, slots, per, levels):
-    devices = table.shape[0]
-    return pl.pallas_call(
-        functools.partial(plan_kernel, per, levels),
+def plan(stripes, slots, per, height, levels):
+    members = len(stripes)
+    columns = stripes[0].shape[-1]
+    lines = max(8, 2 * lax.axis_size("cols"))
+    return pl.pallas_call(
+        functools.partial(plan_kernel, levels),
         out_shape=(
-            jax.ShapeDtypeStruct((devices, slots), jnp.int32),
+            jax.ShapeDtypeStruct((members * per, height, columns), stripes[0].dtype),
+            jax.ShapeDtypeStruct((members * lines, slots), jnp.int32),
             jax.ShapeDtypeStruct((8, 128), jnp.int32),
             jax.ShapeDtypeStruct((1,), jnp.int32),
         ),
-        in_specs=[VMEM],
-        out_specs=(VMEM, VMEM, SMEM),
+        in_specs=[VMEM] * members,
+        out_specs=(VMEM, VMEM, VMEM, SMEM),
         compiler_params=pltpu.CompilerParams(vmem_limit_bytes=48 * MIB),
         name="plan",
-    )(table)
-
-
-def list_kernel(list_ref, *refs):
-    *stripe_refs, out_ref, all_ref = refs
-    members = len(stripe_refs)
-    me = lax.axis_index("rows") % members
-    per = stripe_refs[0].shape[0]
-    for d in range(members):
-        all_ref[pl.ds((me ^ d) * per, per)] = stripe_refs[d][...]
+    )(*stripes)
+
+
+def list_kernel(list_ref, all_ref, out_ref):
     for k in range(out_ref.shape[0]):
         out_ref[k] = all_ref[list_ref[0, k]]
 
 
 def listed(numbers, stripes, count):
-    per, height, columns = stripes[0].shape
     return pl.pallas_call(
         list_kernel,
-        out_shape=(
-            jax.ShapeDtypeStruct((count, height, columns), stripes[0].dtype),
-            jax.ShapeDtypeStruct((len(stripes) * per, height, columns), stripes[0].dtype),
-        ),
-        in_specs=[SMEM] + [VMEM] * len(stripes),
-        out_specs=(VMEM, VMEM),
+        out_shape=jax.ShapeDtypeStruct((count, *stripes.shape[1:]), stripes.dtype),
+        in_specs=[SMEM, VMEM],
+        out_specs=VMEM,
         compiler_params=pltpu.CompilerParams(vmem_limit_bytes=24 * MIB),
         name="listed_stripes",
-    )(numbers, *stripes)
+    )(numbers, stripes)
 
 
 def pick_kernel(places_ref, own_ref, other_ref, *out_refs):
     members = len(out_refs)
     rows, cols = lax.axis_size("rows"), lax.axis_size("cols")
-    here = own_ref.shape[0]
-    me = lax.axis_index("rows")
-    c = lax.axis_index("cols")
+    here, there = own_ref.shape[0], other_ref.shape[0]
+    lines = places_ref.shape[0] // members
+    line = lax.axis_index("rows") // members * cols + lax.axis_index("cols")
     for d in range(members):
         out_ref = out_refs[d]
-        device = (me ^ d) * cols + c
 
         def body(s, carry):
-            place = places_ref[device, s]
-
-            @pl.when(place < here)
-            def _():
-                out_ref[s] = own_ref[jnp.minimum(place, here - 1)]
-
-            @pl.when(place >= here)
-            def _():
-                out_ref[s] = other_ref[jnp.clip(place - here, 0, other_ref.shape[0] - 1)]
-
+            place = places_ref[d * lines + line, s]
+            own = own_ref[jnp.minimum(place, here - 1)]
+            other = other_ref[jnp.clip(place - here, 0, there - 1)]
+            out_ref[s] = lax.select(place < here, own, other)
             return carry
 
-        lax.fori_loop(0, out_ref.shape[0], body, 0)
+        lax.fori_loop(0, out_ref.shape[0], body, 0, unroll=True)
 
 
 def pick(places, own, other, members):
@@ -265,7 +278,7 @@
     def refine(precision):
         w = inverse[...]
         residual = matmul_nt(matmul(w, scaled[...], precision), w, precision) - identity
-        inverse[...] = w - matmul(residual * half, w, precision)
+        inverse[...] = w - matmul(residual * half, w, lax.Precision.DEFAULT)
         return jnp.sum(residual * residual)
 
     inverse[...] = identity - (scaled[...] - identity) * half
@@ -328,9 +341,11 @@
 
 
 def exchange(pieces, rows):
-    return [pieces[0]] + [
-        lax.ppermute(piece, "rows", [(r, r ^ d) for r in range(rows)]) for d, piece in enumerate(pieces) if d
-    ]
+    far = sorted(range(2, len(pieces)), key=lambda d: (-d.bit_count(), -d))
+    arrived = [pieces[0]] + [None] * (len(pieces) - 1)
+    for d in [1, *far]:
+        arrived[d] = lax.ppermute(pieces[d], "rows", [(r, r ^ d) for r in range(rows)])
+    return arrived
 
 
 def fetch(sketch, block_cols, counts, slots, width):
@@ -340,19 +355,22 @@
     columns = sketch.shape[1]
     sketch = sketch.reshape(-1, members, height, columns)
     per = sketch.shape[0]
-    devices = rows * cols
-    table, *stripes = cut(block_cols, counts, sketch, devices)
-    stripes = exchange(stripes, rows)
-    table = lax.all_to_all(table, ("rows", "cols"), split_axis=0, concat_axis=0, tiled=True)
     swap = [(r, (r + members) % rows) for r in range(rows)]
+    row = table_row(block_cols, counts, columns, sketch.dtype)
+    if cols == 2:
+        here = row + lax.ppermute(row, "cols", [(0, 1), (1, 0)])
+    else:
+        here = lax.psum(row, "cols")
+    across = lax.ppermute(here, "rows", swap)
+    stripes = exchange(cut(sketch, here, across), rows)
     largest = min(per * members, slots * members, 128)
     levels = tuple(level for level in LEVELS if level < largest)
-    places, numbers, level = plan(table, slots, per, levels)
+    own, places, numbers, level = plan(stripes, slots, per, height, levels)
 
     def with_other(count):
         def run():
-            sent, own = listed(numbers, stripes, count)
-            return pick(places, own, lax.ppermute(sent, "rows", swap), members)
+            other = lax.ppermute(listed(numbers, own, count), "rows", swap)
+            return pick(places, own, other, members)
 
         return run
 

time: 168 us -> 170 us (1.012)
  blocking collectives: 43 us -> 26.2 us
  waiting for transfers between devices: 26.3 us -> 41.3 us
  starting transfers between devices: 21.3 us -> 28 us
  Pallas kernels: 71.6 us -> 69.7 us
    all_to_all x1 -> x0, blocking collectives: 18.7 us -> none  [fetch(): lax.all_to_all(table, ('rows', 'cols'), split_axis=0, concat_axis=0, tile...]
    ppermute x15 -> x17, waiting for transfers between devices: 23.7 us -> 38.6 us  [the longest x14 25.2 us: exchange(): lax.ppermute(pieces[d], 'rows', [(r, r ^ d) for r in range(rows)])]
    ppermute x15 -> x17, starting transfers between devices: 21.3 us -> 27.9 us  [the longest x14 20.9 us: exchange(): lax.ppermute(pieces[d], 'rows', [(r, r ^ d) for r in range(rows)])]
    all_to_all x1, blocking collectives: 11.8 us -> 13.7 us  [local(): lax.all_to_all(pieces, 'rows', split_axis=0, concat_axis=0, tiled=True)]
    pallas_call x3 -> x4, Pallas kernels: 3.66 us -> 3.46 us  [the longest x1 1.41 us: plan(): pl.pallas_call(functools.partial(plan_kernel, levels), out_shape=(jax.Sha...]
  transfers between devices with their start and end apart: 16 -> 18, of which waited for: 9 -> 16; matrix products, arithmetic and copies ran while one was open for 0% -> 0% of each run, Pallas kernels for 1% -> 0%
where the time goes in v5:
time: 170 us
  Pallas kernels  69.7 us (41%)
  waiting for transfers between devices  41.3 us (24%)
  starting transfers between devices  28 us (16%)
  blocking collectives  26.2 us (15%)
  between operations  2.02 us (1%)
    pallas_call x1, Pallas kernels, factor_and_basis(): pl.pallas_call(functools.partial(factor_kernel, total_rows), out_shape=(j...  62.2 us
    ppermute x14, waiting for transfers between devices, exchange(): lax.ppermute(pieces[d], 'rows', [(r, r ^ d) for r in range(rows)])  25.2 us
    ppermute x14, starting transfers between devices, exchange(): lax.ppermute(pieces[d], 'rows', [(r, r ^ d) for r in range(rows)])  20.9 us
    all_to_all x1, blocking collectives, local(): lax.all_to_all(pieces, 'rows', split_axis=0, concat_axis=0, tiled=True)  13.7 us
    all_to_all x1, blocking collectives, spread(): return lax.all_to_all(copies, axes, split_axis=0, concat_axis=0, tiled=True)  12.5 us
    ppermute x1, waiting for transfers between devices, run(): other = lax.ppermute(listed(numbers, own, count), 'rows', swap)  10.8 us
    ppermute x1, starting transfers between devices, fetch(): across = lax.ppermute(here, 'rows', swap)  3.93 us
  transfers between devices with their start and end apart: 18, of which 16 were waited for; matrix products, arithmetic and copies ran while one was open for 0% of the time, Pallas kernels for 0%

profile of v5, /device:TPU:0, one launch (start us, length us, event | category | flops | bytes accessed | tf_op | source)
XLA Modules:
  0.0 169.7 jit_solution(995876182169018850)
XLA Ops:
  1.3 1.3 table_row.1
  2.6 0.5 collective-permute-start.7
  3.0 1.0 collective-permute-done.7
  4.1 0.7 add.3.here_ref
  4.8 3.9 %collective-permute-start.8 = (bf16[16,256]{1,0:T(8,128)(2,1)S(1)}, bf16[16,256]{1,0:T(8,128)(2,1)S(1)}, u32[]{:S(2)}, u32[]{:S(2)}) collective-permute-start(bf16[16,256]{1,0:T(8,128)(2,1)S(1)} %add.3.here_ref), channel_id=1, source_target_pairs={{0,16},{2,18},{4,20},{6,22},{8,24},{10,26},{12,28},{14,30},{16,0},... | collective-permute-start | bytes 24584 | tf_op jit(solution)/shard_map/ppermute | solution.py:364
  8.7 1.6 collective-permute-done.8.across_ref
  10.3 0.0 copy-start
  10.3 1.6 copy-done
  11.9 0.1 cut_stripes.1
  12.0 1.9 %collective-permute-start.9 = (bf16[33,16,256]{2,1,0:T(8,128)(2,1)S(1)}, bf16[33,16,256]{2,1,0:T(8,128)(2,1)S(1)}, u32[]{:S(2)}, u32[]{:S(2)}) collective-permute-start(bf16[33,16,256]{2,1,0:T(8,128)(2,1)S(1)} %get-tuple-element.88), channel_id=1, source_target_pairs={{0,2},{2,0},{4,6},{6,4},{8,10},{10,8},{12,14},{14,12},{16,18},{18,... | collective-permute-start | bytes 811016 | tf_op jit(solution)/shard_map/ppermute | solution.py:347
  13.9 1.5 collective-permute-start.10
  15.5 0.1 collective-permute-start.11
  15.6 1.9 %collective-permute-start.12 = (bf16[33,16,256]{2,1,0:T(8,128)(2,1)S(1)}, bf16[33,16,256]{2,1,0:T(8,128)(2,1)S(1)}, u32[]{:S(2)}, u32[]{:S(2)}) collective-permute-start(bf16[33,16,256]{2,1,0:T(8,128)(2,1)S(1)} %get-tuple-element.91), channel_id=1, source_target_pairs={{0,8},{2,10},{4,12},{6,14},{8,0},{10,2},{12,4},{14,6},{16,24},{18,... | collective-permute-start | bytes 811016 | tf_op jit(solution)/shard_map/ppermute | solution.py:347
  17.5 1.4 collective-permute-start.13
  18.9 3.6 %collective-permute-done.9.refs_1_ = bf16[33,16,256]{2,1,0:T(8,128)(2,1)S(1)} collective-permute-done((bf16[33,16,256]{2,1,0:T(8,128)(2,1)S(1)}, bf16[33,16,256]{2,1,0:T(8,128)(2,1)S(1)}, u32[]{:S(2)}, u32[]{:S(2)}) %collective-permute-start.9) | collective-permute-done | bytes 270368 | tf_op jit(solution)/shard_map/ppermute | solution.py:347
  22.5 3.2 %collective-permute-start.14 = (bf16[33,16,256]{2,1,0:T(8,128)(2,1)S(1)}, bf16[33,16,256]{2,1,0:T(8,128)(2,1)S(1)}, u32[]{:S(2)}, u32[]{:S(2)}) collective-permute-start(bf16[33,16,256]{2,1,0:T(8,128)(2,1)S(1)} %get-tuple-element.93), channel_id=1, source_target_pairs={{0,12},{2,14},{4,8},{6,10},{8,4},{10,6},{12,0},{14,2},{16,28},{18,... | collective-permute-start | bytes 811016 | tf_op jit(solution)/shard_map/ppermute | solution.py:347
  25.7 0.0 collective-permute-done.10.refs_2_
  25.7 2.1 %collective-permute-start.15 = (bf16[33,16,256]{2,1,0:T(8,128)(2,1)S(1)}, bf16[33,16,256]{2,1,0:T(8,128)(2,1)S(1)}, u32[]{:S(2)}, u32[]{:S(2)}) collective-permute-start(bf16[33,16,256]{2,1,0:T(8,128)(2,1)S(1)} %get-tuple-element.94), channel_id=1, source_target_pairs={{0,14},{2,12},{4,10},{6,8},{8,6},{10,4},{12,2},{14,0},{16,30},{18,... | collective-permute-start | bytes 811016 | tf_op jit(solution)/shard_map/ppermute | solution.py:347
  27.8 4.0 %collective-permute-done.11.refs_3_ = bf16[33,16,256]{2,1,0:T(8,128)(2,1)S(1)} collective-permute-done((bf16[33,16,256]{2,1,0:T(8,128)(2,1)S(1)}, bf16[33,16,256]{2,1,0:T(8,128)(2,1)S(1)}, u32[]{:S(2)}, u32[]{:S(2)}) %collective-permute-start.11) | collective-permute-done | bytes 270368 | tf_op jit(solution)/shard_map/ppermute | solution.py:347
  31.7 0.0 collective-permute-done.12.refs_4_
  31.7 0.3 collective-permute-done.13.refs_5_
  32.1 5.8 %collective-permute-done.14.refs_6_ = bf16[33,16,256]{2,1,0:T(8,128)(2,1)S(1)} collective-permute-done((bf16[33,16,256]{2,1,0:T(8,128)(2,1)S(1)}, bf16[33,16,256]{2,1,0:T(8,128)(2,1)S(1)}, u32[]{:S(2)}, u32[]{:S(2)}) %collective-permute-start.14) | collective-permute-done | bytes 270368 | tf_op jit(solution)/shard_map/ppermute | solution.py:347
  37.9 3.9 %collective-permute-done.15.refs_7_ = bf16[33,16,256]{2,1,0:T(8,128)(2,1)S(1)} collective-permute-done((bf16[33,16,256]{2,1,0:T(8,128)(2,1)S(1)}, bf16[33,16,256]{2,1,0:T(8,128)(2,1)S(1)}, u32[]{:S(2)}, u32[]{:S(2)}) %collective-permute-start.15) | collective-permute-done | bytes 270368 | tf_op jit(solution)/shard_map/ppermute | solution.py:347
  41.8 1.4 plan.1
  43.8 0.0 copy-start.1
  43.8 0.0 copy-start.2
  43.8 15.5 %conditional.1 = ((bf16[8,32,256]{2,1,0:T(8,128)(2,1)S(1)}, bf16[8,32,256]{2,1,0:T(8,128)(2,1)S(1)}, bf16[8,32,256]{2,1,0:T(8,128)(2,1)S(1)}, bf16[8,32,256]{2,1...) conditional(s32[]{:T(128)} %bitcast.1, ...), branch_computations={%region_0.0_spmd, %region_1.0_spmd, %region_2.0_spmd, %region_3.0_... | conditional | bytes 4194352 | solution.py:377
  43.9 0.6 listed_stripes.10
  44.5 2.7 %collective-permute-start.3 = (bf16[18,32,256]{2,1,0:T(8,128)(2,1)S(1)}, bf16[18,32,256]{2,1,0:T(8,128)(2,1)S(1)}, u32[]{:S(2)}, u32[]{:S(2)}) collective-permute-start(bf16[18,32,256]{2,1,0:T(8,128)(2,1)S(1)} %listed_stripes.10), channel_id=1, source_target_pairs={{0,16},{2,18},{4,20},{6,22},{8,24},{10,26},{12,28},{14,30},{16,0},... | collective-permute-start | bytes 884744 | tf_op jit(solution)/shard_map/cond/branch_3_fun/ppermute | solution.py:372
  47.2 10.8 %collective-permute-done.3.other_ref = bf16[18,32,256]{2,1,0:T(8,128)(2,1)S(1)} collective-permute-done((bf16[18,32,256]{2,1,0:T(8,128)(2,1)S(1)}, bf16[18,32,256]{2,1,0:T(8,128)(2,1)S(1)}, u32[]{:S(2)}, u32[]{:S(2)}) %collective-permute-start.3) | collective-permute-done | bytes 294944 | tf_op jit(solution)/shard_map/cond/branch_3_fun/ppermute | solution.py:372
  58.0 1.4 pick_stripes.10
  59.4 0.6 collective-permute-start.16
  60.0 1.0 collective-permute-start.17
  61.0 2.0 %collective-permute-start.18 = (bf16[8,32,256]{2,1,0:T(8,128)(2,1)S(1)}, bf16[8,32,256]{2,1,0:T(8,128)(2,1)S(1)}, u32[]{:S(2)}, u32[]{:S(2)}) collective-permute-start(bf16[8,32,256]{2,1,0:T(8,128)(2,1)S(1)} %get-tuple-element.102), channel_id=1, source_target_pairs={{0,6},{2,4},{4,2},{6,0},{8,14},{10,12},{12,10},{14,8},{16,22},{18,... | collective-permute-start | bytes 393224 | tf_op jit(solution)/shard_map/ppermute | solution.py:347
  62.9 0.7 collective-permute-start.19
  63.6 1.4 collective-permute-start.20
  65.0 0.3 collective-permute-done.16.refs_1_
  65.2 1.0 collective-permute-start.21
  66.3 0.3 collective-permute-done.17.refs_2_
  66.6 2.2 %collective-permute-start.22 = (bf16[8,32,256]{2,1,0:T(8,128)(2,1)S(1)}, bf16[8,32,256]{2,1,0:T(8,128)(2,1)S(1)}, u32[]{:S(2)}, u32[]{:S(2)}) collective-permute-start(bf16[8,32,256]{2,1,0:T(8,128)(2,1)S(1)} %get-tuple-element.106), channel_id=1, source_target_pairs={{0,14},{2,12},{4,10},{6,8},{8,6},{10,4},{12,2},{14,0},{16,30},{18,... | collective-permute-start | bytes 393224 | tf_op jit(solution)/shard_map/ppermute | solution.py:347
  68.8 0.2 collective-permute-done.18.refs_3_
  69.0 0.4 collective-permute-done.19.refs_4_
  69.4 2.8 %collective-permute-done.20.refs_5_ = bf16[8,32,256]{2,1,0:T(8,128)(2,1)S(1)} collective-permute-done((bf16[8,32,256]{2,1,0:T(8,128)(2,1)S(1)}, bf16[8,32,256]{2,1,0:T(8,128)(2,1)S(1)}, u32[]{:S(2)}, u32[]{:S(2)}) %collective-permute-start.20) | collective-permute-done | bytes 131104 | tf_op jit(solution)/shard_map/ppermute | solution.py:347
  72.1 1.9 %collective-permute-done.21.refs_6_ = bf16[8,32,256]{2,1,0:T(8,128)(2,1)S(1)} collective-permute-done((bf16[8,32,256]{2,1,0:T(8,128)(2,1)S(1)}, bf16[8,32,256]{2,1,0:T(8,128)(2,1)S(1)}, u32[]{:S(2)}, u32[]{:S(2)}) %collective-permute-start.21) | collective-permute-done | bytes 131104 | tf_op jit(solution)/shard_map/ppermute | solution.py:347
  74.1 1.7 collective-permute-done.22.refs_7_
  75.7 0.0 copy-done.1
  75.7 0.0 copy-done.2
  75.7 1.3 block_products.1.mine_ref
  77.0 0.1 collective-permute-start.23
  77.1 2.6 %collective-permute-done.23.other_ref = f32[1024,256]{1,0:T(8,128)S(1)} collective-permute-done((f32[1024,256]{1,0:T(8,128)S(1)}, f32[1024,256]{1,0:T(8,128)S(1)}, u32[]{:S(2)}, u32[]{:S(2)}) %collective-permute-start.23) | collective-permute-done | bytes 1048608 | tf_op jit(solution)/shard_map/ppermute | solution.py:391
  79.8 1.5 sum_and_gram.1
  81.2 13.7 %all_to_all.10 = f32[16,16,128]{2,1,0:T(8,128)S(1)} all-to-all(f32[16,16,128]{2,1,0:T(8,128)S(1)} %bitcast.6), channel_id=1, replica_groups=mesh['rows'=16,'cols'=2] {'rows'}, dimensions={0} | all-to-all | bytes 262144 | tf_op jit(solution)/shard_map/all_to_all | solution.py:394
  95.0 12.5 %all_to_all.11 = f32[32,16,128]{2,1,0:T(8,128)S(1)} all-to-all(f32[32,16,128]{2,1,0:T(8,128)S(1)} %broadcast_in_dim.2), channel_id=1, replica_groups=mesh['rows'=16,'cols'=2] {'rows','cols'}, dimensions={0} | all-to-all | bytes 524288 | tf_op jit(solution)/shard_map/all_to_all | solution.py:340
  107.5 62.2 %factor_and_basis.1 = (f32[512,256]{1,0:T(8,128)}, f32[256,256]{1,0:T(8,128)}) custom-call(f32[16,2,16,128]{3,2,1,0:T(8,128)S(1)} %bitcast.5, f32[512,256]{1,0:T(8,128)S(1)} %get-tuple-element.108.own_ref), custom_call_target="tpu_custom_call" | custom-call | tf_op jit(solution)/shard_map/factor_and_basis/pallas_call | solution.py:324
  (2 shorter events, 0.0 us)
Async XLA Ops:
  2.6 1.5 collective-permute-start.7
  4.8 5.6 %collective-permute-start.8 = (bf16[16,256]{1,0:T(8,128)(2,1)S(1)}, bf16[16,256]{1,0:T(8,128)(2,1)S(1)}, u32[]{:S(2)}, u32[]{:S(2)}) collective-permute-start(bf16[16,256]{1,0:T(8,128)(2,1)S(1)} %add.3.here_ref), channel_id=1, source_target_pairs={{0,16},{2,18},{4,20},{6,22},{8,24},{10,26},{12,28},{14,30},{16,0},... | collective-permute-start | bytes 24584 | tf_op jit(solution)/shard_map/ppermute | solution.py:364
  10.3 1.6 copy-start
  12.0 10.5 %collective-permute-start.9 = (bf16[33,16,256]{2,1,0:T(8,128)(2,1)S(1)}, bf16[33,16,256]{2,1,0:T(8,128)(2,1)S(1)}, u32[]{:S(2)}, u32[]{:S(2)}) collective-permute-start(bf16[33,16,256]{2,1,0:T(8,128)(2,1)S(1)} %get-tuple-element.88), channel_id=1, source_target_pairs={{0,2},{2,0},{4,6},{6,4},{8,10},{10,8},{12,14},{14,12},{16,18},{18,... | collective-permute-start | bytes 811016 | tf_op jit(solution)/shard_map/ppermute | solution.py:347
  13.9 11.8 %collective-permute-start.10 = (bf16[33,16,256]{2,1,0:T(8,128)(2,1)S(1)}, bf16[33,16,256]{2,1,0:T(8,128)(2,1)S(1)}, u32[]{:S(2)}, u32[]{:S(2)}) collective-permute-start(bf16[33,16,256]{2,1,0:T(8,128)(2,1)S(1)} %get-tuple-element.89), channel_id=1, source_target_pairs={{0,4},{2,6},{4,0},{6,2},{8,12},{10,14},{12,8},{14,10},{16,20},{18,... | collective-permute-start | bytes 811016 | tf_op jit(solution)/shard_map/ppermute | solution.py:347
  15.5 16.3 %collective-permute-start.11 = (bf16[33,16,256]{2,1,0:T(8,128)(2,1)S(1)}, bf16[33,16,256]{2,1,0:T(8,128)(2,1)S(1)}, u32[]{:S(2)}, u32[]{:S(2)}) collective-permute-start(bf16[33,16,256]{2,1,0:T(8,128)(2,1)S(1)} %get-tuple-element.90), channel_id=1, source_target_pairs={{0,6},{2,4},{4,2},{6,0},{8,14},{10,12},{12,10},{14,8},{16,22},{18,... | collective-permute-start | bytes 811016 | tf_op jit(solution)/shard_map/ppermute | solution.py:347
  15.6 16.1 %collective-permute-start.12 = (bf16[33,16,256]{2,1,0:T(8,128)(2,1)S(1)}, bf16[33,16,256]{2,1,0:T(8,128)(2,1)S(1)}, u32[]{:S(2)}, u32[]{:S(2)}) collective-permute-start(bf16[33,16,256]{2,1,0:T(8,128)(2,1)S(1)} %get-tuple-element.91), channel_id=1, source_target_pairs={{0,8},{2,10},{4,12},{6,14},{8,0},{10,2},{12,4},{14,6},{16,24},{18,... | collective-permute-start | bytes 811016 | tf_op jit(solution)/shard_map/ppermute | solution.py:347
  17.5 14.6 %collective-permute-start.13 = (bf16[33,16,256]{2,1,0:T(8,128)(2,1)S(1)}, bf16[33,16,256]{2,1,0:T(8,128)(2,1)S(1)}, u32[]{:S(2)}, u32[]{:S(2)}) collective-permute-start(bf16[33,16,256]{2,1,0:T(8,128)(2,1)S(1)} %get-tuple-element.92), channel_id=1, source_target_pairs={{0,10},{2,8},{4,14},{6,12},{8,2},{10,0},{12,6},{14,4},{16,26},{18,... | collective-permute-start | bytes 811016 | tf_op jit(solution)/shard_map/ppermute | solution.py:347
  22.5 15.4 %collective-permute-start.14 = (bf16[33,16,256]{2,1,0:T(8,128)(2,1)S(1)}, bf16[33,16,256]{2,1,0:T(8,128)(2,1)S(1)}, u32[]{:S(2)}, u32[]{:S(2)}) collective-permute-start(bf16[33,16,256]{2,1,0:T(8,128)(2,1)S(1)} %get-tuple-element.93), channel_id=1, source_target_pairs={{0,12},{2,14},{4,8},{6,10},{8,4},{10,6},{12,0},{14,2},{16,28},{18,... | collective-permute-start | bytes 811016 | tf_op jit(solution)/shard_map/ppermute | solution.py:347
  25.7 16.1 %collective-permute-start.15 = (bf16[33,16,256]{2,1,0:T(8,128)(2,1)S(1)}, bf16[33,16,256]{2,1,0:T(8,128)(2,1)S(1)}, u32[]{:S(2)}, u32[]{:S(2)}) collective-permute-start(bf16[33,16,256]{2,1,0:T(8,128)(2,1)S(1)} %get-tuple-element.94), channel_id=1, source_target_pairs={{0,14},{2,12},{4,10},{6,8},{8,6},{10,4},{12,2},{14,0},{16,30},{18,... | collective-permute-start | bytes 811016 | tf_op jit(solution)/shard_map/ppermute | solution.py:347
  43.8 31.9 %copy-start.1 = (bf16[8,256,256]{2,1,0:T(8,128)(2,1)S(1)}, bf16[8,256,256]{2,1,0:T(8,128)(2,1)}, u32[]{:S(2)}) copy-start(bf16[8,256,256]{2,1,0:T(8,128)(2,1)} %blocks_ref.1) | copy-start | bytes 3145732
  43.8 31.9 %copy-start.2 = (s32[8]{0:T(128)S(1)}, s32[8]{0:T(128)}, u32[]{:S(2)}) copy-start(s32[8]{0:T(128)} %rows_ref.1) | copy-start | bytes 100
  44.5 13.4 %collective-permute-start.3 = (bf16[18,32,256]{2,1,0:T(8,128)(2,1)S(1)}, bf16[18,32,256]{2,1,0:T(8,128)(2,1)S(1)}, u32[]{:S(2)}, u32[]{:S(2)}) collective-permute-start(bf16[18,32,256]{2,1,0:T(8,128)(2,1)S(1)} %listed_stripes.10), channel_id=1, source_target_pairs={{0,16},{2,18},{4,20},{6,22},{8,24},{10,26},{12,28},{14,30},{16,0},... | collective-permute-start | bytes 884744 | tf_op jit(solution)/shard_map/cond/branch_3_fun/ppermute | solution.py:372
  59.4 5.9 %collective-permute-start.16 = (bf16[8,32,256]{2,1,0:T(8,128)(2,1)S(1)}, bf16[8,32,256]{2,1,0:T(8,128)(2,1)S(1)}, u32[]{:S(2)}, u32[]{:S(2)}) collective-permute-start(bf16[8,32,256]{2,1,0:T(8,128)(2,1)S(1)} %get-tuple-element.100), channel_id=1, source_target_pairs={{0,2},{2,0},{4,6},{6,4},{8,10},{10,8},{12,14},{14,12},{16,18},{18,... | collective-permute-start | bytes 393224 | tf_op jit(solution)/shard_map/ppermute | solution.py:347
  60.0 6.6 %collective-permute-start.17 = (bf16[8,32,256]{2,1,0:T(8,128)(2,1)S(1)}, bf16[8,32,256]{2,1,0:T(8,128)(2,1)S(1)}, u32[]{:S(2)}, u32[]{:S(2)}) collective-permute-start(bf16[8,32,256]{2,1,0:T(8,128)(2,1)S(1)} %get-tuple-element.101), channel_id=1, source_target_pairs={{0,4},{2,6},{4,0},{6,2},{8,12},{10,14},{12,8},{14,10},{16,20},{18,... | collective-permute-start | bytes 393224 | tf_op jit(solution)/shard_map/ppermute | solution.py:347
  61.0 8.0 %collective-permute-start.18 = (bf16[8,32,256]{2,1,0:T(8,128)(2,1)S(1)}, bf16[8,32,256]{2,1,0:T(8,128)(2,1)S(1)}, u32[]{:S(2)}, u32[]{:S(2)}) collective-permute-start(bf16[8,32,256]{2,1,0:T(8,128)(2,1)S(1)} %get-tuple-element.102), channel_id=1, source_target_pairs={{0,6},{2,4},{4,2},{6,0},{8,14},{10,12},{12,10},{14,8},{16,22},{18,... | collective-permute-start | bytes 393224 | tf_op jit(solution)/shard_map/ppermute | solution.py:347
  62.9 6.4 %collective-permute-start.19 = (bf16[8,32,256]{2,1,0:T(8,128)(2,1)S(1)}, bf16[8,32,256]{2,1,0:T(8,128)(2,1)S(1)}, u32[]{:S(2)}, u32[]{:S(2)}) collective-permute-start(bf16[8,32,256]{2,1,0:T(8,128)(2,1)S(1)} %get-tuple-element.103), channel_id=1, source_target_pairs={{0,8},{2,10},{4,12},{6,14},{8,0},{10,2},{12,4},{14,6},{16,24},{18,... | collective-permute-start | bytes 393224 | tf_op jit(solution)/shard_map/ppermute | solution.py:347
  63.6 8.5 %collective-permute-start.20 = (bf16[8,32,256]{2,1,0:T(8,128)(2,1)S(1)}, bf16[8,32,256]{2,1,0:T(8,128)(2,1)S(1)}, u32[]{:S(2)}, u32[]{:S(2)}) collective-permute-start(bf16[8,32,256]{2,1,0:T(8,128)(2,1)S(1)} %get-tuple-element.104), channel_id=1, source_target_pairs={{0,10},{2,8},{4,14},{6,12},{8,2},{10,0},{12,6},{14,4},{16,26},{18,... | collective-permute-start | bytes 393224 | tf_op jit(solution)/shard_map/ppermute | solution.py:347
  65.2 8.8 %collective-permute-start.21 = (bf16[8,32,256]{2,1,0:T(8,128)(2,1)S(1)}, bf16[8,32,256]{2,1,0:T(8,128)(2,1)S(1)}, u32[]{:S(2)}, u32[]{:S(2)}) collective-permute-start(bf16[8,32,256]{2,1,0:T(8,128)(2,1)S(1)} %get-tuple-element.105), channel_id=1, source_target_pairs={{0,12},{2,14},{4,8},{6,10},{8,4},{10,6},{12,0},{14,2},{16,28},{18,... | collective-permute-start | bytes 393224 | tf_op jit(solution)/shard_map/ppermute | solution.py:347
  66.6 9.2 %collective-permute-start.22 = (bf16[8,32,256]{2,1,0:T(8,128)(2,1)S(1)}, bf16[8,32,256]{2,1,0:T(8,128)(2,1)S(1)}, u32[]{:S(2)}, u32[]{:S(2)}) collective-permute-start(bf16[8,32,256]{2,1,0:T(8,128)(2,1)S(1)} %get-tuple-element.106), channel_id=1, source_target_pairs={{0,14},{2,12},{4,10},{6,8},{8,6},{10,4},{12,2},{14,0},{16,30},{18,... | collective-permute-start | bytes 393224 | tf_op jit(solution)/shard_map/ppermute | solution.py:347
  77.0 2.7 %collective-permute-start.23 = (f32[1024,256]{1,0:T(8,128)S(1)}, f32[1024,256]{1,0:T(8,128)S(1)}, u32[]{:S(2)}, u32[]{:S(2)}) collective-permute-start(f32[1024,256]{1,0:T(8,128)S(1)} %block_products.1.mine_ref), channel_id=1, source_target_pairs={{0,1},{1,0},{2,3},{3,2},{4,5},{5,4},{6,7},{7,6},{8,9},{9,8},{10,11... | collective-permute-start | bytes 3145736 | tf_op jit(solution)/shard_map/ppermute | solution.py:391

commit v6 on v5

--- a/solution.py
+++ b/solution.py
@@ -18,52 +18,66 @@
 TABLE_ROWS = 16
 
 
-def row_kernel(cols_ref, counts_ref, out_ref):
-    slots = cols_ref.shape[0]
-    rows, cols = lax.axis_size("rows"), lax.axis_size("cols")
-    mine = lax.axis_index("rows") // (rows // 2) * cols + lax.axis_index("cols")
-    row = lax.broadcasted_iota(jnp.int32, out_ref.shape, 0)
-    lane = lax.broadcasted_iota(jnp.int32, out_ref.shape, 1)
-    table = jnp.where(lane == slots, counts_ref[0], 0)
-    for s in range(slots):
-        table = jnp.where(lane == s, cols_ref[s], table)
-    out_ref[...] = jnp.where(row == mine, table, 0).astype(jnp.float32).astype(out_ref.dtype)
-
-
-def table_row(block_cols, counts, columns, dtype):
-    return pl.pallas_call(
-        row_kernel,
-        out_shape=jax.ShapeDtypeStruct((TABLE_ROWS, columns), dtype),
-        in_specs=[SMEM, SMEM],
-        out_specs=VMEM,
-        name="table_row",
-    )(block_cols, counts)
-
-
-def cut_kernel(sketch_ref, here_ref, across_ref, *out_refs):
+def distances(members):
+    return [0, 1, 2, *range(members - 1, 2, -1)]
+
+
+def cut_kernel(sketch_ref, *out_refs):
     members = len(out_refs)
     me = lax.axis_index("rows") % members
-    blocks, _, height, columns = sketch_ref.shape
-    unit = out_refs[0].shape[1]
-    pieces = blocks * height // unit
-    table = (here_ref[...].astype(jnp.float32) + across_ref[...].astype(jnp.float32)).astype(here_ref.dtype)
-    for d in range(members):
-        out_refs[d][:pieces] = sketch_ref[:, me ^ d].reshape(pieces, unit, columns)
-        out_refs[d][pieces:] = table.reshape(-1, unit, columns)
-
-
-def cut(sketch, here, across):
+    for ref, d in zip(out_refs, distances(members)):
+        ref[...] = sketch_ref[:, me ^ d].reshape(ref.shape)
+
+
+def cut(sketch):
     blocks, members, height, columns = sketch.shape
     unit = min(height, TABLE_ROWS)
-    pieces = (blocks * height + TABLE_ROWS) // unit
+    size = sketch.size * sketch.dtype.itemsize
     return pl.pallas_call(
         cut_kernel,
-        out_shape=(jax.ShapeDtypeStruct((pieces, unit, columns), sketch.dtype),) * members,
-        in_specs=[VMEM] * 3,
+        out_shape=(jax.ShapeDtypeStruct((blocks * height // unit, unit, columns), sketch.dtype),) * members,
+        in_specs=[VMEM],
         out_specs=(VMEM,) * members,
         compiler_params=pltpu.CompilerParams(vmem_limit_bytes=24 * MIB),
+        cost_estimate=pl.CostEstimate(flops=0, bytes_accessed=2 * size, transcendentals=0),
         name="cut_stripes",
-    )(sketch, here, across)
+    )(sketch)
+
+
+def stamp_kernel(*refs):
+    members = (len(refs) - 4) // 2
+    line_refs, stripe_refs, out_refs = refs[:4], refs[4 : 4 + members], refs[4 + members :]
+    cols = lax.axis_size("cols")
+    half, c = lax.axis_index("rows") // members, lax.axis_index("cols")
+    pieces = stripe_refs[0].shape[0]
+    row = lax.broadcasted_iota(jnp.int32, (TABLE_ROWS, 128), 0)
+    table = jnp.zeros((TABLE_ROWS, 128), jnp.int32)
+    if cols == 2:
+        places = [half * 2 + c, half * 2 + 1 - c, (1 - half) * 2 + c, (1 - half) * 2 + 1 - c]
+        for place, line_ref in zip(places, line_refs):
+            table = jnp.where(row == place, line_ref[...], table)
+    else:
+        for k in range(cols):
+            table = jnp.where(row == half * cols + k, line_refs[0][k : k + 1], table)
+            table = jnp.where(row == (1 - half) * cols + k, line_refs[1][k : k + 1], table)
+    table = table.astype(jnp.float32).astype(out_refs[0].dtype)
+    for stripe_ref, out_ref in zip(stripe_refs, out_refs):
+        out_ref[:pieces] = stripe_ref[...]
+        out_ref[pieces:, :, :128] = table.reshape(-1, out_ref.shape[1], 128)
+
+
+def stamp(lines, stripes):
+    pieces, unit, columns = stripes[0].shape
+    pieces += TABLE_ROWS // unit
+    members = len(stripes)
+    return pl.pallas_call(
+        stamp_kernel,
+        out_shape=(jax.ShapeDtypeStruct((pieces, unit, columns), stripes[0].dtype),) * members,
+        in_specs=[VMEM] * (4 + members),
+        out_specs=(VMEM,) * members,
+        compiler_params=pltpu.CompilerParams(vmem_limit_bytes=24 * MIB),
+        name="stamp_stripes",
+    )(*lines, *stripes)
 
 
 def plan_kernel(levels, *refs):
@@ -81,9 +95,9 @@
     pieces = per * height // unit
     lines = places_ref.shape[0] // members
     tables = []
-    for d in range(members):
-        all_ref[pl.ds((me ^ d) * per, per)] = stripe_refs[d][:pieces].reshape(per, height, columns)
-        tables.append(stripe_refs[d][pieces:].reshape(TABLE_ROWS, columns).astype(jnp.float32)[:lines])
+    for ref, d in zip(stripe_refs, distances(members)):
+        all_ref[pl.ds((me ^ d) * per, per)] = ref[:pieces].reshape(per, height, columns)
+        tables.append(ref[pieces:, :, :128].reshape(TABLE_ROWS, 128).astype(jnp.float32)[:lines])
     table = jnp.concatenate(tables, axis=0).astype(jnp.int32)
     block = lax.broadcasted_iota(jnp.int32, (members * lines, panel), 1)
     line = lax.broadcasted_iota(jnp.int32, (members * lines, panel), 0) % lines
@@ -193,8 +207,8 @@
     columns = out_ref.shape[1]
     members = len(chosen_refs)
     me = lax.axis_index("rows") % members
-    for d in range(members):
-        whole[me ^ d] = chosen_refs[d][...]
+    for ref, d in zip(chosen_refs, distances(members) if members > 1 else [0]):
+        whole[me ^ d] = ref[...]
     out_ref[...] = jnp.zeros_like(out_ref)
     for s in range(slots):
 
@@ -220,15 +234,23 @@
     )(block_rows, counts, blocks, *chosen)
 
 
-def gram_kernel(mine_ref, other_ref, own_ref, gram_ref, slab):
+def gram_kernel(mine_ref, other_ref, own_ref, *refs):
+    *gram_refs, slab = refs
     c = lax.axis_index("cols")
-    share, width = own_ref.shape[0], gram_ref.shape[1]
+    me = lax.axis_index("rows") % len(gram_refs)
+    share, (height, width) = own_ref.shape[0], gram_refs[0].shape
     slab[...] = mine_ref[...] + other_ref[...]
     own_ref[...] = slab[pl.ds(pl.multiple_of(c * share, share), share), :]
     right = slab[:, pl.ds(pl.multiple_of(c * width, width), width)]
-    gram_ref[...] = lax.dot_general(
+    gram = lax.dot_general(
         slab[...], right, (((0,), (0,)), ((), ())), precision=HIGHEST, preferred_element_type=jnp.float32
     )
+    for q in range(len(gram_refs)):
+        for d in range(len(gram_refs)):
+
+            @pl.when(me ^ d == q)
+            def _():
+                gram_refs[d][...] = gram[q * height : (q + 1) * height]
 
 
 def sum_and_gram(mine, other):
@@ -237,14 +259,33 @@
         gram_kernel,
         out_shape=(
             jax.ShapeDtypeStruct((rows // 2, columns), jnp.float32),
-            jax.ShapeDtypeStruct((columns, columns // 2), jnp.float32),
+            *[jax.ShapeDtypeStruct((columns // 4, columns // 2), jnp.float32)] * 4,
         ),
         in_specs=[VMEM, VMEM],
-        out_specs=(VMEM, VMEM),
+        out_specs=(VMEM,) * 5,
         scratch_shapes=[pltpu.VMEM((rows, columns), jnp.float32)],
         compiler_params=pltpu.CompilerParams(vmem_limit_bytes=24 * MIB),
         name="sum_and_gram",
     )(mine, other)
+
+
+def stack_kernel(*refs):
+    *quarter_refs, out_ref = refs
+    me = lax.axis_index("rows") % len(quarter_refs)
+    height = quarter_refs[0].shape[0]
+    for d, ref in enumerate(quarter_refs):
+        out_ref[pl.ds(pl.multiple_of((me ^ d) * height, height), height), :] = ref[...]
+
+
+def stack(quarters):
+    height, width = quarters[0].shape
+    return pl.pallas_call(
+        stack_kernel,
+        out_shape=jax.ShapeDtypeStruct((len(quarters) * height, width), jnp.float32),
+        in_specs=[VMEM] * len(quarters),
+        out_specs=VMEM,
+        name="stack_quarters",
+    )(*quarters)
 
 
 def matmul(a, b, precision):
@@ -257,11 +298,16 @@
     )
 
 
-def factor_kernel(total_rows, gram_ref, own_ref, basis_ref, factor_ref, whole, scaled, inverse):
+def factor_kernel(total_rows, *refs):
+    *gram_refs, own_ref, basis_ref, factor_ref, whole, scaled, inverse = refs
     n = factor_ref.shape[0]
-    width = gram_ref.shape[-1]
-    for c in range(n // width):
-        whole[:, c * width : (c + 1) * width] = gram_ref[:, c].reshape(n, width)
+    if len(gram_refs) == 1:
+        whole[...] = gram_refs[0][...]
+    else:
+        c = lax.axis_index("cols")
+        width = n // 2
+        whole[:, pl.ds(pl.multiple_of(c * width, width), width)] = gram_refs[0][...]
+        whole[:, pl.ds(pl.multiple_of((1 - c) * width, width), width)] = gram_refs[1][...]
     row_ids = lax.broadcasted_iota(jnp.int32, (n, n), 0)
     col_ids = lax.broadcasted_iota(jnp.int32, (n, n), 1)
     diagonal = row_ids == col_ids
@@ -319,7 +365,7 @@
     basis_ref[...] = matmul_nt(own_ref[...] * up_across, w, HIGHEST) * root_rows
 
 
-def factor_and_basis(total_rows, gram, own):
+def factor_and_basis(total_rows, grams, own):
     columns = own.shape[1]
     return pl.pallas_call(
         functools.partial(factor_kernel, total_rows),
@@ -327,48 +373,55 @@
             jax.ShapeDtypeStruct(own.shape, jnp.float32),
             jax.ShapeDtypeStruct((columns, columns), jnp.float32),
         ),
-        in_specs=[VMEM, VMEM],
+        in_specs=[VMEM] * (len(grams) + 1),
         out_specs=(VMEM, VMEM),
         scratch_shapes=[pltpu.VMEM((columns, columns), jnp.float32)] * 3,
         compiler_params=pltpu.CompilerParams(vmem_limit_bytes=24 * MIB),
         name="factor_and_basis",
-    )(gram, own)
-
-
-def spread(piece, axes, devices):
-    copies = jnp.broadcast_to(piece[None], (devices, *piece.shape))
-    return lax.all_to_all(copies, axes, split_axis=0, concat_axis=0, tiled=True)
+    )(*grams, own)
+
+
+def moved(piece, rows, d):
+    return lax.ppermute(piece, "rows", [(r, r ^ d) for r in range(rows)])
 
 
 def exchange(pieces, rows):
-    far = sorted(range(2, len(pieces)), key=lambda d: (-d.bit_count(), -d))
-    arrived = [pieces[0]] + [None] * (len(pieces) - 1)
-    for d in [1, *far]:
-        arrived[d] = lax.ppermute(pieces[d], "rows", [(r, r ^ d) for r in range(rows)])
-    return arrived
+    order = distances(len(pieces))
+    return [moved(piece, rows, d) if d else piece for piece, d in zip(pieces, order)]
+
+
+def table_lines(block_cols, counts):
+    rows, cols = lax.axis_size("rows"), lax.axis_size("cols")
+    line = jnp.concatenate([block_cols, counts, jnp.zeros((128 - block_cols.shape[0] - 1,), jnp.int32)])[None]
+    swap = [(r, (r + rows // 2) % rows) for r in range(rows)]
+    if cols != 2:
+        lines = lax.all_gather(line, "cols", axis=0, tiled=True)
+        lines = [lines, lax.ppermute(lines, "rows", swap)]
+        return [*lines, *lines]
+    across = [(r * 2 + c, to * 2 + 1 - c) for r, to in swap for c in range(2)]
+    return [
+        line,
+        lax.ppermute(line, "cols", [(0, 1), (1, 0)]),
+        lax.ppermute(line, "rows", swap),
+        lax.ppermute(line, ("rows", "cols"), across),
+    ]
 
 
 def fetch(sketch, block_cols, counts, slots, width):
-    rows, cols = lax.axis_size("rows"), lax.axis_size("cols")
+    rows = lax.axis_size("rows")
     members = rows // 2
     height = width // members
     columns = sketch.shape[1]
     sketch = sketch.reshape(-1, members, height, columns)
     per = sketch.shape[0]
-    swap = [(r, (r + members) % rows) for r in range(rows)]
-    row = table_row(block_cols, counts, columns, sketch.dtype)
-    if cols == 2:
-        here = row + lax.ppermute(row, "cols", [(0, 1), (1, 0)])
-    else:
-        here = lax.psum(row, "cols")
-    across = lax.ppermute(here, "rows", swap)
-    stripes = exchange(cut(sketch, here, across), rows)
+    stripes = exchange(stamp(table_lines(block_cols, counts), cut(sketch)), rows)
     largest = min(per * members, slots * members, 128)
     levels = tuple(level for level in LEVELS if level < largest)
     own, places, numbers, level = plan(stripes, slots, per, height, levels)
 
     def with_other(count):
         def run():
+            swap = [(r, (r + members) % rows) for r in range(rows)]
             other = lax.ppermute(listed(numbers, own, count), "rows", swap)
             return pick(places, own, other, members)
 
@@ -376,6 +429,15 @@
 
     picked = lax.switch(level[0], [with_other(count) for count in (*levels, largest)])
     return exchange(picked, rows)
+
+
+def gram_halves(quarters, rows):
+    first, *rest = quarters
+    for d, quarter in enumerate(rest):
+        first = first + moved(quarter, rows, d + 1)
+    total = (first + moved(first, rows, 4)) + (moved(first, rows, 8) + moved(first, rows, 12))
+    half = stack([total] + [moved(total, rows, d) for d in range(1, 4)])
+    return half, lax.ppermute(half, "cols", [(0, 1), (1, 0)])
 
 
 def local(sketch, blocks, block_rows, block_cols, counts):
@@ -384,21 +446,17 @@
     rows, cols = lax.axis_size("rows"), lax.axis_size("cols")
     chosen = fetch(sketch, block_cols, counts, slots, width)
     if chosen[0].shape[1] % 16:
-        order = lax.axis_index("rows") % len(chosen) ^ jnp.arange(len(chosen))
+        order = jnp.argsort(lax.axis_index("rows") % len(chosen) ^ jnp.array(distances(len(chosen))))
         chosen = [jnp.stack(chosen)[order].swapaxes(0, 1).reshape(1, slots, width, columns)[0]]
     partial_rows = block_products(block_rows, counts, blocks, chosen)
-    if cols == 2:
+    if (rows, cols) == (16, 2):
         other = lax.ppermute(partial_rows, "cols", [(0, 1), (1, 0)])
-        own, gram = sum_and_gram(partial_rows, other)
-        pieces = gram.reshape(rows, -1, columns // 2)
-        pieces = lax.all_to_all(pieces, "rows", split_axis=0, concat_axis=0, tiled=True)
-        gram = spread(jnp.sum(pieces, axis=0), ("rows", "cols"), rows * cols)
-        gram = gram.reshape(rows, cols, -1, columns // 2)
+        own, *quarters = sum_and_gram(partial_rows, other)
+        grams = gram_halves(quarters, rows)
     else:
         own = lax.psum_scatter(partial_rows, "cols", scatter_dimension=0, tiled=True)
-        gram = lax.psum(matmul(own.T, own, HIGHEST), ("rows", "cols"))
-        gram = gram.reshape(1, 1, columns, columns)
-    return factor_and_basis(RB * width * rows, gram, own)
+        grams = [lax.psum(matmul(own.T, own, HIGHEST), ("rows", "cols"))]
+    return factor_and_basis(RB * width * rows, grams, own)
 
 
 def solution(mesh):

time: 170 us -> 171 us (level)
  blocking collectives: 26.2 us -> 0 us
  waiting for transfers between devices: 41.3 us -> 55.1 us
  starting transfers between devices: 28 us -> 38.3 us
  local copies, waits for them, and re-layouts: 1.62 us -> 3.7 us
    all_to_all x2 -> x0, blocking collectives: 26.2 us -> none  [the longest x1 13.7 us: local(): lax.all_to_all(pieces, 'rows', split_axis=0, concat_axis=0, tiled=True)]
    ppermute x16 -> x27, waiting for transfers between devices: 27.8 us -> 41 us  [the longest x23 37.4 us: moved(): return lax.ppermute(piece, 'rows', [(r, r ^ d) for r in range(rows)])]
    ppermute x16 -> x27, starting transfers between devices: 25.3 us -> 36.5 us  [the longest x23 32.3 us: moved(): return lax.ppermute(piece, 'rows', [(r, r ^ d) for r in range(rows)])]
    unnamed x6 -> x16, local copies, waits for them, and re-layouts: 1.6 us -> 3.7 us
  transfers between devices with their start and end apart: 18 -> 29, of which waited for: 16 -> 20; matrix products, arithmetic and copies ran while one was open for 0% -> 0% of each run, Pallas kernels for 0% -> 0%
where the time goes in v6:
time: 171 us; the launch traced here: 170 us
  Pallas kernels  69.9 us (41%)
  waiting for transfers between devices  55.1 us (32%)
  starting transfers between devices  38.3 us (22%)
  local copies, waits for them, and re-layouts  3.7 us (2%)
  between operations  2.07 us (1%)
    pallas_call x1, Pallas kernels, factor_and_basis(): pl.pallas_call(functools.partial(factor_kernel, total_rows), out_shape=(j...  62.1 us
    ppermute x23, waiting for transfers between devices, moved(): return lax.ppermute(piece, 'rows', [(r, r ^ d) for r in range(rows)])  37.4 us
    ppermute x23, starting transfers between devices, moved(): return lax.ppermute(piece, 'rows', [(r, r ^ d) for r in range(rows)])  32.3 us
    ppermute x1, waiting for transfers between devices, run(): other = lax.ppermute(listed(numbers, own, count), 'rows', swap)  11.5 us
    unnamed x16, local copies, waits for them, and re-layouts  3.7 us
    ppermute x1, starting transfers between devices, table_lines(): lax.ppermute(line, ('rows', 'cols'), across)  3.48 us
  transfers between devices with their start and end apart: 29, of which 20 were waited for; matrix products, arithmetic and copies ran while one was open for 0% of the time, Pallas kernels for 0%

profile of v6, /device:TPU:0, one launch (start us, length us, event | category | flops | bytes accessed | tf_op | source)
XLA Modules:
  0.0 169.8 jit_solution(16005903115064985162)
XLA Ops:
  1.3 0.7 add_bitcast_fusion.refs_0_
  2.0 3.5 %collective-permute-start.9 = (s32[1,128]{1,0:T(1,128)S(1)}, s32[1,128]{1,0:T(1,128)S(1)}, u32[]{:S(2)}, u32[]{:S(2)}) collective-permute-start(s32[1,128]{1,0:T(1,128)S(1)} %add_bitcast_fusion.refs_0_), channel_id=1, source_target_pairs={{0,17},{1,16},{2,19},{3,18},{4,21},{5,20},{6,23},{7,22},{8,25},{9,... | collective-permute-start | bytes 1544 | tf_op jit(solution)/shard_map/ppermute | solution.py:406
  5.5 0.6 collective-permute-start.8
  6.1 0.0 collective-permute-start.7
  6.2 1.6 copy-done
  7.8 0.1 cut_stripes.1
  7.9 2.0 %collective-permute-done.8.refs_2_ = s32[1,128]{1,0:T(1,128)S(1)} collective-permute-done((s32[1,128]{1,0:T(1,128)S(1)}, s32[1,128]{1,0:T(1,128)S(1)}, u32[]{:S(2)}, u32[]{:S(2)}) %collective-permute-start.8) | collective-permute-done | bytes 544 | tf_op jit(solution)/shard_map/ppermute | solution.py:405
  9.9 0.1 stamp_stripes.1
  10.1 1.6 collective-permute-start.10
  11.6 1.5 collective-permute-start.11
  13.2 1.5 collective-permute-start.12
  14.7 1.4 collective-permute-start.13
  16.1 2.5 %collective-permute-start.14 = (bf16[33,16,256]{2,1,0:T(8,128)(2,1)S(1)}, bf16[33,16,256]{2,1,0:T(8,128)(2,1)S(1)}, u32[]{:S(2)}, u32[]{:S(2)}) collective-permute-start(bf16[33,16,256]{2,1,0:T(8,128)(2,1)S(1)} %get-tuple-element.111), channel_id=1, source_target_pairs={{0,10},{2,8},{4,14},{6,12},{8,2},{10,0},{12,6},{14,4},{16,26},{18,... | collective-permute-start | bytes 811016 | tf_op jit(solution)/shard_map/ppermute | solution.py:385
  18.6 5.3 %collective-permute-done.10.refs_1_ = bf16[33,16,256]{2,1,0:T(8,128)(2,1)S(1)} collective-permute-done((bf16[33,16,256]{2,1,0:T(8,128)(2,1)S(1)}, bf16[33,16,256]{2,1,0:T(8,128)(2,1)S(1)}, u32[]{:S(2)}, u32[]{:S(2)}) %collective-permute-start.10) | collective-permute-done | bytes 270368 | tf_op jit(solution)/shard_map/ppermute | solution.py:385
  23.9 1.6 collective-permute-start.15
  25.4 5.4 %collective-permute-done.11.refs_2_ = bf16[33,16,256]{2,1,0:T(8,128)(2,1)S(1)} collective-permute-done((bf16[33,16,256]{2,1,0:T(8,128)(2,1)S(1)}, bf16[33,16,256]{2,1,0:T(8,128)(2,1)S(1)}, u32[]{:S(2)}, u32[]{:S(2)}) %collective-permute-start.11) | collective-permute-done | bytes 270368 | tf_op jit(solution)/shard_map/ppermute | solution.py:385
  30.9 1.5 collective-permute-start.16
  32.4 2.7 %collective-permute-done.14.refs_5_ = bf16[33,16,256]{2,1,0:T(8,128)(2,1)S(1)} collective-permute-done((bf16[33,16,256]{2,1,0:T(8,128)(2,1)S(1)}, bf16[33,16,256]{2,1,0:T(8,128)(2,1)S(1)}, u32[]{:S(2)}, u32[]{:S(2)}) %collective-permute-start.14) | collective-permute-done | bytes 270368 | tf_op jit(solution)/shard_map/ppermute | solution.py:385
  35.0 3.8 %collective-permute-done.15.refs_6_ = bf16[33,16,256]{2,1,0:T(8,128)(2,1)S(1)} collective-permute-done((bf16[33,16,256]{2,1,0:T(8,128)(2,1)S(1)}, bf16[33,16,256]{2,1,0:T(8,128)(2,1)S(1)}, u32[]{:S(2)}, u32[]{:S(2)}) %collective-permute-start.15) | collective-permute-done | bytes 270368 | tf_op jit(solution)/shard_map/ppermute | solution.py:385
  38.8 0.9 collective-permute-done.16.refs_7_
  39.8 1.4 plan.1
  41.8 0.0 copy-start.1
  41.8 0.0 copy-start.3
  41.9 15.2 %conditional.1 = ((bf16[8,32,256]{2,1,0:T(8,128)(2,1)S(1)}, bf16[8,32,256]{2,1,0:T(8,128)(2,1)S(1)}, bf16[8,32,256]{2,1,0:T(8,128)(2,1)S(1)}, bf16[8,32,256]{2,1...) conditional(s32[]{:T(128)} %bitcast.2, ...), branch_computations={%region_0.0_spmd, %region_1.0_spmd, %region_2.0_spmd, %region_3.0_... | conditional | bytes 4194352 | solution.py:430
  41.9 0.6 listed_stripes.9
  42.5 1.7 collective-permute-start.2
  44.2 11.5 %collective-permute-done.2.other_ref = bf16[16,32,256]{2,1,0:T(8,128)(2,1)S(1)} collective-permute-done((bf16[16,32,256]{2,1,0:T(8,128)(2,1)S(1)}, bf16[16,32,256]{2,1,0:T(8,128)(2,1)S(1)}, u32[]{:S(2)}, u32[]{:S(2)}) %collective-permute-start.2) | collective-permute-done | bytes 262176 | tf_op jit(solution)/shard_map/cond/branch_2_fun/ppermute | solution.py:425
  55.7 1.4 pick_stripes.9
  57.1 2.0 %collective-permute-start.17 = (bf16[8,32,256]{2,1,0:T(8,128)(2,1)S(1)}, bf16[8,32,256]{2,1,0:T(8,128)(2,1)S(1)}, u32[]{:S(2)}, u32[]{:S(2)}) collective-permute-start(bf16[8,32,256]{2,1,0:T(8,128)(2,1)S(1)} %get-tuple-element.119), channel_id=1, source_target_pairs={{0,2},{2,0},{4,6},{6,4},{8,10},{10,8},{12,14},{14,12},{16,18},{18,... | collective-permute-start | bytes 393224 | tf_op jit(solution)/shard_map/ppermute | solution.py:385
  59.1 0.6 collective-permute-start.18
  59.8 0.7 collective-permute-start.19
  60.5 2.5 %collective-permute-start.20 = (bf16[8,32,256]{2,1,0:T(8,128)(2,1)S(1)}, bf16[8,32,256]{2,1,0:T(8,128)(2,1)S(1)}, u32[]{:S(2)}, u32[]{:S(2)}) collective-permute-start(bf16[8,32,256]{2,1,0:T(8,128)(2,1)S(1)} %get-tuple-element.122), channel_id=1, source_target_pairs={{0,12},{2,14},{4,8},{6,10},{8,4},{10,6},{12,0},{14,2},{16,28},{18,... | collective-permute-start | bytes 393224 | tf_op jit(solution)/shard_map/ppermute | solution.py:385
  62.9 0.6 collective-permute-start.21
  63.5 2.1 %collective-permute-start.22 = (bf16[8,32,256]{2,1,0:T(8,128)(2,1)S(1)}, bf16[8,32,256]{2,1,0:T(8,128)(2,1)S(1)}, u32[]{:S(2)}, u32[]{:S(2)}) collective-permute-start(bf16[8,32,256]{2,1,0:T(8,128)(2,1)S(1)} %get-tuple-element.124), channel_id=1, source_target_pairs={{0,8},{2,10},{4,12},{6,14},{8,0},{10,2},{12,4},{14,6},{16,24},{18,... | collective-permute-start | bytes 393224 | tf_op jit(solution)/shard_map/ppermute | solution.py:385
  65.6 5.4 %collective-permute-done.18.refs_2_ = bf16[8,32,256]{2,1,0:T(8,128)(2,1)S(1)} collective-permute-done((bf16[8,32,256]{2,1,0:T(8,128)(2,1)S(1)}, bf16[8,32,256]{2,1,0:T(8,128)(2,1)S(1)}, u32[]{:S(2)}, u32[]{:S(2)}) %collective-permute-start.18) | collective-permute-done | bytes 131104 | tf_op jit(solution)/shard_map/ppermute | solution.py:385
  71.0 0.7 collective-permute-start.23
  71.8 0.5 collective-permute-done.21.refs_5_
  72.3 0.3 collective-permute-done.22.refs_6_
  72.6 4.3 %collective-permute-done.23.refs_7_ = bf16[8,32,256]{2,1,0:T(8,128)(2,1)S(1)} collective-permute-done((bf16[8,32,256]{2,1,0:T(8,128)(2,1)S(1)}, bf16[8,32,256]{2,1,0:T(8,128)(2,1)S(1)}, u32[]{:S(2)}, u32[]{:S(2)}) %collective-permute-start.23) | collective-permute-done | bytes 131104 | tf_op jit(solution)/shard_map/ppermute | solution.py:385
  76.9 1.1 block_products.1.mine_ref
  78.0 0.1 collective-permute-start.24
  78.1 2.6 %collective-permute-done.24.other_ref = f32[1024,256]{1,0:T(8,128)S(1)} collective-permute-done((f32[1024,256]{1,0:T(8,128)S(1)}, f32[1024,256]{1,0:T(8,128)S(1)}, u32[]{:S(2)}, u32[]{:S(2)}) %collective-permute-start.24) | collective-permute-done | bytes 1048608 | tf_op jit(solution)/shard_map/ppermute | solution.py:453
  80.8 1.5 sum_and_gram.1
  82.3 0.1 collective-permute-start.25
  82.3 1.4 collective-permute-start.26
  83.8 2.0 %collective-permute-start.27 = (f32[64,128]{1,0:T(8,128)S(1)}, f32[64,128]{1,0:T(8,128)S(1)}, u32[]{:S(2)}, u32[]{:S(2)}) collective-permute-start(f32[64,128]{1,0:T(8,128)S(1)} %get-tuple-element.129), channel_id=1, source_target_pairs={{0,6},{2,4},{4,2},{6,0},{8,14},{10,12},{12,10},{14,8},{16,22},{18,... | collective-permute-start | bytes 98312 | tf_op jit(solution)/shard_map/ppermute | solution.py:385
  85.8 0.4 collective-permute-done.25
  86.2 0.1 collective-permute-done.26
  86.3 2.3 %collective-permute-done.27 = f32[64,128]{1,0:T(8,128)S(1)} collective-permute-done((f32[64,128]{1,0:T(8,128)S(1)}, f32[64,128]{1,0:T(8,128)S(1)}, u32[]{:S(2)}, u32[]{:S(2)}) %collective-permute-start.27) | collective-permute-done | bytes 32800 | tf_op jit(solution)/shard_map/ppermute | solution.py:385
  88.6 2.6 %collective-permute-start.30 = (f32[64,128]{1,0:T(8,128)S(1)}, f32[64,128]{1,0:T(8,128)S(1)}, u32[]{:S(2)}, u32[]{:S(2)}) collective-permute-start(f32[64,128]{1,0:T(8,128)S(1)} %add_add_fusion.1), channel_id=1, source_target_pairs={{0,24},{2,26},{4,28},{6,30},{8,16},{10,18},{12,20},{14,22},{16,8},... | collective-permute-start | bytes 98312 | tf_op jit(solution)/shard_map/ppermute | solution.py:385
  91.3 1.8 %collective-permute-start.28 = (f32[64,128]{1,0:T(8,128)S(1)}, f32[64,128]{1,0:T(8,128)S(1)}, u32[]{:S(2)}, u32[]{:S(2)}) collective-permute-start(f32[64,128]{1,0:T(8,128)S(1)} %add_add_fusion.1), channel_id=1, source_target_pairs={{0,8},{2,10},{4,12},{6,14},{8,0},{10,2},{12,4},{14,6},{16,24},{18,... | collective-permute-start | bytes 98312 | tf_op jit(solution)/shard_map/ppermute | solution.py:385
  93.1 1.3 collective-permute-done.30
  94.4 1.7 collective-permute-done.29
  96.1 0.0 copy-start.4
  96.1 2.6 %collective-permute-start.33 = (f32[64,128]{1,0:T(8,128)S(1)}, f32[64,128]{1,0:T(8,128)S(1)}, u32[]{:S(2)}, u32[]{:S(2)}) collective-permute-start(f32[64,128]{1,0:T(8,128)S(1)} %add_add_fusion.refs_0_), channel_id=1, source_target_pairs={{0,6},{2,4},{4,2},{6,0},{8,14},{10,12},{12,10},{14,8},{16,22},{18,... | collective-permute-start | bytes 98312 | tf_op jit(solution)/shard_map/ppermute | solution.py:385
  98.6 1.0 collective-permute-start.31
  99.6 1.3 collective-permute-done.33.refs_3_
  101.0 1.6 collective-permute-done.32.refs_2_
  102.6 0.6 copy-done.6
  103.2 0.6 copy-done.7
  103.8 1.5 stack_quarters.1.refs_0_
  105.2 1.6 collective-permute-done.34.refs_1_
  106.8 0.9 copy-done.2
  107.7 62.1 %factor_and_basis.1 = (f32[512,256]{1,0:T(8,128)}, f32[256,256]{1,0:T(8,128)}) custom-call(f32[256,128]{1,0:T(8,128)S(1)} %copy-done.2, f32[256,128]{1,0:T(8,128)S(1)} %collective-permute-done.34.refs_1_, f32[512,256]{1,0:T(8,128)S(1)} %get-tuple-element.130.refs_2_), custom_call_target="tpu_custom_call" | custom-call | tf_op jit(solution)/shard_map/factor_and_basis/pallas_call | solution.py:370
  (24 shorter events, 0.1 us)
Async XLA Ops:
  2.0 5.9 %collective-permute-start.9 = (s32[1,128]{1,0:T(1,128)S(1)}, s32[1,128]{1,0:T(1,128)S(1)}, u32[]{:S(2)}, u32[]{:S(2)}) collective-permute-start(s32[1,128]{1,0:T(1,128)S(1)} %add_bitcast_fusion.refs_0_), channel_id=1, source_target_pairs={{0,17},{1,16},{2,19},{3,18},{4,21},{5,20},{6,23},{7,22},{8,25},{9,... | collective-permute-start | bytes 1544 | tf_op jit(solution)/shard_map/ppermute | solution.py:406
  5.5 4.4 %collective-permute-start.8 = (s32[1,128]{1,0:T(1,128)S(1)}, s32[1,128]{1,0:T(1,128)S(1)}, u32[]{:S(2)}, u32[]{:S(2)}) collective-permute-start(s32[1,128]{1,0:T(1,128)S(1)} %add_bitcast_fusion.refs_0_), channel_id=1, source_target_pairs={{0,16},{2,18},{4,20},{6,22},{8,24},{10,26},{12,28},{14,30},{16,0},... | collective-permute-start | bytes 1544 | tf_op jit(solution)/shard_map/ppermute | solution.py:405
  6.1 3.8 %collective-permute-start.7 = (s32[1,128]{1,0:T(1,128)S(1)}, s32[1,128]{1,0:T(1,128)S(1)}, u32[]{:S(2)}, u32[]{:S(2)}) collective-permute-start(s32[1,128]{1,0:T(1,128)S(1)} %add_bitcast_fusion.refs_0_), channel_id=1, source_target_pairs={{0,1},{1,0},{2,3},{3,2},{4,5},{5,4},{6,7},{7,6},{8,9},{9,8},{10,11... | collective-permute-start | bytes 1544 | tf_op jit(solution)/shard_map/ppermute | solution.py:404
  6.2 1.6 copy-start
  10.1 13.8 %collective-permute-start.10 = (bf16[33,16,256]{2,1,0:T(8,128)(2,1)S(1)}, bf16[33,16,256]{2,1,0:T(8,128)(2,1)S(1)}, u32[]{:S(2)}, u32[]{:S(2)}) collective-permute-start(bf16[33,16,256]{2,1,0:T(8,128)(2,1)S(1)} %get-tuple-element.107), channel_id=1, source_target_pairs={{0,2},{2,0},{4,6},{6,4},{8,10},{10,8},{12,14},{14,12},{16,18},{18,... | collective-permute-start | bytes 811016 | tf_op jit(solution)/shard_map/ppermute | solution.py:385
  11.6 19.2 %collective-permute-start.11 = (bf16[33,16,256]{2,1,0:T(8,128)(2,1)S(1)}, bf16[33,16,256]{2,1,0:T(8,128)(2,1)S(1)}, u32[]{:S(2)}, u32[]{:S(2)}) collective-permute-start(bf16[33,16,256]{2,1,0:T(8,128)(2,1)S(1)} %get-tuple-element.108), channel_id=1, source_target_pairs={{0,4},{2,6},{4,0},{6,2},{8,12},{10,14},{12,8},{14,10},{16,20},{18,... | collective-permute-start | bytes 811016 | tf_op jit(solution)/shard_map/ppermute | solution.py:385
  13.2 19.2 %collective-permute-start.12 = (bf16[33,16,256]{2,1,0:T(8,128)(2,1)S(1)}, bf16[33,16,256]{2,1,0:T(8,128)(2,1)S(1)}, u32[]{:S(2)}, u32[]{:S(2)}) collective-permute-start(bf16[33,16,256]{2,1,0:T(8,128)(2,1)S(1)} %get-tuple-element.109), channel_id=1, source_target_pairs={{0,14},{2,12},{4,10},{6,8},{8,6},{10,4},{12,2},{14,0},{16,30},{18,... | collective-permute-start | bytes 811016 | tf_op jit(solution)/shard_map/ppermute | solution.py:385
  14.7 17.7 %collective-permute-start.13 = (bf16[33,16,256]{2,1,0:T(8,128)(2,1)S(1)}, bf16[33,16,256]{2,1,0:T(8,128)(2,1)S(1)}, u32[]{:S(2)}, u32[]{:S(2)}) collective-permute-start(bf16[33,16,256]{2,1,0:T(8,128)(2,1)S(1)} %get-tuple-element.110), channel_id=1, source_target_pairs={{0,12},{2,14},{4,8},{6,10},{8,4},{10,6},{12,0},{14,2},{16,28},{18,... | collective-permute-start | bytes 811016 | tf_op jit(solution)/shard_map/ppermute | solution.py:385
  16.1 19.0 %collective-permute-start.14 = (bf16[33,16,256]{2,1,0:T(8,128)(2,1)S(1)}, bf16[33,16,256]{2,1,0:T(8,128)(2,1)S(1)}, u32[]{:S(2)}, u32[]{:S(2)}) collective-permute-start(bf16[33,16,256]{2,1,0:T(8,128)(2,1)S(1)} %get-tuple-element.111), channel_id=1, source_target_pairs={{0,10},{2,8},{4,14},{6,12},{8,2},{10,0},{12,6},{14,4},{16,26},{18,... | collective-permute-start | bytes 811016 | tf_op jit(solution)/shard_map/ppermute | solution.py:385
  23.9 15.0 %collective-permute-start.15 = (bf16[33,16,256]{2,1,0:T(8,128)(2,1)S(1)}, bf16[33,16,256]{2,1,0:T(8,128)(2,1)S(1)}, u32[]{:S(2)}, u32[]{:S(2)}) collective-permute-start(bf16[33,16,256]{2,1,0:T(8,128)(2,1)S(1)} %get-tuple-element.112), channel_id=1, source_target_pairs={{0,8},{2,10},{4,12},{6,14},{8,0},{10,2},{12,4},{14,6},{16,24},{18,... | collective-permute-start | bytes 811016 | tf_op jit(solution)/shard_map/ppermute | solution.py:385
  30.9 8.9 %collective-permute-start.16 = (bf16[33,16,256]{2,1,0:T(8,128)(2,1)S(1)}, bf16[33,16,256]{2,1,0:T(8,128)(2,1)S(1)}, u32[]{:S(2)}, u32[]{:S(2)}) collective-permute-start(bf16[33,16,256]{2,1,0:T(8,128)(2,1)S(1)} %get-tuple-element.113), channel_id=1, source_target_pairs={{0,6},{2,4},{4,2},{6,0},{8,14},{10,12},{12,10},{14,8},{16,22},{18,... | collective-permute-start | bytes 811016 | tf_op jit(solution)/shard_map/ppermute | solution.py:385
  41.8 35.1 %copy-start.1 = (bf16[8,256,256]{2,1,0:T(8,128)(2,1)S(1)}, bf16[8,256,256]{2,1,0:T(8,128)(2,1)}, u32[]{:S(2)}) copy-start(bf16[8,256,256]{2,1,0:T(8,128)(2,1)} %blocks_ref.1) | copy-start | bytes 3145732
  41.8 35.1 %copy-start.3 = (s32[8]{0:T(128)S(1)}, s32[8]{0:T(128)}, u32[]{:S(2)}) copy-start(s32[8]{0:T(128)} %rows_ref.1) | copy-start | bytes 100
  42.5 13.2 %collective-permute-start.2 = (bf16[16,32,256]{2,1,0:T(8,128)(2,1)S(1)}, bf16[16,32,256]{2,1,0:T(8,128)(2,1)S(1)}, u32[]{:S(2)}, u32[]{:S(2)}) collective-permute-start(bf16[16,32,256]{2,1,0:T(8,128)(2,1)S(1)} %listed_stripes.9), channel_id=1, source_target_pairs={{0,16},{2,18},{4,20},{6,22},{8,24},{10,26},{12,28},{14,30},{16,0},... | collective-permute-start | bytes 786440 | tf_op jit(solution)/shard_map/cond/branch_2_fun/ppermute | solution.py:425
  57.1 6.4 %collective-permute-start.17 = (bf16[8,32,256]{2,1,0:T(8,128)(2,1)S(1)}, bf16[8,32,256]{2,1,0:T(8,128)(2,1)S(1)}, u32[]{:S(2)}, u32[]{:S(2)}) collective-permute-start(bf16[8,32,256]{2,1,0:T(8,128)(2,1)S(1)} %get-tuple-element.119), channel_id=1, source_target_pairs={{0,2},{2,0},{4,6},{6,4},{8,10},{10,8},{12,14},{14,12},{16,18},{18,... | collective-permute-start | bytes 393224 | tf_op jit(solution)/shard_map/ppermute | solution.py:385
  59.1 11.9 %collective-permute-start.18 = (bf16[8,32,256]{2,1,0:T(8,128)(2,1)S(1)}, bf16[8,32,256]{2,1,0:T(8,128)(2,1)S(1)}, u32[]{:S(2)}, u32[]{:S(2)}) collective-permute-start(bf16[8,32,256]{2,1,0:T(8,128)(2,1)S(1)} %get-tuple-element.120), channel_id=1, source_target_pairs={{0,4},{2,6},{4,0},{6,2},{8,12},{10,14},{12,8},{14,10},{16,20},{18,... | collective-permute-start | bytes 393224 | tf_op jit(solution)/shard_map/ppermute | solution.py:385
  59.8 12.0 %collective-permute-start.19 = (bf16[8,32,256]{2,1,0:T(8,128)(2,1)S(1)}, bf16[8,32,256]{2,1,0:T(8,128)(2,1)S(1)}, u32[]{:S(2)}, u32[]{:S(2)}) collective-permute-start(bf16[8,32,256]{2,1,0:T(8,128)(2,1)S(1)} %get-tuple-element.121), channel_id=1, source_target_pairs={{0,14},{2,12},{4,10},{6,8},{8,6},{10,4},{12,2},{14,0},{16,30},{18,... | collective-permute-start | bytes 393224 | tf_op jit(solution)/shard_map/ppermute | solution.py:385
  60.5 11.3 %collective-permute-start.20 = (bf16[8,32,256]{2,1,0:T(8,128)(2,1)S(1)}, bf16[8,32,256]{2,1,0:T(8,128)(2,1)S(1)}, u32[]{:S(2)}, u32[]{:S(2)}) collective-permute-start(bf16[8,32,256]{2,1,0:T(8,128)(2,1)S(1)} %get-tuple-element.122), channel_id=1, source_target_pairs={{0,12},{2,14},{4,8},{6,10},{8,4},{10,6},{12,0},{14,2},{16,28},{18,... | collective-permute-start | bytes 393224 | tf_op jit(solution)/shard_map/ppermute | solution.py:385
  62.9 9.3 %collective-permute-start.21 = (bf16[8,32,256]{2,1,0:T(8,128)(2,1)S(1)}, bf16[8,32,256]{2,1,0:T(8,128)(2,1)S(1)}, u32[]{:S(2)}, u32[]{:S(2)}) collective-permute-start(bf16[8,32,256]{2,1,0:T(8,128)(2,1)S(1)} %get-tuple-element.123), channel_id=1, source_target_pairs={{0,10},{2,8},{4,14},{6,12},{8,2},{10,0},{12,6},{14,4},{16,26},{18,... | collective-permute-start | bytes 393224 | tf_op jit(solution)/shard_map/ppermute | solution.py:385
  63.5 9.1 %collective-permute-start.22 = (bf16[8,32,256]{2,1,0:T(8,128)(2,1)S(1)}, bf16[8,32,256]{2,1,0:T(8,128)(2,1)S(1)}, u32[]{:S(2)}, u32[]{:S(2)}) collective-permute-start(bf16[8,32,256]{2,1,0:T(8,128)(2,1)S(1)} %get-tuple-element.124), channel_id=1, source_target_pairs={{0,8},{2,10},{4,12},{6,14},{8,0},{10,2},{12,4},{14,6},{16,24},{18,... | collective-permute-start | bytes 393224 | tf_op jit(solution)/shard_map/ppermute | solution.py:385
  71.0 5.9 %collective-permute-start.23 = (bf16[8,32,256]{2,1,0:T(8,128)(2,1)S(1)}, bf16[8,32,256]{2,1,0:T(8,128)(2,1)S(1)}, u32[]{:S(2)}, u32[]{:S(2)}) collective-permute-start(bf16[8,32,256]{2,1,0:T(8,128)(2,1)S(1)} %get-tuple-element.125), channel_id=1, source_target_pairs={{0,6},{2,4},{4,2},{6,0},{8,14},{10,12},{12,10},{14,8},{16,22},{18,... | collective-permute-start | bytes 393224 | tf_op jit(solution)/shard_map/ppermute | solution.py:385
  78.0 2.7 %collective-permute-start.24 = (f32[1024,256]{1,0:T(8,128)S(1)}, f32[1024,256]{1,0:T(8,128)S(1)}, u32[]{:S(2)}, u32[]{:S(2)}) collective-permute-start(f32[1024,256]{1,0:T(8,128)S(1)} %block_products.1.mine_ref), channel_id=1, source_target_pairs={{0,1},{1,0},{2,3},{3,2},{4,5},{5,4},{6,7},{7,6},{8,9},{9,8},{10,11... | collective-permute-start | bytes 3145736 | tf_op jit(solution)/shard_map/ppermute | solution.py:453
  82.3 4.0 %collective-permute-start.25 = (f32[64,128]{1,0:T(8,128)S(1)}, f32[64,128]{1,0:T(8,128)S(1)}, u32[]{:S(2)}, u32[]{:S(2)}) collective-permute-start(f32[64,128]{1,0:T(8,128)S(1)} %get-tuple-element.127), channel_id=1, source_target_pairs={{0,2},{2,0},{4,6},{6,4},{8,10},{10,8},{12,14},{14,12},{16,18},{18,... | collective-permute-start | bytes 98312 | tf_op jit(solution)/shard_map/ppermute | solution.py:385
  82.3 4.0 %collective-permute-start.26 = (f32[64,128]{1,0:T(8,128)S(1)}, f32[64,128]{1,0:T(8,128)S(1)}, u32[]{:S(2)}, u32[]{:S(2)}) collective-permute-start(f32[64,128]{1,0:T(8,128)S(1)} %get-tuple-element.128), channel_id=1, source_target_pairs={{0,4},{2,6},{4,0},{6,2},{8,12},{10,14},{12,8},{14,10},{16,20},{18,... | collective-permute-start | bytes 98312 | tf_op jit(solution)/shard_map/ppermute | solution.py:385
  83.8 4.8 %collective-permute-start.27 = (f32[64,128]{1,0:T(8,128)S(1)}, f32[64,128]{1,0:T(8,128)S(1)}, u32[]{:S(2)}, u32[]{:S(2)}) collective-permute-start(f32[64,128]{1,0:T(8,128)S(1)} %get-tuple-element.129), channel_id=1, source_target_pairs={{0,6},{2,4},{4,2},{6,0},{8,14},{10,12},{12,10},{14,8},{16,22},{18,... | collective-permute-start | bytes 98312 | tf_op jit(solution)/shard_map/ppermute | solution.py:385
  88.6 5.8 %collective-permute-start.30 = (f32[64,128]{1,0:T(8,128)S(1)}, f32[64,128]{1,0:T(8,128)S(1)}, u32[]{:S(2)}, u32[]{:S(2)}) collective-permute-start(f32[64,128]{1,0:T(8,128)S(1)} %add_add_fusion.1), channel_id=1, source_target_pairs={{0,24},{2,26},{4,28},{6,30},{8,16},{10,18},{12,20},{14,22},{16,8},... | collective-permute-start | bytes 98312 | tf_op jit(solution)/shard_map/ppermute | solution.py:385
  91.2 4.8 %collective-permute-start.29 = (f32[64,128]{1,0:T(8,128)S(1)}, f32[64,128]{1,0:T(8,128)S(1)}, u32[]{:S(2)}, u32[]{:S(2)}) collective-permute-start(f32[64,128]{1,0:T(8,128)S(1)} %add_add_fusion.1), channel_id=1, source_target_pairs={{0,16},{2,18},{4,20},{6,22},{8,24},{10,26},{12,28},{14,30},{16,0},... | collective-permute-start | bytes 98312 | tf_op jit(solution)/shard_map/ppermute | solution.py:385
  91.3 4.8 %collective-permute-start.28 = (f32[64,128]{1,0:T(8,128)S(1)}, f32[64,128]{1,0:T(8,128)S(1)}, u32[]{:S(2)}, u32[]{:S(2)}) collective-permute-start(f32[64,128]{1,0:T(8,128)S(1)} %add_add_fusion.1), channel_id=1, source_target_pairs={{0,8},{2,10},{4,12},{6,14},{8,0},{10,2},{12,4},{14,6},{16,24},{18,... | collective-permute-start | bytes 98312 | tf_op jit(solution)/shard_map/ppermute | solution.py:385
  96.1 6.5 %copy-start.4 = (f32[64,128]{1,0:T(8,128)}, f32[64,128]{1,0:T(8,128)S(1)}, u32[]{:S(2)}) copy-start(f32[64,128]{1,0:T(8,128)S(1)} %add_add_fusion.refs_0_) | copy-start | bytes 98308
  96.1 4.9 %collective-permute-start.33 = (f32[64,128]{1,0:T(8,128)S(1)}, f32[64,128]{1,0:T(8,128)S(1)}, u32[]{:S(2)}, u32[]{:S(2)}) collective-permute-start(f32[64,128]{1,0:T(8,128)S(1)} %add_add_fusion.refs_0_), channel_id=1, source_target_pairs={{0,6},{2,4},{4,2},{6,0},{8,14},{10,12},{12,10},{14,8},{16,22},{18,... | collective-permute-start | bytes 98312 | tf_op jit(solution)/shard_map/ppermute | solution.py:385
  98.6 3.9 %collective-permute-start.32 = (f32[64,128]{1,0:T(8,128)S(1)}, f32[64,128]{1,0:T(8,128)S(1)}, u32[]{:S(2)}, u32[]{:S(2)}) collective-permute-start(f32[64,128]{1,0:T(8,128)S(1)} %add_add_fusion.refs_0_), channel_id=1, source_target_pairs={{0,4},{2,6},{4,0},{6,2},{8,12},{10,14},{12,8},{14,10},{16,20},{18,... | collective-permute-start | bytes 98312 | tf_op jit(solution)/shard_map/ppermute | solution.py:385
  98.6 3.9 %collective-permute-start.31 = (f32[64,128]{1,0:T(8,128)S(1)}, f32[64,128]{1,0:T(8,128)S(1)}, u32[]{:S(2)}, u32[]{:S(2)}) collective-permute-start(f32[64,128]{1,0:T(8,128)S(1)} %add_add_fusion.refs_0_), channel_id=1, source_target_pairs={{0,2},{2,0},{4,6},{6,4},{8,10},{10,8},{12,14},{14,12},{16,18},{18,... | collective-permute-start | bytes 98312 | tf_op jit(solution)/shard_map/ppermute | solution.py:385
  101.0 1.6 copy-start.5
  102.6 0.6 copy-start.6
  103.2 0.6 copy-start.7
  105.2 1.6 collective-permute-start.34
  106.8 0.9 copy-start.2

commit v7 on v5

--- a/solution.py
+++ b/solution.py
@@ -14,130 +14,156 @@
 MIB = 1024 * 1024
 
 
-LEVELS = (12, 14, 16, 18, 20, 24)
-TABLE_ROWS = 16
-
-
-def row_kernel(cols_ref, counts_ref, out_ref):
+ACROSS = (12, 14, 16, 18, 20, 24)
+WITHIN = (6, 7, 8)
+
+
+def table_kernel(cols_ref, counts_ref, out_ref):
     slots = cols_ref.shape[0]
-    rows, cols = lax.axis_size("rows"), lax.axis_size("cols")
-    mine = lax.axis_index("rows") // (rows // 2) * cols + lax.axis_index("cols")
-    row = lax.broadcasted_iota(jnp.int32, out_ref.shape, 0)
-    lane = lax.broadcasted_iota(jnp.int32, out_ref.shape, 1)
+    lane = lax.broadcasted_iota(jnp.int32, out_ref.shape, 2)
     table = jnp.where(lane == slots, counts_ref[0], 0)
     for s in range(slots):
         table = jnp.where(lane == s, cols_ref[s], table)
-    out_ref[...] = jnp.where(row == mine, table, 0).astype(jnp.float32).astype(out_ref.dtype)
-
-
-def table_row(block_cols, counts, columns, dtype):
-    return pl.pallas_call(
-        row_kernel,
-        out_shape=jax.ShapeDtypeStruct((TABLE_ROWS, columns), dtype),
+    out_ref[...] = table
+
+
+def table_copies(block_cols, counts, devices):
+    return pl.pallas_call(
+        table_kernel,
+        out_shape=jax.ShapeDtypeStruct((devices, 1, 128), jnp.int32),
         in_specs=[SMEM, SMEM],
         out_specs=VMEM,
-        name="table_row",
+        name="table_copies",
     )(block_cols, counts)
 
 
-def cut_kernel(sketch_ref, here_ref, across_ref, *out_refs):
-    members = len(out_refs)
-    me = lax.axis_index("rows") % members
-    blocks, _, height, columns = sketch_ref.shape
-    unit = out_refs[0].shape[1]
-    pieces = blocks * height // unit
-    table = (here_ref[...].astype(jnp.float32) + across_ref[...].astype(jnp.float32)).astype(here_ref.dtype)
-    for d in range(members):
-        out_refs[d][:pieces] = sketch_ref[:, me ^ d].reshape(pieces, unit, columns)
-        out_refs[d][pieces:] = table.reshape(-1, unit, columns)
-
-
-def cut(sketch, here, across):
-    blocks, members, height, columns = sketch.shape
-    unit = min(height, TABLE_ROWS)
-    pieces = (blocks * height + TABLE_ROWS) // unit
-    return pl.pallas_call(
-        cut_kernel,
-        out_shape=(jax.ShapeDtypeStruct((pieces, unit, columns), sketch.dtype),) * members,
-        in_specs=[VMEM] * 3,
-        out_specs=(VMEM,) * members,
-        compiler_params=pltpu.CompilerParams(vmem_limit_bytes=24 * MIB),
-        name="cut_stripes",
-    )(sketch, here, across)
-
-
-def plan_kernel(levels, *refs):
-    *stripe_refs, all_ref, places_ref, list_ref, level_ref = refs
+def plan_kernel(per, within, across, table_ref, places_ref, lists_ref, *level_refs):
+    devices = table_ref.shape[0]
+    slots = places_ref.shape[1]
     rows, cols = lax.axis_size("rows"), lax.axis_size("cols")
-    members = len(stripe_refs)
-    me = lax.axis_index("rows") % members
-    half = lax.axis_index("rows") // members
-    c = lax.axis_index("cols")
-    part, height, columns = all_ref.shape
-    per = part // members
-    panel = part * 2
-    slots = places_ref.shape[1]
-    unit = stripe_refs[0].shape[1]
-    pieces = per * height // unit
-    lines = places_ref.shape[0] // members
-    tables = []
-    for d in range(members):
-        all_ref[pl.ds((me ^ d) * per, per)] = stripe_refs[d][:pieces].reshape(per, height, columns)
-        tables.append(stripe_refs[d][pieces:].reshape(TABLE_ROWS, columns).astype(jnp.float32)[:lines])
-    table = jnp.concatenate(tables, axis=0).astype(jnp.int32)
-    block = lax.broadcasted_iota(jnp.int32, (members * lines, panel), 1)
-    line = lax.broadcasted_iota(jnp.int32, (members * lines, panel), 0) % lines
+    panel = per * rows
+    part = panel // 2
+    table = table_ref[:, 0, :]
+    block = lax.broadcasted_iota(jnp.int32, (devices, panel), 1)
+    device = lax.broadcasted_iota(jnp.int32, (devices, panel), 0)
+    side, core = device // (devices // 2), device % cols
     asked = [(table[:, s : s + 1] == block) & (s < table[:, slots : slots + 1]) for s in range(slots)]
-    some = functools.reduce(jnp.logical_or, asked) & (line // cols != block // part)
-    some = jnp.where(some, 1.0, 0.0)
-    touched = functools.reduce(jnp.maximum, [some[d * lines : (d + 1) * lines] for d in range(members)])
-    most = jnp.max(jnp.sum(touched, axis=1, keepdims=True)).astype(jnp.int32)
-    level_ref[0] = sum((most > level).astype(jnp.int32) for level in levels)
-    touched = touched.astype(jnp.bfloat16)
+    some = functools.reduce(jnp.logical_or, asked)
+    lines = -(-cols // 8) * 8
+    line = lax.broadcasted_iota(jnp.int32, (3 * lines, panel), 0)
+    asks = jnp.zeros((3 * lines, panel), jnp.float32)
+    for c in range(cols):
+        for h in range(2):
+            found = jnp.max(jnp.where(some & (core == c) & (side == h), 1.0, 0.0), axis=0, keepdims=True)
+            asks = jnp.where(line == c, jnp.maximum(asks, found), asks)
+            asks = jnp.where((line == lines * (1 + h) + c) & (block[:1] // part != h), found, asks)
     first = lax.broadcasted_iota(jnp.int32, (panel, panel), 0)
     second = lax.broadcasted_iota(jnp.int32, (panel, panel), 1)
-    after = jnp.where(first > second, 1.0, 0.0).astype(jnp.bfloat16)
+    after = first > second
+    near = jnp.where(after & (first // per == second // per), 1.0, 0.0).astype(jnp.bfloat16)
+    after = jnp.where(after, 1.0, 0.0).astype(jnp.bfloat16)
     same = jnp.where(first == second, 1.0, 0.0).astype(jnp.bfloat16)
     nt = (((1,), (1,)), ((), ()))
-    rank = lax.dot_general(touched, after, nt, preferred_element_type=jnp.float32)
-    line = lax.broadcasted_iota(jnp.int32, (lines, panel), 0)
-    rank = jnp.sum(jnp.where(line == half * cols + c, rank, 0.0), axis=0, keepdims=True)
+
+    def ranks(a, b):
+        return lax.dot_general(a, b, nt, preferred_element_type=jnp.float32)
+
+    short = asks.astype(jnp.bfloat16)
+    near_rank = ranks(short, near)
+    far_rank = ranks(short, after)
+    longest = jnp.max(jnp.where(line < lines, near_rank + asks, 0.0)).astype(jnp.int32)
+    level_refs[0][0] = sum((longest > level).astype(jnp.int32) for level in within)
+    longest = jnp.max(jnp.where(line < lines, 0.0, far_rank + asks)).astype(jnp.int32)
+    level_refs[1][0] = sum((longest > level).astype(jnp.int32) for level in across)
+    me = lax.axis_index("rows")
+    half, c = me // (rows // 2), lax.axis_index("cols")
+
+    def row(values, number):
+        return jnp.sum(jnp.where(line == number, values, 0.0), axis=0, keepdims=True)
+
     ids = lax.broadcasted_iota(jnp.int32, (1, panel), 1)
-    place = jnp.where(ids // part == half, ids - half * part, part + rank.astype(jnp.int32))
+    here = ids // per * per - half * part + row(near_rank, c).astype(jnp.int32)
+    there = part + row(far_rank, lines * (1 + half) + c).astype(jnp.int32)
+    place = jnp.where(ids // part == half, here, there)
     slot = lax.broadcasted_iota(jnp.int32, places_ref.shape, 1)
     places = jnp.zeros(places_ref.shape, jnp.int32)
     for s in range(slots):
         found = jnp.sum(jnp.where(asked[s], place, 0), axis=1, keepdims=True)
         places = jnp.where(slot == s, found, places)
     places_ref[...] = places
-    line = lax.broadcasted_iota(jnp.int32, (panel, lines), 1)
-    mine = line == (1 - half) * cols + c
-    there = lax.dot_general(same, touched, nt, preferred_element_type=jnp.float32)
-    there = jnp.sum(jnp.where(mine, there, 0.0), axis=1, keepdims=True)
-    rank = lax.dot_general(after, touched, nt, preferred_element_type=jnp.float32)
-    rank = jnp.sum(jnp.where(mine, rank, 0.0), axis=1, keepdims=True).astype(jnp.int32)
-    ids = lax.broadcasted_iota(jnp.int32, (panel, list_ref.shape[1]), 0)
-    number = lax.broadcasted_iota(jnp.int32, (panel, list_ref.shape[1]), 1)
-    listed = jnp.where((there > 0.5) & (rank == number), ids - half * part, 0)
-    list_ref[...] = jnp.broadcast_to(jnp.sum(listed, axis=0, keepdims=True), list_ref.shape)
-
-
-def plan(stripes, slots, per, height, levels):
-    members = len(stripes)
-    columns = stripes[0].shape[-1]
-    lines = max(8, 2 * lax.axis_size("cols"))
-    return pl.pallas_call(
-        functools.partial(plan_kernel, levels),
+    line = lax.broadcasted_iota(jnp.int32, (panel, 3 * lines), 1)
+
+    def column(values, number):
+        return jnp.sum(jnp.where(line == number, values, 0.0), axis=1, keepdims=True)
+
+    turned, near_rank, far_rank = ranks(same, short), ranks(near, short), ranks(after, short)
+    ids = lax.broadcasted_iota(jnp.int32, (panel, 1), 0)
+    number = lax.broadcasted_iota(jnp.int32, (panel, lists_ref.shape[1]), 1)
+    near_rank = column(near_rank, c).astype(jnp.int32)
+    here = ids // per * per - half * part + near_rank
+    other = lines * (2 - half) + c
+    sent = (column(turned, other) > 0.5) & (column(far_rank, other).astype(jnp.int32) == number)
+    sent = jnp.sum(jnp.where(sent, here, 0), axis=0, keepdims=True)
+    kept = (column(turned, c) > 0.5) & (ids // per == me) & (near_rank == number)
+    kept = jnp.sum(jnp.where(kept, ids % per, 0), axis=0, keepdims=True)
+    lists_ref[...] = jnp.where(lax.broadcasted_iota(jnp.int32, lists_ref.shape, 0) == 0, sent, kept)
+
+
+def plan(table, slots, per, within, across):
+    devices = table.shape[0]
+    return pl.pallas_call(
+        functools.partial(plan_kernel, per, within, across),
         out_shape=(
-            jax.ShapeDtypeStruct((members * per, height, columns), stripes[0].dtype),
-            jax.ShapeDtypeStruct((members * lines, slots), jnp.int32),
+            jax.ShapeDtypeStruct((devices, slots), jnp.int32),
             jax.ShapeDtypeStruct((8, 128), jnp.int32),
             jax.ShapeDtypeStruct((1,), jnp.int32),
+            jax.ShapeDtypeStruct((1,), jnp.int32),
         ),
-        in_specs=[VMEM] * members,
-        out_specs=(VMEM, VMEM, VMEM, SMEM),
+        in_specs=[VMEM],
+        out_specs=(VMEM, VMEM, SMEM, SMEM),
         compiler_params=pltpu.CompilerParams(vmem_limit_bytes=48 * MIB),
         name="plan",
+    )(table)
+
+
+def cut_kernel(lists_ref, sketch_ref, *out_refs):
+    members = len(out_refs)
+    me = lax.axis_index("rows") % members
+    for k in range(out_refs[0].shape[0]):
+        for d, out_ref in enumerate(out_refs):
+            out_ref[k] = sketch_ref[lists_ref[1, k], me ^ d]
+
+
+def cut(lists, sketch, count):
+    _, members, height, columns = sketch.shape
+    return pl.pallas_call(
+        cut_kernel,
+        out_shape=(jax.ShapeDtypeStruct((count, height, columns), sketch.dtype),) * members,
+        in_specs=[SMEM, VMEM],
+        out_specs=(VMEM,) * members,
+        compiler_params=pltpu.CompilerParams(vmem_limit_bytes=24 * MIB),
+        name="cut_stripes",
+    )(lists, sketch)
+
+
+def order_kernel(*refs):
+    *stripe_refs, all_ref = refs
+    members = len(stripe_refs)
+    me = lax.axis_index("rows") % members
+    per = all_ref.shape[0] // members
+    for d, ref in enumerate(stripe_refs):
+        all_ref[pl.ds((me ^ d) * per, ref.shape[0])] = ref[...]
+
+
+def order(stripes, per):
+    _, height, columns = stripes[0].shape
+    return pl.pallas_call(
+        order_kernel,
+        out_shape=jax.ShapeDtypeStruct((len(stripes) * per, height, columns), stripes[0].dtype),
+        in_specs=[VMEM] * len(stripes),
+        out_specs=VMEM,
+        compiler_params=pltpu.CompilerParams(vmem_limit_bytes=24 * MIB),
+        name="order_stripes",
     )(*stripes)
 
 
@@ -159,15 +185,15 @@
 
 def pick_kernel(places_ref, own_ref, other_ref, *out_refs):
     members = len(out_refs)
-    rows, cols = lax.axis_size("rows"), lax.axis_size("cols")
+    cols = lax.axis_size("cols")
     here, there = own_ref.shape[0], other_ref.shape[0]
-    lines = places_ref.shape[0] // members
-    line = lax.axis_index("rows") // members * cols + lax.axis_index("cols")
+    me = lax.axis_index("rows")
+    c = lax.axis_index("cols")
     for d in range(members):
         out_ref = out_refs[d]
 
         def body(s, carry):
-            place = places_ref[d * lines + line, s]
+            place = places_ref[(me ^ d) * cols + c, s]
             own = own_ref[jnp.minimum(place, here - 1)]
             other = other_ref[jnp.clip(place - here, 0, there - 1)]
             out_ref[s] = lax.select(place < here, own, other)
@@ -355,26 +381,30 @@
     columns = sketch.shape[1]
     sketch = sketch.reshape(-1, members, height, columns)
     per = sketch.shape[0]
-    swap = [(r, (r + members) % rows) for r in range(rows)]
-    row = table_row(block_cols, counts, columns, sketch.dtype)
-    if cols == 2:
-        here = row + lax.ppermute(row, "cols", [(0, 1), (1, 0)])
-    else:
-        here = lax.psum(row, "cols")
-    across = lax.ppermute(here, "rows", swap)
-    stripes = exchange(cut(sketch, here, across), rows)
     largest = min(per * members, slots * members, 128)
-    levels = tuple(level for level in LEVELS if level < largest)
-    own, places, numbers, level = plan(stripes, slots, per, height, levels)
-
-    def with_other(count):
+    within = tuple(level for level in WITHIN if level < per)
+    across = tuple(level for level in ACROSS if level < largest)
+    table = table_copies(block_cols, counts, rows * cols)
+    table = lax.all_to_all(table, ("rows", "cols"), split_axis=0, concat_axis=0, tiled=True)
+    places, lists, near, far = plan(table, slots, per, within, across)
+
+    def within_half(count):
         def run():
-            other = lax.ppermute(listed(numbers, own, count), "rows", swap)
+            return order(exchange(cut(lists, sketch, count), rows), per)
+
+        return run
+
+    own = lax.switch(near[0], [within_half(count) for count in (*within, per)])
+
+    def across_halves(count):
+        def run():
+            swap = [(r, (r + members) % rows) for r in range(rows)]
+            other = lax.ppermute(listed(lists, own, count), "rows", swap)
             return pick(places, own, other, members)
 
         return run
 
-    picked = lax.switch(level[0], [with_other(count) for count in (*levels, largest)])
+    picked = lax.switch(far[0], [across_halves(count) for count in (*across, largest)])
     return exchange(picked, rows)
 
 

time: 170 us -> 165 us (0.971); the launches traced: 170 us -> 167 us
  blocking collectives: 26.2 us -> 37.5 us
  starting transfers between devices: 28 us -> 16.9 us
  waiting for transfers between devices: 41.3 us -> 36.5 us
  Pallas kernels: 69.7 us -> 73 us
    all_to_all x0 -> x1, blocking collectives: none -> 14.4 us  [fetch(): lax.all_to_all(table, ('rows', 'cols'), split_axis=0, concat_axis=0, tile...]
    ppermute x14, waiting for transfers between devices: 25.2 us -> 15.6 us  [exchange(): lax.ppermute(pieces[d], 'rows', [(r, r ^ d) for r in range(rows)])]
    ppermute x3 -> x1, starting transfers between devices: 7.04 us -> 0.59 us  [run(): other = lax.ppermute(listed(lists, own, count), 'rows', swap)]
    ppermute x3 -> x1, waiting for transfers between devices: 13.5 us -> 18.2 us  [run(): other = lax.ppermute(listed(lists, own, count), 'rows', swap)]
    ppermute x14, starting transfers between devices: 20.9 us -> 16.2 us  [exchange(): lax.ppermute(pieces[d], 'rows', [(r, r ^ d) for r in range(rows)])]
    all_to_all x1, blocking collectives: 13.7 us -> 10.6 us  [local(): lax.all_to_all(pieces, 'rows', split_axis=0, concat_axis=0, tiled=True)]
    pallas_call x3 -> x4, Pallas kernels: 2.83 us -> 5.24 us  [the longest x1 2.21 us: plan(): pl.pallas_call(functools.partial(plan_kernel, per, within, across), out_s...]
  transfers between devices with their start and end apart: 18 -> 16, of which waited for: 16 -> 10; matrix products, arithmetic and copies ran while one was open for 0% -> 0% of each run, Pallas kernels for 0% -> 0%
where the time goes in v7:
time: 165 us; the launch traced here: 167 us
  Pallas kernels  73 us (44%)
  blocking collectives  37.5 us (23%)
  waiting for transfers between devices  36.5 us (22%)
  starting transfers between devices  16.9 us (10%)
  between operations  2.65 us (2%)
    pallas_call x1, Pallas kernels, factor_and_basis(): pl.pallas_call(functools.partial(factor_kernel, total_rows), out_shape=(j...  62.2 us
    ppermute x1, waiting for transfers between devices, run(): other = lax.ppermute(listed(lists, own, count), 'rows', swap)  18.2 us
    ppermute x14, starting transfers between devices, exchange(): lax.ppermute(pieces[d], 'rows', [(r, r ^ d) for r in range(rows)])  16.2 us
    ppermute x14, waiting for transfers between devices, exchange(): lax.ppermute(pieces[d], 'rows', [(r, r ^ d) for r in range(rows)])  15.6 us
    all_to_all x1, blocking collectives, fetch(): lax.all_to_all(table, ('rows', 'cols'), split_axis=0, concat_axis=0, tile...  14.4 us
    all_to_all x1, blocking collectives, spread(): return lax.all_to_all(copies, axes, split_axis=0, concat_axis=0, tiled=True)  12.5 us
    all_to_all x1, blocking collectives, local(): lax.all_to_all(pieces, 'rows', split_axis=0, concat_axis=0, tiled=True)  10.6 us
  transfers between devices with their start and end apart: 16, of which 10 were waited for; matrix products, arithmetic and copies ran while one was open for 0% of the time, Pallas kernels for 0%

profile of v7, /device:TPU:0, one launch (start us, length us, event | category | flops | bytes accessed | tf_op | source)
XLA Modules:
  0.0 166.7 jit_solution(14016020375437836818)
XLA Ops:
  1.3 1.3 table_copies.1
  2.6 14.4 %all_to_all.15.table_ref = s32[32,1,128]{2,1,0:T(1,128)S(1)} all-to-all(s32[32,1,128]{2,1,0:T(1,128)} %table_copies.1), channel_id=1, replica_groups=mesh['rows'=16,'cols'=2] {'rows','cols'}, dimensions={0} | all-to-all | bytes 32768 | tf_op jit(solution)/shard_map/all_to_all | solution.py:388
  16.9 2.2 %plan.1 = (s32[32,8]{1,0:T(8,128)S(1)}, s32[8,128]{1,0:T(8,128)S(1)}, s32[1]{0:T(128)}, s32[1]{0:T(128)}) custom-call(s32[32,1,128]{2,1,0:T(1,128)S(1)} %all_to_all.15.table_ref), custom_call_target="tpu_custom_call" | custom-call | tf_op jit(solution)/shard_map/plan/pallas_call | solution.py:114
  20.5 15.6 %conditional.2 = (bf16[128,32,256]{2,1,0:T(8,128)(2,1)S(1)}) conditional(s32[]{:T(128)} %bitcast.1, (s32[8,128]{1,0:T(8,128)S(1)}, bf16[16,8,32,256]{3,2,1,0:T(8,128)(2,1)}) %tuple.60, (s32[8,128]{1,0:T(8,128)S(1)}, bf16[16,8,32,256]{3,2,1,0:T(8,128)(2,1)}) %tuple.61, (s32[8,128]{1,0:T(8,128)S(1)}, ...), branch_computations={%region_0.0_spmd, %region_1.0_spmd, %region_2.0_spmd, %region_3.0_... | conditional | bytes 7340320 | solution.py:397
  20.5 1.7 %cut_stripes.4 = (bf16[6,32,256]{2,1,0:T(8,128)(2,1)S(1)}, bf16[6,32,256]{2,1,0:T(8,128)(2,1)S(1)}, bf16[6,32,256]{2,1,0:T(8,128)(2,1)S(1)}, bf16[6,32,256]{2,1,...) custom-call(s32[8,128]{1,0:T(8,128)S(1)} %get-tuple-element.60.lists, ...), custom_call_target="tpu_custom_call" | custom-call | tf_op jit(solution)/shard_map/cond/branch_0_fun/cut_stripes/pallas_call | solution.py:139
  22.2 0.6 collective-permute-start
  22.8 0.6 collective-permute-start.1
  23.4 2.3 %collective-permute-start.2 = (bf16[6,32,256]{2,1,0:T(8,128)(2,1)S(1)}, bf16[6,32,256]{2,1,0:T(8,128)(2,1)S(1)}, u32[]{:S(2)}, u32[]{:S(2)}) collective-permute-start(bf16[6,32,256]{2,1,0:T(8,128)(2,1)S(1)} %get-tuple-element.68), channel_id=1, source_target_pairs={{0,6},{2,4},{4,2},{6,0},{8,14},{10,12},{12,10},{14,8},{16,22},{18,... | collective-permute-start | bytes 294920 | tf_op jit(solution)/shard_map/cond/branch_0_fun/ppermute | solution.py:373
  25.7 0.6 collective-permute-start.3
  26.3 1.4 collective-permute-start.4
  27.7 0.0 collective-permute-done.refs_1_
  27.7 0.7 collective-permute-start.5
  28.4 0.7 collective-permute-done.1.refs_2_
  29.0 2.6 %collective-permute-start.6 = (bf16[6,32,256]{2,1,0:T(8,128)(2,1)S(1)}, bf16[6,32,256]{2,1,0:T(8,128)(2,1)S(1)}, u32[]{:S(2)}, u32[]{:S(2)}) collective-permute-start(bf16[6,32,256]{2,1,0:T(8,128)(2,1)S(1)} %get-tuple-element.72), channel_id=1, source_target_pairs={{0,14},{2,12},{4,10},{6,8},{8,6},{10,4},{12,2},{14,0},{16,30},{18,... | collective-permute-start | bytes 294920 | tf_op jit(solution)/shard_map/cond/branch_0_fun/ppermute | solution.py:373
  31.6 0.0 collective-permute-done.2.refs_3_
  31.6 0.0 collective-permute-done.3.refs_4_
  31.6 1.9 %collective-permute-done.4.refs_5_ = bf16[6,32,256]{2,1,0:T(8,128)(2,1)S(1)} collective-permute-done((bf16[6,32,256]{2,1,0:T(8,128)(2,1)S(1)}, bf16[6,32,256]{2,1,0:T(8,128)(2,1)S(1)}, u32[]{:S(2)}, u32[]{:S(2)}) %collective-permute-start.4) | collective-permute-done | bytes 98336 | tf_op jit(solution)/shard_map/cond/branch_0_fun/ppermute | solution.py:373
  33.4 1.5 collective-permute-done.5.refs_6_
  34.9 1.1 collective-permute-done.6.refs_7_
  36.0 0.1 order_stripes.4
  36.1 0.0 copy-start
  36.1 0.0 copy-start.1
  36.1 21.4 %conditional.3 = ((bf16[8,32,256]{2,1,0:T(8,128)(2,1)S(1)}, bf16[8,32,256]{2,1,0:T(8,128)(2,1)S(1)}, bf16[8,32,256]{2,1,0:T(8,128)(2,1)}, bf16[8,32,256]{2,1,0:T...) conditional(s32[]{:T(128)} %bitcast, (s32[8,128]{1,0:T(8,128)S(1)}, ...), branch_computations={%region_4.0_spmd, %region_5.0_spmd, %region_6.0_spmd, %region_7.0_... | conditional | bytes 4194352 | solution.py:407
  36.1 0.6 listed_stripes.12
  36.8 0.6 collective-permute-start.33
  37.4 18.2 %collective-permute-done.33.other_ref = bf16[24,32,256]{2,1,0:T(8,128)(2,1)S(1)} collective-permute-done((bf16[24,32,256]{2,1,0:T(8,128)(2,1)S(1)}, bf16[24,32,256]{2,1,0:T(8,128)(2,1)S(1)}, u32[]{:S(2)}, u32[]{:S(2)}) %collective-permute-start.33) | collective-permute-done | bytes 393248 | tf_op jit(solution)/shard_map/cond/branch_5_fun/ppermute | solution.py:402
  55.6 1.9 %pick_stripes.12 = (bf16[8,32,256]{2,1,0:T(8,128)(2,1)S(1)}, bf16[8,32,256]{2,1,0:T(8,128)(2,1)S(1)}, bf16[8,32,256]{2,1,0:T(8,128)(2,1)}, bf16[8,32,256]{2,1,0:...) custom-call(s32[32,8]{1,0:T(8,128)S(1)} %get-tuple-element.118.place, ...), custom_call_target="tpu_custom_call" | custom-call | tf_op jit(solution)/shard_map/cond/branch_5_fun/pick_stripes/pallas_call | solution.py:206
  57.5 0.9 collective-permute-start.35
  58.4 1.5 collective-permute-start.36
  59.9 1.1 collective-permute-start.37
  61.0 0.0 collective-permute-start.38
  61.0 2.3 %collective-permute-start.39 = (bf16[8,32,256]{2,1,0:T(8,128)(2,1)}, bf16[8,32,256]{2,1,0:T(8,128)(2,1)S(1)}, u32[]{:S(2)}, u32[]{:S(2)}) collective-permute-start(bf16[8,32,256]{2,1,0:T(8,128)(2,1)} %get-tuple-element.149), channel_id=1, source_target_pairs={{0,10},{2,8},{4,14},{6,12},{8,2},{10,0},{12,6},{14,4},{16,26},{18,... | collective-permute-start | bytes 393224 | tf_op jit(solution)/shard_map/ppermute | solution.py:373
  63.4 0.0 collective-permute-done.35.refs_1_
  63.4 0.9 collective-permute-start.40
  64.3 2.1 %collective-permute-done.36.refs_2_ = bf16[8,32,256]{2,1,0:T(8,128)(2,1)S(1)} collective-permute-done((bf16[8,32,256]{2,1,0:T(8,128)(2,1)}, bf16[8,32,256]{2,1,0:T(8,128)(2,1)S(1)}, u32[]{:S(2)}, u32[]{:S(2)}) %collective-permute-start.36) | collective-permute-done | bytes 131104 | tf_op jit(solution)/shard_map/ppermute | solution.py:373
  66.4 0.7 collective-permute-start.41
  67.1 0.0 collective-permute-done.37.refs_3_
  67.1 0.0 collective-permute-done.38.refs_4_
  67.2 3.6 %collective-permute-done.39.refs_5_ = bf16[8,32,256]{2,1,0:T(8,128)(2,1)S(1)} collective-permute-done((bf16[8,32,256]{2,1,0:T(8,128)(2,1)}, bf16[8,32,256]{2,1,0:T(8,128)(2,1)S(1)}, u32[]{:S(2)}, u32[]{:S(2)}) %collective-permute-start.39) | collective-permute-done | bytes 131104 | tf_op jit(solution)/shard_map/ppermute | solution.py:373
  70.8 2.4 %collective-permute-done.40.refs_6_ = bf16[8,32,256]{2,1,0:T(8,128)(2,1)S(1)} collective-permute-done((bf16[8,32,256]{2,1,0:T(8,128)(2,1)}, bf16[8,32,256]{2,1,0:T(8,128)(2,1)S(1)}, u32[]{:S(2)}, u32[]{:S(2)}) %collective-permute-start.40) | collective-permute-done | bytes 131104 | tf_op jit(solution)/shard_map/ppermute | solution.py:373
  73.2 2.3 %collective-permute-done.41.refs_7_ = bf16[8,32,256]{2,1,0:T(8,128)(2,1)S(1)} collective-permute-done((bf16[8,32,256]{2,1,0:T(8,128)(2,1)}, bf16[8,32,256]{2,1,0:T(8,128)(2,1)S(1)}, u32[]{:S(2)}, u32[]{:S(2)}) %collective-permute-start.41) | collective-permute-done | bytes 131104 | tf_op jit(solution)/shard_map/ppermute | solution.py:373
  75.5 0.0 copy-done
  75.5 0.0 copy-done.1
  75.5 1.7 block_products.1.mine_ref
  77.2 0.1 collective-permute-start.42
  77.2 2.6 %collective-permute-done.42.other_ref = f32[1024,256]{1,0:T(8,128)S(1)} collective-permute-done((f32[1024,256]{1,0:T(8,128)S(1)}, f32[1024,256]{1,0:T(8,128)S(1)}, u32[]{:S(2)}, u32[]{:S(2)}) %collective-permute-start.42) | collective-permute-done | bytes 1048608 | tf_op jit(solution)/shard_map/ppermute | solution.py:421
  79.9 1.4 sum_and_gram.1
  81.3 10.6 %all_to_all.16 = f32[16,16,128]{2,1,0:T(8,128)S(1)} all-to-all(f32[16,16,128]{2,1,0:T(8,128)S(1)} %bitcast.6), channel_id=1, replica_groups=mesh['rows'=16,'cols'=2] {'rows'}, dimensions={0} | all-to-all | bytes 262144 | tf_op jit(solution)/shard_map/all_to_all | solution.py:424
  92.0 12.5 %all_to_all.17 = f32[32,16,128]{2,1,0:T(8,128)S(1)} all-to-all(f32[32,16,128]{2,1,0:T(8,128)S(1)} %broadcast_in_dim.2), channel_id=1, replica_groups=mesh['rows'=16,'cols'=2] {'rows','cols'}, dimensions={0} | all-to-all | bytes 524288 | tf_op jit(solution)/shard_map/all_to_all | solution.py:366
  104.5 62.2 %factor_and_basis.1 = (f32[512,256]{1,0:T(8,128)}, f32[256,256]{1,0:T(8,128)}) custom-call(f32[16,2,16,128]{3,2,1,0:T(8,128)S(1)} %bitcast.5, f32[512,256]{1,0:T(8,128)S(1)} %get-tuple-element.153.own_ref), custom_call_target="tpu_custom_call" | custom-call | tf_op jit(solution)/shard_map/factor_and_basis/pallas_call | solution.py:350
  (2 shorter events, 0.0 us)
Async XLA Ops:
  22.2 5.6 %collective-permute-start = (bf16[6,32,256]{2,1,0:T(8,128)(2,1)S(1)}, bf16[6,32,256]{2,1,0:T(8,128)(2,1)S(1)}, u32[]{:S(2)}, u32[]{:S(2)}) collective-permute-start(bf16[6,32,256]{2,1,0:T(8,128)(2,1)S(1)} %get-tuple-element.66), channel_id=1, source_target_pairs={{0,2},{2,0},{4,6},{6,4},{8,10},{10,8},{12,14},{14,12},{16,18},{18,... | collective-permute-start | bytes 294920 | tf_op jit(solution)/shard_map/cond/branch_0_fun/ppermute | solution.py:373
  22.8 6.3 %collective-permute-start.1 = (bf16[6,32,256]{2,1,0:T(8,128)(2,1)S(1)}, bf16[6,32,256]{2,1,0:T(8,128)(2,1)S(1)}, u32[]{:S(2)}, u32[]{:S(2)}) collective-permute-start(bf16[6,32,256]{2,1,0:T(8,128)(2,1)S(1)} %get-tuple-element.67), channel_id=1, source_target_pairs={{0,4},{2,6},{4,0},{6,2},{8,12},{10,14},{12,8},{14,10},{16,20},{18,... | collective-permute-start | bytes 294920 | tf_op jit(solution)/shard_map/cond/branch_0_fun/ppermute | solution.py:373
  23.4 8.2 %collective-permute-start.2 = (bf16[6,32,256]{2,1,0:T(8,128)(2,1)S(1)}, bf16[6,32,256]{2,1,0:T(8,128)(2,1)S(1)}, u32[]{:S(2)}, u32[]{:S(2)}) collective-permute-start(bf16[6,32,256]{2,1,0:T(8,128)(2,1)S(1)} %get-tuple-element.68), channel_id=1, source_target_pairs={{0,6},{2,4},{4,2},{6,0},{8,14},{10,12},{12,10},{14,8},{16,22},{18,... | collective-permute-start | bytes 294920 | tf_op jit(solution)/shard_map/cond/branch_0_fun/ppermute | solution.py:373
  25.7 5.9 %collective-permute-start.3 = (bf16[6,32,256]{2,1,0:T(8,128)(2,1)S(1)}, bf16[6,32,256]{2,1,0:T(8,128)(2,1)S(1)}, u32[]{:S(2)}, u32[]{:S(2)}) collective-permute-start(bf16[6,32,256]{2,1,0:T(8,128)(2,1)S(1)} %get-tuple-element.69), channel_id=1, source_target_pairs={{0,8},{2,10},{4,12},{6,14},{8,0},{10,2},{12,4},{14,6},{16,24},{18,... | collective-permute-start | bytes 294920 | tf_op jit(solution)/shard_map/cond/branch_0_fun/ppermute | solution.py:373
  26.3 7.1 %collective-permute-start.4 = (bf16[6,32,256]{2,1,0:T(8,128)(2,1)S(1)}, bf16[6,32,256]{2,1,0:T(8,128)(2,1)S(1)}, u32[]{:S(2)}, u32[]{:S(2)}) collective-permute-start(bf16[6,32,256]{2,1,0:T(8,128)(2,1)S(1)} %get-tuple-element.70), channel_id=1, source_target_pairs={{0,10},{2,8},{4,14},{6,12},{8,2},{10,0},{12,6},{14,4},{16,26},{18,... | collective-permute-start | bytes 294920 | tf_op jit(solution)/shard_map/cond/branch_0_fun/ppermute | solution.py:373
  27.7 7.2 %collective-permute-start.5 = (bf16[6,32,256]{2,1,0:T(8,128)(2,1)S(1)}, bf16[6,32,256]{2,1,0:T(8,128)(2,1)S(1)}, u32[]{:S(2)}, u32[]{:S(2)}) collective-permute-start(bf16[6,32,256]{2,1,0:T(8,128)(2,1)S(1)} %get-tuple-element.71), channel_id=1, source_target_pairs={{0,12},{2,14},{4,8},{6,10},{8,4},{10,6},{12,0},{14,2},{16,28},{18,... | collective-permute-start | bytes 294920 | tf_op jit(solution)/shard_map/cond/branch_0_fun/ppermute | solution.py:373
  29.0 7.0 %collective-permute-start.6 = (bf16[6,32,256]{2,1,0:T(8,128)(2,1)S(1)}, bf16[6,32,256]{2,1,0:T(8,128)(2,1)S(1)}, u32[]{:S(2)}, u32[]{:S(2)}) collective-permute-start(bf16[6,32,256]{2,1,0:T(8,128)(2,1)S(1)} %get-tuple-element.72), channel_id=1, source_target_pairs={{0,14},{2,12},{4,10},{6,8},{8,6},{10,4},{12,2},{14,0},{16,30},{18,... | collective-permute-start | bytes 294920 | tf_op jit(solution)/shard_map/cond/branch_0_fun/ppermute | solution.py:373
  36.1 39.4 %copy-start = (bf16[8,256,256]{2,1,0:T(8,128)(2,1)S(1)}, bf16[8,256,256]{2,1,0:T(8,128)(2,1)}, u32[]{:S(2)}) copy-start(bf16[8,256,256]{2,1,0:T(8,128)(2,1)} %blocks_ref.1) | copy-start | bytes 3145732
  36.1 39.4 %copy-start.1 = (s32[8]{0:T(128)S(1)}, s32[8]{0:T(128)}, u32[]{:S(2)}) copy-start(s32[8]{0:T(128)} %rows_ref.1) | copy-start | bytes 100
  36.8 18.8 %collective-permute-start.33 = (bf16[24,32,256]{2,1,0:T(8,128)(2,1)S(1)}, bf16[24,32,256]{2,1,0:T(8,128)(2,1)S(1)}, u32[]{:S(2)}, u32[]{:S(2)}) collective-permute-start(bf16[24,32,256]{2,1,0:T(8,128)(2,1)S(1)} %listed_stripes.12), channel_id=1, source_target_pairs={{0,16},{2,18},{4,20},{6,22},{8,24},{10,26},{12,28},{14,30},{16,0},... | collective-permute-start | bytes 1179656 | tf_op jit(solution)/shard_map/cond/branch_5_fun/ppermute | solution.py:402
  57.5 5.8 %collective-permute-start.35 = (bf16[8,32,256]{2,1,0:T(8,128)(2,1)S(1)}, bf16[8,32,256]{2,1,0:T(8,128)(2,1)S(1)}, u32[]{:S(2)}, u32[]{:S(2)}) collective-permute-start(bf16[8,32,256]{2,1,0:T(8,128)(2,1)S(1)} %get-tuple-element.145), channel_id=1, source_target_pairs={{0,2},{2,0},{4,6},{6,4},{8,10},{10,8},{12,14},{14,12},{16,18},{18,... | collective-permute-start | bytes 393224 | tf_op jit(solution)/shard_map/ppermute | solution.py:373
  58.4 8.0 %collective-permute-start.36 = (bf16[8,32,256]{2,1,0:T(8,128)(2,1)}, bf16[8,32,256]{2,1,0:T(8,128)(2,1)S(1)}, u32[]{:S(2)}, u32[]{:S(2)}) collective-permute-start(bf16[8,32,256]{2,1,0:T(8,128)(2,1)} %get-tuple-element.146), channel_id=1, source_target_pairs={{0,4},{2,6},{4,0},{6,2},{8,12},{10,14},{12,8},{14,10},{16,20},{18,... | collective-permute-start | bytes 393224 | tf_op jit(solution)/shard_map/ppermute | solution.py:373
  59.9 7.2 %collective-permute-start.37 = (bf16[8,32,256]{2,1,0:T(8,128)(2,1)}, bf16[8,32,256]{2,1,0:T(8,128)(2,1)S(1)}, u32[]{:S(2)}, u32[]{:S(2)}) collective-permute-start(bf16[8,32,256]{2,1,0:T(8,128)(2,1)} %get-tuple-element.147), channel_id=1, source_target_pairs={{0,6},{2,4},{4,2},{6,0},{8,14},{10,12},{12,10},{14,8},{16,22},{18,... | collective-permute-start | bytes 393224 | tf_op jit(solution)/shard_map/ppermute | solution.py:373
  61.0 6.1 %collective-permute-start.38 = (bf16[8,32,256]{2,1,0:T(8,128)(2,1)}, bf16[8,32,256]{2,1,0:T(8,128)(2,1)S(1)}, u32[]{:S(2)}, u32[]{:S(2)}) collective-permute-start(bf16[8,32,256]{2,1,0:T(8,128)(2,1)} %get-tuple-element.148), channel_id=1, source_target_pairs={{0,8},{2,10},{4,12},{6,14},{8,0},{10,2},{12,4},{14,6},{16,24},{18,... | collective-permute-start | bytes 393224 | tf_op jit(solution)/shard_map/ppermute | solution.py:373
  61.0 9.8 %collective-permute-start.39 = (bf16[8,32,256]{2,1,0:T(8,128)(2,1)}, bf16[8,32,256]{2,1,0:T(8,128)(2,1)S(1)}, u32[]{:S(2)}, u32[]{:S(2)}) collective-permute-start(bf16[8,32,256]{2,1,0:T(8,128)(2,1)} %get-tuple-element.149), channel_id=1, source_target_pairs={{0,10},{2,8},{4,14},{6,12},{8,2},{10,0},{12,6},{14,4},{16,26},{18,... | collective-permute-start | bytes 393224 | tf_op jit(solution)/shard_map/ppermute | solution.py:373
  63.4 9.9 %collective-permute-start.40 = (bf16[8,32,256]{2,1,0:T(8,128)(2,1)}, bf16[8,32,256]{2,1,0:T(8,128)(2,1)S(1)}, u32[]{:S(2)}, u32[]{:S(2)}) collective-permute-start(bf16[8,32,256]{2,1,0:T(8,128)(2,1)} %get-tuple-element.150), channel_id=1, source_target_pairs={{0,12},{2,14},{4,8},{6,10},{8,4},{10,6},{12,0},{14,2},{16,28},{18,... | collective-permute-start | bytes 393224 | tf_op jit(solution)/shard_map/ppermute | solution.py:373
  66.4 9.0 %collective-permute-start.41 = (bf16[8,32,256]{2,1,0:T(8,128)(2,1)}, bf16[8,32,256]{2,1,0:T(8,128)(2,1)S(1)}, u32[]{:S(2)}, u32[]{:S(2)}) collective-permute-start(bf16[8,32,256]{2,1,0:T(8,128)(2,1)} %get-tuple-element.151), channel_id=1, source_target_pairs={{0,14},{2,12},{4,10},{6,8},{8,6},{10,4},{12,2},{14,0},{16,30},{18,... | collective-permute-start | bytes 393224 | tf_op jit(solution)/shard_map/ppermute | solution.py:373
  77.2 2.7 %collective-permute-start.42 = (f32[1024,256]{1,0:T(8,128)S(1)}, f32[1024,256]{1,0:T(8,128)S(1)}, u32[]{:S(2)}, u32[]{:S(2)}) collective-permute-start(f32[1024,256]{1,0:T(8,128)S(1)} %block_products.1.mine_ref), channel_id=1, source_target_pairs={{0,1},{1,0},{2,3},{3,2},{4,5},{5,4},{6,7},{7,6},{8,9},{9,8},{10,11... | collective-permute-start | bytes 3145736 | tf_op jit(solution)/shard_map/ppermute | solution.py:421

commit v8 on v7

--- a/solution.py
+++ b/solution.py
@@ -126,24 +126,46 @@
     )(table)
 
 
-def cut_kernel(lists_ref, sketch_ref, *out_refs):
-    members = len(out_refs)
+def distances(members):
+    return [0, *sorted(range(1, members), key=lambda d: (-d.bit_count(), -d))]
+
+
+def turn_kernel(sketch_ref, out_ref):
+    members = out_ref.shape[0]
     me = lax.axis_index("rows") % members
+    for i, d in enumerate(distances(members)):
+        out_ref[i] = sketch_ref[:, me ^ d]
+
+
+def turn(sketch):
+    blocks, members, height, columns = sketch.shape
+    return pl.pallas_call(
+        turn_kernel,
+        out_shape=jax.ShapeDtypeStruct((members, blocks, height, columns), sketch.dtype),
+        in_specs=[VMEM],
+        out_specs=VMEM,
+        compiler_params=pltpu.CompilerParams(vmem_limit_bytes=24 * MIB),
+        cost_estimate=pl.CostEstimate(flops=0, bytes_accessed=4 * sketch.size, transcendentals=0),
+        name="turn_stripes",
+    )(sketch)
+
+
+def cut_kernel(lists_ref, stripes_ref, *out_refs):
     for k in range(out_refs[0].shape[0]):
-        for d, out_ref in enumerate(out_refs):
-            out_ref[k] = sketch_ref[lists_ref[1, k], me ^ d]
-
-
-def cut(lists, sketch, count):
-    _, members, height, columns = sketch.shape
+        for i, out_ref in enumerate(out_refs):
+            out_ref[k] = stripes_ref[i, lists_ref[1, k]]
+
+
+def cut(lists, stripes, count):
+    members, _, height, columns = stripes.shape
     return pl.pallas_call(
         cut_kernel,
-        out_shape=(jax.ShapeDtypeStruct((count, height, columns), sketch.dtype),) * members,
+        out_shape=(jax.ShapeDtypeStruct((count, height, columns), stripes.dtype),) * members,
         in_specs=[SMEM, VMEM],
         out_specs=(VMEM,) * members,
         compiler_params=pltpu.CompilerParams(vmem_limit_bytes=24 * MIB),
         name="cut_stripes",
-    )(lists, sketch)
+    )(lists, stripes)
 
 
 def order_kernel(*refs):
@@ -151,7 +173,7 @@
     members = len(stripe_refs)
     me = lax.axis_index("rows") % members
     per = all_ref.shape[0] // members
-    for d, ref in enumerate(stripe_refs):
+    for ref, d in zip(stripe_refs, distances(members)):
         all_ref[pl.ds((me ^ d) * per, ref.shape[0])] = ref[...]
 
 
@@ -189,8 +211,7 @@
     here, there = own_ref.shape[0], other_ref.shape[0]
     me = lax.axis_index("rows")
     c = lax.axis_index("cols")
-    for d in range(members):
-        out_ref = out_refs[d]
+    for d, out_ref in zip(distances(members), out_refs):
 
         def body(s, carry):
             place = places_ref[(me ^ d) * cols + c, s]
@@ -219,8 +240,8 @@
     columns = out_ref.shape[1]
     members = len(chosen_refs)
     me = lax.axis_index("rows") % members
-    for d in range(members):
-        whole[me ^ d] = chosen_refs[d][...]
+    for ref, d in zip(chosen_refs, distances(members) if members > 1 else [0]):
+        whole[me ^ d] = ref[...]
     out_ref[...] = jnp.zeros_like(out_ref)
     for s in range(slots):
 
@@ -367,11 +388,11 @@
 
 
 def exchange(pieces, rows):
-    far = sorted(range(2, len(pieces)), key=lambda d: (-d.bit_count(), -d))
-    arrived = [pieces[0]] + [None] * (len(pieces) - 1)
-    for d in [1, *far]:
-        arrived[d] = lax.ppermute(pieces[d], "rows", [(r, r ^ d) for r in range(rows)])
-    return arrived
+    order = distances(len(pieces))
+    return [
+        lax.ppermute(piece, "rows", [(r, r ^ d) for r in range(rows)]) if d else piece
+        for piece, d in zip(pieces, order)
+    ]
 
 
 def fetch(sketch, block_cols, counts, slots, width):
@@ -384,13 +405,14 @@
     largest = min(per * members, slots * members, 128)
     within = tuple(level for level in WITHIN if level < per)
     across = tuple(level for level in ACROSS if level < largest)
+    stripes = turn(sketch)
     table = table_copies(block_cols, counts, rows * cols)
     table = lax.all_to_all(table, ("rows", "cols"), split_axis=0, concat_axis=0, tiled=True)
     places, lists, near, far = plan(table, slots, per, within, across)
 
     def within_half(count):
         def run():
-            return order(exchange(cut(lists, sketch, count), rows), per)
+            return order(exchange(cut(lists, stripes, count), rows), per)
 
         return run
 
@@ -414,7 +436,7 @@
     rows, cols = lax.axis_size("rows"), lax.axis_size("cols")
     chosen = fetch(sketch, block_cols, counts, slots, width)
     if chosen[0].shape[1] % 16:
-        order = lax.axis_index("rows") % len(chosen) ^ jnp.arange(len(chosen))
+        order = jnp.argsort(lax.axis_index("rows") % len(chosen) ^ jnp.array(distances(len(chosen))))
         chosen = [jnp.stack(chosen)[order].swapaxes(0, 1).reshape(1, slots, width, columns)[0]]
     partial_rows = block_products(block_rows, counts, blocks, chosen)
     if cols == 2:

time: 165 us -> 160 us (0.970); the launches traced: 167 us -> 160 us
  blocking collectives: 37.5 us -> 24 us
  starting transfers between devices: 16.9 us -> 25.9 us
  waiting for transfers between devices: 36.5 us -> 34.2 us
    all_to_all x1 -> x0, blocking collectives: 14.4 us -> none  [fetch(): lax.all_to_all(table, ('rows', 'cols'), split_axis=0, concat_axis=0, tile...]
    all_to_all x0 -> x1, starting transfers between devices: none -> 7.3 us  [fetch(): lax.all_to_all(table, ('rows', 'cols'), split_axis=0, concat_axis=0, tile...]
    ppermute x1, waiting for transfers between devices: 18.2 us -> 12.2 us  [run(): other = lax.ppermute(listed(lists, own, count), 'rows', swap)]
    all_to_all x0 -> x1, waiting for transfers between devices: none -> 5.34 us  [fetch(): lax.all_to_all(table, ('rows', 'cols'), split_axis=0, concat_axis=0, tile...]
    ppermute x14, starting transfers between devices: 16.2 us -> 18.1 us  [exchange(): lax.ppermute(piece, 'rows', [(r, r ^ d) for r in range(rows)])]
  transfers between devices with their start and end apart: 16 -> 17, of which waited for: 10 -> 15; matrix products, arithmetic and copies ran while one was open for 0% -> 0% of each run, Pallas kernels for 0% -> 0%
where the time goes in v8:
time: 160 us
  Pallas kernels  71.5 us (45%)
  waiting for transfers between devices  34.2 us (21%)
  starting transfers between devices  25.9 us (16%)
  blocking collectives  24 us (15%)
  between operations  2.67 us (2%)
  local copies, waits for them, and re-layouts  1.62 us (1%)
    pallas_call x1, Pallas kernels, factor_and_basis(): pl.pallas_call(functools.partial(factor_kernel, total_rows), out_shape=(j...  62.2 us
    ppermute x14, starting transfers between devices, exchange(): lax.ppermute(piece, 'rows', [(r, r ^ d) for r in range(rows)])  18.1 us
    ppermute x14, waiting for transfers between devices, exchange(): lax.ppermute(piece, 'rows', [(r, r ^ d) for r in range(rows)])  14 us
    all_to_all x1, blocking collectives, spread(): return lax.all_to_all(copies, axes, split_axis=0, concat_axis=0, tiled=True)  12.5 us
    ppermute x1, waiting for transfers between devices, run(): other = lax.ppermute(listed(lists, own, count), 'rows', swap)  12.2 us
    all_to_all x1, blocking collectives, local(): lax.all_to_all(pieces, 'rows', split_axis=0, concat_axis=0, tiled=True)  11.5 us
    all_to_all x1, starting transfers between devices, fetch(): lax.all_to_all(table, ('rows', 'cols'), split_axis=0, concat_axis=0, tile...  7.3 us
    all_to_all x1, waiting for transfers between devices, fetch(): lax.all_to_all(table, ('rows', 'cols'), split_axis=0, concat_axis=0, tile...  5.34 us
  transfers between devices with their start and end apart: 17, of which 15 were waited for; matrix products, arithmetic and copies ran while one was open for 0% of the time, Pallas kernels for 0%

profile of v8, /device:TPU:0, one launch (start us, length us, event | category | flops | bytes accessed | tf_op | source)
XLA Modules:
  0.0 160.0 jit_solution(12801256369088543865)
XLA Ops:
  1.3 1.3 table_copies.1
  2.6 7.3 %all-to-all-start = ((s32[32,1,128]{2,1,0:T(1,128)}), s32[32,1,128]{2,1,0:T(1,128)S(1)}, u32[]{:S(2)}, u32[]{:S(2)}) async-start(s32[32,1,128]{2,1,0:T(1,128)} %table_copies.1), calls=%async_computation | async-start | bytes 32768 | tf_op jit(solution)/shard_map/all_to_all | solution.py:410
  9.9 0.0 copy-start
  9.9 1.6 copy-done
  11.5 0.1 turn_stripes.1
  11.6 5.3 %all-to-all-done.table_ref = s32[32,1,128]{2,1,0:T(1,128)S(1)} async-done(((s32[32,1,128]{2,1,0:T(1,128)}), s32[32,1,128]{2,1,0:T(1,128)S(1)}, u32[]{:S(2)}, u32[]{:S(2)}) %all-to-all-start) | async-done | bytes 16416 | tf_op jit(solution)/shard_map/all_to_all | solution.py:410
  16.9 2.2 %plan.1 = (s32[32,8]{1,0:T(8,128)S(1)}, s32[8,128]{1,0:T(8,128)S(1)}, s32[1]{0:T(128)}, s32[1]{0:T(128)}) custom-call(s32[32,1,128]{2,1,0:T(1,128)S(1)} %all-to-all-done.table_ref), custom_call_target="tpu_custom_call" | custom-call | tf_op jit(solution)/shard_map/plan/pallas_call | solution.py:114
  20.5 16.0 %conditional.2 = (bf16[128,32,256]{2,1,0:T(8,128)(2,1)S(1)}) conditional(s32[]{:T(128)} %bitcast.1, (s32[8,128]{1,0:T(8,128)S(1)}, bf16[8,16,32,256]{3,2,1,0:T(8,128)(2,1)S(1)}) %tuple.40, (s32[8,128]{1,0:T(8,128)S(1)}, bf16[8,16,32,256]{3,2,1,0:T(8,128)(2,1)S(1)}) %tuple.40, (s32[8,128]{1,0:T(8,128)S(1)}, ...), branch_computations={%region_0.0_spmd, %region_1.0_spmd, %region_2.0_spmd, %region_3.0_... | conditional | bytes 7340320 | solution.py:419
  20.5 0.7 cut_stripes.5
  21.2 0.7 collective-permute-start.7
  21.8 2.3 %collective-permute-start.8 = (bf16[7,32,256]{2,1,0:T(8,128)(2,1)S(1)}, bf16[7,32,256]{2,1,0:T(8,128)(2,1)S(1)}, u32[]{:S(2)}, u32[]{:S(2)}) collective-permute-start(bf16[7,32,256]{2,1,0:T(8,128)(2,1)S(1)} %get-tuple-element.77), channel_id=1, source_target_pairs={{0,12},{2,14},{4,8},{6,10},{8,4},{10,6},{12,0},{14,2},{16,28},{18,... | collective-permute-start | bytes 344072 | tf_op jit(solution)/shard_map/cond/branch_1_fun/ppermute | solution.py:393
  24.1 1.5 collective-permute-start.9
  25.6 0.6 collective-permute-start.10
  26.2 1.4 collective-permute-start.11
  27.7 2.4 %collective-permute-done.7.refs_1_ = bf16[7,32,256]{2,1,0:T(8,128)(2,1)S(1)} collective-permute-done((bf16[7,32,256]{2,1,0:T(8,128)(2,1)S(1)}, bf16[7,32,256]{2,1,0:T(8,128)(2,1)S(1)}, u32[]{:S(2)}, u32[]{:S(2)}) %collective-permute-start.7) | collective-permute-done | bytes 114720 | tf_op jit(solution)/shard_map/cond/branch_1_fun/ppermute | solution.py:393
  30.1 0.4 collective-permute-start.12
  30.5 1.0 collective-permute-done.8.refs_2_
  31.5 1.3 collective-permute-start.13
  32.8 0.2 collective-permute-done.9.refs_3_
  33.1 1.6 %collective-permute-done.10.refs_4_ = bf16[7,32,256]{2,1,0:T(8,128)(2,1)S(1)} collective-permute-done((bf16[7,32,256]{2,1,0:T(8,128)(2,1)S(1)}, bf16[7,32,256]{2,1,0:T(8,128)(2,1)S(1)}, u32[]{:S(2)}, u32[]{:S(2)}) %collective-permute-start.10) | collective-permute-done | bytes 114720 | tf_op jit(solution)/shard_map/cond/branch_1_fun/ppermute | solution.py:393
  34.7 0.0 collective-permute-done.11.refs_5_
  34.7 0.6 collective-permute-done.12.refs_6_
  35.3 1.0 collective-permute-done.13.refs_7_
  36.3 0.1 order_stripes.5
  36.4 0.0 copy-start.1
  36.4 0.0 copy-start.2
  36.4 15.3 %conditional.3 = ((bf16[8,32,256]{2,1,0:T(8,128)(2,1)S(1)}, bf16[8,32,256]{2,1,0:T(8,128)(2,1)S(1)}, bf16[8,32,256]{2,1,0:T(8,128)(2,1)}, bf16[8,32,256]{2,1,0:T...) conditional(s32[]{:T(128)} %bitcast, (s32[8,128]{1,0:T(8,128)S(1)}, ...), branch_computations={%region_4.0_spmd, %region_5.0_spmd, %region_6.0_spmd, %region_7.0_... | conditional | bytes 4194352 | solution.py:429
  36.5 0.6 listed_stripes.9
  37.1 0.5 collective-permute-start.30
  37.6 12.2 %collective-permute-done.30.other_ref = bf16[16,32,256]{2,1,0:T(8,128)(2,1)S(1)} collective-permute-done((bf16[16,32,256]{2,1,0:T(8,128)(2,1)S(1)}, bf16[16,32,256]{2,1,0:T(8,128)(2,1)S(1)}, u32[]{:S(2)}, u32[]{:S(2)}) %collective-permute-start.30) | collective-permute-done | bytes 262176 | tf_op jit(solution)/shard_map/cond/branch_2_fun/ppermute | solution.py:424
  49.8 1.9 %pick_stripes.9 = (bf16[8,32,256]{2,1,0:T(8,128)(2,1)S(1)}, bf16[8,32,256]{2,1,0:T(8,128)(2,1)S(1)}, bf16[8,32,256]{2,1,0:T(8,128)(2,1)}, bf16[8,32,256]{2,1,0:T...) custom-call(s32[32,8]{1,0:T(8,128)S(1)} %get-tuple-element.109.place, ...), custom_call_target="tpu_custom_call" | custom-call | tf_op jit(solution)/shard_map/cond/branch_2_fun/pick_stripes/pallas_call | solution.py:227
  51.7 0.0 collective-permute-start.35
  51.7 3.2 %collective-permute-start.36 = (bf16[8,32,256]{2,1,0:T(8,128)(2,1)}, bf16[8,32,256]{2,1,0:T(8,128)(2,1)S(1)}, u32[]{:S(2)}, u32[]{:S(2)}) collective-permute-start(bf16[8,32,256]{2,1,0:T(8,128)(2,1)} %get-tuple-element.146), channel_id=1, source_target_pairs={{0,12},{2,14},{4,8},{6,10},{8,4},{10,6},{12,0},{14,2},{16,28},{18,... | collective-permute-start | bytes 393224 | tf_op jit(solution)/shard_map/ppermute | solution.py:393
  54.9 0.7 collective-permute-start.37
  55.6 1.5 collective-permute-start.38
  57.0 1.8 %collective-permute-start.39 = (bf16[8,32,256]{2,1,0:T(8,128)(2,1)}, bf16[8,32,256]{2,1,0:T(8,128)(2,1)S(1)}, u32[]{:S(2)}, u32[]{:S(2)}) collective-permute-start(bf16[8,32,256]{2,1,0:T(8,128)(2,1)} %get-tuple-element.149), channel_id=1, source_target_pairs={{0,8},{2,10},{4,12},{6,14},{8,0},{10,2},{12,4},{14,6},{16,24},{18,... | collective-permute-start | bytes 393224 | tf_op jit(solution)/shard_map/ppermute | solution.py:393
  58.9 2.1 %collective-permute-done.35.refs_1_ = bf16[8,32,256]{2,1,0:T(8,128)(2,1)S(1)} collective-permute-done((bf16[8,32,256]{2,1,0:T(8,128)(2,1)S(1)}, bf16[8,32,256]{2,1,0:T(8,128)(2,1)S(1)}, u32[]{:S(2)}, u32[]{:S(2)}) %collective-permute-start.35) | collective-permute-done | bytes 131104 | tf_op jit(solution)/shard_map/ppermute | solution.py:393
  61.0 1.3 collective-permute-start.40
  62.3 0.9 collective-permute-done.36.refs_2_
  63.2 1.3 collective-permute-start.41
  64.5 1.2 collective-permute-done.37.refs_3_
  65.7 0.5 collective-permute-done.38.refs_4_
  66.2 0.0 collective-permute-done.39.refs_5_
  66.3 1.0 collective-permute-done.40.refs_6_
  67.3 1.4 collective-permute-done.41.refs_7_
  68.6 0.0 copy-done.1
  68.6 0.0 copy-done.2
  68.6 0.9 block_products.1.mine_ref
  69.6 0.1 collective-permute-start.42
  69.7 2.6 %collective-permute-done.42.other_ref = f32[1024,256]{1,0:T(8,128)S(1)} collective-permute-done((f32[1024,256]{1,0:T(8,128)S(1)}, f32[1024,256]{1,0:T(8,128)S(1)}, u32[]{:S(2)}, u32[]{:S(2)}) %collective-permute-start.42) | collective-permute-done | bytes 1048608 | tf_op jit(solution)/shard_map/ppermute | solution.py:443
  72.3 1.5 sum_and_gram.1
  73.8 11.5 %all_to_all.15 = f32[16,16,128]{2,1,0:T(8,128)S(1)} all-to-all(f32[16,16,128]{2,1,0:T(8,128)S(1)} %bitcast.7), channel_id=1, replica_groups=mesh['rows'=16,'cols'=2] {'rows'}, dimensions={0} | all-to-all | bytes 262144 | tf_op jit(solution)/shard_map/all_to_all | solution.py:446
  85.3 12.5 %all_to_all.16 = f32[32,16,128]{2,1,0:T(8,128)S(1)} all-to-all(f32[32,16,128]{2,1,0:T(8,128)S(1)} %broadcast_in_dim.2), channel_id=1, replica_groups=mesh['rows'=16,'cols'=2] {'rows','cols'}, dimensions={0} | all-to-all | bytes 524288 | tf_op jit(solution)/shard_map/all_to_all | solution.py:387
  97.8 62.2 %factor_and_basis.1 = (f32[512,256]{1,0:T(8,128)}, f32[256,256]{1,0:T(8,128)}) custom-call(f32[16,2,16,128]{3,2,1,0:T(8,128)S(1)} %bitcast.6, f32[512,256]{1,0:T(8,128)S(1)} %get-tuple-element.153.own_ref), custom_call_target="tpu_custom_call" | custom-call | tf_op jit(solution)/shard_map/factor_and_basis/pallas_call | solution.py:371
  (2 shorter events, 0.0 us)
Async XLA Ops:
  2.6 14.4 %all-to-all-start = ((s32[32,1,128]{2,1,0:T(1,128)}), s32[32,1,128]{2,1,0:T(1,128)S(1)}, u32[]{:S(2)}, u32[]{:S(2)}) async-start(s32[32,1,128]{2,1,0:T(1,128)} %table_copies.1), calls=%async_computation | async-start | bytes 32768 | tf_op jit(solution)/shard_map/all_to_all | solution.py:410
  9.9 1.6 copy-start
  21.2 8.9 %collective-permute-start.7 = (bf16[7,32,256]{2,1,0:T(8,128)(2,1)S(1)}, bf16[7,32,256]{2,1,0:T(8,128)(2,1)S(1)}, u32[]{:S(2)}, u32[]{:S(2)}) collective-permute-start(bf16[7,32,256]{2,1,0:T(8,128)(2,1)S(1)} %get-tuple-element.76), channel_id=1, source_target_pairs={{0,14},{2,12},{4,10},{6,8},{8,6},{10,4},{12,2},{14,0},{16,30},{18,... | collective-permute-start | bytes 344072 | tf_op jit(solution)/shard_map/cond/branch_1_fun/ppermute | solution.py:393
  21.8 9.7 %collective-permute-start.8 = (bf16[7,32,256]{2,1,0:T(8,128)(2,1)S(1)}, bf16[7,32,256]{2,1,0:T(8,128)(2,1)S(1)}, u32[]{:S(2)}, u32[]{:S(2)}) collective-permute-start(bf16[7,32,256]{2,1,0:T(8,128)(2,1)S(1)} %get-tuple-element.77), channel_id=1, source_target_pairs={{0,12},{2,14},{4,8},{6,10},{8,4},{10,6},{12,0},{14,2},{16,28},{18,... | collective-permute-start | bytes 344072 | tf_op jit(solution)/shard_map/cond/branch_1_fun/ppermute | solution.py:393
  24.1 8.9 %collective-permute-start.9 = (bf16[7,32,256]{2,1,0:T(8,128)(2,1)S(1)}, bf16[7,32,256]{2,1,0:T(8,128)(2,1)S(1)}, u32[]{:S(2)}, u32[]{:S(2)}) collective-permute-start(bf16[7,32,256]{2,1,0:T(8,128)(2,1)S(1)} %get-tuple-element.78), channel_id=1, source_target_pairs={{0,10},{2,8},{4,14},{6,12},{8,2},{10,0},{12,6},{14,4},{16,26},{18,... | collective-permute-start | bytes 344072 | tf_op jit(solution)/shard_map/cond/branch_1_fun/ppermute | solution.py:393
  25.6 9.0 %collective-permute-start.10 = (bf16[7,32,256]{2,1,0:T(8,128)(2,1)S(1)}, bf16[7,32,256]{2,1,0:T(8,128)(2,1)S(1)}, u32[]{:S(2)}, u32[]{:S(2)}) collective-permute-start(bf16[7,32,256]{2,1,0:T(8,128)(2,1)S(1)} %get-tuple-element.79), channel_id=1, source_target_pairs={{0,6},{2,4},{4,2},{6,0},{8,14},{10,12},{12,10},{14,8},{16,22},{18,... | collective-permute-start | bytes 344072 | tf_op jit(solution)/shard_map/cond/branch_1_fun/ppermute | solution.py:393
  26.2 8.4 %collective-permute-start.11 = (bf16[7,32,256]{2,1,0:T(8,128)(2,1)S(1)}, bf16[7,32,256]{2,1,0:T(8,128)(2,1)S(1)}, u32[]{:S(2)}, u32[]{:S(2)}) collective-permute-start(bf16[7,32,256]{2,1,0:T(8,128)(2,1)S(1)} %get-tuple-element.80), channel_id=1, source_target_pairs={{0,8},{2,10},{4,12},{6,14},{8,0},{10,2},{12,4},{14,6},{16,24},{18,... | collective-permute-start | bytes 344072 | tf_op jit(solution)/shard_map/cond/branch_1_fun/ppermute | solution.py:393
  30.1 5.2 %collective-permute-start.12 = (bf16[7,32,256]{2,1,0:T(8,128)(2,1)S(1)}, bf16[7,32,256]{2,1,0:T(8,128)(2,1)S(1)}, u32[]{:S(2)}, u32[]{:S(2)}) collective-permute-start(bf16[7,32,256]{2,1,0:T(8,128)(2,1)S(1)} %get-tuple-element.81), channel_id=1, source_target_pairs={{0,4},{2,6},{4,0},{6,2},{8,12},{10,14},{12,8},{14,10},{16,20},{18,... | collective-permute-start | bytes 344072 | tf_op jit(solution)/shard_map/cond/branch_1_fun/ppermute | solution.py:393
  31.5 4.8 %collective-permute-start.13 = (bf16[7,32,256]{2,1,0:T(8,128)(2,1)S(1)}, bf16[7,32,256]{2,1,0:T(8,128)(2,1)S(1)}, u32[]{:S(2)}, u32[]{:S(2)}) collective-permute-start(bf16[7,32,256]{2,1,0:T(8,128)(2,1)S(1)} %get-tuple-element.82), channel_id=1, source_target_pairs={{0,2},{2,0},{4,6},{6,4},{8,10},{10,8},{12,14},{14,12},{16,18},{18,... | collective-permute-start | bytes 344072 | tf_op jit(solution)/shard_map/cond/branch_1_fun/ppermute | solution.py:393
  36.4 32.2 %copy-start.1 = (bf16[8,256,256]{2,1,0:T(8,128)(2,1)S(1)}, bf16[8,256,256]{2,1,0:T(8,128)(2,1)}, u32[]{:S(2)}) copy-start(bf16[8,256,256]{2,1,0:T(8,128)(2,1)} %blocks_ref.1) | copy-start | bytes 3145732
  36.4 32.2 %copy-start.2 = (s32[8]{0:T(128)S(1)}, s32[8]{0:T(128)}, u32[]{:S(2)}) copy-start(s32[8]{0:T(128)} %rows_ref.1) | copy-start | bytes 100
  37.1 12.7 %collective-permute-start.30 = (bf16[16,32,256]{2,1,0:T(8,128)(2,1)S(1)}, bf16[16,32,256]{2,1,0:T(8,128)(2,1)S(1)}, u32[]{:S(2)}, u32[]{:S(2)}) collective-permute-start(bf16[16,32,256]{2,1,0:T(8,128)(2,1)S(1)} %listed_stripes.9), channel_id=1, source_target_pairs={{0,16},{2,18},{4,20},{6,22},{8,24},{10,26},{12,28},{14,30},{16,0},... | collective-permute-start | bytes 786440 | tf_op jit(solution)/shard_map/cond/branch_2_fun/ppermute | solution.py:424
  51.7 9.3 %collective-permute-start.35 = (bf16[8,32,256]{2,1,0:T(8,128)(2,1)S(1)}, bf16[8,32,256]{2,1,0:T(8,128)(2,1)S(1)}, u32[]{:S(2)}, u32[]{:S(2)}) collective-permute-start(bf16[8,32,256]{2,1,0:T(8,128)(2,1)S(1)} %get-tuple-element.145), channel_id=1, source_target_pairs={{0,14},{2,12},{4,10},{6,8},{8,6},{10,4},{12,2},{14,0},{16,30},{18,... | collective-permute-start | bytes 393224 | tf_op jit(solution)/shard_map/ppermute | solution.py:393
  51.7 11.5 %collective-permute-start.36 = (bf16[8,32,256]{2,1,0:T(8,128)(2,1)}, bf16[8,32,256]{2,1,0:T(8,128)(2,1)S(1)}, u32[]{:S(2)}, u32[]{:S(2)}) collective-permute-start(bf16[8,32,256]{2,1,0:T(8,128)(2,1)} %get-tuple-element.146), channel_id=1, source_target_pairs={{0,12},{2,14},{4,8},{6,10},{8,4},{10,6},{12,0},{14,2},{16,28},{18,... | collective-permute-start | bytes 393224 | tf_op jit(solution)/shard_map/ppermute | solution.py:393
  54.9 10.8 %collective-permute-start.37 = (bf16[8,32,256]{2,1,0:T(8,128)(2,1)}, bf16[8,32,256]{2,1,0:T(8,128)(2,1)S(1)}, u32[]{:S(2)}, u32[]{:S(2)}) collective-permute-start(bf16[8,32,256]{2,1,0:T(8,128)(2,1)} %get-tuple-element.147), channel_id=1, source_target_pairs={{0,10},{2,8},{4,14},{6,12},{8,2},{10,0},{12,6},{14,4},{16,26},{18,... | collective-permute-start | bytes 393224 | tf_op jit(solution)/shard_map/ppermute | solution.py:393
  55.6 10.7 %collective-permute-start.38 = (bf16[8,32,256]{2,1,0:T(8,128)(2,1)}, bf16[8,32,256]{2,1,0:T(8,128)(2,1)S(1)}, u32[]{:S(2)}, u32[]{:S(2)}) collective-permute-start(bf16[8,32,256]{2,1,0:T(8,128)(2,1)} %get-tuple-element.148), channel_id=1, source_target_pairs={{0,6},{2,4},{4,2},{6,0},{8,14},{10,12},{12,10},{14,8},{16,22},{18,... | collective-permute-start | bytes 393224 | tf_op jit(solution)/shard_map/ppermute | solution.py:393
  57.0 9.2 %collective-permute-start.39 = (bf16[8,32,256]{2,1,0:T(8,128)(2,1)}, bf16[8,32,256]{2,1,0:T(8,128)(2,1)S(1)}, u32[]{:S(2)}, u32[]{:S(2)}) collective-permute-start(bf16[8,32,256]{2,1,0:T(8,128)(2,1)} %get-tuple-element.149), channel_id=1, source_target_pairs={{0,8},{2,10},{4,12},{6,14},{8,0},{10,2},{12,4},{14,6},{16,24},{18,... | collective-permute-start | bytes 393224 | tf_op jit(solution)/shard_map/ppermute | solution.py:393
  61.0 6.3 %collective-permute-start.40 = (bf16[8,32,256]{2,1,0:T(8,128)(2,1)}, bf16[8,32,256]{2,1,0:T(8,128)(2,1)S(1)}, u32[]{:S(2)}, u32[]{:S(2)}) collective-permute-start(bf16[8,32,256]{2,1,0:T(8,128)(2,1)} %get-tuple-element.150), channel_id=1, source_target_pairs={{0,4},{2,6},{4,0},{6,2},{8,12},{10,14},{12,8},{14,10},{16,20},{18,... | collective-permute-start | bytes 393224 | tf_op jit(solution)/shard_map/ppermute | solution.py:393
  63.2 5.4 %collective-permute-start.41 = (bf16[8,32,256]{2,1,0:T(8,128)(2,1)}, bf16[8,32,256]{2,1,0:T(8,128)(2,1)S(1)}, u32[]{:S(2)}, u32[]{:S(2)}) collective-permute-start(bf16[8,32,256]{2,1,0:T(8,128)(2,1)} %get-tuple-element.151), channel_id=1, source_target_pairs={{0,2},{2,0},{4,6},{6,4},{8,10},{10,8},{12,14},{14,12},{16,18},{18,... | collective-permute-start | bytes 393224 | tf_op jit(solution)/shard_map/ppermute | solution.py:393
  69.6 2.7 %collective-permute-start.42 = (f32[1024,256]{1,0:T(8,128)S(1)}, f32[1024,256]{1,0:T(8,128)S(1)}, u32[]{:S(2)}, u32[]{:S(2)}) collective-permute-start(f32[1024,256]{1,0:T(8,128)S(1)} %block_products.1.mine_ref), channel_id=1, source_target_pairs={{0,1},{1,0},{2,3},{3,2},{4,5},{5,4},{6,7},{7,6},{8,9},{9,8},{10,11... | collective-permute-start | bytes 3145736 | tf_op jit(solution)/shard_map/ppermute | solution.py:443

commit v9 on v8

--- a/solution.py
+++ b/solution.py
@@ -15,7 +15,7 @@
 
 
 ACROSS = (12, 14, 16, 18, 20, 24)
-WITHIN = (6, 7, 8)
+WITHIN = 8
 
 
 def table_kernel(cols_ref, counts_ref, out_ref):
@@ -37,30 +37,44 @@
     )(block_cols, counts)
 
 
-def plan_kernel(per, within, across, table_ref, places_ref, lists_ref, *level_refs):
+def over(values, size):
+    return values >> (size.bit_length() - 1)
+
+
+def plan_kernel(slots, per, within, across, table_ref, places_ref, lists_ref, *level_refs):
     devices = table_ref.shape[0]
-    slots = places_ref.shape[1]
     rows, cols = lax.axis_size("rows"), lax.axis_size("cols")
     panel = per * rows
     part = panel // 2
-    table = table_ref[:, 0, :]
-    block = lax.broadcasted_iota(jnp.int32, (devices, panel), 1)
-    device = lax.broadcasted_iota(jnp.int32, (devices, panel), 0)
-    side, core = device // (devices // 2), device % cols
-    asked = [(table[:, s : s + 1] == block) & (s < table[:, slots : slots + 1]) for s in range(slots)]
-    some = functools.reduce(jnp.logical_or, asked)
+    groups = [range(at, min(at + 64, devices)) for at in range(0, devices, 64)]
+
+    def read(group):
+        table = table_ref[group.start : group.stop, 0, :]
+        lane = lax.broadcasted_iota(jnp.int32, table.shape, 1)
+        counts = table[:, slots : slots + 1]
+        table = jnp.where(lane < counts, table, -1)
+        block = lax.broadcasted_iota(jnp.int32, (len(group), panel), 1)
+        return table, counts, [table[:, s : s + 1] == block for s in range(slots)]
+
     lines = -(-cols // 8) * 8
     line = lax.broadcasted_iota(jnp.int32, (3 * lines, panel), 0)
+    ids = lax.broadcasted_iota(jnp.int32, (1, panel), 1)
     asks = jnp.zeros((3 * lines, panel), jnp.float32)
-    for c in range(cols):
-        for h in range(2):
-            found = jnp.max(jnp.where(some & (core == c) & (side == h), 1.0, 0.0), axis=0, keepdims=True)
-            asks = jnp.where(line == c, jnp.maximum(asks, found), asks)
-            asks = jnp.where((line == lines * (1 + h) + c) & (block[:1] // part != h), found, asks)
+    for group in groups:
+        _, _, asked = read(group)
+        some = jnp.where(functools.reduce(jnp.logical_or, asked), 1.0, 0.0).astype(jnp.bfloat16)
+        shape = (3 * lines, len(group))
+        number = lax.broadcasted_iota(jnp.int32, shape, 0)
+        device = lax.broadcasted_iota(jnp.int32, shape, 1) + group.start
+        core, side = device & (cols - 1), over(device, devices // 2)
+        reads = (number == core) | (number == lines * (1 + side) + core)
+        asks += jnp.dot(jnp.where(reads, 1.0, 0.0).astype(jnp.bfloat16), some, preferred_element_type=jnp.float32)
+    own_half = (line >= lines) & (over(line - lines, lines) == over(lax.broadcasted_iota(jnp.int32, line.shape, 1), part))
+    asks = jnp.where((asks > 0.5) & jnp.logical_not(own_half), 1.0, 0.0)
     first = lax.broadcasted_iota(jnp.int32, (panel, panel), 0)
     second = lax.broadcasted_iota(jnp.int32, (panel, panel), 1)
     after = first > second
-    near = jnp.where(after & (first // per == second // per), 1.0, 0.0).astype(jnp.bfloat16)
+    near = jnp.where(after & ((first ^ second) < per), 1.0, 0.0).astype(jnp.bfloat16)
     after = jnp.where(after, 1.0, 0.0).astype(jnp.bfloat16)
     same = jnp.where(first == second, 1.0, 0.0).astype(jnp.bfloat16)
     nt = (((1,), (1,)), ((), ()))
@@ -72,25 +86,26 @@
     near_rank = ranks(short, near)
     far_rank = ranks(short, after)
     longest = jnp.max(jnp.where(line < lines, near_rank + asks, 0.0)).astype(jnp.int32)
-    level_refs[0][0] = sum((longest > level).astype(jnp.int32) for level in within)
+    level_refs[0][0] = (longest > within).astype(jnp.int32)
     longest = jnp.max(jnp.where(line < lines, 0.0, far_rank + asks)).astype(jnp.int32)
     level_refs[1][0] = sum((longest > level).astype(jnp.int32) for level in across)
     me = lax.axis_index("rows")
-    half, c = me // (rows // 2), lax.axis_index("cols")
+    half, c = over(me, rows // 2), lax.axis_index("cols")
 
     def row(values, number):
         return jnp.sum(jnp.where(line == number, values, 0.0), axis=0, keepdims=True)
 
-    ids = lax.broadcasted_iota(jnp.int32, (1, panel), 1)
-    here = ids // per * per - half * part + row(near_rank, c).astype(jnp.int32)
+    here = (ids & -per) - half * part + row(near_rank, c).astype(jnp.int32)
     there = part + row(far_rank, lines * (1 + half) + c).astype(jnp.int32)
-    place = jnp.where(ids // part == half, here, there)
-    slot = lax.broadcasted_iota(jnp.int32, places_ref.shape, 1)
-    places = jnp.zeros(places_ref.shape, jnp.int32)
-    for s in range(slots):
-        found = jnp.sum(jnp.where(asked[s], place, 0), axis=1, keepdims=True)
-        places = jnp.where(slot == s, found, places)
-    places_ref[...] = places
+    place = jnp.where(over(ids, part) == half, here, there)
+    for group in groups:
+        table, _, asked = read(group)
+        lane = lax.broadcasted_iota(jnp.int32, table.shape, 1)
+        places = jnp.zeros(table.shape, jnp.int32)
+        for s in range(slots):
+            found = jnp.sum(jnp.where(asked[s], place, 0), axis=1, keepdims=True)
+            places = jnp.where(lane == s, found, places)
+        places_ref[group.start : group.stop] = places
     line = lax.broadcasted_iota(jnp.int32, (panel, 3 * lines), 1)
 
     def column(values, number):
@@ -100,21 +115,21 @@
     ids = lax.broadcasted_iota(jnp.int32, (panel, 1), 0)
     number = lax.broadcasted_iota(jnp.int32, (panel, lists_ref.shape[1]), 1)
     near_rank = column(near_rank, c).astype(jnp.int32)
-    here = ids // per * per - half * part + near_rank
+    here = (ids & -per) - half * part + near_rank
     other = lines * (2 - half) + c
     sent = (column(turned, other) > 0.5) & (column(far_rank, other).astype(jnp.int32) == number)
     sent = jnp.sum(jnp.where(sent, here, 0), axis=0, keepdims=True)
-    kept = (column(turned, c) > 0.5) & (ids // per == me) & (near_rank == number)
-    kept = jnp.sum(jnp.where(kept, ids % per, 0), axis=0, keepdims=True)
+    kept = (column(turned, c) > 0.5) & (over(ids, per) == me) & (near_rank == number)
+    kept = jnp.sum(jnp.where(kept, ids & (per - 1), 0), axis=0, keepdims=True)
     lists_ref[...] = jnp.where(lax.broadcasted_iota(jnp.int32, lists_ref.shape, 0) == 0, sent, kept)
 
 
 def plan(table, slots, per, within, across):
     devices = table.shape[0]
     return pl.pallas_call(
-        functools.partial(plan_kernel, per, within, across),
+        functools.partial(plan_kernel, slots, per, within, across),
         out_shape=(
-            jax.ShapeDtypeStruct((devices, slots), jnp.int32),
+            jax.ShapeDtypeStruct((devices, 128), jnp.int32),
             jax.ShapeDtypeStruct((8, 128), jnp.int32),
             jax.ShapeDtypeStruct((1,), jnp.int32),
             jax.ShapeDtypeStruct((1,), jnp.int32),
@@ -150,17 +165,17 @@
     )(sketch)
 
 
-def cut_kernel(lists_ref, stripes_ref, *out_refs):
+def cut_kernel(start, lists_ref, stripes_ref, *out_refs):
     for k in range(out_refs[0].shape[0]):
         for i, out_ref in enumerate(out_refs):
-            out_ref[k] = stripes_ref[i, lists_ref[1, k]]
-
-
-def cut(lists, stripes, count):
+            out_ref[k] = stripes_ref[i, lists_ref[1, start + k]]
+
+
+def cut(lists, stripes, start, stop):
     members, _, height, columns = stripes.shape
     return pl.pallas_call(
-        cut_kernel,
-        out_shape=(jax.ShapeDtypeStruct((count, height, columns), stripes.dtype),) * members,
+        functools.partial(cut_kernel, start),
+        out_shape=(jax.ShapeDtypeStruct((stop - start, height, columns), stripes.dtype),) * members,
         in_specs=[SMEM, VMEM],
         out_specs=(VMEM,) * members,
         compiler_params=pltpu.CompilerParams(vmem_limit_bytes=24 * MIB),
@@ -168,20 +183,22 @@
     )(lists, stripes)
 
 
-def order_kernel(*refs):
+def order_kernel(members, *refs):
     *stripe_refs, all_ref = refs
-    members = len(stripe_refs)
     me = lax.axis_index("rows") % members
     per = all_ref.shape[0] // members
-    for ref, d in zip(stripe_refs, distances(members)):
-        all_ref[pl.ds((me ^ d) * per, ref.shape[0])] = ref[...]
-
-
-def order(stripes, per):
+    for i, d in enumerate(distances(members)):
+        at = (me ^ d) * per
+        for ref in stripe_refs[i::members]:
+            all_ref[pl.ds(at, ref.shape[0])] = ref[...]
+            at = at + ref.shape[0]
+
+
+def order(stripes, members, per):
     _, height, columns = stripes[0].shape
     return pl.pallas_call(
-        order_kernel,
-        out_shape=jax.ShapeDtypeStruct((len(stripes) * per, height, columns), stripes[0].dtype),
+        functools.partial(order_kernel, members),
+        out_shape=jax.ShapeDtypeStruct((members * per, height, columns), stripes[0].dtype),
         in_specs=[VMEM] * len(stripes),
         out_specs=VMEM,
         compiler_params=pltpu.CompilerParams(vmem_limit_bytes=24 * MIB),
@@ -205,30 +222,25 @@
     )(numbers, stripes)
 
 
-def pick_kernel(places_ref, own_ref, other_ref, *out_refs):
-    members = len(out_refs)
-    cols = lax.axis_size("cols")
-    here, there = own_ref.shape[0], other_ref.shape[0]
-    me = lax.axis_index("rows")
-    c = lax.axis_index("cols")
-    for d, out_ref in zip(distances(members), out_refs):
-
-        def body(s, carry):
-            place = places_ref[(me ^ d) * cols + c, s]
-            own = own_ref[jnp.minimum(place, here - 1)]
-            other = other_ref[jnp.clip(place - here, 0, there - 1)]
-            out_ref[s] = lax.select(place < here, own, other)
-            return carry
-
-        lax.fori_loop(0, out_ref.shape[0], body, 0, unroll=True)
-
-
-def pick(places, own, other, members):
+def pick_kernel(places_ref, own_ref, other_ref, *refs):
+    *out_refs, whole = refs
+    here = own_ref.shape[0]
+    whole[:here] = own_ref[...]
+    whole[here:] = other_ref[...]
+    for d, out_ref in zip(distances(len(out_refs)), out_refs):
+        device = (lax.axis_index("rows") ^ d) * lax.axis_size("cols") + lax.axis_index("cols")
+        for s in range(out_ref.shape[0]):
+            out_ref[s] = whole[jnp.minimum(places_ref[device, s], whole.shape[0] - 1)]
+
+
+def pick(places, own, other, slots, members):
+    shape = own.shape[1:]
     return pl.pallas_call(
         pick_kernel,
-        out_shape=(jax.ShapeDtypeStruct((places.shape[1], *own.shape[1:]), own.dtype),) * members,
+        out_shape=(jax.ShapeDtypeStruct((slots, *shape), own.dtype),) * members,
         in_specs=[SMEM, VMEM, VMEM],
         out_specs=(VMEM,) * members,
+        scratch_shapes=[pltpu.VMEM((own.shape[0] + other.shape[0], *shape), own.dtype)],
         compiler_params=pltpu.CompilerParams(vmem_limit_bytes=24 * MIB),
         name="pick_stripes",
     )(places, own, other)
@@ -304,7 +316,17 @@
     )
 
 
-def factor_kernel(total_rows, gram_ref, own_ref, basis_ref, factor_ref, whole, scaled, inverse):
+def split_matmul(times, passes, a, b):
+    a_high, b_high = a.astype(jnp.bfloat16), b.astype(jnp.bfloat16)
+    result = times(a_high, b_high, None)
+    if passes == 3:
+        a_low = (a - a_high.astype(jnp.float32)).astype(jnp.bfloat16)
+        b_low = (b - b_high.astype(jnp.float32)).astype(jnp.bfloat16)
+        result += times(a_high, b_low, None) + times(a_low, b_high, None)
+    return result
+
+
+def factor_kernel(total_rows, gram_ref, own_ref, basis_ref, factor_ref, whole, scaled, inverse, product):
     n = factor_ref.shape[0]
     width = gram_ref.shape[-1]
     for c in range(n // width):
@@ -322,21 +344,28 @@
     up_across = 1.0 / across
     scaled[...] = gram * up_down * up_across
 
-    def refine(precision):
+    def refine(times, times_nt):
         w = inverse[...]
-        residual = matmul_nt(matmul(w, scaled[...], precision), w, precision) - identity
-        inverse[...] = w - matmul(residual * half, w, lax.Precision.DEFAULT)
+        upper = times(w, scaled[...])
+        residual = times_nt(upper, w) - identity
+        step = residual * half
+        inverse[...] = w - matmul(step, w, lax.Precision.DEFAULT)
+        product[...] = upper - matmul(step, upper, lax.Precision.DEFAULT)
         return jnp.sum(residual * residual)
 
+    def exactly(times):
+        return functools.partial(times, precision=HIGHEST)
+
     inverse[...] = identity - (scaled[...] - identity) * half
-    refine(lax.Precision.DEFAULT)
+    for passes in (1, 3):
+        refine(functools.partial(split_matmul, matmul, passes), functools.partial(split_matmul, matmul_nt, passes))
 
     def going(state):
         step, size = state
         return (step < 8) & (size > 1e-6)
 
     def advance(state):
-        return state[0] + 1, refine(HIGHEST)
+        return state[0] + 1, refine(exactly(matmul), exactly(matmul_nt))
 
     _, size = lax.while_loop(going, advance, (jnp.int32(0), jnp.float32(1.0)))
 
@@ -357,11 +386,11 @@
             return carry
 
         lax.fori_loop(0, n, eliminate, 0)
-        scaled[...] = whole[...] * up_down * up_across
+        product[...] = matmul(inverse[...], whole[...] * up_down * up_across, HIGHEST)
 
     w = inverse[...]
     root_rows = jnp.sqrt(jnp.float32(total_rows))
-    upper = matmul(w, scaled[...], HIGHEST) * across / root_rows
+    upper = product[...] * across / root_rows
     factor_ref[...] = jnp.where(row_ids <= col_ids, upper, 0.0)
     basis_ref[...] = matmul_nt(own_ref[...] * up_across, w, HIGHEST) * root_rows
 
@@ -376,7 +405,7 @@
         ),
         in_specs=[VMEM, VMEM],
         out_specs=(VMEM, VMEM),
-        scratch_shapes=[pltpu.VMEM((columns, columns), jnp.float32)] * 3,
+        scratch_shapes=[pltpu.VMEM((columns, columns), jnp.float32)] * 4,
         compiler_params=pltpu.CompilerParams(vmem_limit_bytes=24 * MIB),
         name="factor_and_basis",
     )(gram, own)
@@ -403,26 +432,27 @@
     sketch = sketch.reshape(-1, members, height, columns)
     per = sketch.shape[0]
     largest = min(per * members, slots * members, 128)
-    within = tuple(level for level in WITHIN if level < per)
+    within = min(per, WITHIN)
     across = tuple(level for level in ACROSS if level < largest)
     stripes = turn(sketch)
     table = table_copies(block_cols, counts, rows * cols)
     table = lax.all_to_all(table, ("rows", "cols"), split_axis=0, concat_axis=0, tiled=True)
-    places, lists, near, far = plan(table, slots, per, within, across)
-
-    def within_half(count):
-        def run():
-            return order(exchange(cut(lists, stripes, count), rows), per)
-
-        return run
-
-    own = lax.switch(near[0], [within_half(count) for count in (*within, per)])
+    places, lists, more, far = plan(table, slots, per, within, across)
+    first = exchange(cut(lists, stripes, 0, within), rows)
+
+    def as_sent():
+        return order(first, members, per)
+
+    def with_rest():
+        return order(first + exchange(cut(lists, stripes, within, per), rows), members, per)
+
+    own = lax.cond(more[0] > 0, with_rest, as_sent) if within < per else as_sent()
 
     def across_halves(count):
         def run():
             swap = [(r, (r + members) % rows) for r in range(rows)]
             other = lax.ppermute(listed(lists, own, count), "rows", swap)
-            return pick(places, own, other, members)
+            return pick(places, own, other, slots, members)
 
         return run
 

time: 160 us -> 162 us (1.012); the launches traced: 160 us -> 159 us
  transfers between devices with their start and end apart: 17 -> 17, of which waited for: 15 -> 14; matrix products, arithmetic and copies ran while one was open for 0% -> 0% of each run, Pallas kernels for 0% -> 0%
where the time goes in v9:
time: 162 us; the launch traced here: 159 us
  Pallas kernels  70 us (43%)
  waiting for transfers between devices  35 us (22%)
  starting transfers between devices  25.8 us (16%)
  blocking collectives  23.4 us (14%)
  between operations  2.7 us (2%)
  local copies, waits for them, and re-layouts  1.62 us (1%)
    pallas_call x1, Pallas kernels, factor_and_basis(): pl.pallas_call(functools.partial(factor_kernel, total_rows), out_shape=(j...  61.8 us
    ppermute x14, starting transfers between devices, exchange(): lax.ppermute(piece, 'rows', [(r, r ^ d) for r in range(rows)])  17.9 us
    ppermute x14, waiting for transfers between devices, exchange(): lax.ppermute(piece, 'rows', [(r, r ^ d) for r in range(rows)])  14.5 us
    ppermute x1, waiting for transfers between devices, run(): other = lax.ppermute(listed(lists, own, count), 'rows', swap)  12.5 us
    all_to_all x1, blocking collectives, spread(): return lax.all_to_all(copies, axes, split_axis=0, concat_axis=0, tiled=True)  12.5 us
    all_to_all x1, blocking collectives, local(): lax.all_to_all(pieces, 'rows', split_axis=0, concat_axis=0, tiled=True)  10.9 us
    all_to_all x1, starting transfers between devices, fetch(): lax.all_to_all(table, ('rows', 'cols'), split_axis=0, concat_axis=0, tile...  7.3 us
    all_to_all x1, waiting for transfers between devices, fetch(): lax.all_to_all(table, ('rows', 'cols'), split_axis=0, concat_axis=0, tile...  5.34 us
  transfers between devices with their start and end apart: 17, of which 14 were waited for; matrix products, arithmetic and copies ran while one was open for 0% of the time, Pallas kernels for 0%

profile of v9, /device:TPU:0, one launch (start us, length us, event | category | flops | bytes accessed | tf_op | source)
XLA Modules:
  0.0 158.6 jit_solution(12491457955989524362)
XLA Ops:
  1.3 1.3 table_copies.1
  2.6 7.3 %all-to-all-start = ((s32[32,1,128]{2,1,0:T(1,128)}), s32[32,1,128]{2,1,0:T(1,128)S(1)}, u32[]{:S(2)}, u32[]{:S(2)}) async-start(s32[32,1,128]{2,1,0:T(1,128)} %table_copies.1), calls=%async_computation | async-start | bytes 32768 | tf_op jit(solution)/shard_map/all_to_all | solution.py:439
  9.9 0.0 copy-start
  9.9 1.6 copy-done
  11.5 0.1 turn_stripes.1.stripes_ref
  11.6 5.3 %all-to-all-done.table_ref = s32[32,1,128]{2,1,0:T(1,128)S(1)} async-done(((s32[32,1,128]{2,1,0:T(1,128)}), s32[32,1,128]{2,1,0:T(1,128)S(1)}, u32[]{:S(2)}, u32[]{:S(2)}) %all-to-all-start) | async-done | bytes 16416 | tf_op jit(solution)/shard_map/all_to_all | solution.py:439
  16.9 1.2 plan.1
  18.1 0.7 cut_stripes.3
  18.8 0.7 collective-permute-start.14
  19.5 2.3 %collective-permute-start.15 = (bf16[8,32,256]{2,1,0:T(8,128)(2,1)S(1)}, bf16[8,32,256]{2,1,0:T(8,128)(2,1)S(1)}, u32[]{:S(2)}, u32[]{:S(2)}) collective-permute-start(bf16[8,32,256]{2,1,0:T(8,128)(2,1)S(1)} %get-tuple-element.157), channel_id=1, source_target_pairs={{0,12},{2,14},{4,8},{6,10},{8,4},{10,6},{12,0},{14,2},{16,28},{18,... | collective-permute-start | bytes 393224 | tf_op jit(solution)/shard_map/ppermute | solution.py:422
  21.8 1.5 collective-permute-start.16
  23.3 0.6 collective-permute-start.17
  23.9 1.4 collective-permute-start.18
  25.3 2.9 %collective-permute-done.14 = bf16[8,32,256]{2,1,0:T(8,128)(2,1)S(1)} collective-permute-done((bf16[8,32,256]{2,1,0:T(8,128)(2,1)S(1)}, bf16[8,32,256]{2,1,0:T(8,128)(2,1)S(1)}, u32[]{:S(2)}, u32[]{:S(2)}) %collective-permute-start.14) | collective-permute-done | bytes 131104 | tf_op jit(solution)/shard_map/ppermute | solution.py:422
  28.3 0.5 collective-permute-start.19
  28.8 1.5 collective-permute-done.15
  30.2 1.3 collective-permute-start.20
  32.9 0.0 collective-permute-done.16
  32.9 0.7 collective-permute-done.17
  33.6 0.0 collective-permute-done.18
  33.6 0.8 collective-permute-done.19
  34.4 0.8 collective-permute-done.20
  35.2 0.1 conditional.2
  35.2 0.1 order_stripes.2
  35.3 0.0 copy-start.1
  35.3 0.0 copy-start.2
  35.3 15.6 %conditional.3 = ((bf16[8,32,256]{2,1,0:T(8,128)(2,1)S(1)}, bf16[8,32,256]{2,1,0:T(8,128)(2,1)S(1)}, bf16[8,32,256]{2,1,0:T(8,128)(2,1)}, bf16[8,32,256]{2,1,0:T...) conditional(s32[]{:T(128)} %bitcast, (s32[8,128]{1,0:T(8,128)S(1)}, ...), branch_computations={%region_2.0_spmd, %region_3.0_spmd, %region_4.0_spmd, %region_5.0_... | conditional | bytes 4194352 | solution.py:459
  35.4 0.6 listed_stripes.9
  36.0 0.5 collective-permute-start.9
  36.5 12.5 %collective-permute-done.9.other_ref = bf16[16,32,256]{2,1,0:T(8,128)(2,1)S(1)} collective-permute-done((bf16[16,32,256]{2,1,0:T(8,128)(2,1)S(1)}, bf16[16,32,256]{2,1,0:T(8,128)(2,1)S(1)}, u32[]{:S(2)}, u32[]{:S(2)}) %collective-permute-start.9) | collective-permute-done | bytes 262176 | tf_op jit(solution)/shard_map/cond/branch_2_fun/ppermute | solution.py:454
  49.0 1.8 %pick_stripes.9 = (bf16[8,32,256]{2,1,0:T(8,128)(2,1)S(1)}, bf16[8,32,256]{2,1,0:T(8,128)(2,1)S(1)}, bf16[8,32,256]{2,1,0:T(8,128)(2,1)}, bf16[8,32,256]{2,1,0:T...) custom-call(s32[32,128]{1,0:T(8,128)S(1)} %get-tuple-element.113.pla, ...), custom_call_target="tpu_custom_call" | custom-call | tf_op jit(solution)/shard_map/cond/branch_2_fun/pick_stripes/pallas_call | solution.py:238
  50.9 0.0 collective-permute-start.21
  50.9 3.8 %collective-permute-start.22 = (bf16[8,32,256]{2,1,0:T(8,128)(2,1)}, bf16[8,32,256]{2,1,0:T(8,128)(2,1)S(1)}, u32[]{:S(2)}, u32[]{:S(2)}) collective-permute-start(bf16[8,32,256]{2,1,0:T(8,128)(2,1)} %get-tuple-element.166), channel_id=1, source_target_pairs={{0,12},{2,14},{4,8},{6,10},{8,4},{10,6},{12,0},{14,2},{16,28},{18,... | collective-permute-start | bytes 393224 | tf_op jit(solution)/shard_map/ppermute | solution.py:422
  54.7 0.0 collective-permute-start.23
  54.7 1.5 collective-permute-start.24
  56.2 2.1 %collective-permute-start.25 = (bf16[8,32,256]{2,1,0:T(8,128)(2,1)}, bf16[8,32,256]{2,1,0:T(8,128)(2,1)S(1)}, u32[]{:S(2)}, u32[]{:S(2)}) collective-permute-start(bf16[8,32,256]{2,1,0:T(8,128)(2,1)} %get-tuple-element.169), channel_id=1, source_target_pairs={{0,8},{2,10},{4,12},{6,14},{8,0},{10,2},{12,4},{14,6},{16,24},{18,... | collective-permute-start | bytes 393224 | tf_op jit(solution)/shard_map/ppermute | solution.py:422
  58.2 1.6 collective-permute-done.21.refs_1_
  59.8 1.6 %collective-permute-start.26 = (bf16[8,32,256]{2,1,0:T(8,128)(2,1)}, bf16[8,32,256]{2,1,0:T(8,128)(2,1)S(1)}, u32[]{:S(2)}, u32[]{:S(2)}) collective-permute-start(bf16[8,32,256]{2,1,0:T(8,128)(2,1)} %get-tuple-element.170), channel_id=1, source_target_pairs={{0,4},{2,6},{4,0},{6,2},{8,12},{10,14},{12,8},{14,10},{16,20},{18,... | collective-permute-start | bytes 393224 | tf_op jit(solution)/shard_map/ppermute | solution.py:422
  61.4 1.7 %collective-permute-done.22.refs_2_ = bf16[8,32,256]{2,1,0:T(8,128)(2,1)S(1)} collective-permute-done((bf16[8,32,256]{2,1,0:T(8,128)(2,1)}, bf16[8,32,256]{2,1,0:T(8,128)(2,1)S(1)}, u32[]{:S(2)}, u32[]{:S(2)}) %collective-permute-start.22) | collective-permute-done | bytes 131104 | tf_op jit(solution)/shard_map/ppermute | solution.py:422
  63.1 0.6 collective-permute-start.27
  63.7 1.4 collective-permute-done.23.refs_3_
  65.1 0.0 collective-permute-done.24.refs_4_
  65.1 1.1 collective-permute-done.25.refs_5_
  66.2 0.3 collective-permute-done.26.refs_6_
  66.5 1.8 %collective-permute-done.27.refs_7_ = bf16[8,32,256]{2,1,0:T(8,128)(2,1)S(1)} collective-permute-done((bf16[8,32,256]{2,1,0:T(8,128)(2,1)}, bf16[8,32,256]{2,1,0:T(8,128)(2,1)S(1)}, u32[]{:S(2)}, u32[]{:S(2)}) %collective-permute-start.27) | collective-permute-done | bytes 131104 | tf_op jit(solution)/shard_map/ppermute | solution.py:422
  68.2 0.0 copy-done.1
  68.2 0.0 copy-done.2
  68.3 0.9 block_products.1.mine_ref
  69.2 0.1 collective-permute-start.28
  69.3 2.6 %collective-permute-done.28.other_ref = f32[1024,256]{1,0:T(8,128)S(1)} collective-permute-done((f32[1024,256]{1,0:T(8,128)S(1)}, f32[1024,256]{1,0:T(8,128)S(1)}, u32[]{:S(2)}, u32[]{:S(2)}) %collective-permute-start.28) | collective-permute-done | bytes 1048608 | tf_op jit(solution)/shard_map/ppermute | solution.py:473
  71.9 1.4 sum_and_gram.1
  73.4 10.9 %all_to_all.15 = f32[16,16,128]{2,1,0:T(8,128)S(1)} all-to-all(f32[16,16,128]{2,1,0:T(8,128)S(1)} %bitcast.7), channel_id=1, replica_groups=mesh['rows'=16,'cols'=2] {'rows'}, dimensions={0} | all-to-all | bytes 262144 | tf_op jit(solution)/shard_map/all_to_all | solution.py:476
  84.3 12.5 %all_to_all.16 = f32[32,16,128]{2,1,0:T(8,128)S(1)} all-to-all(f32[32,16,128]{2,1,0:T(8,128)S(1)} %broadcast_in_dim.2), channel_id=1, replica_groups=mesh['rows'=16,'cols'=2] {'rows','cols'}, dimensions={0} | all-to-all | bytes 524288 | tf_op jit(solution)/shard_map/all_to_all | solution.py:416
  96.8 61.8 %factor_and_basis.1 = (f32[512,256]{1,0:T(8,128)}, f32[256,256]{1,0:T(8,128)}) custom-call(f32[16,2,16,128]{3,2,1,0:T(8,128)S(1)} %bitcast.6, f32[512,256]{1,0:T(8,128)S(1)} %get-tuple-element.173.own_ref), custom_call_target="tpu_custom_call" | custom-call | tf_op jit(solution)/shard_map/factor_and_basis/pallas_call | solution.py:400
  (2 shorter events, 0.0 us)
Async XLA Ops:
  2.6 14.4 %all-to-all-start = ((s32[32,1,128]{2,1,0:T(1,128)}), s32[32,1,128]{2,1,0:T(1,128)S(1)}, u32[]{:S(2)}, u32[]{:S(2)}) async-start(s32[32,1,128]{2,1,0:T(1,128)} %table_copies.1), calls=%async_computation | async-start | bytes 32768 | tf_op jit(solution)/shard_map/all_to_all | solution.py:439
  9.9 1.6 %copy-start = (bf16[4096,256]{1,0:T(8,128)(2,1)S(1)}, bf16[4096,256]{1,0:T(8,128)(2,1)}, u32[]{:S(2)}) copy-start(bf16[4096,256]{1,0:T(8,128)(2,1)} %param.14) | copy-start | bytes 6291460
  18.8 9.4 %collective-permute-start.14 = (bf16[8,32,256]{2,1,0:T(8,128)(2,1)S(1)}, bf16[8,32,256]{2,1,0:T(8,128)(2,1)S(1)}, u32[]{:S(2)}, u32[]{:S(2)}) collective-permute-start(bf16[8,32,256]{2,1,0:T(8,128)(2,1)S(1)} %get-tuple-element.156), channel_id=1, source_target_pairs={{0,14},{2,12},{4,10},{6,8},{8,6},{10,4},{12,2},{14,0},{16,30},{18,... | collective-permute-start | bytes 393224 | tf_op jit(solution)/shard_map/ppermute | solution.py:422
  19.5 10.7 %collective-permute-start.15 = (bf16[8,32,256]{2,1,0:T(8,128)(2,1)S(1)}, bf16[8,32,256]{2,1,0:T(8,128)(2,1)S(1)}, u32[]{:S(2)}, u32[]{:S(2)}) collective-permute-start(bf16[8,32,256]{2,1,0:T(8,128)(2,1)S(1)} %get-tuple-element.157), channel_id=1, source_target_pairs={{0,12},{2,14},{4,8},{6,10},{8,4},{10,6},{12,0},{14,2},{16,28},{18,... | collective-permute-start | bytes 393224 | tf_op jit(solution)/shard_map/ppermute | solution.py:422
  21.8 11.1 %collective-permute-start.16 = (bf16[8,32,256]{2,1,0:T(8,128)(2,1)S(1)}, bf16[8,32,256]{2,1,0:T(8,128)(2,1)S(1)}, u32[]{:S(2)}, u32[]{:S(2)}) collective-permute-start(bf16[8,32,256]{2,1,0:T(8,128)(2,1)S(1)} %get-tuple-element.158), channel_id=1, source_target_pairs={{0,10},{2,8},{4,14},{6,12},{8,2},{10,0},{12,6},{14,4},{16,26},{18,... | collective-permute-start | bytes 393224 | tf_op jit(solution)/shard_map/ppermute | solution.py:422
  23.3 10.3 %collective-permute-start.17 = (bf16[8,32,256]{2,1,0:T(8,128)(2,1)S(1)}, bf16[8,32,256]{2,1,0:T(8,128)(2,1)S(1)}, u32[]{:S(2)}, u32[]{:S(2)}) collective-permute-start(bf16[8,32,256]{2,1,0:T(8,128)(2,1)S(1)} %get-tuple-element.159), channel_id=1, source_target_pairs={{0,6},{2,4},{4,2},{6,0},{8,14},{10,12},{12,10},{14,8},{16,22},{18,... | collective-permute-start | bytes 393224 | tf_op jit(solution)/shard_map/ppermute | solution.py:422
  23.9 9.7 %collective-permute-start.18 = (bf16[8,32,256]{2,1,0:T(8,128)(2,1)S(1)}, bf16[8,32,256]{2,1,0:T(8,128)(2,1)S(1)}, u32[]{:S(2)}, u32[]{:S(2)}) collective-permute-start(bf16[8,32,256]{2,1,0:T(8,128)(2,1)S(1)} %get-tuple-element.160), channel_id=1, source_target_pairs={{0,8},{2,10},{4,12},{6,14},{8,0},{10,2},{12,4},{14,6},{16,24},{18,... | collective-permute-start | bytes 393224 | tf_op jit(solution)/shard_map/ppermute | solution.py:422
  28.3 6.1 %collective-permute-start.19 = (bf16[8,32,256]{2,1,0:T(8,128)(2,1)S(1)}, bf16[8,32,256]{2,1,0:T(8,128)(2,1)S(1)}, u32[]{:S(2)}, u32[]{:S(2)}) collective-permute-start(bf16[8,32,256]{2,1,0:T(8,128)(2,1)S(1)} %get-tuple-element.161), channel_id=1, source_target_pairs={{0,4},{2,6},{4,0},{6,2},{8,12},{10,14},{12,8},{14,10},{16,20},{18,... | collective-permute-start | bytes 393224 | tf_op jit(solution)/shard_map/ppermute | solution.py:422
  30.2 5.0 %collective-permute-start.20 = (bf16[8,32,256]{2,1,0:T(8,128)(2,1)S(1)}, bf16[8,32,256]{2,1,0:T(8,128)(2,1)S(1)}, u32[]{:S(2)}, u32[]{:S(2)}) collective-permute-start(bf16[8,32,256]{2,1,0:T(8,128)(2,1)S(1)} %get-tuple-element.162), channel_id=1, source_target_pairs={{0,2},{2,0},{4,6},{6,4},{8,10},{10,8},{12,14},{14,12},{16,18},{18,... | collective-permute-start | bytes 393224 | tf_op jit(solution)/shard_map/ppermute | solution.py:422
  35.3 33.0 %copy-start.1 = (bf16[8,256,256]{2,1,0:T(8,128)(2,1)S(1)}, bf16[8,256,256]{2,1,0:T(8,128)(2,1)}, u32[]{:S(2)}) copy-start(bf16[8,256,256]{2,1,0:T(8,128)(2,1)} %blocks_ref.1) | copy-start | bytes 3145732
  35.3 33.0 %copy-start.2 = (s32[8]{0:T(128)S(1)}, s32[8]{0:T(128)}, u32[]{:S(2)}) copy-start(s32[8]{0:T(128)} %rows_ref.1) | copy-start | bytes 100
  36.0 13.1 %collective-permute-start.9 = (bf16[16,32,256]{2,1,0:T(8,128)(2,1)S(1)}, bf16[16,32,256]{2,1,0:T(8,128)(2,1)S(1)}, u32[]{:S(2)}, u32[]{:S(2)}) collective-permute-start(bf16[16,32,256]{2,1,0:T(8,128)(2,1)S(1)} %listed_stripes.9), channel_id=1, source_target_pairs={{0,16},{2,18},{4,20},{6,22},{8,24},{10,26},{12,28},{14,30},{16,0},... | collective-permute-start | bytes 786440 | tf_op jit(solution)/shard_map/cond/branch_2_fun/ppermute | solution.py:454
  50.9 8.9 %collective-permute-start.21 = (bf16[8,32,256]{2,1,0:T(8,128)(2,1)S(1)}, bf16[8,32,256]{2,1,0:T(8,128)(2,1)S(1)}, u32[]{:S(2)}, u32[]{:S(2)}) collective-permute-start(bf16[8,32,256]{2,1,0:T(8,128)(2,1)S(1)} %get-tuple-element.165), channel_id=1, source_target_pairs={{0,14},{2,12},{4,10},{6,8},{8,6},{10,4},{12,2},{14,0},{16,30},{18,... | collective-permute-start | bytes 393224 | tf_op jit(solution)/shard_map/ppermute | solution.py:422
  50.9 12.2 %collective-permute-start.22 = (bf16[8,32,256]{2,1,0:T(8,128)(2,1)}, bf16[8,32,256]{2,1,0:T(8,128)(2,1)S(1)}, u32[]{:S(2)}, u32[]{:S(2)}) collective-permute-start(bf16[8,32,256]{2,1,0:T(8,128)(2,1)} %get-tuple-element.166), channel_id=1, source_target_pairs={{0,12},{2,14},{4,8},{6,10},{8,4},{10,6},{12,0},{14,2},{16,28},{18,... | collective-permute-start | bytes 393224 | tf_op jit(solution)/shard_map/ppermute | solution.py:422
  54.7 10.4 %collective-permute-start.23 = (bf16[8,32,256]{2,1,0:T(8,128)(2,1)}, bf16[8,32,256]{2,1,0:T(8,128)(2,1)S(1)}, u32[]{:S(2)}, u32[]{:S(2)}) collective-permute-start(bf16[8,32,256]{2,1,0:T(8,128)(2,1)} %get-tuple-element.167), channel_id=1, source_target_pairs={{0,10},{2,8},{4,14},{6,12},{8,2},{10,0},{12,6},{14,4},{16,26},{18,... | collective-permute-start | bytes 393224 | tf_op jit(solution)/shard_map/ppermute | solution.py:422
  54.7 10.4 %collective-permute-start.24 = (bf16[8,32,256]{2,1,0:T(8,128)(2,1)}, bf16[8,32,256]{2,1,0:T(8,128)(2,1)S(1)}, u32[]{:S(2)}, u32[]{:S(2)}) collective-permute-start(bf16[8,32,256]{2,1,0:T(8,128)(2,1)} %get-tuple-element.168), channel_id=1, source_target_pairs={{0,6},{2,4},{4,2},{6,0},{8,14},{10,12},{12,10},{14,8},{16,22},{18,... | collective-permute-start | bytes 393224 | tf_op jit(solution)/shard_map/ppermute | solution.py:422
  56.2 10.0 %collective-permute-start.25 = (bf16[8,32,256]{2,1,0:T(8,128)(2,1)}, bf16[8,32,256]{2,1,0:T(8,128)(2,1)S(1)}, u32[]{:S(2)}, u32[]{:S(2)}) collective-permute-start(bf16[8,32,256]{2,1,0:T(8,128)(2,1)} %get-tuple-element.169), channel_id=1, source_target_pairs={{0,8},{2,10},{4,12},{6,14},{8,0},{10,2},{12,4},{14,6},{16,24},{18,... | collective-permute-start | bytes 393224 | tf_op jit(solution)/shard_map/ppermute | solution.py:422
  59.8 6.7 %collective-permute-start.26 = (bf16[8,32,256]{2,1,0:T(8,128)(2,1)}, bf16[8,32,256]{2,1,0:T(8,128)(2,1)S(1)}, u32[]{:S(2)}, u32[]{:S(2)}) collective-permute-start(bf16[8,32,256]{2,1,0:T(8,128)(2,1)} %get-tuple-element.170), channel_id=1, source_target_pairs={{0,4},{2,6},{4,0},{6,2},{8,12},{10,14},{12,8},{14,10},{16,20},{18,... | collective-permute-start | bytes 393224 | tf_op jit(solution)/shard_map/ppermute | solution.py:422
  63.1 5.2 %collective-permute-start.27 = (bf16[8,32,256]{2,1,0:T(8,128)(2,1)}, bf16[8,32,256]{2,1,0:T(8,128)(2,1)S(1)}, u32[]{:S(2)}, u32[]{:S(2)}) collective-permute-start(bf16[8,32,256]{2,1,0:T(8,128)(2,1)} %get-tuple-element.171), channel_id=1, source_target_pairs={{0,2},{2,0},{4,6},{6,4},{8,10},{10,8},{12,14},{14,12},{16,18},{18,... | collective-permute-start | bytes 393224 | tf_op jit(solution)/shard_map/ppermute | solution.py:422
  69.2 2.7 %collective-permute-start.28 = (f32[1024,256]{1,0:T(8,128)S(1)}, f32[1024,256]{1,0:T(8,128)S(1)}, u32[]{:S(2)}, u32[]{:S(2)}) collective-permute-start(f32[1024,256]{1,0:T(8,128)S(1)} %block_products.1.mine_ref), channel_id=1, source_target_pairs={{0,1},{1,0},{2,3},{3,2},{4,5},{5,4},{6,7},{7,6},{8,9},{9,8},{10,11... | collective-permute-start | bytes 3145736 | tf_op jit(solution)/shard_map/ppermute | solution.py:473

commit v10 on v9

--- a/solution.py
+++ b/solution.py
@@ -165,10 +165,17 @@
     )(sketch)
 
 
+def copy_group(out_ref, refs):
+    for at in range(0, len(refs), 8):
+        values = [ref[...] for ref in refs[at : at + 8]]
+        for k, value in enumerate(values):
+            out_ref[at + k] = value
+
+
 def cut_kernel(start, lists_ref, stripes_ref, *out_refs):
-    for k in range(out_refs[0].shape[0]):
-        for i, out_ref in enumerate(out_refs):
-            out_ref[k] = stripes_ref[i, lists_ref[1, start + k]]
+    numbers = [lists_ref[1, start + k] for k in range(out_refs[0].shape[0])]
+    for i, out_ref in enumerate(out_refs):
+        copy_group(out_ref, [stripes_ref.at[i, number] for number in numbers])
 
 
 def cut(lists, stripes, start, stop):
@@ -207,8 +214,7 @@
 
 
 def list_kernel(list_ref, all_ref, out_ref):
-    for k in range(out_ref.shape[0]):
-        out_ref[k] = all_ref[list_ref[0, k]]
+    copy_group(out_ref, [all_ref.at[list_ref[0, k]] for k in range(out_ref.shape[0])])
 
 
 def listed(numbers, stripes, count):
@@ -229,8 +235,8 @@
     whole[here:] = other_ref[...]
     for d, out_ref in zip(distances(len(out_refs)), out_refs):
         device = (lax.axis_index("rows") ^ d) * lax.axis_size("cols") + lax.axis_index("cols")
-        for s in range(out_ref.shape[0]):
-            out_ref[s] = whole[jnp.minimum(places_ref[device, s], whole.shape[0] - 1)]
+        last = whole.shape[0] - 1
+        copy_group(out_ref, [whole.at[jnp.minimum(places_ref[device, s], last)] for s in range(out_ref.shape[0])])
 
 
 def pick(places, own, other, slots, members):
@@ -246,14 +252,14 @@
     )(places, own, other)
 
 
-def product_kernel(rows_ref, counts_ref, blocks_ref, *refs):
+def product_kernel(start, rows_ref, counts_ref, blocks_ref, *refs):
     *chosen_refs, out_ref, whole = refs
     slots, width, _ = blocks_ref.shape
     columns = out_ref.shape[1]
     members = len(chosen_refs)
     me = lax.axis_index("rows") % members
     for ref, d in zip(chosen_refs, distances(members) if members > 1 else [0]):
-        whole[me ^ d] = ref[...]
+        whole[me ^ d] = ref[:, :, start : start + columns]
     out_ref[...] = jnp.zeros_like(out_ref)
     for s in range(slots):
 
@@ -265,24 +271,26 @@
             out_ref[at, :] += product
 
 
-def block_products(block_rows, counts, blocks, chosen):
+def block_products(block_rows, counts, blocks, chosen, start, stop):
     _, width, _ = blocks.shape
-    columns = chosen[0].shape[-1]
-    return pl.pallas_call(
-        product_kernel,
+    columns = stop - start
+    return pl.pallas_call(
+        functools.partial(product_kernel, start),
         out_shape=jax.ShapeDtypeStruct((RB * width, columns), jnp.float32),
         in_specs=[SMEM, SMEM, VMEM] + [VMEM] * len(chosen),
         out_specs=VMEM,
-        scratch_shapes=[pltpu.VMEM((len(chosen), *chosen[0].shape), chosen[0].dtype)],
+        scratch_shapes=[pltpu.VMEM((len(chosen), *chosen[0].shape[:2], columns), chosen[0].dtype)],
         compiler_params=pltpu.CompilerParams(vmem_limit_bytes=24 * MIB),
         name="block_products",
     )(block_rows, counts, blocks, *chosen)
 
 
-def gram_kernel(mine_ref, other_ref, own_ref, gram_ref, slab):
+def gram_kernel(*refs):
+    mine_refs, other_refs, (own_ref, gram_ref, slab) = refs[:2], refs[2:4], refs[4:]
     c = lax.axis_index("cols")
     share, width = own_ref.shape[0], gram_ref.shape[1]
-    slab[...] = mine_ref[...] + other_ref[...]
+    for i, (mine_ref, other_ref) in enumerate(zip(mine_refs, other_refs)):
+        slab[:, i * width : (i + 1) * width] = mine_ref[...] + other_ref[...]
     own_ref[...] = slab[pl.ds(pl.multiple_of(c * share, share), share), :]
     right = slab[:, pl.ds(pl.multiple_of(c * width, width), width)]
     gram_ref[...] = lax.dot_general(
@@ -291,19 +299,20 @@
 
 
 def sum_and_gram(mine, other):
-    rows, columns = mine.shape
+    rows, width = mine[0].shape
+    columns = 2 * width
     return pl.pallas_call(
         gram_kernel,
         out_shape=(
             jax.ShapeDtypeStruct((rows // 2, columns), jnp.float32),
-            jax.ShapeDtypeStruct((columns, columns // 2), jnp.float32),
+            jax.ShapeDtypeStruct((columns, width), jnp.float32),
         ),
-        in_specs=[VMEM, VMEM],
+        in_specs=[VMEM] * 4,
         out_specs=(VMEM, VMEM),
         scratch_shapes=[pltpu.VMEM((rows, columns), jnp.float32)],
         compiler_params=pltpu.CompilerParams(vmem_limit_bytes=24 * MIB),
         name="sum_and_gram",
-    )(mine, other)
+    )(*mine, *other)
 
 
 def matmul(a, b, precision):
@@ -468,15 +477,16 @@
     if chosen[0].shape[1] % 16:
         order = jnp.argsort(lax.axis_index("rows") % len(chosen) ^ jnp.array(distances(len(chosen))))
         chosen = [jnp.stack(chosen)[order].swapaxes(0, 1).reshape(1, slots, width, columns)[0]]
-    partial_rows = block_products(block_rows, counts, blocks, chosen)
     if cols == 2:
-        other = lax.ppermute(partial_rows, "cols", [(0, 1), (1, 0)])
-        own, gram = sum_and_gram(partial_rows, other)
+        halves = ((0, columns // 2), (columns // 2, columns))
+        mine = [block_products(block_rows, counts, blocks, chosen, *half) for half in halves]
+        own, gram = sum_and_gram(mine, [lax.ppermute(half, "cols", [(0, 1), (1, 0)]) for half in mine])
         pieces = gram.reshape(rows, -1, columns // 2)
         pieces = lax.all_to_all(pieces, "rows", split_axis=0, concat_axis=0, tiled=True)
         gram = spread(jnp.sum(pieces, axis=0), ("rows", "cols"), rows * cols)
         gram = gram.reshape(rows, cols, -1, columns // 2)
     else:
+        partial_rows = block_products(block_rows, counts, blocks, chosen, 0, columns)
         own = lax.psum_scatter(partial_rows, "cols", scatter_dimension=0, tiled=True)
         gram = lax.psum(matmul(own.T, own, HIGHEST), ("rows", "cols"))
         gram = gram.reshape(1, 1, columns, columns)

time: 162 us -> 160 us (0.988); the launches traced: 159 us -> 160 us
  Pallas kernels: 70 us -> 72.5 us
    pallas_call x1 -> x2, Pallas kernels: 0.93 us -> 3.47 us  [block_products(): pl.pallas_call(functools.partial(product_kernel, start), out_shape=jax.Sh...]
  transfers between devices with their start and end apart: 17 -> 18, of which waited for: 14 -> 15; matrix products, arithmetic and copies ran while one was open for 0% -> 0% of each run, Pallas kernels for 0% -> 1%
where the time goes in v10:
time: 160 us
  Pallas kernels  72.5 us (45%)
  waiting for transfers between devices  34.3 us (21%)
  starting transfers between devices  25.9 us (16%)
  blocking collectives  23.1 us (14%)
  between operations  2.72 us (2%)
  local copies, waits for them, and re-layouts  1.62 us (1%)
    pallas_call x1, Pallas kernels, factor_and_basis(): pl.pallas_call(functools.partial(factor_kernel, total_rows), out_shape=(j...  61.8 us
    ppermute x14, starting transfers between devices, exchange(): lax.ppermute(piece, 'rows', [(r, r ^ d) for r in range(rows)])  17.9 us
    ppermute x14, waiting for transfers between devices, exchange(): lax.ppermute(piece, 'rows', [(r, r ^ d) for r in range(rows)])  14.5 us
    ppermute x1, waiting for transfers between devices, run(): other = lax.ppermute(listed(lists, own, count), 'rows', swap)  12.5 us
    all_to_all x1, blocking collectives, spread(): return lax.all_to_all(copies, axes, split_axis=0, concat_axis=0, tiled=True)  12.5 us
    all_to_all x1, blocking collectives, local(): lax.all_to_all(pieces, 'rows', split_axis=0, concat_axis=0, tiled=True)  10.6 us
    all_to_all x1, starting transfers between devices, fetch(): lax.all_to_all(table, ('rows', 'cols'), split_axis=0, concat_axis=0, tile...  7.3 us
    all_to_all x1, waiting for transfers between devices, fetch(): lax.all_to_all(table, ('rows', 'cols'), split_axis=0, concat_axis=0, tile...  5.34 us
  transfers between devices with their start and end apart: 18, of which 15 were waited for; matrix products, arithmetic and copies ran while one was open for 0% of the time, Pallas kernels for 1%

profile of v10, /device:TPU:0, one launch (start us, length us, event | category | flops | bytes accessed | tf_op | source)
XLA Modules:
  0.0 160.2 jit_solution(14764130379364241636)
XLA Ops:
  1.3 1.3 table_copies.1
  2.6 7.3 %all-to-all-start = ((s32[32,1,128]{2,1,0:T(1,128)}), s32[32,1,128]{2,1,0:T(1,128)S(1)}, u32[]{:S(2)}, u32[]{:S(2)}) async-start(s32[32,1,128]{2,1,0:T(1,128)} %table_copies.1), calls=%async_computation | async-start | bytes 32768 | tf_op jit(solution)/shard_map/all_to_all | solution.py:448
  9.9 0.0 copy-start.1
  9.9 1.6 copy-done.1
  11.5 0.1 turn_stripes.1.stripes_ref
  11.6 5.3 %all-to-all-done.table_ref = s32[32,1,128]{2,1,0:T(1,128)S(1)} async-done(((s32[32,1,128]{2,1,0:T(1,128)}), s32[32,1,128]{2,1,0:T(1,128)S(1)}, u32[]{:S(2)}, u32[]{:S(2)}) %all-to-all-start) | async-done | bytes 16416 | tf_op jit(solution)/shard_map/all_to_all | solution.py:448
  16.9 1.2 plan.1
  18.1 0.7 cut_stripes.3
  18.8 0.7 collective-permute-start.14
  19.5 2.3 %collective-permute-start.15 = (bf16[8,32,256]{2,1,0:T(8,128)(2,1)S(1)}, bf16[8,32,256]{2,1,0:T(8,128)(2,1)S(1)}, u32[]{:S(2)}, u32[]{:S(2)}) collective-permute-start(bf16[8,32,256]{2,1,0:T(8,128)(2,1)S(1)} %get-tuple-element.157), channel_id=1, source_target_pairs={{0,12},{2,14},{4,8},{6,10},{8,4},{10,6},{12,0},{14,2},{16,28},{18,... | collective-permute-start | bytes 393224 | tf_op jit(solution)/shard_map/ppermute | solution.py:431
  21.8 1.5 collective-permute-start.16
  23.3 0.6 collective-permute-start.17
  23.9 1.4 collective-permute-start.18
  25.3 2.9 %collective-permute-done.14 = bf16[8,32,256]{2,1,0:T(8,128)(2,1)S(1)} collective-permute-done((bf16[8,32,256]{2,1,0:T(8,128)(2,1)S(1)}, bf16[8,32,256]{2,1,0:T(8,128)(2,1)S(1)}, u32[]{:S(2)}, u32[]{:S(2)}) %collective-permute-start.14) | collective-permute-done | bytes 131104 | tf_op jit(solution)/shard_map/ppermute | solution.py:431
  28.3 0.5 collective-permute-start.19
  28.8 1.5 collective-permute-done.15
  30.2 1.3 collective-permute-start.20
  32.9 0.0 collective-permute-done.16
  32.9 0.7 collective-permute-done.17
  33.6 0.0 collective-permute-done.18
  33.6 0.8 collective-permute-done.19
  34.4 0.8 collective-permute-done.20
  35.2 0.1 conditional.2
  35.2 0.1 order_stripes.2
  35.3 0.0 copy-start
  35.3 0.0 copy-start.2
  35.3 15.6 %conditional.3 = ((bf16[8,32,256]{2,1,0:T(8,128)(2,1)S(1)}, bf16[8,32,256]{2,1,0:T(8,128)(2,1)S(1)}, bf16[8,32,256]{2,1,0:T(8,128)(2,1)}, bf16[8,32,256]{2,1,0:T...) conditional(s32[]{:T(128)} %bitcast, (s32[8,128]{1,0:T(8,128)S(1)}, ...), branch_computations={%region_2.0_spmd, %region_3.0_spmd, %region_4.0_spmd, %region_5.0_... | conditional | bytes 4194352 | solution.py:468
  35.4 0.6 listed_stripes.9
  36.0 0.5 collective-permute-start.9
  36.5 12.5 %collective-permute-done.9.other_ref = bf16[16,32,256]{2,1,0:T(8,128)(2,1)S(1)} collective-permute-done((bf16[16,32,256]{2,1,0:T(8,128)(2,1)S(1)}, bf16[16,32,256]{2,1,0:T(8,128)(2,1)S(1)}, u32[]{:S(2)}, u32[]{:S(2)}) %collective-permute-start.9) | collective-permute-done | bytes 262176 | tf_op jit(solution)/shard_map/cond/branch_2_fun/ppermute | solution.py:463
  49.0 1.8 %pick_stripes.9 = (bf16[8,32,256]{2,1,0:T(8,128)(2,1)S(1)}, bf16[8,32,256]{2,1,0:T(8,128)(2,1)S(1)}, bf16[8,32,256]{2,1,0:T(8,128)(2,1)}, bf16[8,32,256]{2,1,0:T...) custom-call(s32[32,128]{1,0:T(8,128)S(1)} %get-tuple-element.113.pla, ...), custom_call_target="tpu_custom_call" | custom-call | tf_op jit(solution)/shard_map/cond/branch_2_fun/pick_stripes/pallas_call | solution.py:244
  50.9 0.0 collective-permute-start.21
  50.9 3.8 %collective-permute-start.22 = (bf16[8,32,256]{2,1,0:T(8,128)(2,1)}, bf16[8,32,256]{2,1,0:T(8,128)(2,1)S(1)}, u32[]{:S(2)}, u32[]{:S(2)}) collective-permute-start(bf16[8,32,256]{2,1,0:T(8,128)(2,1)} %get-tuple-element.166), channel_id=1, source_target_pairs={{0,12},{2,14},{4,8},{6,10},{8,4},{10,6},{12,0},{14,2},{16,28},{18,... | collective-permute-start | bytes 393224 | tf_op jit(solution)/shard_map/ppermute | solution.py:431
  54.7 0.0 collective-permute-start.23
  54.7 1.5 collective-permute-start.24
  56.2 2.1 %collective-permute-start.25 = (bf16[8,32,256]{2,1,0:T(8,128)(2,1)}, bf16[8,32,256]{2,1,0:T(8,128)(2,1)S(1)}, u32[]{:S(2)}, u32[]{:S(2)}) collective-permute-start(bf16[8,32,256]{2,1,0:T(8,128)(2,1)} %get-tuple-element.169), channel_id=1, source_target_pairs={{0,8},{2,10},{4,12},{6,14},{8,0},{10,2},{12,4},{14,6},{16,24},{18,... | collective-permute-start | bytes 393224 | tf_op jit(solution)/shard_map/ppermute | solution.py:431
  58.2 1.6 collective-permute-done.21.refs_1_
  59.8 1.6 %collective-permute-start.26 = (bf16[8,32,256]{2,1,0:T(8,128)(2,1)}, bf16[8,32,256]{2,1,0:T(8,128)(2,1)S(1)}, u32[]{:S(2)}, u32[]{:S(2)}) collective-permute-start(bf16[8,32,256]{2,1,0:T(8,128)(2,1)} %get-tuple-element.170), channel_id=1, source_target_pairs={{0,4},{2,6},{4,0},{6,2},{8,12},{10,14},{12,8},{14,10},{16,20},{18,... | collective-permute-start | bytes 393224 | tf_op jit(solution)/shard_map/ppermute | solution.py:431
  61.4 1.7 %collective-permute-done.22.refs_2_ = bf16[8,32,256]{2,1,0:T(8,128)(2,1)S(1)} collective-permute-done((bf16[8,32,256]{2,1,0:T(8,128)(2,1)}, bf16[8,32,256]{2,1,0:T(8,128)(2,1)S(1)}, u32[]{:S(2)}, u32[]{:S(2)}) %collective-permute-start.22) | collective-permute-done | bytes 131104 | tf_op jit(solution)/shard_map/ppermute | solution.py:431
  63.1 0.6 collective-permute-start.27
  63.7 1.4 collective-permute-done.23.refs_3_
  65.1 0.0 collective-permute-done.24.refs_4_
  65.1 1.1 collective-permute-done.25.refs_5_
  66.2 0.3 collective-permute-done.26.refs_6_
  66.5 1.8 %collective-permute-done.27.refs_7_ = bf16[8,32,256]{2,1,0:T(8,128)(2,1)S(1)} collective-permute-done((bf16[8,32,256]{2,1,0:T(8,128)(2,1)}, bf16[8,32,256]{2,1,0:T(8,128)(2,1)S(1)}, u32[]{:S(2)}, u32[]{:S(2)}) %collective-permute-start.27) | collective-permute-done | bytes 131104 | tf_op jit(solution)/shard_map/ppermute | solution.py:431
  68.3 0.0 copy-done
  68.3 0.0 copy-done.2
  68.3 1.7 %block_products.2.refs_0_ = f32[1024,128]{1,0:T(8,128)S(1)} custom-call(s32[8]{0:T(128)S(1)} %copy-done.2, s32[1]{0:T(128)S(6)} %copy.65.counts_ref, bf16[8,256,256]{2,1,0:T(8,128)(2,1)S(1)} %copy-done, bf16[8,32,256]{2,1,0:T(8,128)(2,1)S(1)} %get-tuple-element.164.refs_0_, bf16[8,32,256]{2,1,0:T(8,128)(2,1)S(1)} %collective-permute-done.21.refs_1_, ...), custom_call_target="tpu_custom_call" | custom-call | tf_op jit(solution)/shard_map/block_products/pallas_call | solution.py:277
  70.0 0.1 collective-permute-start.28
  70.1 1.7 %block_products.3.refs_1_ = f32[1024,128]{1,0:T(8,128)S(1)} custom-call(s32[8]{0:T(128)S(1)} %copy-done.2, s32[1]{0:T(128)S(6)} %copy.65.counts_ref, bf16[8,256,256]{2,1,0:T(8,128)(2,1)S(1)} %copy-done, bf16[8,32,256]{2,1,0:T(8,128)(2,1)S(1)} %get-tuple-element.164.refs_0_, bf16[8,32,256]{2,1,0:T(8,128)(2,1)S(1)} %collective-permute-done.21.refs_1_, ...), custom_call_target="tpu_custom_call" | custom-call | tf_op jit(solution)/shard_map/block_products/pallas_call | solution.py:277
  71.8 0.1 collective-permute-start.29
  71.9 0.1 collective-permute-done.28.refs_2_
  72.0 1.8 %collective-permute-done.29.refs_3_ = f32[1024,128]{1,0:T(8,128)S(1)} collective-permute-done((f32[1024,128]{1,0:T(8,128)S(1)}, f32[1024,128]{1,0:T(8,128)S(1)}, u32[]{:S(2)}, u32[]{:S(2)}) %collective-permute-start.29) | collective-permute-done | bytes 524320 | tf_op jit(solution)/shard_map/ppermute | solution.py:483
  73.8 1.4 sum_and_gram.1
  75.2 10.6 %all_to_all.15 = f32[16,16,128]{2,1,0:T(8,128)S(1)} all-to-all(f32[16,16,128]{2,1,0:T(8,128)S(1)} %bitcast.7), channel_id=1, replica_groups=mesh['rows'=16,'cols'=2] {'rows'}, dimensions={0} | all-to-all | bytes 262144 | tf_op jit(solution)/shard_map/all_to_all | solution.py:485
  85.9 12.5 %all_to_all.16 = f32[32,16,128]{2,1,0:T(8,128)S(1)} all-to-all(f32[32,16,128]{2,1,0:T(8,128)S(1)} %broadcast_in_dim.2), channel_id=1, replica_groups=mesh['rows'=16,'cols'=2] {'rows','cols'}, dimensions={0} | all-to-all | bytes 524288 | tf_op jit(solution)/shard_map/all_to_all | solution.py:425
  98.4 61.8 %factor_and_basis.1 = (f32[512,256]{1,0:T(8,128)}, f32[256,256]{1,0:T(8,128)}) custom-call(f32[16,2,16,128]{3,2,1,0:T(8,128)S(1)} %bitcast.6, f32[512,256]{1,0:T(8,128)S(1)} %get-tuple-element.173.own_ref), custom_call_target="tpu_custom_call" | custom-call | tf_op jit(solution)/shard_map/factor_and_basis/pallas_call | solution.py:409
  (2 shorter events, 0.0 us)
Async XLA Ops:
  2.6 14.4 %all-to-all-start = ((s32[32,1,128]{2,1,0:T(1,128)}), s32[32,1,128]{2,1,0:T(1,128)S(1)}, u32[]{:S(2)}, u32[]{:S(2)}) async-start(s32[32,1,128]{2,1,0:T(1,128)} %table_copies.1), calls=%async_computation | async-start | bytes 32768 | tf_op jit(solution)/shard_map/all_to_all | solution.py:448
  9.9 1.6 copy-start.1
  18.8 9.4 %collective-permute-start.14 = (bf16[8,32,256]{2,1,0:T(8,128)(2,1)S(1)}, bf16[8,32,256]{2,1,0:T(8,128)(2,1)S(1)}, u32[]{:S(2)}, u32[]{:S(2)}) collective-permute-start(bf16[8,32,256]{2,1,0:T(8,128)(2,1)S(1)} %get-tuple-element.156), channel_id=1, source_target_pairs={{0,14},{2,12},{4,10},{6,8},{8,6},{10,4},{12,2},{14,0},{16,30},{18,... | collective-permute-start | bytes 393224 | tf_op jit(solution)/shard_map/ppermute | solution.py:431
  19.5 10.7 %collective-permute-start.15 = (bf16[8,32,256]{2,1,0:T(8,128)(2,1)S(1)}, bf16[8,32,256]{2,1,0:T(8,128)(2,1)S(1)}, u32[]{:S(2)}, u32[]{:S(2)}) collective-permute-start(bf16[8,32,256]{2,1,0:T(8,128)(2,1)S(1)} %get-tuple-element.157), channel_id=1, source_target_pairs={{0,12},{2,14},{4,8},{6,10},{8,4},{10,6},{12,0},{14,2},{16,28},{18,... | collective-permute-start | bytes 393224 | tf_op jit(solution)/shard_map/ppermute | solution.py:431
  21.8 11.1 %collective-permute-start.16 = (bf16[8,32,256]{2,1,0:T(8,128)(2,1)S(1)}, bf16[8,32,256]{2,1,0:T(8,128)(2,1)S(1)}, u32[]{:S(2)}, u32[]{:S(2)}) collective-permute-start(bf16[8,32,256]{2,1,0:T(8,128)(2,1)S(1)} %get-tuple-element.158), channel_id=1, source_target_pairs={{0,10},{2,8},{4,14},{6,12},{8,2},{10,0},{12,6},{14,4},{16,26},{18,... | collective-permute-start | bytes 393224 | tf_op jit(solution)/shard_map/ppermute | solution.py:431
  23.3 10.3 %collective-permute-start.17 = (bf16[8,32,256]{2,1,0:T(8,128)(2,1)S(1)}, bf16[8,32,256]{2,1,0:T(8,128)(2,1)S(1)}, u32[]{:S(2)}, u32[]{:S(2)}) collective-permute-start(bf16[8,32,256]{2,1,0:T(8,128)(2,1)S(1)} %get-tuple-element.159), channel_id=1, source_target_pairs={{0,6},{2,4},{4,2},{6,0},{8,14},{10,12},{12,10},{14,8},{16,22},{18,... | collective-permute-start | bytes 393224 | tf_op jit(solution)/shard_map/ppermute | solution.py:431
  23.9 9.7 %collective-permute-start.18 = (bf16[8,32,256]{2,1,0:T(8,128)(2,1)S(1)}, bf16[8,32,256]{2,1,0:T(8,128)(2,1)S(1)}, u32[]{:S(2)}, u32[]{:S(2)}) collective-permute-start(bf16[8,32,256]{2,1,0:T(8,128)(2,1)S(1)} %get-tuple-element.160), channel_id=1, source_target_pairs={{0,8},{2,10},{4,12},{6,14},{8,0},{10,2},{12,4},{14,6},{16,24},{18,... | collective-permute-start | bytes 393224 | tf_op jit(solution)/shard_map/ppermute | solution.py:431
  28.3 6.1 %collective-permute-start.19 = (bf16[8,32,256]{2,1,0:T(8,128)(2,1)S(1)}, bf16[8,32,256]{2,1,0:T(8,128)(2,1)S(1)}, u32[]{:S(2)}, u32[]{:S(2)}) collective-permute-start(bf16[8,32,256]{2,1,0:T(8,128)(2,1)S(1)} %get-tuple-element.161), channel_id=1, source_target_pairs={{0,4},{2,6},{4,0},{6,2},{8,12},{10,14},{12,8},{14,10},{16,20},{18,... | collective-permute-start | bytes 393224 | tf_op jit(solution)/shard_map/ppermute | solution.py:431
  30.2 5.0 %collective-permute-start.20 = (bf16[8,32,256]{2,1,0:T(8,128)(2,1)S(1)}, bf16[8,32,256]{2,1,0:T(8,128)(2,1)S(1)}, u32[]{:S(2)}, u32[]{:S(2)}) collective-permute-start(bf16[8,32,256]{2,1,0:T(8,128)(2,1)S(1)} %get-tuple-element.162), channel_id=1, source_target_pairs={{0,2},{2,0},{4,6},{6,4},{8,10},{10,8},{12,14},{14,12},{16,18},{18,... | collective-permute-start | bytes 393224 | tf_op jit(solution)/shard_map/ppermute | solution.py:431
  35.3 33.0 %copy-start = (bf16[8,256,256]{2,1,0:T(8,128)(2,1)S(1)}, bf16[8,256,256]{2,1,0:T(8,128)(2,1)}, u32[]{:S(2)}) copy-start(bf16[8,256,256]{2,1,0:T(8,128)(2,1)} %blocks_ref.3) | copy-start | bytes 3145732
  35.3 33.0 %copy-start.2 = (s32[8]{0:T(128)S(1)}, s32[8]{0:T(128)}, u32[]{:S(2)}) copy-start(s32[8]{0:T(128)} %rows_ref.3) | copy-start | bytes 100
  36.0 13.1 %collective-permute-start.9 = (bf16[16,32,256]{2,1,0:T(8,128)(2,1)S(1)}, bf16[16,32,256]{2,1,0:T(8,128)(2,1)S(1)}, u32[]{:S(2)}, u32[]{:S(2)}) collective-permute-start(bf16[16,32,256]{2,1,0:T(8,128)(2,1)S(1)} %listed_stripes.9), channel_id=1, source_target_pairs={{0,16},{2,18},{4,20},{6,22},{8,24},{10,26},{12,28},{14,30},{16,0},... | collective-permute-start | bytes 786440 | tf_op jit(solution)/shard_map/cond/branch_2_fun/ppermute | solution.py:463
  50.9 8.9 %collective-permute-start.21 = (bf16[8,32,256]{2,1,0:T(8,128)(2,1)S(1)}, bf16[8,32,256]{2,1,0:T(8,128)(2,1)S(1)}, u32[]{:S(2)}, u32[]{:S(2)}) collective-permute-start(bf16[8,32,256]{2,1,0:T(8,128)(2,1)S(1)} %get-tuple-element.165), channel_id=1, source_target_pairs={{0,14},{2,12},{4,10},{6,8},{8,6},{10,4},{12,2},{14,0},{16,30},{18,... | collective-permute-start | bytes 393224 | tf_op jit(solution)/shard_map/ppermute | solution.py:431
  50.9 12.2 %collective-permute-start.22 = (bf16[8,32,256]{2,1,0:T(8,128)(2,1)}, bf16[8,32,256]{2,1,0:T(8,128)(2,1)S(1)}, u32[]{:S(2)}, u32[]{:S(2)}) collective-permute-start(bf16[8,32,256]{2,1,0:T(8,128)(2,1)} %get-tuple-element.166), channel_id=1, source_target_pairs={{0,12},{2,14},{4,8},{6,10},{8,4},{10,6},{12,0},{14,2},{16,28},{18,... | collective-permute-start | bytes 393224 | tf_op jit(solution)/shard_map/ppermute | solution.py:431
  54.7 10.4 %collective-permute-start.23 = (bf16[8,32,256]{2,1,0:T(8,128)(2,1)}, bf16[8,32,256]{2,1,0:T(8,128)(2,1)S(1)}, u32[]{:S(2)}, u32[]{:S(2)}) collective-permute-start(bf16[8,32,256]{2,1,0:T(8,128)(2,1)} %get-tuple-element.167), channel_id=1, source_target_pairs={{0,10},{2,8},{4,14},{6,12},{8,2},{10,0},{12,6},{14,4},{16,26},{18,... | collective-permute-start | bytes 393224 | tf_op jit(solution)/shard_map/ppermute | solution.py:431
  54.7 10.4 %collective-permute-start.24 = (bf16[8,32,256]{2,1,0:T(8,128)(2,1)}, bf16[8,32,256]{2,1,0:T(8,128)(2,1)S(1)}, u32[]{:S(2)}, u32[]{:S(2)}) collective-permute-start(bf16[8,32,256]{2,1,0:T(8,128)(2,1)} %get-tuple-element.168), channel_id=1, source_target_pairs={{0,6},{2,4},{4,2},{6,0},{8,14},{10,12},{12,10},{14,8},{16,22},{18,... | collective-permute-start | bytes 393224 | tf_op jit(solution)/shard_map/ppermute | solution.py:431
  56.2 10.0 %collective-permute-start.25 = (bf16[8,32,256]{2,1,0:T(8,128)(2,1)}, bf16[8,32,256]{2,1,0:T(8,128)(2,1)S(1)}, u32[]{:S(2)}, u32[]{:S(2)}) collective-permute-start(bf16[8,32,256]{2,1,0:T(8,128)(2,1)} %get-tuple-element.169), channel_id=1, source_target_pairs={{0,8},{2,10},{4,12},{6,14},{8,0},{10,2},{12,4},{14,6},{16,24},{18,... | collective-permute-start | bytes 393224 | tf_op jit(solution)/shard_map/ppermute | solution.py:431
  59.8 6.7 %collective-permute-start.26 = (bf16[8,32,256]{2,1,0:T(8,128)(2,1)}, bf16[8,32,256]{2,1,0:T(8,128)(2,1)S(1)}, u32[]{:S(2)}, u32[]{:S(2)}) collective-permute-start(bf16[8,32,256]{2,1,0:T(8,128)(2,1)} %get-tuple-element.170), channel_id=1, source_target_pairs={{0,4},{2,6},{4,0},{6,2},{8,12},{10,14},{12,8},{14,10},{16,20},{18,... | collective-permute-start | bytes 393224 | tf_op jit(solution)/shard_map/ppermute | solution.py:431
  63.1 5.2 %collective-permute-start.27 = (bf16[8,32,256]{2,1,0:T(8,128)(2,1)}, bf16[8,32,256]{2,1,0:T(8,128)(2,1)S(1)}, u32[]{:S(2)}, u32[]{:S(2)}) collective-permute-start(bf16[8,32,256]{2,1,0:T(8,128)(2,1)} %get-tuple-element.171), channel_id=1, source_target_pairs={{0,2},{2,0},{4,6},{6,4},{8,10},{10,8},{12,14},{14,12},{16,18},{18,... | collective-permute-start | bytes 393224 | tf_op jit(solution)/shard_map/ppermute | solution.py:431
  70.0 2.0 %collective-permute-start.28 = (f32[1024,128]{1,0:T(8,128)S(1)}, f32[1024,128]{1,0:T(8,128)S(1)}, u32[]{:S(2)}, u32[]{:S(2)}) collective-permute-start(f32[1024,128]{1,0:T(8,128)S(1)} %block_products.2.refs_0_), channel_id=1, source_target_pairs={{0,1},{1,0},{2,3},{3,2},{4,5},{5,4},{6,7},{7,6},{8,9},{9,8},{10,11... | collective-permute-start | bytes 1572872 | tf_op jit(solution)/shard_map/ppermute | solution.py:483
  71.8 2.0 %collective-permute-start.29 = (f32[1024,128]{1,0:T(8,128)S(1)}, f32[1024,128]{1,0:T(8,128)S(1)}, u32[]{:S(2)}, u32[]{:S(2)}) collective-permute-start(f32[1024,128]{1,0:T(8,128)S(1)} %block_products.3.refs_1_), channel_id=1, source_target_pairs={{0,1},{1,0},{2,3},{3,2},{4,5},{5,4},{6,7},{7,6},{8,9},{9,8},{10,11... | collective-permute-start | bytes 1572872 | tf_op jit(solution)/shard_map/ppermute | solution.py:483

commit v11 on v9

--- a/solution.py
+++ b/solution.py
@@ -14,7 +14,7 @@
 MIB = 1024 * 1024
 
 
-ACROSS = (12, 14, 16, 18, 20, 24)
+ACROSS = (*range(11, 21), 22, 24, 28, 36)
 WITHIN = 8
 
 
@@ -433,7 +433,7 @@
     per = sketch.shape[0]
     largest = min(per * members, slots * members, 128)
     within = min(per, WITHIN)
-    across = tuple(level for level in ACROSS if level < largest)
+    across = tuple(level for level in ACROSS if level < largest and members <= 8)
     stripes = turn(sketch)
     table = table_copies(block_cols, counts, rows * cols)
     table = lax.all_to_all(table, ("rows", "cols"), split_axis=0, concat_axis=0, tiled=True)

time: 162 us -> 158 us (0.975); the launches traced: 159 us -> 157 us
  waiting for transfers between devices: 35 us -> 32.9 us
    ppermute x1, waiting for transfers between devices: 12.5 us -> 10.4 us  [run(): other = lax.ppermute(listed(lists, own, count), 'rows', swap)]
where the time goes in v11:
time: 158 us; the launch traced here: 157 us
  Pallas kernels  70.3 us (44%)
  waiting for transfers between devices  32.9 us (21%)
  starting transfers between devices  25.8 us (16%)
  blocking collectives  23.4 us (15%)
  between operations  2.7 us (2%)
  local copies, waits for them, and re-layouts  1.62 us (1%)
    pallas_call x1, Pallas kernels, factor_and_basis(): pl.pallas_call(functools.partial(factor_kernel, total_rows), out_shape=(j...  61.8 us
    ppermute x14, starting transfers between devices, exchange(): lax.ppermute(piece, 'rows', [(r, r ^ d) for r in range(rows)])  17.9 us
    ppermute x14, waiting for transfers between devices, exchange(): lax.ppermute(piece, 'rows', [(r, r ^ d) for r in range(rows)])  14.5 us
    all_to_all x1, blocking collectives, spread(): return lax.all_to_all(copies, axes, split_axis=0, concat_axis=0, tiled=True)  12.5 us
    all_to_all x1, blocking collectives, local(): lax.all_to_all(pieces, 'rows', split_axis=0, concat_axis=0, tiled=True)  10.9 us
    ppermute x1, waiting for transfers between devices, run(): other = lax.ppermute(listed(lists, own, count), 'rows', swap)  10.4 us
    all_to_all x1, starting transfers between devices, fetch(): lax.all_to_all(table, ('rows', 'cols'), split_axis=0, concat_axis=0, tile...  7.3 us
    all_to_all x1, waiting for transfers between devices, fetch(): lax.all_to_all(table, ('rows', 'cols'), split_axis=0, concat_axis=0, tile...  5.34 us
  transfers between devices with their start and end apart: 17, of which 14 were waited for; matrix products, arithmetic and copies ran while one was open for 0% of the time, Pallas kernels for 0%

profile of v11, /device:TPU:0, one launch (start us, length us, event | category | flops | bytes accessed | tf_op | source)
XLA Modules:
  0.0 156.9 jit_solution(14963074241695090557)
XLA Ops:
  1.3 1.3 table_copies.1
  2.6 7.3 %all-to-all-start = ((s32[32,1,128]{2,1,0:T(1,128)}), s32[32,1,128]{2,1,0:T(1,128)S(1)}, u32[]{:S(2)}, u32[]{:S(2)}) async-start(s32[32,1,128]{2,1,0:T(1,128)} %table_copies.1), calls=%async_computation | async-start | bytes 32768 | tf_op jit(solution)/shard_map/all_to_all | solution.py:439
  9.9 0.0 copy-start
  9.9 1.6 %copy-done = bf16[4096,256]{1,0:T(8,128)(2,1)S(1)} copy-done((bf16[4096,256]{1,0:T(8,128)(2,1)S(1)}, bf16[4096,256]{1,0:T(8,128)(2,1)}, u32[]{:S(2)}) %copy-start) | copy-done | bytes 2097176
  11.5 0.1 turn_stripes.1.stripes_ref
  11.6 5.3 %all-to-all-done.table_ref = s32[32,1,128]{2,1,0:T(1,128)S(1)} async-done(((s32[32,1,128]{2,1,0:T(1,128)}), s32[32,1,128]{2,1,0:T(1,128)S(1)}, u32[]{:S(2)}, u32[]{:S(2)}) %all-to-all-start) | async-done | bytes 16416 | tf_op jit(solution)/shard_map/all_to_all | solution.py:439
  16.9 1.2 plan.1
  18.1 0.7 cut_stripes.3
  18.8 0.7 collective-permute-start.22
  19.5 2.3 %collective-permute-start.23 = (bf16[8,32,256]{2,1,0:T(8,128)(2,1)S(1)}, bf16[8,32,256]{2,1,0:T(8,128)(2,1)S(1)}, u32[]{:S(2)}, u32[]{:S(2)}) collective-permute-start(bf16[8,32,256]{2,1,0:T(8,128)(2,1)S(1)} %get-tuple-element.229), channel_id=1, source_target_pairs={{0,12},{2,14},{4,8},{6,10},{8,4},{10,6},{12,0},{14,2},{16,28},{18,... | collective-permute-start | bytes 393224 | tf_op jit(solution)/shard_map/ppermute | solution.py:422
  21.8 1.5 collective-permute-start.24
  23.3 0.6 collective-permute-start.25
  23.9 1.4 collective-permute-start.26
  25.3 2.9 %collective-permute-done.22 = bf16[8,32,256]{2,1,0:T(8,128)(2,1)S(1)} collective-permute-done((bf16[8,32,256]{2,1,0:T(8,128)(2,1)S(1)}, bf16[8,32,256]{2,1,0:T(8,128)(2,1)S(1)}, u32[]{:S(2)}, u32[]{:S(2)}) %collective-permute-start.22) | collective-permute-done | bytes 131104 | tf_op jit(solution)/shard_map/ppermute | solution.py:422
  28.3 0.5 collective-permute-start.27
  28.8 1.5 collective-permute-done.23
  30.2 1.3 collective-permute-start.28
  32.9 0.0 collective-permute-done.24
  32.9 0.7 collective-permute-done.25
  33.6 0.0 collective-permute-done.26
  33.6 0.8 collective-permute-done.27
  34.4 0.8 collective-permute-done.28
  35.2 0.1 conditional.2
  35.2 0.1 order_stripes.2
  35.3 0.0 copy-start.1
  35.3 0.0 copy-start.2
  35.3 13.4 %conditional.3 = ((bf16[8,32,256]{2,1,0:T(8,128)(2,1)S(1)}, bf16[8,32,256]{2,1,0:T(8,128)(2,1)S(1)}, bf16[8,32,256]{2,1,0:T(8,128)(2,1)}, bf16[8,32,256]{2,1,0:T...) conditional(s32[]{:T(128)} %bitcast, (s32[8,128]{1,0:T(8,128)S(1)}, ...), branch_computations={%region_2.0_spmd, %region_3.0_spmd, %region_4.0_spmd, %region_5.0_... | conditional | bytes 4194352 | solution.py:459
  35.4 0.6 listed_stripes.17
  36.0 0.5 collective-permute-start.9
  36.5 10.4 %collective-permute-done.9.other_ref = bf16[13,32,256]{2,1,0:T(8,128)(2,1)S(1)} collective-permute-done((bf16[13,32,256]{2,1,0:T(8,128)(2,1)S(1)}, bf16[13,32,256]{2,1,0:T(8,128)(2,1)S(1)}, u32[]{:S(2)}, u32[]{:S(2)}) %collective-permute-start.9) | collective-permute-done | bytes 213024 | tf_op jit(solution)/shard_map/cond/branch_2_fun/ppermute | solution.py:454
  46.9 1.8 %pick_stripes.17 = (bf16[8,32,256]{2,1,0:T(8,128)(2,1)S(1)}, bf16[8,32,256]{2,1,0:T(8,128)(2,1)S(1)}, bf16[8,32,256]{2,1,0:T(8,128)(2,1)}, bf16[8,32,256]{2,1,0:...) custom-call(s32[32,128]{1,0:T(8,128)S(1)} %get-tuple-element.161.pla, ...), custom_call_target="tpu_custom_call" | custom-call | tf_op jit(solution)/shard_map/cond/branch_2_fun/pick_stripes/pallas_call | solution.py:238
  48.8 0.0 collective-permute-start.29
  48.8 3.8 %collective-permute-start.30 = (bf16[8,32,256]{2,1,0:T(8,128)(2,1)}, bf16[8,32,256]{2,1,0:T(8,128)(2,1)S(1)}, u32[]{:S(2)}, u32[]{:S(2)}) collective-permute-start(bf16[8,32,256]{2,1,0:T(8,128)(2,1)} %get-tuple-element.238), channel_id=1, source_target_pairs={{0,12},{2,14},{4,8},{6,10},{8,4},{10,6},{12,0},{14,2},{16,28},{18,... | collective-permute-start | bytes 393224 | tf_op jit(solution)/shard_map/ppermute | solution.py:422
  52.6 0.0 collective-permute-start.31
  52.6 1.5 collective-permute-start.32
  54.0 2.1 %collective-permute-start.33 = (bf16[8,32,256]{2,1,0:T(8,128)(2,1)}, bf16[8,32,256]{2,1,0:T(8,128)(2,1)S(1)}, u32[]{:S(2)}, u32[]{:S(2)}) collective-permute-start(bf16[8,32,256]{2,1,0:T(8,128)(2,1)} %get-tuple-element.241), channel_id=1, source_target_pairs={{0,8},{2,10},{4,12},{6,14},{8,0},{10,2},{12,4},{14,6},{16,24},{18,... | collective-permute-start | bytes 393224 | tf_op jit(solution)/shard_map/ppermute | solution.py:422
  56.1 1.6 collective-permute-done.29.refs_1_
  57.7 1.6 %collective-permute-start.34 = (bf16[8,32,256]{2,1,0:T(8,128)(2,1)}, bf16[8,32,256]{2,1,0:T(8,128)(2,1)S(1)}, u32[]{:S(2)}, u32[]{:S(2)}) collective-permute-start(bf16[8,32,256]{2,1,0:T(8,128)(2,1)} %get-tuple-element.242), channel_id=1, source_target_pairs={{0,4},{2,6},{4,0},{6,2},{8,12},{10,14},{12,8},{14,10},{16,20},{18,... | collective-permute-start | bytes 393224 | tf_op jit(solution)/shard_map/ppermute | solution.py:422
  59.3 1.7 %collective-permute-done.30.refs_2_ = bf16[8,32,256]{2,1,0:T(8,128)(2,1)S(1)} collective-permute-done((bf16[8,32,256]{2,1,0:T(8,128)(2,1)}, bf16[8,32,256]{2,1,0:T(8,128)(2,1)S(1)}, u32[]{:S(2)}, u32[]{:S(2)}) %collective-permute-start.30) | collective-permute-done | bytes 131104 | tf_op jit(solution)/shard_map/ppermute | solution.py:422
  61.0 0.6 collective-permute-start.35
  61.5 1.4 collective-permute-done.31.refs_3_
  62.9 0.0 collective-permute-done.32.refs_4_
  62.9 0.9 collective-permute-done.33.refs_5_
  63.8 0.5 collective-permute-done.34.refs_6_
  64.4 1.8 %collective-permute-done.35.refs_7_ = bf16[8,32,256]{2,1,0:T(8,128)(2,1)S(1)} collective-permute-done((bf16[8,32,256]{2,1,0:T(8,128)(2,1)}, bf16[8,32,256]{2,1,0:T(8,128)(2,1)S(1)}, u32[]{:S(2)}, u32[]{:S(2)}) %collective-permute-start.35) | collective-permute-done | bytes 131104 | tf_op jit(solution)/shard_map/ppermute | solution.py:422
  66.1 0.0 copy-done.1
  66.1 0.0 copy-done.2
  66.1 1.3 block_products.1.mine_ref
  67.4 0.1 collective-permute-start.36
  67.5 2.6 %collective-permute-done.36.other_ref = f32[1024,256]{1,0:T(8,128)S(1)} collective-permute-done((f32[1024,256]{1,0:T(8,128)S(1)}, f32[1024,256]{1,0:T(8,128)S(1)}, u32[]{:S(2)}, u32[]{:S(2)}) %collective-permute-start.36) | collective-permute-done | bytes 1048608 | tf_op jit(solution)/shard_map/ppermute | solution.py:473
  70.2 1.4 sum_and_gram.1
  71.6 10.9 %all_to_all.15 = f32[16,16,128]{2,1,0:T(8,128)S(1)} all-to-all(f32[16,16,128]{2,1,0:T(8,128)S(1)} %bitcast.7), channel_id=1, replica_groups=mesh['rows'=16,'cols'=2] {'rows'}, dimensions={0} | all-to-all | bytes 262144 | tf_op jit(solution)/shard_map/all_to_all | solution.py:476
  82.5 12.5 %all_to_all.16 = f32[32,16,128]{2,1,0:T(8,128)S(1)} all-to-all(f32[32,16,128]{2,1,0:T(8,128)S(1)} %broadcast_in_dim.2), channel_id=1, replica_groups=mesh['rows'=16,'cols'=2] {'rows','cols'}, dimensions={0} | all-to-all | bytes 524288 | tf_op jit(solution)/shard_map/all_to_all | solution.py:416
  95.1 61.8 %factor_and_basis.1 = (f32[512,256]{1,0:T(8,128)}, f32[256,256]{1,0:T(8,128)}) custom-call(f32[16,2,16,128]{3,2,1,0:T(8,128)S(1)} %bitcast.6, f32[512,256]{1,0:T(8,128)S(1)} %get-tuple-element.245.own_ref), custom_call_target="tpu_custom_call" | custom-call | tf_op jit(solution)/shard_map/factor_and_basis/pallas_call | solution.py:400
  (2 shorter events, 0.0 us)
Async XLA Ops:
  2.6 14.4 %all-to-all-start = ((s32[32,1,128]{2,1,0:T(1,128)}), s32[32,1,128]{2,1,0:T(1,128)S(1)}, u32[]{:S(2)}, u32[]{:S(2)}) async-start(s32[32,1,128]{2,1,0:T(1,128)} %table_copies.1), calls=%async_computation | async-start | bytes 32768 | tf_op jit(solution)/shard_map/all_to_all | solution.py:439
  9.9 1.6 %copy-start = (bf16[4096,256]{1,0:T(8,128)(2,1)S(1)}, bf16[4096,256]{1,0:T(8,128)(2,1)}, u32[]{:S(2)}) copy-start(bf16[4096,256]{1,0:T(8,128)(2,1)} %param.22) | copy-start | bytes 6291460
  18.8 9.4 %collective-permute-start.22 = (bf16[8,32,256]{2,1,0:T(8,128)(2,1)S(1)}, bf16[8,32,256]{2,1,0:T(8,128)(2,1)S(1)}, u32[]{:S(2)}, u32[]{:S(2)}) collective-permute-start(bf16[8,32,256]{2,1,0:T(8,128)(2,1)S(1)} %get-tuple-element.228), channel_id=1, source_target_pairs={{0,14},{2,12},{4,10},{6,8},{8,6},{10,4},{12,2},{14,0},{16,30},{18,... | collective-permute-start | bytes 393224 | tf_op jit(solution)/shard_map/ppermute | solution.py:422
  19.5 10.7 %collective-permute-start.23 = (bf16[8,32,256]{2,1,0:T(8,128)(2,1)S(1)}, bf16[8,32,256]{2,1,0:T(8,128)(2,1)S(1)}, u32[]{:S(2)}, u32[]{:S(2)}) collective-permute-start(bf16[8,32,256]{2,1,0:T(8,128)(2,1)S(1)} %get-tuple-element.229), channel_id=1, source_target_pairs={{0,12},{2,14},{4,8},{6,10},{8,4},{10,6},{12,0},{14,2},{16,28},{18,... | collective-permute-start | bytes 393224 | tf_op jit(solution)/shard_map/ppermute | solution.py:422
  21.8 11.1 %collective-permute-start.24 = (bf16[8,32,256]{2,1,0:T(8,128)(2,1)S(1)}, bf16[8,32,256]{2,1,0:T(8,128)(2,1)S(1)}, u32[]{:S(2)}, u32[]{:S(2)}) collective-permute-start(bf16[8,32,256]{2,1,0:T(8,128)(2,1)S(1)} %get-tuple-element.230), channel_id=1, source_target_pairs={{0,10},{2,8},{4,14},{6,12},{8,2},{10,0},{12,6},{14,4},{16,26},{18,... | collective-permute-start | bytes 393224 | tf_op jit(solution)/shard_map/ppermute | solution.py:422
  23.3 10.3 %collective-permute-start.25 = (bf16[8,32,256]{2,1,0:T(8,128)(2,1)S(1)}, bf16[8,32,256]{2,1,0:T(8,128)(2,1)S(1)}, u32[]{:S(2)}, u32[]{:S(2)}) collective-permute-start(bf16[8,32,256]{2,1,0:T(8,128)(2,1)S(1)} %get-tuple-element.231), channel_id=1, source_target_pairs={{0,6},{2,4},{4,2},{6,0},{8,14},{10,12},{12,10},{14,8},{16,22},{18,... | collective-permute-start | bytes 393224 | tf_op jit(solution)/shard_map/ppermute | solution.py:422
  23.9 9.7 %collective-permute-start.26 = (bf16[8,32,256]{2,1,0:T(8,128)(2,1)S(1)}, bf16[8,32,256]{2,1,0:T(8,128)(2,1)S(1)}, u32[]{:S(2)}, u32[]{:S(2)}) collective-permute-start(bf16[8,32,256]{2,1,0:T(8,128)(2,1)S(1)} %get-tuple-element.232), channel_id=1, source_target_pairs={{0,8},{2,10},{4,12},{6,14},{8,0},{10,2},{12,4},{14,6},{16,24},{18,... | collective-permute-start | bytes 393224 | tf_op jit(solution)/shard_map/ppermute | solution.py:422
  28.3 6.1 %collective-permute-start.27 = (bf16[8,32,256]{2,1,0:T(8,128)(2,1)S(1)}, bf16[8,32,256]{2,1,0:T(8,128)(2,1)S(1)}, u32[]{:S(2)}, u32[]{:S(2)}) collective-permute-start(bf16[8,32,256]{2,1,0:T(8,128)(2,1)S(1)} %get-tuple-element.233), channel_id=1, source_target_pairs={{0,4},{2,6},{4,0},{6,2},{8,12},{10,14},{12,8},{14,10},{16,20},{18,... | collective-permute-start | bytes 393224 | tf_op jit(solution)/shard_map/ppermute | solution.py:422
  30.2 5.0 %collective-permute-start.28 = (bf16[8,32,256]{2,1,0:T(8,128)(2,1)S(1)}, bf16[8,32,256]{2,1,0:T(8,128)(2,1)S(1)}, u32[]{:S(2)}, u32[]{:S(2)}) collective-permute-start(bf16[8,32,256]{2,1,0:T(8,128)(2,1)S(1)} %get-tuple-element.234), channel_id=1, source_target_pairs={{0,2},{2,0},{4,6},{6,4},{8,10},{10,8},{12,14},{14,12},{16,18},{18,... | collective-permute-start | bytes 393224 | tf_op jit(solution)/shard_map/ppermute | solution.py:422
  35.3 30.8 %copy-start.1 = (bf16[8,256,256]{2,1,0:T(8,128)(2,1)S(1)}, bf16[8,256,256]{2,1,0:T(8,128)(2,1)}, u32[]{:S(2)}) copy-start(bf16[8,256,256]{2,1,0:T(8,128)(2,1)} %blocks_ref.1) | copy-start | bytes 3145732
  35.3 30.8 %copy-start.2 = (s32[8]{0:T(128)S(1)}, s32[8]{0:T(128)}, u32[]{:S(2)}) copy-start(s32[8]{0:T(128)} %rows_ref.1) | copy-start | bytes 100
  36.0 11.0 %collective-permute-start.9 = (bf16[13,32,256]{2,1,0:T(8,128)(2,1)S(1)}, bf16[13,32,256]{2,1,0:T(8,128)(2,1)S(1)}, u32[]{:S(2)}, u32[]{:S(2)}) collective-permute-start(bf16[13,32,256]{2,1,0:T(8,128)(2,1)S(1)} %listed_stripes.17), channel_id=1, source_target_pairs={{0,16},{2,18},{4,20},{6,22},{8,24},{10,26},{12,28},{14,30},{16,0},... | collective-permute-start | bytes 638984 | tf_op jit(solution)/shard_map/cond/branch_2_fun/ppermute | solution.py:454
  48.8 8.9 %collective-permute-start.29 = (bf16[8,32,256]{2,1,0:T(8,128)(2,1)S(1)}, bf16[8,32,256]{2,1,0:T(8,128)(2,1)S(1)}, u32[]{:S(2)}, u32[]{:S(2)}) collective-permute-start(bf16[8,32,256]{2,1,0:T(8,128)(2,1)S(1)} %get-tuple-element.237), channel_id=1, source_target_pairs={{0,14},{2,12},{4,10},{6,8},{8,6},{10,4},{12,2},{14,0},{16,30},{18,... | collective-permute-start | bytes 393224 | tf_op jit(solution)/shard_map/ppermute | solution.py:422
  48.8 12.2 %collective-permute-start.30 = (bf16[8,32,256]{2,1,0:T(8,128)(2,1)}, bf16[8,32,256]{2,1,0:T(8,128)(2,1)S(1)}, u32[]{:S(2)}, u32[]{:S(2)}) collective-permute-start(bf16[8,32,256]{2,1,0:T(8,128)(2,1)} %get-tuple-element.238), channel_id=1, source_target_pairs={{0,12},{2,14},{4,8},{6,10},{8,4},{10,6},{12,0},{14,2},{16,28},{18,... | collective-permute-start | bytes 393224 | tf_op jit(solution)/shard_map/ppermute | solution.py:422
  52.6 10.3 %collective-permute-start.31 = (bf16[8,32,256]{2,1,0:T(8,128)(2,1)}, bf16[8,32,256]{2,1,0:T(8,128)(2,1)S(1)}, u32[]{:S(2)}, u32[]{:S(2)}) collective-permute-start(bf16[8,32,256]{2,1,0:T(8,128)(2,1)} %get-tuple-element.239), channel_id=1, source_target_pairs={{0,10},{2,8},{4,14},{6,12},{8,2},{10,0},{12,6},{14,4},{16,26},{18,... | collective-permute-start | bytes 393224 | tf_op jit(solution)/shard_map/ppermute | solution.py:422
  52.6 10.3 %collective-permute-start.32 = (bf16[8,32,256]{2,1,0:T(8,128)(2,1)}, bf16[8,32,256]{2,1,0:T(8,128)(2,1)S(1)}, u32[]{:S(2)}, u32[]{:S(2)}) collective-permute-start(bf16[8,32,256]{2,1,0:T(8,128)(2,1)} %get-tuple-element.240), channel_id=1, source_target_pairs={{0,6},{2,4},{4,2},{6,0},{8,14},{10,12},{12,10},{14,8},{16,22},{18,... | collective-permute-start | bytes 393224 | tf_op jit(solution)/shard_map/ppermute | solution.py:422
  54.0 9.8 %collective-permute-start.33 = (bf16[8,32,256]{2,1,0:T(8,128)(2,1)}, bf16[8,32,256]{2,1,0:T(8,128)(2,1)S(1)}, u32[]{:S(2)}, u32[]{:S(2)}) collective-permute-start(bf16[8,32,256]{2,1,0:T(8,128)(2,1)} %get-tuple-element.241), channel_id=1, source_target_pairs={{0,8},{2,10},{4,12},{6,14},{8,0},{10,2},{12,4},{14,6},{16,24},{18,... | collective-permute-start | bytes 393224 | tf_op jit(solution)/shard_map/ppermute | solution.py:422
  57.7 6.7 %collective-permute-start.34 = (bf16[8,32,256]{2,1,0:T(8,128)(2,1)}, bf16[8,32,256]{2,1,0:T(8,128)(2,1)S(1)}, u32[]{:S(2)}, u32[]{:S(2)}) collective-permute-start(bf16[8,32,256]{2,1,0:T(8,128)(2,1)} %get-tuple-element.242), channel_id=1, source_target_pairs={{0,4},{2,6},{4,0},{6,2},{8,12},{10,14},{12,8},{14,10},{16,20},{18,... | collective-permute-start | bytes 393224 | tf_op jit(solution)/shard_map/ppermute | solution.py:422
  61.0 5.2 %collective-permute-start.35 = (bf16[8,32,256]{2,1,0:T(8,128)(2,1)}, bf16[8,32,256]{2,1,0:T(8,128)(2,1)S(1)}, u32[]{:S(2)}, u32[]{:S(2)}) collective-permute-start(bf16[8,32,256]{2,1,0:T(8,128)(2,1)} %get-tuple-element.243), channel_id=1, source_target_pairs={{0,2},{2,0},{4,6},{6,4},{8,10},{10,8},{12,14},{14,12},{16,18},{18,... | collective-permute-start | bytes 393224 | tf_op jit(solution)/shard_map/ppermute | solution.py:422
  67.4 2.7 %collective-permute-start.36 = (f32[1024,256]{1,0:T(8,128)S(1)}, f32[1024,256]{1,0:T(8,128)S(1)}, u32[]{:S(2)}, u32[]{:S(2)}) collective-permute-start(f32[1024,256]{1,0:T(8,128)S(1)} %block_products.1.mine_ref), channel_id=1, source_target_pairs={{0,1},{1,0},{2,3},{3,2},{4,5},{5,4},{6,7},{7,6},{8,9},{9,8},{10,11... | collective-permute-start | bytes 3145736 | tf_op jit(solution)/shard_map/ppermute | solution.py:473

commit v12 on v11

--- a/solution.py
+++ b/solution.py
@@ -15,7 +15,7 @@
 
 
 ACROSS = (*range(11, 21), 22, 24, 28, 36)
-WITHIN = 8
+WITHIN = (5, 6, 7, 8, 9, 10, 12)
 
 
 def table_kernel(cols_ref, counts_ref, out_ref):
@@ -86,7 +86,7 @@
     near_rank = ranks(short, near)
     far_rank = ranks(short, after)
     longest = jnp.max(jnp.where(line < lines, near_rank + asks, 0.0)).astype(jnp.int32)
-    level_refs[0][0] = (longest > within).astype(jnp.int32)
+    level_refs[0][0] = sum((longest > level).astype(jnp.int32) for level in within)
     longest = jnp.max(jnp.where(line < lines, 0.0, far_rank + asks)).astype(jnp.int32)
     level_refs[1][0] = sum((longest > level).astype(jnp.int32) for level in across)
     me = lax.axis_index("rows")
@@ -165,17 +165,17 @@
     )(sketch)
 
 
-def cut_kernel(start, lists_ref, stripes_ref, *out_refs):
+def cut_kernel(lists_ref, stripes_ref, *out_refs):
     for k in range(out_refs[0].shape[0]):
         for i, out_ref in enumerate(out_refs):
-            out_ref[k] = stripes_ref[i, lists_ref[1, start + k]]
-
-
-def cut(lists, stripes, start, stop):
+            out_ref[k] = stripes_ref[i, lists_ref[1, k]]
+
+
+def cut(lists, stripes, count):
     members, _, height, columns = stripes.shape
     return pl.pallas_call(
-        functools.partial(cut_kernel, start),
-        out_shape=(jax.ShapeDtypeStruct((stop - start, height, columns), stripes.dtype),) * members,
+        cut_kernel,
+        out_shape=(jax.ShapeDtypeStruct((count, height, columns), stripes.dtype),) * members,
         in_specs=[SMEM, VMEM],
         out_specs=(VMEM,) * members,
         compiler_params=pltpu.CompilerParams(vmem_limit_bytes=24 * MIB),
@@ -183,22 +183,20 @@
     )(lists, stripes)
 
 
-def order_kernel(members, *refs):
+def order_kernel(*refs):
     *stripe_refs, all_ref = refs
+    members = len(stripe_refs)
     me = lax.axis_index("rows") % members
     per = all_ref.shape[0] // members
-    for i, d in enumerate(distances(members)):
-        at = (me ^ d) * per
-        for ref in stripe_refs[i::members]:
-            all_ref[pl.ds(at, ref.shape[0])] = ref[...]
-            at = at + ref.shape[0]
-
-
-def order(stripes, members, per):
+    for ref, d in zip(stripe_refs, distances(members)):
+        all_ref[pl.ds((me ^ d) * per, ref.shape[0])] = ref[...]
+
+
+def order(stripes, per):
     _, height, columns = stripes[0].shape
     return pl.pallas_call(
-        functools.partial(order_kernel, members),
-        out_shape=jax.ShapeDtypeStruct((members * per, height, columns), stripes[0].dtype),
+        order_kernel,
+        out_shape=jax.ShapeDtypeStruct((len(stripes) * per, height, columns), stripes[0].dtype),
         in_specs=[VMEM] * len(stripes),
         out_specs=VMEM,
         compiler_params=pltpu.CompilerParams(vmem_limit_bytes=24 * MIB),
@@ -432,21 +430,20 @@
     sketch = sketch.reshape(-1, members, height, columns)
     per = sketch.shape[0]
     largest = min(per * members, slots * members, 128)
-    within = min(per, WITHIN)
+    within = tuple(level for level in WITHIN if level < per)
     across = tuple(level for level in ACROSS if level < largest and members <= 8)
     stripes = turn(sketch)
     table = table_copies(block_cols, counts, rows * cols)
     table = lax.all_to_all(table, ("rows", "cols"), split_axis=0, concat_axis=0, tiled=True)
-    places, lists, more, far = plan(table, slots, per, within, across)
-    first = exchange(cut(lists, stripes, 0, within), rows)
-
-    def as_sent():
-        return order(first, members, per)
-
-    def with_rest():
-        return order(first + exchange(cut(lists, stripes, within, per), rows), members, per)
-
-    own = lax.cond(more[0] > 0, with_rest, as_sent) if within < per else as_sent()
+    places, lists, near, far = plan(table, slots, per, within, across)
+
+    def within_half(count):
+        def run():
+            return order(exchange(cut(lists, stripes, count), rows), per)
+
+        return run
+
+    own = lax.switch(near[0], [within_half(count) for count in (*within, per)])
 
     def across_halves(count):
         def run():

time: 158 us -> 158 us (level); the launches traced: 157 us -> 155 us
  waiting for transfers between devices: 32.9 us -> 29.2 us
    ppermute x14, waiting for transfers between devices: 14.5 us -> 10.5 us  [exchange(): lax.ppermute(piece, 'rows', [(r, r ^ d) for r in range(rows)])]
  transfers between devices with their start and end apart: 17 -> 17, of which waited for: 14 -> 13; matrix products, arithmetic and copies ran while one was open for 0% -> 0% of each run, Pallas kernels for 0% -> 0%
where the time goes in v12:
time: 158 us; the launch traced here: 155 us
  Pallas kernels  71.4 us (45%)
  waiting for transfers between devices  29.2 us (18%)
  starting transfers between devices  26.9 us (17%)
  blocking collectives  23.1 us (15%)
  between operations  2.67 us (2%)
  local copies, waits for them, and re-layouts  1.62 us (1%)
    pallas_call x1, Pallas kernels, factor_and_basis(): pl.pallas_call(functools.partial(factor_kernel, total_rows), out_shape=(j...  62 us
    ppermute x14, starting transfers between devices, exchange(): lax.ppermute(piece, 'rows', [(r, r ^ d) for r in range(rows)])  18.8 us
    all_to_all x1, blocking collectives, spread(): return lax.all_to_all(copies, axes, split_axis=0, concat_axis=0, tiled=True)  12.5 us
    ppermute x1, waiting for transfers between devices, run(): other = lax.ppermute(listed(lists, own, count), 'rows', swap)  10.7 us
    all_to_all x1, blocking collectives, local(): lax.all_to_all(pieces, 'rows', split_axis=0, concat_axis=0, tiled=True)  10.6 us
    ppermute x14, waiting for transfers between devices, exchange(): lax.ppermute(piece, 'rows', [(r, r ^ d) for r in range(rows)])  10.5 us
    all_to_all x1, starting transfers between devices, fetch(): lax.all_to_all(table, ('rows', 'cols'), split_axis=0, concat_axis=0, tile...  7.3 us
    all_to_all x1, waiting for transfers between devices, fetch(): lax.all_to_all(table, ('rows', 'cols'), split_axis=0, concat_axis=0, tile...  5.34 us
  transfers between devices with their start and end apart: 17, of which 13 were waited for; matrix products, arithmetic and copies ran while one was open for 0% of the time, Pallas kernels for 0%

profile of v12, /device:TPU:0, one launch (start us, length us, event | category | flops | bytes accessed | tf_op | source)
XLA Modules:
  0.0 155.0 jit_solution(15846705773309679997)
XLA Ops:
  1.3 1.3 table_copies.1
  2.6 7.3 %all-to-all-start = ((s32[32,1,128]{2,1,0:T(1,128)}), s32[32,1,128]{2,1,0:T(1,128)S(1)}, u32[]{:S(2)}, u32[]{:S(2)}) async-start(s32[32,1,128]{2,1,0:T(1,128)} %table_copies.1), calls=%async_computation | async-start | bytes 32768 | tf_op jit(solution)/shard_map/all_to_all | solution.py:437
  9.9 0.0 copy-start
  9.9 1.6 %copy-done = bf16[4096,256]{1,0:T(8,128)(2,1)S(1)} copy-done((bf16[4096,256]{1,0:T(8,128)(2,1)S(1)}, bf16[4096,256]{1,0:T(8,128)(2,1)}, u32[]{:S(2)}) %copy-start) | copy-done | bytes 2097176
  11.5 0.1 turn_stripes.1
  11.6 5.3 %all-to-all-done.table_ref = s32[32,1,128]{2,1,0:T(1,128)S(1)} async-done(((s32[32,1,128]{2,1,0:T(1,128)}), s32[32,1,128]{2,1,0:T(1,128)S(1)}, u32[]{:S(2)}, u32[]{:S(2)}) %all-to-all-start) | async-done | bytes 16416 | tf_op jit(solution)/shard_map/all_to_all | solution.py:437
  16.9 1.2 plan.1
  19.4 13.5 %conditional.2 = (bf16[128,32,256]{2,1,0:T(8,128)(2,1)S(1)}) conditional(s32[]{:T(128)} %bitcast.1, (s32[8,128]{1,0:T(8,128)S(1)}, bf16[8,16,32,256]{3,2,1,0:T(8,128)(2,1)S(1)}) %tuple.76, (s32[8,128]{1,0:T(8,128)S(1)}, bf16[8,16,32,256]{3,2,1,0:T(8,128)(2,1)S(1)}) %tuple.76, (s32[8,128]{1,0:T(8,128)S(1)}, ...), branch_computations={%region_0.0_spmd, %region_1.0_spmd, %region_2.0_spmd, %region_3.0_... | conditional | bytes 7340320 | solution.py:446
  19.5 0.6 cut_stripes.8
  20.1 0.7 collective-permute-start
  20.8 2.3 %collective-permute-start.1 = (bf16[5,32,256]{2,1,0:T(8,128)(2,1)S(1)}, bf16[5,32,256]{2,1,0:T(8,128)(2,1)S(1)}, u32[]{:S(2)}, u32[]{:S(2)}) collective-permute-start(bf16[5,32,256]{2,1,0:T(8,128)(2,1)S(1)} %get-tuple-element.132), channel_id=1, source_target_pairs={{0,12},{2,14},{4,8},{6,10},{8,4},{10,6},{12,0},{14,2},{16,28},{18,... | collective-permute-start | bytes 245768 | tf_op jit(solution)/shard_map/cond/branch_0_fun/ppermute | solution.py:420
  23.1 1.5 collective-permute-start.2
  24.6 0.6 collective-permute-start.3
  25.2 1.4 collective-permute-start.4
  26.6 0.9 collective-permute-done.refs_1_
  27.5 0.9 collective-permute-start.5
  28.5 0.0 collective-permute-done.1.refs_2_
  28.5 1.3 collective-permute-start.6
  29.7 0.2 collective-permute-done.2.refs_3_
  29.9 1.6 %collective-permute-done.3.refs_4_ = bf16[5,32,256]{2,1,0:T(8,128)(2,1)S(1)} collective-permute-done((bf16[5,32,256]{2,1,0:T(8,128)(2,1)S(1)}, bf16[5,32,256]{2,1,0:T(8,128)(2,1)S(1)}, u32[]{:S(2)}, u32[]{:S(2)}) %collective-permute-start.3) | collective-permute-done | bytes 81952 | tf_op jit(solution)/shard_map/cond/branch_0_fun/ppermute | solution.py:420
  31.5 0.0 collective-permute-done.4.refs_5_
  31.5 0.7 collective-permute-done.5.refs_6_
  32.2 0.7 collective-permute-done.6.refs_7_
  32.9 0.1 order_stripes.8
  33.0 0.0 copy-start.1
  33.0 0.0 copy-start.2
  33.0 13.9 %conditional.3 = ((bf16[8,32,256]{2,1,0:T(8,128)(2,1)S(1)}, bf16[8,32,256]{2,1,0:T(8,128)(2,1)S(1)}, bf16[8,32,256]{2,1,0:T(8,128)(2,1)}, bf16[8,32,256]{2,1,0:T...) conditional(s32[]{:T(128)} %bitcast, (s32[8,128]{1,0:T(8,128)S(1)}, ...), branch_computations={%region_8.0_spmd, %region_9.0_spmd, %region_10.0_spmd, %region_11.... | conditional | bytes 4194352 | solution.py:456
  33.1 0.6 listed_stripes.18
  33.7 0.7 collective-permute-start.59
  34.4 10.7 %collective-permute-done.59.other_ref = bf16[14,32,256]{2,1,0:T(8,128)(2,1)S(1)} collective-permute-done((bf16[14,32,256]{2,1,0:T(8,128)(2,1)S(1)}, bf16[14,32,256]{2,1,0:T(8,128)(2,1)S(1)}, u32[]{:S(2)}, u32[]{:S(2)}) %collective-permute-start.59) | collective-permute-done | bytes 229408 | tf_op jit(solution)/shard_map/cond/branch_3_fun/ppermute | solution.py:451
  45.0 1.8 %pick_stripes.18 = (bf16[8,32,256]{2,1,0:T(8,128)(2,1)S(1)}, bf16[8,32,256]{2,1,0:T(8,128)(2,1)S(1)}, bf16[8,32,256]{2,1,0:T(8,128)(2,1)}, bf16[8,32,256]{2,1,0:...) custom-call(s32[32,128]{1,0:T(8,128)S(1)} %get-tuple-element.220.pla, ...), custom_call_target="tpu_custom_call" | custom-call | tf_op jit(solution)/shard_map/cond/branch_3_fun/pick_stripes/pallas_call | solution.py:236
  46.9 0.0 collective-permute-start.71
  46.9 3.0 %collective-permute-start.72 = (bf16[8,32,256]{2,1,0:T(8,128)(2,1)}, bf16[8,32,256]{2,1,0:T(8,128)(2,1)S(1)}, u32[]{:S(2)}, u32[]{:S(2)}) collective-permute-start(bf16[8,32,256]{2,1,0:T(8,128)(2,1)} %get-tuple-element.278), channel_id=1, source_target_pairs={{0,12},{2,14},{4,8},{6,10},{8,4},{10,6},{12,0},{14,2},{16,28},{18,... | collective-permute-start | bytes 393224 | tf_op jit(solution)/shard_map/ppermute | solution.py:420
  49.9 0.9 collective-permute-start.73
  50.7 1.5 collective-permute-start.74
  52.2 1.8 %collective-permute-start.75 = (bf16[8,32,256]{2,1,0:T(8,128)(2,1)}, bf16[8,32,256]{2,1,0:T(8,128)(2,1)S(1)}, u32[]{:S(2)}, u32[]{:S(2)}) collective-permute-start(bf16[8,32,256]{2,1,0:T(8,128)(2,1)} %get-tuple-element.281), channel_id=1, source_target_pairs={{0,8},{2,10},{4,12},{6,14},{8,0},{10,2},{12,4},{14,6},{16,24},{18,... | collective-permute-start | bytes 393224 | tf_op jit(solution)/shard_map/ppermute | solution.py:420
  54.0 1.8 %collective-permute-done.71.refs_1_ = bf16[8,32,256]{2,1,0:T(8,128)(2,1)S(1)} collective-permute-done((bf16[8,32,256]{2,1,0:T(8,128)(2,1)S(1)}, bf16[8,32,256]{2,1,0:T(8,128)(2,1)S(1)}, u32[]{:S(2)}, u32[]{:S(2)}) %collective-permute-start.71) | collective-permute-done | bytes 131104 | tf_op jit(solution)/shard_map/ppermute | solution.py:420
  55.8 1.5 collective-permute-start.76
  57.3 0.0 collective-permute-done.72.refs_2_
  57.3 1.5 collective-permute-start.77
  58.8 1.9 %collective-permute-done.73.refs_3_ = bf16[8,32,256]{2,1,0:T(8,128)(2,1)S(1)} collective-permute-done((bf16[8,32,256]{2,1,0:T(8,128)(2,1)}, bf16[8,32,256]{2,1,0:T(8,128)(2,1)S(1)}, u32[]{:S(2)}, u32[]{:S(2)}) %collective-permute-start.73) | collective-permute-done | bytes 131104 | tf_op jit(solution)/shard_map/ppermute | solution.py:420
  60.7 0.0 collective-permute-done.74.refs_4_
  60.8 0.1 collective-permute-done.75.refs_5_
  60.8 1.1 collective-permute-done.76.refs_6_
  61.9 1.5 collective-permute-done.77.refs_7_
  63.5 0.0 copy-done.1
  63.5 0.0 copy-done.2
  63.5 2.2 %block_products.1.mine_ref = f32[1024,256]{1,0:T(8,128)S(1)} custom-call(s32[8]{0:T(128)S(1)} %copy-done.2, s32[1]{0:T(128)S(6)} %copy.135.counts_ref, bf16[8,256,256]{2,1,0:T(8,128)(2,1)S(1)} %copy-done.1, bf16[8,32,256]{2,1,0:T(8,128)(2,1)S(1)} %get-tuple-element.276.refs_0_, bf16[8,32,256]{2,1,0:T(8,128)(2,1)S(1)} %collective-permute-done.71.refs_1_, ...), custom_call_target="tpu_custom_call" | custom-call | tf_op jit(solution)/shard_map/block_products/pallas_call | solution.py:269
  65.7 0.1 collective-permute-start.78
  65.8 2.6 %collective-permute-done.78.other_ref = f32[1024,256]{1,0:T(8,128)S(1)} collective-permute-done((f32[1024,256]{1,0:T(8,128)S(1)}, f32[1024,256]{1,0:T(8,128)S(1)}, u32[]{:S(2)}, u32[]{:S(2)}) %collective-permute-start.78) | collective-permute-done | bytes 1048608 | tf_op jit(solution)/shard_map/ppermute | solution.py:470
  68.4 1.4 sum_and_gram.1
  69.9 10.6 %all_to_all.15 = f32[16,16,128]{2,1,0:T(8,128)S(1)} all-to-all(f32[16,16,128]{2,1,0:T(8,128)S(1)} %bitcast.7), channel_id=1, replica_groups=mesh['rows'=16,'cols'=2] {'rows'}, dimensions={0} | all-to-all | bytes 262144 | tf_op jit(solution)/shard_map/all_to_all | solution.py:473
  80.5 12.5 %all_to_all.16 = f32[32,16,128]{2,1,0:T(8,128)S(1)} all-to-all(f32[32,16,128]{2,1,0:T(8,128)S(1)} %broadcast_in_dim.2), channel_id=1, replica_groups=mesh['rows'=16,'cols'=2] {'rows','cols'}, dimensions={0} | all-to-all | bytes 524288 | tf_op jit(solution)/shard_map/all_to_all | solution.py:414
  93.0 62.0 %factor_and_basis.1 = (f32[512,256]{1,0:T(8,128)}, f32[256,256]{1,0:T(8,128)}) custom-call(f32[16,2,16,128]{3,2,1,0:T(8,128)S(1)} %bitcast.6, f32[512,256]{1,0:T(8,128)S(1)} %get-tuple-element.285.own_ref), custom_call_target="tpu_custom_call" | custom-call | tf_op jit(solution)/shard_map/factor_and_basis/pallas_call | solution.py:398
  (2 shorter events, 0.0 us)
Async XLA Ops:
  2.6 14.4 %all-to-all-start = ((s32[32,1,128]{2,1,0:T(1,128)}), s32[32,1,128]{2,1,0:T(1,128)S(1)}, u32[]{:S(2)}, u32[]{:S(2)}) async-start(s32[32,1,128]{2,1,0:T(1,128)} %table_copies.1), calls=%async_computation | async-start | bytes 32768 | tf_op jit(solution)/shard_map/all_to_all | solution.py:437
  9.9 1.6 %copy-start = (bf16[4096,256]{1,0:T(8,128)(2,1)S(1)}, bf16[4096,256]{1,0:T(8,128)(2,1)}, u32[]{:S(2)}) copy-start(bf16[4096,256]{1,0:T(8,128)(2,1)} %param.28) | copy-start | bytes 6291460
  20.1 7.4 %collective-permute-start = (bf16[5,32,256]{2,1,0:T(8,128)(2,1)S(1)}, bf16[5,32,256]{2,1,0:T(8,128)(2,1)S(1)}, u32[]{:S(2)}, u32[]{:S(2)}) collective-permute-start(bf16[5,32,256]{2,1,0:T(8,128)(2,1)S(1)} %get-tuple-element.128), channel_id=1, source_target_pairs={{0,14},{2,12},{4,10},{6,8},{8,6},{10,4},{12,2},{14,0},{16,30},{18,... | collective-permute-start | bytes 245768 | tf_op jit(solution)/shard_map/cond/branch_0_fun/ppermute | solution.py:420
  20.8 7.7 %collective-permute-start.1 = (bf16[5,32,256]{2,1,0:T(8,128)(2,1)S(1)}, bf16[5,32,256]{2,1,0:T(8,128)(2,1)S(1)}, u32[]{:S(2)}, u32[]{:S(2)}) collective-permute-start(bf16[5,32,256]{2,1,0:T(8,128)(2,1)S(1)} %get-tuple-element.132), channel_id=1, source_target_pairs={{0,12},{2,14},{4,8},{6,10},{8,4},{10,6},{12,0},{14,2},{16,28},{18,... | collective-permute-start | bytes 245768 | tf_op jit(solution)/shard_map/cond/branch_0_fun/ppermute | solution.py:420
  23.1 6.8 %collective-permute-start.2 = (bf16[5,32,256]{2,1,0:T(8,128)(2,1)S(1)}, bf16[5,32,256]{2,1,0:T(8,128)(2,1)S(1)}, u32[]{:S(2)}, u32[]{:S(2)}) collective-permute-start(bf16[5,32,256]{2,1,0:T(8,128)(2,1)S(1)} %get-tuple-element.133), channel_id=1, source_target_pairs={{0,10},{2,8},{4,14},{6,12},{8,2},{10,0},{12,6},{14,4},{16,26},{18,... | collective-permute-start | bytes 245768 | tf_op jit(solution)/shard_map/cond/branch_0_fun/ppermute | solution.py:420
  24.6 6.9 %collective-permute-start.3 = (bf16[5,32,256]{2,1,0:T(8,128)(2,1)S(1)}, bf16[5,32,256]{2,1,0:T(8,128)(2,1)S(1)}, u32[]{:S(2)}, u32[]{:S(2)}) collective-permute-start(bf16[5,32,256]{2,1,0:T(8,128)(2,1)S(1)} %get-tuple-element.134), channel_id=1, source_target_pairs={{0,6},{2,4},{4,2},{6,0},{8,14},{10,12},{12,10},{14,8},{16,22},{18,... | collective-permute-start | bytes 245768 | tf_op jit(solution)/shard_map/cond/branch_0_fun/ppermute | solution.py:420
  25.2 6.3 %collective-permute-start.4 = (bf16[5,32,256]{2,1,0:T(8,128)(2,1)S(1)}, bf16[5,32,256]{2,1,0:T(8,128)(2,1)S(1)}, u32[]{:S(2)}, u32[]{:S(2)}) collective-permute-start(bf16[5,32,256]{2,1,0:T(8,128)(2,1)S(1)} %get-tuple-element.138), channel_id=1, source_target_pairs={{0,8},{2,10},{4,12},{6,14},{8,0},{10,2},{12,4},{14,6},{16,24},{18,... | collective-permute-start | bytes 245768 | tf_op jit(solution)/shard_map/cond/branch_0_fun/ppermute | solution.py:420
  27.5 4.6 %collective-permute-start.5 = (bf16[5,32,256]{2,1,0:T(8,128)(2,1)S(1)}, bf16[5,32,256]{2,1,0:T(8,128)(2,1)S(1)}, u32[]{:S(2)}, u32[]{:S(2)}) collective-permute-start(bf16[5,32,256]{2,1,0:T(8,128)(2,1)S(1)} %get-tuple-element.139), channel_id=1, source_target_pairs={{0,4},{2,6},{4,0},{6,2},{8,12},{10,14},{12,8},{14,10},{16,20},{18,... | collective-permute-start | bytes 245768 | tf_op jit(solution)/shard_map/cond/branch_0_fun/ppermute | solution.py:420
  28.5 4.4 %collective-permute-start.6 = (bf16[5,32,256]{2,1,0:T(8,128)(2,1)S(1)}, bf16[5,32,256]{2,1,0:T(8,128)(2,1)S(1)}, u32[]{:S(2)}, u32[]{:S(2)}) collective-permute-start(bf16[5,32,256]{2,1,0:T(8,128)(2,1)S(1)} %get-tuple-element.140), channel_id=1, source_target_pairs={{0,2},{2,0},{4,6},{6,4},{8,10},{10,8},{12,14},{14,12},{16,18},{18,... | collective-permute-start | bytes 245768 | tf_op jit(solution)/shard_map/cond/branch_0_fun/ppermute | solution.py:420
  33.0 30.5 %copy-start.1 = (bf16[8,256,256]{2,1,0:T(8,128)(2,1)S(1)}, bf16[8,256,256]{2,1,0:T(8,128)(2,1)}, u32[]{:S(2)}) copy-start(bf16[8,256,256]{2,1,0:T(8,128)(2,1)} %blocks_ref.1) | copy-start | bytes 3145732
  33.0 30.5 %copy-start.2 = (s32[8]{0:T(128)S(1)}, s32[8]{0:T(128)}, u32[]{:S(2)}) copy-start(s32[8]{0:T(128)} %rows_ref.1) | copy-start | bytes 100
  33.7 11.4 %collective-permute-start.59 = (bf16[14,32,256]{2,1,0:T(8,128)(2,1)S(1)}, bf16[14,32,256]{2,1,0:T(8,128)(2,1)S(1)}, u32[]{:S(2)}, u32[]{:S(2)}) collective-permute-start(bf16[14,32,256]{2,1,0:T(8,128)(2,1)S(1)} %listed_stripes.18), channel_id=1, source_target_pairs={{0,16},{2,18},{4,20},{6,22},{8,24},{10,26},{12,28},{14,30},{16,0},... | collective-permute-start | bytes 688136 | tf_op jit(solution)/shard_map/cond/branch_3_fun/ppermute | solution.py:451
  46.9 8.9 %collective-permute-start.71 = (bf16[8,32,256]{2,1,0:T(8,128)(2,1)S(1)}, bf16[8,32,256]{2,1,0:T(8,128)(2,1)S(1)}, u32[]{:S(2)}, u32[]{:S(2)}) collective-permute-start(bf16[8,32,256]{2,1,0:T(8,128)(2,1)S(1)} %get-tuple-element.277), channel_id=1, source_target_pairs={{0,14},{2,12},{4,10},{6,8},{8,6},{10,4},{12,2},{14,0},{16,30},{18,... | collective-permute-start | bytes 393224 | tf_op jit(solution)/shard_map/ppermute | solution.py:420
  46.9 10.4 %collective-permute-start.72 = (bf16[8,32,256]{2,1,0:T(8,128)(2,1)}, bf16[8,32,256]{2,1,0:T(8,128)(2,1)S(1)}, u32[]{:S(2)}, u32[]{:S(2)}) collective-permute-start(bf16[8,32,256]{2,1,0:T(8,128)(2,1)} %get-tuple-element.278), channel_id=1, source_target_pairs={{0,12},{2,14},{4,8},{6,10},{8,4},{10,6},{12,0},{14,2},{16,28},{18,... | collective-permute-start | bytes 393224 | tf_op jit(solution)/shard_map/ppermute | solution.py:420
  49.9 10.9 %collective-permute-start.73 = (bf16[8,32,256]{2,1,0:T(8,128)(2,1)}, bf16[8,32,256]{2,1,0:T(8,128)(2,1)S(1)}, u32[]{:S(2)}, u32[]{:S(2)}) collective-permute-start(bf16[8,32,256]{2,1,0:T(8,128)(2,1)} %get-tuple-element.279), channel_id=1, source_target_pairs={{0,10},{2,8},{4,14},{6,12},{8,2},{10,0},{12,6},{14,4},{16,26},{18,... | collective-permute-start | bytes 393224 | tf_op jit(solution)/shard_map/ppermute | solution.py:420
  50.7 10.0 %collective-permute-start.74 = (bf16[8,32,256]{2,1,0:T(8,128)(2,1)}, bf16[8,32,256]{2,1,0:T(8,128)(2,1)S(1)}, u32[]{:S(2)}, u32[]{:S(2)}) collective-permute-start(bf16[8,32,256]{2,1,0:T(8,128)(2,1)} %get-tuple-element.280), channel_id=1, source_target_pairs={{0,6},{2,4},{4,2},{6,0},{8,14},{10,12},{12,10},{14,8},{16,22},{18,... | collective-permute-start | bytes 393224 | tf_op jit(solution)/shard_map/ppermute | solution.py:420
  52.2 8.7 %collective-permute-start.75 = (bf16[8,32,256]{2,1,0:T(8,128)(2,1)}, bf16[8,32,256]{2,1,0:T(8,128)(2,1)S(1)}, u32[]{:S(2)}, u32[]{:S(2)}) collective-permute-start(bf16[8,32,256]{2,1,0:T(8,128)(2,1)} %get-tuple-element.281), channel_id=1, source_target_pairs={{0,8},{2,10},{4,12},{6,14},{8,0},{10,2},{12,4},{14,6},{16,24},{18,... | collective-permute-start | bytes 393224 | tf_op jit(solution)/shard_map/ppermute | solution.py:420
  55.8 6.1 %collective-permute-start.76 = (bf16[8,32,256]{2,1,0:T(8,128)(2,1)}, bf16[8,32,256]{2,1,0:T(8,128)(2,1)S(1)}, u32[]{:S(2)}, u32[]{:S(2)}) collective-permute-start(bf16[8,32,256]{2,1,0:T(8,128)(2,1)} %get-tuple-element.282), channel_id=1, source_target_pairs={{0,4},{2,6},{4,0},{6,2},{8,12},{10,14},{12,8},{14,10},{16,20},{18,... | collective-permute-start | bytes 393224 | tf_op jit(solution)/shard_map/ppermute | solution.py:420
  57.3 6.2 %collective-permute-start.77 = (bf16[8,32,256]{2,1,0:T(8,128)(2,1)}, bf16[8,32,256]{2,1,0:T(8,128)(2,1)S(1)}, u32[]{:S(2)}, u32[]{:S(2)}) collective-permute-start(bf16[8,32,256]{2,1,0:T(8,128)(2,1)} %get-tuple-element.283), channel_id=1, source_target_pairs={{0,2},{2,0},{4,6},{6,4},{8,10},{10,8},{12,14},{14,12},{16,18},{18,... | collective-permute-start | bytes 393224 | tf_op jit(solution)/shard_map/ppermute | solution.py:420
  65.7 2.7 %collective-permute-start.78 = (f32[1024,256]{1,0:T(8,128)S(1)}, f32[1024,256]{1,0:T(8,128)S(1)}, u32[]{:S(2)}, u32[]{:S(2)}) collective-permute-start(f32[1024,256]{1,0:T(8,128)S(1)} %block_products.1.mine_ref), channel_id=1, source_target_pairs={{0,1},{1,0},{2,3},{3,2},{4,5},{5,4},{6,7},{7,6},{8,9},{9,8},{10,11... | collective-permute-start | bytes 3145736 | tf_op jit(solution)/shard_map/ppermute | solution.py:470

commit v13 on v12

--- a/solution.py
+++ b/solution.py
@@ -98,6 +98,7 @@
     here = (ids & -per) - half * part + row(near_rank, c).astype(jnp.int32)
     there = part + row(far_rank, lines * (1 + half) + c).astype(jnp.int32)
     place = jnp.where(over(ids, part) == half, here, there)
+    chosen = jnp.zeros(places_ref.shape, jnp.float32)
     for group in groups:
         table, _, asked = read(group)
         lane = lax.broadcasted_iota(jnp.int32, table.shape, 1)
@@ -105,7 +106,19 @@
         for s in range(slots):
             found = jnp.sum(jnp.where(asked[s], place, 0), axis=1, keepdims=True)
             places = jnp.where(lane == s, found, places)
-        places_ref[group.start : group.stop] = places
+        shape = (places_ref.shape[0], len(group))
+        number = lax.broadcasted_iota(jnp.int32, shape, 0)
+        device = lax.broadcasted_iota(jnp.int32, shape, 1) + group.start
+        reads = functools.reduce(
+            jnp.logical_or,
+            [(number == i) & (device == (me ^ d) * cols + c) for i, d in enumerate(distances(shape[0]))],
+        )
+        chosen += jnp.dot(
+            jnp.where(reads, 1.0, 0.0).astype(jnp.bfloat16),
+            places.astype(jnp.float32).astype(jnp.bfloat16),
+            preferred_element_type=jnp.float32,
+        )
+    places_ref[...] = chosen.astype(jnp.int32)
     line = lax.broadcasted_iota(jnp.int32, (panel, 3 * lines), 1)
 
     def column(values, number):
@@ -129,7 +142,7 @@
     return pl.pallas_call(
         functools.partial(plan_kernel, slots, per, within, across),
         out_shape=(
-            jax.ShapeDtypeStruct((devices, 128), jnp.int32),
+            jax.ShapeDtypeStruct((lax.axis_size("rows") // 2, 128), jnp.int32),
             jax.ShapeDtypeStruct((8, 128), jnp.int32),
             jax.ShapeDtypeStruct((1,), jnp.int32),
             jax.ShapeDtypeStruct((1,), jnp.int32),
@@ -225,10 +238,9 @@
     here = own_ref.shape[0]
     whole[:here] = own_ref[...]
     whole[here:] = other_ref[...]
-    for d, out_ref in zip(distances(len(out_refs)), out_refs):
-        device = (lax.axis_index("rows") ^ d) * lax.axis_size("cols") + lax.axis_index("cols")
+    for i, out_ref in enumerate(out_refs):
         for s in range(out_ref.shape[0]):
-            out_ref[s] = whole[jnp.minimum(places_ref[device, s], whole.shape[0] - 1)]
+            out_ref[s] = whole[jnp.minimum(places_ref[i, s], whole.shape[0] - 1)]
 
 
 def pick(places, own, other, slots, members):

time: 158 us -> 157 us (level); the launches traced: 155 us -> 158 us
  waiting for transfers between devices: 29.2 us -> 33.5 us
    ppermute x14, waiting for transfers between devices: 10.5 us -> 15.8 us  [exchange(): lax.ppermute(piece, 'rows', [(r, r ^ d) for r in range(rows)])]
  transfers between devices with their start and end apart: 17 -> 17, of which waited for: 13 -> 15; matrix products, arithmetic and copies ran while one was open for 0% -> 0% of each run, Pallas kernels for 0% -> 0%
where the time goes in v13:
time: 157 us; the launch traced here: 158 us
  Pallas kernels  70.4 us (45%)
  waiting for transfers between devices  33.5 us (21%)
  starting transfers between devices  25.7 us (16%)
  blocking collectives  23.5 us (15%)
  between operations  2.67 us (2%)
  local copies, waits for them, and re-layouts  1.62 us (1%)
    pallas_call x1, Pallas kernels, factor_and_basis(): pl.pallas_call(functools.partial(factor_kernel, total_rows), out_shape=(j...  61.8 us
    ppermute x14, starting transfers between devices, exchange(): lax.ppermute(piece, 'rows', [(r, r ^ d) for r in range(rows)])  17.8 us
    ppermute x14, waiting for transfers between devices, exchange(): lax.ppermute(piece, 'rows', [(r, r ^ d) for r in range(rows)])  15.8 us
    all_to_all x1, blocking collectives, spread(): return lax.all_to_all(copies, axes, split_axis=0, concat_axis=0, tiled=True)  12.5 us
    all_to_all x1, blocking collectives, local(): lax.all_to_all(pieces, 'rows', split_axis=0, concat_axis=0, tiled=True)  11 us
    ppermute x1, waiting for transfers between devices, run(): other = lax.ppermute(listed(lists, own, count), 'rows', swap)  9.73 us
    all_to_all x1, starting transfers between devices, fetch(): lax.all_to_all(table, ('rows', 'cols'), split_axis=0, concat_axis=0, tile...  7.3 us
    all_to_all x1, waiting for transfers between devices, fetch(): lax.all_to_all(table, ('rows', 'cols'), split_axis=0, concat_axis=0, tile...  5.34 us
  transfers between devices with their start and end apart: 17, of which 15 were waited for; matrix products, arithmetic and copies ran while one was open for 0% of the time, Pallas kernels for 0%

profile of v13, /device:TPU:0, one launch (start us, length us, event | category | flops | bytes accessed | tf_op | source)
XLA Modules:
  0.0 157.6 jit_solution(2601679661138497543)
XLA Ops:
  1.3 1.3 table_copies.1
  2.6 7.3 %all-to-all-start = ((s32[32,1,128]{2,1,0:T(1,128)}), s32[32,1,128]{2,1,0:T(1,128)S(1)}, u32[]{:S(2)}, u32[]{:S(2)}) async-start(s32[32,1,128]{2,1,0:T(1,128)} %table_copies.1), calls=%async_computation | async-start | bytes 32768 | tf_op jit(solution)/shard_map/all_to_all | solution.py:449
  9.9 0.0 copy-start
  9.9 1.6 %copy-done = bf16[4096,256]{1,0:T(8,128)(2,1)S(1)} copy-done((bf16[4096,256]{1,0:T(8,128)(2,1)S(1)}, bf16[4096,256]{1,0:T(8,128)(2,1)}, u32[]{:S(2)}) %copy-start) | copy-done | bytes 2097176
  11.5 0.1 turn_stripes.1
  11.6 5.3 %all-to-all-done.table_ref = s32[32,1,128]{2,1,0:T(1,128)S(1)} async-done(((s32[32,1,128]{2,1,0:T(1,128)}), s32[32,1,128]{2,1,0:T(1,128)S(1)}, u32[]{:S(2)}, u32[]{:S(2)}) %all-to-all-start) | async-done | bytes 16416 | tf_op jit(solution)/shard_map/all_to_all | solution.py:449
  16.9 1.3 plan.1
  19.5 17.2 %conditional.2 = (bf16[128,32,256]{2,1,0:T(8,128)(2,1)S(1)}) conditional(s32[]{:T(128)} %bitcast.1, (s32[8,128]{1,0:T(8,128)S(1)}, bf16[8,16,32,256]{3,2,1,0:T(8,128)(2,1)S(1)}) %tuple.76, (s32[8,128]{1,0:T(8,128)S(1)}, bf16[8,16,32,256]{3,2,1,0:T(8,128)(2,1)S(1)}) %tuple.76, (s32[8,128]{1,0:T(8,128)S(1)}, ...), branch_computations={%region_0.0_spmd, %region_1.0_spmd, %region_2.0_spmd, %region_3.0_... | conditional | bytes 7340320 | solution.py:458
  19.6 0.7 cut_stripes.11
  20.2 0.7 collective-permute-start.21
  20.9 2.3 %collective-permute-start.22 = (bf16[8,32,256]{2,1,0:T(8,128)(2,1)S(1)}, bf16[8,32,256]{2,1,0:T(8,128)(2,1)S(1)}, u32[]{:S(2)}, u32[]{:S(2)}) collective-permute-start(bf16[8,32,256]{2,1,0:T(8,128)(2,1)S(1)} %get-tuple-element.165), channel_id=1, source_target_pairs={{0,12},{2,14},{4,8},{6,10},{8,4},{10,6},{12,0},{14,2},{16,28},{18,... | collective-permute-start | bytes 393224 | tf_op jit(solution)/shard_map/cond/branch_3_fun/ppermute | solution.py:432
  23.2 1.5 collective-permute-start.23
  24.7 0.6 collective-permute-start.24
  25.3 1.4 collective-permute-start.25
  26.8 2.9 %collective-permute-done.21.refs_1_ = bf16[8,32,256]{2,1,0:T(8,128)(2,1)S(1)} collective-permute-done((bf16[8,32,256]{2,1,0:T(8,128)(2,1)S(1)}, bf16[8,32,256]{2,1,0:T(8,128)(2,1)S(1)}, u32[]{:S(2)}, u32[]{:S(2)}) %collective-permute-start.21) | collective-permute-done | bytes 131104 | tf_op jit(solution)/shard_map/cond/branch_3_fun/ppermute | solution.py:432
  29.7 0.5 collective-permute-start.26
  30.2 1.5 collective-permute-done.22.refs_2_
  31.6 1.3 collective-permute-start.27
  33.0 0.3 collective-permute-done.23.refs_3_
  33.3 1.7 %collective-permute-done.24.refs_4_ = bf16[8,32,256]{2,1,0:T(8,128)(2,1)S(1)} collective-permute-done((bf16[8,32,256]{2,1,0:T(8,128)(2,1)S(1)}, bf16[8,32,256]{2,1,0:T(8,128)(2,1)S(1)}, u32[]{:S(2)}, u32[]{:S(2)}) %collective-permute-start.24) | collective-permute-done | bytes 131104 | tf_op jit(solution)/shard_map/cond/branch_3_fun/ppermute | solution.py:432
  35.0 0.0 collective-permute-done.25.refs_5_
  35.0 0.8 collective-permute-done.26.refs_6_
  35.8 0.8 collective-permute-done.27.refs_7_
  36.6 0.1 order_stripes.11
  36.7 0.0 copy-start.1
  36.7 0.0 copy-start.2
  36.7 12.5 %conditional.3 = ((bf16[8,32,256]{2,1,0:T(8,128)(2,1)S(1)}, bf16[8,32,256]{2,1,0:T(8,128)(2,1)S(1)}, bf16[8,32,256]{2,1,0:T(8,128)(2,1)S(1)}, bf16[8,32,256]{2,1...) conditional(s32[]{:T(128)} %bitcast, (s32[8,128]{1,0:T(8,128)S(1)}, ...), branch_computations={%region_8.0_spmd, %region_9.0_spmd, %region_10.0_spmd, %region_11.... | conditional | bytes 4194352 | solution.py:468
  36.8 0.6 listed_stripes.16
  37.4 0.5 collective-permute-start.57
  37.9 9.7 %collective-permute-done.57.other_ref = bf16[12,32,256]{2,1,0:T(8,128)(2,1)S(1)} collective-permute-done((bf16[12,32,256]{2,1,0:T(8,128)(2,1)S(1)}, bf16[12,32,256]{2,1,0:T(8,128)(2,1)S(1)}, u32[]{:S(2)}, u32[]{:S(2)}) %collective-permute-start.57) | collective-permute-done | bytes 196640 | tf_op jit(solution)/shard_map/cond/branch_1_fun/ppermute | solution.py:463
  47.7 1.6 %pick_stripes.16 = (bf16[8,32,256]{2,1,0:T(8,128)(2,1)S(1)}, bf16[8,32,256]{2,1,0:T(8,128)(2,1)S(1)}, bf16[8,32,256]{2,1,0:T(8,128)(2,1)S(1)}, bf16[8,32,256]{2,...) custom-call(s32[8,128]{1,0:T(8,128)S(1)} %get-tuple-element.214.plac, ...), custom_call_target="tpu_custom_call" | custom-call | tf_op jit(solution)/shard_map/cond/branch_1_fun/pick_stripes/pallas_call | solution.py:248
  49.2 0.0 collective-permute-start.71
  49.2 3.8 %collective-permute-start.72 = (bf16[8,32,256]{2,1,0:T(8,128)(2,1)S(1)}, bf16[8,32,256]{2,1,0:T(8,128)(2,1)S(1)}, u32[]{:S(2)}, u32[]{:S(2)}) collective-permute-start(bf16[8,32,256]{2,1,0:T(8,128)(2,1)S(1)} %get-tuple-element.278), channel_id=1, source_target_pairs={{0,12},{2,14},{4,8},{6,10},{8,4},{10,6},{12,0},{14,2},{16,28},{18,... | collective-permute-start | bytes 393224 | tf_op jit(solution)/shard_map/ppermute | solution.py:432
  53.0 0.0 collective-permute-start.73
  53.0 1.5 collective-permute-start.74
  54.5 2.1 %collective-permute-start.75 = (bf16[8,32,256]{2,1,0:T(8,128)(2,1)}, bf16[8,32,256]{2,1,0:T(8,128)(2,1)S(1)}, u32[]{:S(2)}, u32[]{:S(2)}) collective-permute-start(bf16[8,32,256]{2,1,0:T(8,128)(2,1)} %get-tuple-element.281), channel_id=1, source_target_pairs={{0,8},{2,10},{4,12},{6,14},{8,0},{10,2},{12,4},{14,6},{16,24},{18,... | collective-permute-start | bytes 393224 | tf_op jit(solution)/shard_map/ppermute | solution.py:432
  56.6 1.5 collective-permute-done.71.refs_1_
  58.1 1.5 collective-permute-start.76
  59.6 1.7 %collective-permute-done.72.refs_2_ = bf16[8,32,256]{2,1,0:T(8,128)(2,1)S(1)} collective-permute-done((bf16[8,32,256]{2,1,0:T(8,128)(2,1)S(1)}, bf16[8,32,256]{2,1,0:T(8,128)(2,1)S(1)}, u32[]{:S(2)}, u32[]{:S(2)}) %collective-permute-start.72) | collective-permute-done | bytes 131104 | tf_op jit(solution)/shard_map/ppermute | solution.py:432
  61.3 0.6 collective-permute-start.77
  61.9 1.4 collective-permute-done.73.refs_3_
  63.3 0.0 collective-permute-done.74.refs_4_
  63.3 0.3 collective-permute-done.75.refs_5_
  63.7 1.1 collective-permute-done.76.refs_6_
  64.8 1.8 %collective-permute-done.77.refs_7_ = bf16[8,32,256]{2,1,0:T(8,128)(2,1)S(1)} collective-permute-done((bf16[8,32,256]{2,1,0:T(8,128)(2,1)}, bf16[8,32,256]{2,1,0:T(8,128)(2,1)S(1)}, u32[]{:S(2)}, u32[]{:S(2)}) %collective-permute-start.77) | collective-permute-done | bytes 131104 | tf_op jit(solution)/shard_map/ppermute | solution.py:432
  66.5 0.0 copy-done.1
  66.5 0.0 copy-done.2
  66.5 1.5 block_products.1.mine_ref
  68.0 0.1 collective-permute-start.78
  68.1 2.6 %collective-permute-done.78.other_ref = f32[1024,256]{1,0:T(8,128)S(1)} collective-permute-done((f32[1024,256]{1,0:T(8,128)S(1)}, f32[1024,256]{1,0:T(8,128)S(1)}, u32[]{:S(2)}, u32[]{:S(2)}) %collective-permute-start.78) | collective-permute-done | bytes 1048608 | tf_op jit(solution)/shard_map/ppermute | solution.py:482
  70.7 1.5 sum_and_gram.1
  72.2 11.0 %all_to_all.15 = f32[16,16,128]{2,1,0:T(8,128)S(1)} all-to-all(f32[16,16,128]{2,1,0:T(8,128)S(1)} %bitcast.7), channel_id=1, replica_groups=mesh['rows'=16,'cols'=2] {'rows'}, dimensions={0} | all-to-all | bytes 262144 | tf_op jit(solution)/shard_map/all_to_all | solution.py:485
  83.3 12.5 %all_to_all.16 = f32[32,16,128]{2,1,0:T(8,128)S(1)} all-to-all(f32[32,16,128]{2,1,0:T(8,128)S(1)} %broadcast_in_dim.2), channel_id=1, replica_groups=mesh['rows'=16,'cols'=2] {'rows','cols'}, dimensions={0} | all-to-all | bytes 524288 | tf_op jit(solution)/shard_map/all_to_all | solution.py:426
  95.8 61.8 %factor_and_basis.1 = (f32[512,256]{1,0:T(8,128)}, f32[256,256]{1,0:T(8,128)}) custom-call(f32[16,2,16,128]{3,2,1,0:T(8,128)S(1)} %bitcast.6, f32[512,256]{1,0:T(8,128)S(1)} %get-tuple-element.285.own_ref), custom_call_target="tpu_custom_call" | custom-call | tf_op jit(solution)/shard_map/factor_and_basis/pallas_call | solution.py:410
  (2 shorter events, 0.0 us)
Async XLA Ops:
  2.6 14.4 %all-to-all-start = ((s32[32,1,128]{2,1,0:T(1,128)}), s32[32,1,128]{2,1,0:T(1,128)S(1)}, u32[]{:S(2)}, u32[]{:S(2)}) async-start(s32[32,1,128]{2,1,0:T(1,128)} %table_copies.1), calls=%async_computation | async-start | bytes 32768 | tf_op jit(solution)/shard_map/all_to_all | solution.py:449
  9.9 1.6 %copy-start = (bf16[4096,256]{1,0:T(8,128)(2,1)S(1)}, bf16[4096,256]{1,0:T(8,128)(2,1)}, u32[]{:S(2)}) copy-start(bf16[4096,256]{1,0:T(8,128)(2,1)} %param.28) | copy-start | bytes 6291460
  20.2 9.4 %collective-permute-start.21 = (bf16[8,32,256]{2,1,0:T(8,128)(2,1)S(1)}, bf16[8,32,256]{2,1,0:T(8,128)(2,1)S(1)}, u32[]{:S(2)}, u32[]{:S(2)}) collective-permute-start(bf16[8,32,256]{2,1,0:T(8,128)(2,1)S(1)} %get-tuple-element.164), channel_id=1, source_target_pairs={{0,14},{2,12},{4,10},{6,8},{8,6},{10,4},{12,2},{14,0},{16,30},{18,... | collective-permute-start | bytes 393224 | tf_op jit(solution)/shard_map/cond/branch_3_fun/ppermute | solution.py:432
  20.9 10.7 %collective-permute-start.22 = (bf16[8,32,256]{2,1,0:T(8,128)(2,1)S(1)}, bf16[8,32,256]{2,1,0:T(8,128)(2,1)S(1)}, u32[]{:S(2)}, u32[]{:S(2)}) collective-permute-start(bf16[8,32,256]{2,1,0:T(8,128)(2,1)S(1)} %get-tuple-element.165), channel_id=1, source_target_pairs={{0,12},{2,14},{4,8},{6,10},{8,4},{10,6},{12,0},{14,2},{16,28},{18,... | collective-permute-start | bytes 393224 | tf_op jit(solution)/shard_map/cond/branch_3_fun/ppermute | solution.py:432
  23.2 10.1 %collective-permute-start.23 = (bf16[8,32,256]{2,1,0:T(8,128)(2,1)S(1)}, bf16[8,32,256]{2,1,0:T(8,128)(2,1)S(1)}, u32[]{:S(2)}, u32[]{:S(2)}) collective-permute-start(bf16[8,32,256]{2,1,0:T(8,128)(2,1)S(1)} %get-tuple-element.166), channel_id=1, source_target_pairs={{0,10},{2,8},{4,14},{6,12},{8,2},{10,0},{12,6},{14,4},{16,26},{18,... | collective-permute-start | bytes 393224 | tf_op jit(solution)/shard_map/cond/branch_3_fun/ppermute | solution.py:432
  24.7 10.3 %collective-permute-start.24 = (bf16[8,32,256]{2,1,0:T(8,128)(2,1)S(1)}, bf16[8,32,256]{2,1,0:T(8,128)(2,1)S(1)}, u32[]{:S(2)}, u32[]{:S(2)}) collective-permute-start(bf16[8,32,256]{2,1,0:T(8,128)(2,1)S(1)} %get-tuple-element.167), channel_id=1, source_target_pairs={{0,6},{2,4},{4,2},{6,0},{8,14},{10,12},{12,10},{14,8},{16,22},{18,... | collective-permute-start | bytes 393224 | tf_op jit(solution)/shard_map/cond/branch_3_fun/ppermute | solution.py:432
  25.3 9.7 %collective-permute-start.25 = (bf16[8,32,256]{2,1,0:T(8,128)(2,1)S(1)}, bf16[8,32,256]{2,1,0:T(8,128)(2,1)S(1)}, u32[]{:S(2)}, u32[]{:S(2)}) collective-permute-start(bf16[8,32,256]{2,1,0:T(8,128)(2,1)S(1)} %get-tuple-element.168), channel_id=1, source_target_pairs={{0,8},{2,10},{4,12},{6,14},{8,0},{10,2},{12,4},{14,6},{16,24},{18,... | collective-permute-start | bytes 393224 | tf_op jit(solution)/shard_map/cond/branch_3_fun/ppermute | solution.py:432
  29.7 6.1 %collective-permute-start.26 = (bf16[8,32,256]{2,1,0:T(8,128)(2,1)S(1)}, bf16[8,32,256]{2,1,0:T(8,128)(2,1)S(1)}, u32[]{:S(2)}, u32[]{:S(2)}) collective-permute-start(bf16[8,32,256]{2,1,0:T(8,128)(2,1)S(1)} %get-tuple-element.169), channel_id=1, source_target_pairs={{0,4},{2,6},{4,0},{6,2},{8,12},{10,14},{12,8},{14,10},{16,20},{18,... | collective-permute-start | bytes 393224 | tf_op jit(solution)/shard_map/cond/branch_3_fun/ppermute | solution.py:432
  31.6 5.0 %collective-permute-start.27 = (bf16[8,32,256]{2,1,0:T(8,128)(2,1)S(1)}, bf16[8,32,256]{2,1,0:T(8,128)(2,1)S(1)}, u32[]{:S(2)}, u32[]{:S(2)}) collective-permute-start(bf16[8,32,256]{2,1,0:T(8,128)(2,1)S(1)} %get-tuple-element.170), channel_id=1, source_target_pairs={{0,2},{2,0},{4,6},{6,4},{8,10},{10,8},{12,14},{14,12},{16,18},{18,... | collective-permute-start | bytes 393224 | tf_op jit(solution)/shard_map/cond/branch_3_fun/ppermute | solution.py:432
  36.7 29.8 %copy-start.1 = (bf16[8,256,256]{2,1,0:T(8,128)(2,1)S(1)}, bf16[8,256,256]{2,1,0:T(8,128)(2,1)}, u32[]{:S(2)}) copy-start(bf16[8,256,256]{2,1,0:T(8,128)(2,1)} %blocks_ref.1) | copy-start | bytes 3145732
  36.7 29.8 %copy-start.2 = (s32[8]{0:T(128)S(1)}, s32[8]{0:T(128)}, u32[]{:S(2)}) copy-start(s32[8]{0:T(128)} %rows_ref.1) | copy-start | bytes 100
  37.4 10.3 %collective-permute-start.57 = (bf16[12,32,256]{2,1,0:T(8,128)(2,1)S(1)}, bf16[12,32,256]{2,1,0:T(8,128)(2,1)S(1)}, u32[]{:S(2)}, u32[]{:S(2)}) collective-permute-start(bf16[12,32,256]{2,1,0:T(8,128)(2,1)S(1)} %listed_stripes.16), channel_id=1, source_target_pairs={{0,16},{2,18},{4,20},{6,22},{8,24},{10,26},{12,28},{14,30},{16,0},... | collective-permute-start | bytes 589832 | tf_op jit(solution)/shard_map/cond/branch_1_fun/ppermute | solution.py:463
  49.2 8.9 %collective-permute-start.71 = (bf16[8,32,256]{2,1,0:T(8,128)(2,1)S(1)}, bf16[8,32,256]{2,1,0:T(8,128)(2,1)S(1)}, u32[]{:S(2)}, u32[]{:S(2)}) collective-permute-start(bf16[8,32,256]{2,1,0:T(8,128)(2,1)S(1)} %get-tuple-element.277), channel_id=1, source_target_pairs={{0,14},{2,12},{4,10},{6,8},{8,6},{10,4},{12,2},{14,0},{16,30},{18,... | collective-permute-start | bytes 393224 | tf_op jit(solution)/shard_map/ppermute | solution.py:432
  49.2 12.1 %collective-permute-start.72 = (bf16[8,32,256]{2,1,0:T(8,128)(2,1)S(1)}, bf16[8,32,256]{2,1,0:T(8,128)(2,1)S(1)}, u32[]{:S(2)}, u32[]{:S(2)}) collective-permute-start(bf16[8,32,256]{2,1,0:T(8,128)(2,1)S(1)} %get-tuple-element.278), channel_id=1, source_target_pairs={{0,12},{2,14},{4,8},{6,10},{8,4},{10,6},{12,0},{14,2},{16,28},{18,... | collective-permute-start | bytes 393224 | tf_op jit(solution)/shard_map/ppermute | solution.py:432
  53.0 10.3 %collective-permute-start.73 = (bf16[8,32,256]{2,1,0:T(8,128)(2,1)}, bf16[8,32,256]{2,1,0:T(8,128)(2,1)S(1)}, u32[]{:S(2)}, u32[]{:S(2)}) collective-permute-start(bf16[8,32,256]{2,1,0:T(8,128)(2,1)} %get-tuple-element.279), channel_id=1, source_target_pairs={{0,10},{2,8},{4,14},{6,12},{8,2},{10,0},{12,6},{14,4},{16,26},{18,... | collective-permute-start | bytes 393224 | tf_op jit(solution)/shard_map/ppermute | solution.py:432
  53.0 10.3 %collective-permute-start.74 = (bf16[8,32,256]{2,1,0:T(8,128)(2,1)}, bf16[8,32,256]{2,1,0:T(8,128)(2,1)S(1)}, u32[]{:S(2)}, u32[]{:S(2)}) collective-permute-start(bf16[8,32,256]{2,1,0:T(8,128)(2,1)} %get-tuple-element.280), channel_id=1, source_target_pairs={{0,6},{2,4},{4,2},{6,0},{8,14},{10,12},{12,10},{14,8},{16,22},{18,... | collective-permute-start | bytes 393224 | tf_op jit(solution)/shard_map/ppermute | solution.py:432
  54.5 9.1 %collective-permute-start.75 = (bf16[8,32,256]{2,1,0:T(8,128)(2,1)}, bf16[8,32,256]{2,1,0:T(8,128)(2,1)S(1)}, u32[]{:S(2)}, u32[]{:S(2)}) collective-permute-start(bf16[8,32,256]{2,1,0:T(8,128)(2,1)} %get-tuple-element.281), channel_id=1, source_target_pairs={{0,8},{2,10},{4,12},{6,14},{8,0},{10,2},{12,4},{14,6},{16,24},{18,... | collective-permute-start | bytes 393224 | tf_op jit(solution)/shard_map/ppermute | solution.py:432
  58.1 6.6 %collective-permute-start.76 = (bf16[8,32,256]{2,1,0:T(8,128)(2,1)}, bf16[8,32,256]{2,1,0:T(8,128)(2,1)S(1)}, u32[]{:S(2)}, u32[]{:S(2)}) collective-permute-start(bf16[8,32,256]{2,1,0:T(8,128)(2,1)} %get-tuple-element.282), channel_id=1, source_target_pairs={{0,4},{2,6},{4,0},{6,2},{8,12},{10,14},{12,8},{14,10},{16,20},{18,... | collective-permute-start | bytes 393224 | tf_op jit(solution)/shard_map/ppermute | solution.py:432
  61.3 5.2 %collective-permute-start.77 = (bf16[8,32,256]{2,1,0:T(8,128)(2,1)}, bf16[8,32,256]{2,1,0:T(8,128)(2,1)S(1)}, u32[]{:S(2)}, u32[]{:S(2)}) collective-permute-start(bf16[8,32,256]{2,1,0:T(8,128)(2,1)} %get-tuple-element.283), channel_id=1, source_target_pairs={{0,2},{2,0},{4,6},{6,4},{8,10},{10,8},{12,14},{14,12},{16,18},{18,... | collective-permute-start | bytes 393224 | tf_op jit(solution)/shard_map/ppermute | solution.py:432
  68.0 2.7 %collective-permute-start.78 = (f32[1024,256]{1,0:T(8,128)S(1)}, f32[1024,256]{1,0:T(8,128)S(1)}, u32[]{:S(2)}, u32[]{:S(2)}) collective-permute-start(f32[1024,256]{1,0:T(8,128)S(1)} %block_products.1.mine_ref), channel_id=1, source_target_pairs={{0,1},{1,0},{2,3},{3,2},{4,5},{5,4},{6,7},{7,6},{8,9},{9,8},{10,11... | collective-permute-start | bytes 3145736 | tf_op jit(solution)/shard_map/ppermute | solution.py:482
